TPU v7x, 32 devices: a whole 2x2x4 slice. The times are simulated.
32 devices in a mesh: groups: 2 (over x), seq: 16 (over z, y, core).
Axes of the slice: x: 2, y: 2, z: 4, core: 2. Of those that a mesh axis runs over, the one named last changes fastest.
Arguments:
- frames: bfloat16 [4096, 1024], P(('groups', 'seq')), parts along dimension 0, may hold values from -6 to 6
- conv_kernel: bfloat16 [31, 1024], replicated, may hold values from -1 to 1
- norm_gain: bfloat16 [1024], replicated, may hold values from 0.25 to 1.75
- router: bfloat16 [1024, 8], replicated, may hold values from -0.1875 to 0.1875
- expert_in: bfloat16 [16, 1024, 1024], P('seq'), may hold values from -0.1875 to 0.1875
- expert_out: bfloat16 [16, 1024, 1024], P('seq'), may hold values from -0.125 to 0.125
- expert_ids: int32 [4096, 2], P(('groups', 'seq')), parts along dimension 0, may hold values from 0 to 7, all different within a row; in each aligned block of 128 rows (0 to 127, 128 to 255, ...) at most 64 rows name the same one
- out_grad: bfloat16 [4096, 1024], P(('groups', 'seq')), parts along dimension 0, may hold values from -6 to 6
Outputs:
- block_out: bfloat16 [4096, 1024], P(('groups', 'seq')), parts along dimension 0
- frames_grad: bfloat16 [4096, 1024], P(('groups', 'seq')), parts along dimension 0
- kernel_grad: float32 [62, 1024], P('groups'), parts along dimension 0
- gain_grad: float32 [2048], P('groups'), parts along dimension 0
- router_grad: float32 [2048, 8], P('groups'), parts along dimension 0
- expert_in_grad: bfloat16 [32, 1024, 1024], P(('groups', 'seq')), parts along dimension 0
- expert_out_grad: bfloat16 [32, 1024, 1024], P(('groups', 'seq')), parts along dimension 0
There are 2 independent parts, one for each index of `groups`. A program takes and returns all parts, laid end to end along the dimension named above; an argument that names none is the same for every part. Nothing has to cross between parts.
Inputs may be any that keep to these rules, and one draw needn't show every extreme that they name: `expert_ids`: within the rows of one device (128 frames), no expert is named more than 64 times, a bound that some block reaches; a frame's two experts differ.
All inputs are finite; a program needn't handle non-finite values.
Results may differ from a plain program's by a relative error of at most 0.0079.
Values may be sent and summed in bfloat16 or wider, within the bound.
No kernel may reach another device: no remote copies, remote signals or barrier semaphores. Data moves between devices by JAX's collectives and lax.ppermute only.
A program may use at most 128 MiB of HBM per device.

v0:
```python
import functools

import jax
import jax.numpy as jnp
from jax import lax
from jax.experimental import pallas as pl
from jax.experimental.pallas import tpu as pltpu
from jax.sharding import PartitionSpec as P

KSIZE = 31
RIM = 16
LANES = 128
NORM_EPS = 1e-05
F32 = jnp.float32
BF16 = jnp.bfloat16
LAST = (((1,), (1,)), ((), ()))
FIRST = (((0,), (0,)), ((), ()))
VMEM_LIMIT = 32 * 1024 * 1024


def dot(a, b):
    return jnp.dot(a, b, preferred_element_type=F32)


def dot_last(a, b):
    return lax.dot_general(a, b, LAST, preferred_element_type=F32)


def dot_first(a, b):
    return lax.dot_general(a, b, FIRST, preferred_element_type=F32)


def slope_of(values):
    logistic = jax.nn.sigmoid(values)
    return logistic * (1.0 + values * (1.0 - logistic))


def kernel_call(body, out_shape, scratch=(), flops=0, moved=0):
    return pl.pallas_call(
        body,
        out_shape=out_shape,
        scratch_shapes=list(scratch),
        compiler_params=pltpu.CompilerParams(vmem_limit_bytes=VMEM_LIMIT),
        cost_estimate=pl.CostEstimate(flops=flops, bytes_accessed=moved, transcendentals=0),
    )


def choices(ids, experts):
    lane = lax.broadcasted_iota(jnp.int32, (ids.shape[0], experts), 1)
    return (ids[:, 0:1] == lane).astype(F32), (ids[:, 1:2] == lane).astype(F32)


def placements(ids, experts, capacity):
    count = ids.shape[0]
    first, second = choices(ids, experts)
    named = (first + second).astype(BF16)
    row = lax.broadcasted_iota(jnp.int32, (count, count), 0)
    col = lax.broadcasted_iota(jnp.int32, (count, count), 1)
    before = dot((col < row).astype(BF16), named)
    start = lax.broadcasted_iota(jnp.int32, (count, experts), 1).astype(F32) * capacity
    place = before + start
    slot = lax.broadcasted_iota(jnp.int32, (count, experts * capacity), 1)
    picks = []
    for chosen in (first, second):
        at = jnp.sum(chosen * place, axis=1, keepdims=True).astype(jnp.int32)
        picks.append((slot == at).astype(BF16))
    return picks


def pack_kernel(experts, capacity, ids_ref, rows_ref, out_ref):
    first, second = placements(ids_ref[...], experts, capacity)
    out_ref[...] = dot_first(first + second, rows_ref[...]).astype(BF16)


def shifted(pad_ref, lanes, count):
    for rest in range(8):
        block = pad_ref[pl.ds(rest, count + 24), lanes]
        for turn in range(4):
            offset = 8 * turn + rest
            if 1 <= offset <= KSIZE:
                yield offset, block[8 * turn : 8 * turn + count]


def fill_padded(pad_ref, left_ref, mid_ref, right_ref):
    count = mid_ref.shape[0]
    pad_ref[0:RIM, :] = left_ref[...].astype(F32)
    pad_ref[RIM : RIM + count, :] = mid_ref[...].astype(F32)
    pad_ref[RIM + count : 2 * RIM + count, :] = right_ref[...].astype(F32)


def lane_loop(width, body):
    @pl.loop(0, width // LANES)
    def _(step):
        body(pl.ds(pl.multiple_of(step * LANES, LANES), LANES))


def front_kernel(
    experts, capacity, frames_ref, left_ref, right_ref, taps_ref, gain_ref, router_ref, ids_ref,
    conv_ref, mixed_ref, inverse_ref, normed_ref, gates_ref, payload_ref, pad_ref, taps32_ref, square_ref,
):
    count, width = frames_ref.shape
    fill_padded(pad_ref, left_ref, frames_ref, right_ref)
    taps32_ref[...] = taps_ref[...].astype(F32)
    square_ref[...] = jnp.zeros_like(square_ref)

    def conv(lanes):
        total = jnp.zeros((count, LANES), F32)
        for offset, rows in shifted(pad_ref, lanes, count):
            total = total + taps32_ref[offset - 1 : offset, lanes] * rows
        conv_ref[:, lanes] = total
        mixed = pad_ref[RIM : RIM + count, lanes] + total * jax.nn.sigmoid(total)
        mixed_ref[:, lanes] = mixed
        square_ref[...] += mixed * mixed

    lane_loop(width, conv)
    mean = jnp.sum(square_ref[...], axis=1, keepdims=True) / width
    inverse = lax.rsqrt(mean + NORM_EPS)
    inverse_ref[...] = inverse
    normed = (mixed_ref[...] * inverse * gain_ref[...].astype(F32)).astype(BF16)
    normed_ref[...] = normed
    gates_ref[...] = jax.nn.sigmoid(dot(normed, router_ref[...]))
    first, second = placements(ids_ref[...], experts, capacity)
    payload_ref[...] = dot_first(first + second, normed).astype(BF16)


def result_kernel(
    experts, capacity, rows_ref, ids_ref, mixed_ref, grad_ref, normed_ref, gates_ref,
    out_ref, logits_ref, router_ref,
):
    ids = ids_ref[...]
    gates = gates_ref[...]
    upstream = grad_ref[...].astype(F32)
    total = mixed_ref[...]
    added = jnp.zeros_like(total)
    grad_logits = jnp.zeros(gates.shape, F32)
    for pick, chosen in zip(placements(ids, experts, capacity), choices(ids, experts)):
        result = dot(pick, rows_ref[...])
        gate = jnp.sum(chosen * gates, axis=1, keepdims=True)
        added = added + gate * result
        grad_gate = jnp.sum(upstream * result, axis=1, keepdims=True)
        grad_logits = grad_logits + chosen * (grad_gate * gate * (1.0 - gate))
    out_ref[...] = (total + added).astype(BF16)
    grad_logits = grad_logits.astype(BF16)
    logits_ref[...] = grad_logits
    router_ref[...] = dot_first(grad_logits, normed_ref[...])


def back_kernel(
    experts, capacity, rows_ref, ids_ref, logits_ref, router_ref, mixed_ref, inverse_ref, conv_ref, grad_ref, gain_ref,
    mixed_grad_ref, conv_grad_ref, head_ref, tail_ref, gain_out_ref,
):
    count, width = mixed_ref.shape
    first, second = placements(ids_ref[...], experts, capacity)
    grad_normed = dot(first + second, rows_ref[...]) + dot_last(logits_ref[...], router_ref[...])
    mixed = mixed_ref[...]
    inverse = inverse_ref[...]
    gain_out_ref[...] = jnp.sum(grad_normed * mixed * inverse, axis=0, keepdims=True)
    scaled = grad_normed * gain_ref[...].astype(F32)
    mean = jnp.sum(scaled * mixed, axis=1, keepdims=True) / width
    mixed_grad = grad_ref[...].astype(F32) + inverse * scaled - mixed * (inverse * inverse * inverse * mean)
    mixed_grad_ref[...] = mixed_grad
    conv_grad = (mixed_grad * slope_of(conv_ref[...])).astype(BF16)
    conv_grad_ref[...] = conv_grad
    head_ref[...] = conv_grad[0:RIM]
    tail_ref[...] = conv_grad[count - RIM : count]


def taps_kernel(frames_ref, left_ref, right_ref, conv_grad_ref, gain_ref, router_ref, out_ref, pad_ref):
    count, width = frames_ref.shape
    fill_padded(pad_ref, left_ref, frames_ref, right_ref)

    def reduce(lanes):
        grad = conv_grad_ref[:, lanes].astype(F32)
        for offset, rows in shifted(pad_ref, lanes, count):
            out_ref[offset - 1 : offset, lanes] = jnp.sum(grad * rows, axis=0, keepdims=True)

    lane_loop(width, reduce)
    out_ref[KSIZE : KSIZE + 1, :] = gain_ref[...]
    out_ref[KSIZE + 1 :, :] = router_ref[...]


def frames_kernel(mixed_grad_ref, conv_grad_ref, left_ref, right_ref, taps_ref, out_ref, pad_ref, taps32_ref):
    count, width = mixed_grad_ref.shape
    fill_padded(pad_ref, left_ref, conv_grad_ref, right_ref)
    taps32_ref[...] = taps_ref[...].astype(F32)

    def conv(lanes):
        total = mixed_grad_ref[:, lanes]
        for offset, rows in shifted(pad_ref, lanes, count):
            total = total + taps32_ref[KSIZE - offset : KSIZE - offset + 1, lanes] * rows
        out_ref[:, lanes] = total.astype(BF16)

    lane_loop(width, conv)


def rims(head, tail, count):
    ends = count - 1
    left = lax.ppermute(tail, "seq", [(i, i + 1) for i in range(ends)])
    right = lax.ppermute(head, "seq", [(i + 1, i) for i in range(ends)])
    return left, right


def swap(values, count, bit):
    return lax.ppermute(values, "seq", [(i, i ^ bit) for i in range(count)])


def exchange(payload, count):
    groups = [[2 * chip + core for chip in range(count // 2)] for core in range(2)]
    return lax.all_to_all(payload, "seq", 0, 0, axis_index_groups=groups, tiled=True)


def per_device(frames, conv_kernel, norm_gain, router, expert_in, expert_out, expert_ids, out_grad):
    count, width = frames.shape
    devices = lax.axis_size("seq")
    experts = devices // 2
    capacity = 8 * count // devices
    slots = experts * capacity
    gain = norm_gain.reshape(1, width)
    taps = conv_kernel
    shape = jax.ShapeDtypeStruct
    pad = pltpu.VMEM((count + 2 * RIM, width), F32)
    taps32 = pltpu.VMEM((KSIZE, width), F32)

    grad_payload = kernel_call(
        functools.partial(pack_kernel, experts, capacity), shape((slots, width), BF16), moved=1 << 21
    )(expert_ids, out_grad)
    grads = exchange(grad_payload, devices)
    left, right = rims(frames[0:RIM], frames[count - RIM : count], devices)
    weight_in, weight_out = expert_in[0], expert_out[0]
    other_out = swap(weight_out, devices, 1)
    other_in = swap(weight_in, devices, 1)

    conv_out, mixed, inverse, normed, gates, payload = kernel_call(
        functools.partial(front_kernel, experts, capacity),
        (
            shape((count, width), F32),
            shape((count, width), F32),
            shape((count, 1), F32),
            shape((count, width), BF16),
            shape((count, experts), F32),
            shape((slots, width), BF16),
        ),
        (pad, taps32, pltpu.VMEM((count, LANES), F32)),
        moved=1 << 22,
    )(frames, left, right, taps, gain, router, expert_ids)
    rows = exchange(payload, devices)

    hidden = [dot_last(grads, weight) for weight in (weight_out, other_out)]
    mine = (jnp.arange(experts, dtype=jnp.int32) == lax.axis_index("seq") // 2).astype(F32)
    gate = jax.nn.sigmoid(jnp.sum(dot(rows, router) * mine[None, :], axis=1, keepdims=True))
    grad_rows = (gate * grads.astype(F32)).astype(BF16)
    pre_act = [dot(rows, weight) for weight in (weight_in, other_in)]
    active = [jax.nn.silu(values).astype(BF16) for values in pre_act]
    part_out = (dot(active[0], weight_out) + dot(active[1], other_out)).astype(BF16)
    results = exchange(part_out, devices)
    pre_grad = [(gate * h * slope_of(values)).astype(BF16) for h, values in zip(hidden, pre_act)]
    part_in = (dot_last(pre_grad[0], weight_in) + dot_last(pre_grad[1], other_in)).astype(BF16)
    backs = exchange(part_in, devices)
    far_rows, far_grads, far_active, far_pre = [
        swap(values, devices, 1) for values in (rows, grad_rows, active[1], pre_grad[1])
    ]
    expert_out_grad = (dot_first(active[0], grad_rows) + dot_first(far_active, far_grads)).astype(BF16)
    expert_in_grad = (dot_first(rows, pre_grad[0]) + dot_first(far_rows, far_pre)).astype(BF16)

    block_out, grad_logits, router_local = kernel_call(
        functools.partial(result_kernel, experts, capacity),
        (shape((count, width), BF16), shape((count, experts), BF16), shape((experts, width), F32)),
        moved=1 << 22,
    )(results, expert_ids, mixed, out_grad, normed, gates)
    mixed_grad, conv_grad, head, tail, gain_local = kernel_call(
        functools.partial(back_kernel, experts, capacity),
        (
            shape((count, width), F32),
            shape((count, width), BF16),
            shape((RIM, width), BF16),
            shape((RIM, width), BF16),
            shape((1, width), F32),
        ),
        moved=1 << 22,
    )(backs, expert_ids, grad_logits, router, mixed, inverse, conv_out, out_grad, gain)
    grad_left, grad_right = rims(head, tail, devices)
    local = kernel_call(
        taps_kernel, shape((KSIZE + 1 + experts, width), F32), (pad,), moved=1 << 20
    )(frames, left, right, conv_grad, gain_local, router_local)
    frames_grad = kernel_call(
        frames_kernel, shape((count, width), BF16), (pad, taps32), moved=1 << 20
    )(mixed_grad, conv_grad, grad_left, grad_right, taps)
    bit = 1
    while bit < devices:
        local = local + swap(local, devices, bit)
        bit *= 2
    return (
        block_out,
        frames_grad,
        local[0:KSIZE],
        local[KSIZE],
        local[KSIZE + 1 :].T,
        expert_in_grad[None],
        expert_out_grad[None],
    )


def solution(mesh):
    in_specs = (
        P(("groups", "seq"), None),
        P(),
        P(),
        P(),
        P("seq", None, None),
        P("seq", None, None),
        P(("groups", "seq"), None),
        P(("groups", "seq"), None),
    )
    out_specs = (
        P(("groups", "seq"), None),
        P(("groups", "seq"), None),
        P("groups", None),
        P("groups"),
        P("groups", None),
        P(("groups", "seq"), None, None),
        P(("groups", "seq"), None, None),
    )
    return jax.shard_map(
        per_device, mesh=mesh, in_specs=in_specs, out_specs=out_specs, check_vma=False
    )
```

profile of v0, /device:TPU:0, one launch (start us, length us, event | category | flops | bytes accessed | tf_op | source)
XLA Modules:
  0.0 178.8 jit_solution(8916768423924789964)
XLA Ops:
  1.5 2.3 %collective-permute-start = (bf16[16,1024]{1,0:T(8,128)(2,1)S(1)}, bf16[16,1024]{1,0:T(8,128)(2,1)S(1)}, u32[]{:S(2)}, u32[]{:S(2)}) collective-permute-start(bf16[16,1024]{1,0:T(8,128)(2,1)S(1)} %get-tuple-element.36), channel_id=1, source_target_pairs={{0,1},{1,2},{2,3},{3,4},{4,5},{5,6},{6,7},{7,8},{8,9},{9,10},{10,1... | collective-permute-start | bytes 98312 | tf_op jit(solution)/shard_map/ppermute | solution.py:198
  10.8 4.7 %shard_map.135 = (f32[128,1024]{1,0:T(8,128)S(1)}, f32[128,1024]{1,0:T(8,128)S(1)}, f32[128,1]{1,0:T(8,128)S(1)}, bf16[128,1024]{1,0:T(8,128)(2,1)S(1)}, f32[128...) custom-call(bf16[128,1024]{1,0:T(8,128)(2,1)S(1)} %copy-done.1, bf16[16,1024]{1,0:T(8,128)(2,1)S(1)} %collective-permute-done.left_ref, ...), custom_call_target="tpu_custom_call" | custom-call | bytes 4194304 | tf_op jit(solution)/shard_map/pallas_call | solution.py:233
  18.3 7.7 %all-to-all-start = ((bf16[8,64,1024]{2,1,0:T(8,128)(2,1)}), bf16[8,64,1024]{2,1,0:T(8,128)(2,1)S(1)}, u32[]{:S(2)}, u32[]{:S(2)}) async-start(bf16[8,64,1024]{2,1,0:T(8,128)(2,1)} %bitcast), calls=%async_computation | async-start | bytes 2097152 | tf_op jit(solution)/shard_map/all_to_all | solution.py:209
  26.5 1.8 shard_map.137
  28.3 24.4 %all-to-all-done = bf16[8,64,1024]{2,1,0:T(8,128)(2,1)S(1)} async-done(((bf16[8,64,1024]{2,1,0:T(8,128)(2,1)}), bf16[8,64,1024]{2,1,0:T(8,128)(2,1)S(1)}, u32[]{:S(2)}, u32[]{:S(2)}) %all-to-all-start) | async-done | bytes 1048608 | tf_op jit(solution)/shard_map/all_to_all | solution.py:209
  52.6 3.6 %all-to-all-start.2 = ((bf16[8,64,1024]{2,1,0:T(8,128)(2,1)}), bf16[8,64,1024]{2,1,0:T(8,128)(2,1)S(1)}, u32[]{:S(2)}, u32[]{:S(2)}) async-start(bf16[8,64,1024]{2,1,0:T(8,128)(2,1)} %bitcast.6), calls=%async_computation.2 | async-start | bytes 2097152 | tf_op jit(solution)/shard_map/all_to_all | solution.py:209
  56.3 3.0 %fusion.8 = f32[512,1024]{1,0:T(8,128)S(1)} fusion(bf16[512,1024]{1,0:T(8,128)(2,1)S(1)} %bitcast.48, bf16[1,1024,1024]{2,1,0:T(8,128)(2,1)} %param.12), kind=kOutput, calls=%fused_computation.23 | convolution fusion | flops 1073741824 | bytes 5242880 | tf_op jit(solution)/shard_map/dot_general | solution.py:22
  61.0 4.7 %multiply_convert_fusion.3 = (bf16[512,1024]{1,0:T(8,128)(2,1)}, f32[512,1024]{1,0:T(8,128)}) fusion(bf16[512,1024]{1,0:T(8,128)(2,1)S(1)} %bitcast.50, bf16[1024,1024]{1,0:T(8,128)(2,1)} %collective-permute-done.2), kind=kOutput, calls=%fused_computation.7 | convolution fusion | flops 1076363264 | bytes 6291456 | tf_op jit(solution)/shard_map/dot_general | solution.py:22
  65.8 4.2 %add_convert_fusion.3 = bf16[512,1024]{1,0:T(8,128)(2,1)} fusion(f32[512,1024]{1,0:T(8,128)S(1)} %fusion.4, bf16[512,1024]{1,0:T(8,128)(2,1)} %get-tuple-element.37, bf16[1024,1024]{1,0:T(8,128)(2,1)} %collective-permute-done.3), kind=kOutput, calls=%fused_computation.6 | convolution fusion | flops 1074790400 | bytes 6291456 | tf_op jit(solution)/shard_map/dot_general | solution.py:22
  69.9 12.3 %all-to-all-done.2 = bf16[8,64,1024]{2,1,0:T(8,128)(2,1)S(1)} async-done(((bf16[8,64,1024]{2,1,0:T(8,128)(2,1)}), bf16[8,64,1024]{2,1,0:T(8,128)(2,1)S(1)}, u32[]{:S(2)}, u32[]{:S(2)}) %all-to-all-start.2) | async-done | bytes 1048608 | tf_op jit(solution)/shard_map/all_to_all | solution.py:209
  82.2 3.7 %all-to-all-start.1 = ((bf16[8,64,1024]{2,1,0:T(8,128)(2,1)}), bf16[8,64,1024]{2,1,0:T(8,128)(2,1)S(1)}, u32[]{:S(2)}, u32[]{:S(2)}) async-start(bf16[8,64,1024]{2,1,0:T(8,128)(2,1)} %bitcast.56), calls=%async_computation.1 | async-start | bytes 2097152 | tf_op jit(solution)/shard_map/all_to_all | solution.py:209
  86.0 4.0 %multiply_convert_fusion.2 = bf16[512,1024]{1,0:T(8,128)(2,1)S(1)} fusion(f32[512,1024]{1,0:T(8,128)} %copy-done.26, bf16[512,1024]{1,0:T(8,128)(2,1)S(1)} %bitcast.53, f32[512]{0:T(512)S(1)} %add_divide_fusion.2, bf16[1,1024,1024]{2,1,0:T(8,128)(2,1)} %param.13), kind=kOutput, calls=%fused_computation.5 | convolution fusion | flops 1078984704 | bytes 6293504 | tf_op jit(solution)/shard_map/dot_general | solution.py:26
  92.0 3.3 %multiply_convert_fusion.1 = bf16[512,1024]{1,0:T(8,128)(2,1)S(1)} fusion(f32[512,1024]{1,0:T(8,128)S(1)} %copy-done.28, bf16[512,1024]{1,0:T(8,128)(2,1)S(1)} %bitcast.54, bf16[1024,1024]{1,0:T(8,128)(2,1)} %collective-permute-done.3, f32[512]{0:T(512)S(1)} %add_divide_fusion.2), kind=kOutput, calls=%fused_computation.4 | convolution fusion | flops 1078984704 | bytes 6293504 | tf_op jit(solution)/shard_map/dot_general | solution.py:26
  96.3 3.9 %add_convert_fusion.2 = bf16[512,1024]{1,0:T(8,128)(2,1)} fusion(f32[512,1024]{1,0:T(8,128)S(1)} %fusion.6, bf16[512,1024]{1,0:T(8,128)(2,1)S(1)} %multiply_convert_fusion.1, bf16[1024,1024]{1,0:T(8,128)(2,1)} %collective-permute-done.2), kind=kOutput, calls=%fused_computation.3 | convolution fusion | flops 1074790400 | bytes 6291456 | tf_op jit(solution)/shard_map/dot_general | solution.py:26
  100.2 11.6 %all-to-all-done.1 = bf16[8,64,1024]{2,1,0:T(8,128)(2,1)S(1)} async-done(((bf16[8,64,1024]{2,1,0:T(8,128)(2,1)}), bf16[8,64,1024]{2,1,0:T(8,128)(2,1)S(1)}, u32[]{:S(2)}, u32[]{:S(2)}) %all-to-all-start.1) | async-done | bytes 1048608 | tf_op jit(solution)/shard_map/all_to_all | solution.py:209
  111.8 3.6 %all-to-all-start.3 = ((bf16[8,64,1024]{2,1,0:T(8,128)(2,1)}), bf16[8,64,1024]{2,1,0:T(8,128)(2,1)S(1)}, u32[]{:S(2)}, u32[]{:S(2)}) async-start(bf16[8,64,1024]{2,1,0:T(8,128)(2,1)} %bitcast.55), calls=%async_computation.3 | async-start | bytes 2097152 | tf_op jit(solution)/shard_map/all_to_all | solution.py:209
  116.1 2.4 %multiply_convert_fusion = bf16[512,1024]{1,0:T(8,128)(2,1)} fusion(f32[512]{0:T(512)S(1)} %add_divide_fusion.2, bf16[8,64,1024]{2,1,0:T(8,128)(2,1)} %copy-done.19), kind=kLoop, calls=%fused_computation.2 | loop fusion | flops 1572864 | bytes 2099200 | tf_op jit(solution)/shard_map/convert_element_type | solution.py:251
  121.8 19.6 %all-to-all-done.3 = bf16[8,64,1024]{2,1,0:T(8,128)(2,1)S(1)} async-done(((bf16[8,64,1024]{2,1,0:T(8,128)(2,1)}), bf16[8,64,1024]{2,1,0:T(8,128)(2,1)S(1)}, u32[]{:S(2)}, u32[]{:S(2)}) %all-to-all-start.3) | async-done | bytes 1048608 | tf_op jit(solution)/shard_map/all_to_all | solution.py:209
  146.9 2.7 %fusion.10 = f32[1024,1024]{1,0:T(8,128)S(1)} fusion(bf16[512,1024]{1,0:T(8,128)(2,1)} %multiply_convert_fusion, f32[512,1024]{1,0:T(8,128)S(1)} %copy-done.27), kind=kOutput, calls=%fused_computation.25 | convolution fusion | flops 1076363264 | bytes 7340032 | tf_op jit(solution)/shard_map/dot_general | solution.py:30
  152.4 3.7 %collective-permute-done.7 = f32[40,1024]{1,0:T(8,128)S(1)} collective-permute-done((f32[40,1024]{1,0:T(8,128)S(1)}, f32[40,1024]{1,0:T(8,128)S(1)}, u32[]{:S(2)}, u32[]{:S(2)}) %collective-permute-start.7) | collective-permute-done | bytes 163872 | tf_op jit(solution)/shard_map/ppermute | solution.py:204
  156.3 4.2 %fusion = bf16[1,1024,1024]{2,1,0:T(8,128)(2,1)} fusion(f32[1024,1024]{1,0:T(8,128)S(1)} %fusion.12, bf16[512,1024]{1,0:T(8,128)(2,1)} %collective-permute-done.10, bf16[512,1024]{1,0:T(8,128)(2,1)} %collective-permute-done.11), kind=kOutput, calls=%fused_computation.11 | convolution fusion | flops 1075838976 | bytes 8388608 | tf_op jit(solution)/shard_map/dot_general | solution.py:30
  163.3 5.9 %collective-permute-start.9 = (f32[40,1024]{1,0:T(8,128)S(1)}, f32[40,1024]{1,0:T(8,128)S(1)}, u32[]{:S(2)}, u32[]{:S(2)}) collective-permute-start(f32[40,1024]{1,0:T(8,128)S(1)} %add.57), channel_id=1, source_target_pairs={{0,8},{1,9},{2,10},{3,11},{4,12},{5,13},{6,14},{7,15},{8,0},{9,1},... | collective-permute-start | bytes 491528 | tf_op jit(solution)/shard_map/ppermute | solution.py:204
  169.2 4.2 %fusion.1 = bf16[1,1024,1024]{2,1,0:T(8,128)(2,1)} fusion(f32[1024,1024]{1,0:T(8,128)S(1)} %fusion.10, bf16[512,1024]{1,0:T(8,128)(2,1)} %collective-permute-done.12, bf16[512,1024]{1,0:T(8,128)(2,1)} %collective-permute-done.13), kind=kOutput, calls=%fused_computation.12 | convolution fusion | flops 1075838976 | bytes 8388608 | tf_op jit(solution)/shard_map/dot_general | solution.py:30
  173.5 3.4 %shard_map.139 = bf16[128,1024]{1,0:T(8,128)(2,1)} custom-call(f32[128,1024]{1,0:T(8,128)S(1)} %get-tuple-element.29.mixed_grad_ref, bf16[128,1024]{1,0:T(8,128)(2,1)S(1)} %get-tuple-element.30.conv_grad_ref, bf16[16,1024]{1,0:T(8,128)(2,1)S(1)} %collective-permute-done.4.left_ref, bf16[16,1024]{1,0:T(8,128)(2,1)S(1)} %collective-permute-done.5.right_ref, ...), custom_call_target="tpu_custom_call" | custom-call | bytes 1048576 | tf_op jit(solution)/shard_map/pallas_call | solution.py:285
  (103 shorter events, 32.6 us)
Async XLA Ops:
  0.6 25.8 %copy-start = (bf16[128,1024]{1,0:T(8,128)(2,1)S(1)}, bf16[128,1024]{1,0:T(8,128)(2,1)}, u32[]{:S(2)}) copy-start(bf16[128,1024]{1,0:T(8,128)(2,1)} %grad_ref.3) | copy-start | bytes 786436
  1.5 6.0 %collective-permute-start = (bf16[16,1024]{1,0:T(8,128)(2,1)S(1)}, bf16[16,1024]{1,0:T(8,128)(2,1)S(1)}, u32[]{:S(2)}, u32[]{:S(2)}) collective-permute-start(bf16[16,1024]{1,0:T(8,128)(2,1)S(1)} %get-tuple-element.36), channel_id=1, source_target_pairs={{0,1},{1,2},{2,3},{3,4},{4,5},{5,6},{6,7},{7,8},{8,9},{9,10},{10,1... | collective-permute-start | bytes 98312 | tf_op jit(solution)/shard_map/ppermute | solution.py:198
  3.8 5.2 %collective-permute-start.1 = (bf16[16,1024]{1,0:T(8,128)(2,1)S(1)}, bf16[16,1024]{1,0:T(8,128)(2,1)S(1)}, u32[]{:S(2)}, u32[]{:S(2)}) collective-permute-start(bf16[16,1024]{1,0:T(8,128)(2,1)S(1)} %get-tuple-element.35), channel_id=1, source_target_pairs={{1,0},{2,1},{3,2},{4,3},{5,4},{6,5},{7,6},{8,7},{9,8},{10,9},{11,1... | collective-permute-start | bytes 98312 | tf_op jit(solution)/shard_map/ppermute | solution.py:199
  18.3 34.3 %all-to-all-start = ((bf16[8,64,1024]{2,1,0:T(8,128)(2,1)}), bf16[8,64,1024]{2,1,0:T(8,128)(2,1)S(1)}, u32[]{:S(2)}, u32[]{:S(2)}) async-start(bf16[8,64,1024]{2,1,0:T(8,128)(2,1)} %bitcast), calls=%async_computation | async-start | bytes 2097152 | tf_op jit(solution)/shard_map/all_to_all | solution.py:209
  26.0 35.1 %collective-permute-start.2 = (bf16[1024,1024]{1,0:T(8,128)(2,1)}, bf16[1024,1024]{1,0:T(8,128)(2,1)}, u32[]{:S(2)}, u32[]{:S(2)}) collective-permute-start(bf16[1024,1024]{1,0:T(8,128)(2,1)} %bitcast.59), channel_id=1, source_target_pairs={{0,1},{1,0},{2,3},{3,2},{4,5},{5,4},{6,7},{7,6},{8,9},{9,8},{10,11... | collective-permute-start | bytes 6291464 | tf_op jit(solution)/shard_map/ppermute | solution.py:204
  26.4 39.4 %collective-permute-start.3 = (bf16[1024,1024]{1,0:T(8,128)(2,1)}, bf16[1024,1024]{1,0:T(8,128)(2,1)}, u32[]{:S(2)}, u32[]{:S(2)}) collective-permute-start(bf16[1024,1024]{1,0:T(8,128)(2,1)} %bitcast.58), channel_id=1, source_target_pairs={{0,1},{1,0},{2,3},{3,2},{4,5},{5,4},{6,7},{7,6},{8,9},{9,8},{10,11... | collective-permute-start | bytes 6291464 | tf_op jit(solution)/shard_map/ppermute | solution.py:204
  52.6 8.4 %copy-start.17 = (bf16[8,64,1024]{2,1,0:T(8,128)(2,1)}, bf16[8,64,1024]{2,1,0:T(8,128)(2,1)S(1)}, u32[]{:S(2)}) copy-start(bf16[8,64,1024]{2,1,0:T(8,128)(2,1)S(1)} %all-to-all-done) | copy-start | bytes 3145732
  52.6 29.6 %all-to-all-start.2 = ((bf16[8,64,1024]{2,1,0:T(8,128)(2,1)}), bf16[8,64,1024]{2,1,0:T(8,128)(2,1)S(1)}, u32[]{:S(2)}, u32[]{:S(2)}) async-start(bf16[8,64,1024]{2,1,0:T(8,128)(2,1)} %bitcast.6), calls=%async_computation.2 | async-start | bytes 2097152 | tf_op jit(solution)/shard_map/all_to_all | solution.py:209
  82.2 9.1 %copy-start.19 = (bf16[8,64,1024]{2,1,0:T(8,128)(2,1)}, bf16[8,64,1024]{2,1,0:T(8,128)(2,1)S(1)}, u32[]{:S(2)}) copy-start(bf16[8,64,1024]{2,1,0:T(8,128)(2,1)S(1)} %all-to-all-done.2) | copy-start | bytes 3145732
  82.2 29.6 %all-to-all-start.1 = ((bf16[8,64,1024]{2,1,0:T(8,128)(2,1)}), bf16[8,64,1024]{2,1,0:T(8,128)(2,1)S(1)}, u32[]{:S(2)}, u32[]{:S(2)}) async-start(bf16[8,64,1024]{2,1,0:T(8,128)(2,1)} %bitcast.56), calls=%async_computation.1 | async-start | bytes 2097152 | tf_op jit(solution)/shard_map/all_to_all | solution.py:209
  111.8 29.6 %all-to-all-start.3 = ((bf16[8,64,1024]{2,1,0:T(8,128)(2,1)}), bf16[8,64,1024]{2,1,0:T(8,128)(2,1)S(1)}, u32[]{:S(2)}, u32[]{:S(2)}) async-start(bf16[8,64,1024]{2,1,0:T(8,128)(2,1)} %bitcast.55), calls=%async_computation.3 | async-start | bytes 2097152 | tf_op jit(solution)/shard_map/all_to_all | solution.py:209
  115.5 40.8 %collective-permute-start.10 = (bf16[512,1024]{1,0:T(8,128)(2,1)}, bf16[512,1024]{1,0:T(8,128)(2,1)}, u32[]{:S(2)}, u32[]{:S(2)}) collective-permute-start(bf16[512,1024]{1,0:T(8,128)(2,1)} %bitcast.51), channel_id=1, source_target_pairs={{0,1},{1,0},{2,3},{3,2},{4,5},{5,4},{6,7},{7,6},{8,9},{9,8},{10,11... | collective-permute-start | bytes 3145736 | tf_op jit(solution)/shard_map/ppermute | solution.py:204
  115.6 40.7 %collective-permute-start.11 = (bf16[512,1024]{1,0:T(8,128)(2,1)}, bf16[512,1024]{1,0:T(8,128)(2,1)}, u32[]{:S(2)}, u32[]{:S(2)}) collective-permute-start(bf16[512,1024]{1,0:T(8,128)(2,1)} %copy-done.25), channel_id=1, source_target_pairs={{0,1},{1,0},{2,3},{3,2},{4,5},{5,4},{6,7},{7,6},{8,9},{9,8},{10,11... | collective-permute-start | bytes 3145736 | tf_op jit(solution)/shard_map/ppermute | solution.py:204
  118.5 50.7 %collective-permute-start.13 = (bf16[512,1024]{1,0:T(8,128)(2,1)}, bf16[512,1024]{1,0:T(8,128)(2,1)}, u32[]{:S(2)}, u32[]{:S(2)}) collective-permute-start(bf16[512,1024]{1,0:T(8,128)(2,1)} %multiply_convert_fusion), channel_id=1, source_target_pairs={{0,1},{1,0},{2,3},{3,2},{4,5},{5,4},{6,7},{7,6},{8,9},{9,8},{10,11... | collective-permute-start | bytes 3145736 | tf_op jit(solution)/shard_map/ppermute | solution.py:204
  118.6 50.6 %collective-permute-start.12 = (bf16[512,1024]{1,0:T(8,128)(2,1)}, bf16[512,1024]{1,0:T(8,128)(2,1)}, u32[]{:S(2)}, u32[]{:S(2)}) collective-permute-start(bf16[512,1024]{1,0:T(8,128)(2,1)} %get-tuple-element.37), channel_id=1, source_target_pairs={{0,1},{1,0},{2,3},{3,2},{4,5},{5,4},{6,7},{7,6},{8,9},{9,8},{10,11... | collective-permute-start | bytes 3145736 | tf_op jit(solution)/shard_map/ppermute | solution.py:204
  119.0 26.0 %copy-start.2 = (bf16[128,1024]{1,0:T(8,128)(2,1)S(1)}, bf16[128,1024]{1,0:T(8,128)(2,1)}, u32[]{:S(2)}) copy-start(bf16[128,1024]{1,0:T(8,128)(2,1)} %frames_ref.3) | copy-start | bytes 786436
  146.8 4.3 %copy-start.18 = (bf16[8,64,1024]{2,1,0:T(8,128)(2,1)S(1)}, bf16[8,64,1024]{2,1,0:T(8,128)(2,1)}, u32[]{:S(2)}) copy-start(bf16[8,64,1024]{2,1,0:T(8,128)(2,1)} %copy-done.17) | copy-start | bytes 3145732
  146.8 2.8 %collective-permute-start.6 = (f32[40,1024]{1,0:T(8,128)S(1)}, f32[40,1024]{1,0:T(8,128)S(1)}, u32[]{:S(2)}, u32[]{:S(2)}) collective-permute-start(f32[40,1024]{1,0:T(8,128)S(1)} %shard_map.140), channel_id=1, source_target_pairs={{0,1},{1,0},{2,3},{3,2},{4,5},{5,4},{6,7},{7,6},{8,9},{9,8},{10,11... | collective-permute-start | bytes 491528 | tf_op jit(solution)/shard_map/ppermute | solution.py:204
  149.6 6.5 %collective-permute-start.7 = (f32[40,1024]{1,0:T(8,128)S(1)}, f32[40,1024]{1,0:T(8,128)S(1)}, u32[]{:S(2)}, u32[]{:S(2)}) collective-permute-start(f32[40,1024]{1,0:T(8,128)S(1)} %add.55), channel_id=1, source_target_pairs={{0,2},{1,3},{2,0},{3,1},{4,6},{5,7},{6,4},{7,5},{8,10},{9,11},{10,... | collective-permute-start | bytes 491528 | tf_op jit(solution)/shard_map/ppermute | solution.py:204
  156.2 7.1 %collective-permute-start.8 = (f32[40,1024]{1,0:T(8,128)S(1)}, f32[40,1024]{1,0:T(8,128)S(1)}, u32[]{:S(2)}, u32[]{:S(2)}) collective-permute-start(f32[40,1024]{1,0:T(8,128)S(1)} %add.56), channel_id=1, source_target_pairs={{0,4},{1,5},{2,6},{3,7},{4,0},{5,1},{6,2},{7,3},{8,12},{9,13},{10,... | collective-permute-start | bytes 491528 | tf_op jit(solution)/shard_map/ppermute | solution.py:204
  160.5 13.0 %collective-permute-start.4 = (bf16[16,1024]{1,0:T(8,128)(2,1)S(1)}, bf16[16,1024]{1,0:T(8,128)(2,1)S(1)}, u32[]{:S(2)}, u32[]{:S(2)}) collective-permute-start(bf16[16,1024]{1,0:T(8,128)(2,1)S(1)} %get-tuple-element.31), channel_id=1, source_target_pairs={{0,1},{1,2},{2,3},{3,4},{4,5},{5,6},{6,7},{7,8},{8,9},{9,10},{10,1... | collective-permute-start | bytes 98312 | tf_op jit(solution)/shard_map/ppermute | solution.py:198
  161.9 11.5 %collective-permute-start.5 = (bf16[16,1024]{1,0:T(8,128)(2,1)S(1)}, bf16[16,1024]{1,0:T(8,128)(2,1)S(1)}, u32[]{:S(2)}, u32[]{:S(2)}) collective-permute-start(bf16[16,1024]{1,0:T(8,128)(2,1)S(1)} %get-tuple-element.32), channel_id=1, source_target_pairs={{1,0},{2,1},{3,2},{4,3},{5,4},{6,5},{7,6},{8,7},{9,8},{10,9},{11,1... | collective-permute-start | bytes 98312 | tf_op jit(solution)/shard_map/ppermute | solution.py:199
  163.3 10.2 %copy-start.8 = (bf16[31,1024]{1,0:T(8,128)(2,1)S(1)}, bf16[31,1024]{1,0:T(8,128)(2,1)}, u32[]{:S(2)}) copy-start(bf16[31,1024]{1,0:T(8,128)(2,1)} %taps_ref.3) | copy-start | bytes 190468
  163.3 13.6 %collective-permute-start.9 = (f32[40,1024]{1,0:T(8,128)S(1)}, f32[40,1024]{1,0:T(8,128)S(1)}, u32[]{:S(2)}, u32[]{:S(2)}) collective-permute-start(f32[40,1024]{1,0:T(8,128)S(1)} %add.57), channel_id=1, source_target_pairs={{0,8},{1,9},{2,10},{3,11},{4,12},{5,13},{6,14},{7,15},{8,0},{9,1},... | collective-permute-start | bytes 491528 | tf_op jit(solution)/shard_map/ppermute | solution.py:204
  (23 other events, 40.2 us)
where the time goes:
time: 180 us; the launch traced here: 179 us
  waiting for transfers between devices  73.2 us (41%)
  matrix products  38.5 us (21%)
  starting transfers between devices  34.2 us (19%)
  local copies, waits for them, and re-layouts  15.2 us (8%)
  Pallas kernels  14.1 us (8%)
  other arithmetic  2.54 us (1%)
    all_to_all x4, waiting for transfers between devices, exchange(): lax.all_to_all(payload, 'seq', 0, 0, axis_index_groups=groups, tiled=True)  67.9 us
    all_to_all x4, starting transfers between devices, exchange(): lax.all_to_all(payload, 'seq', 0, 0, axis_index_groups=groups, tiled=True)  18.6 us
    dot_general x5, matrix products, dot(): return jnp.dot(a, b, preferred_element_type=F32)  13.6 us
    dot_general x4, matrix products, dot_last(): return lax.dot_general(a, b, LAST, preferred_element_type=F32)  12.5 us
    dot_general x4, matrix products, dot_first(): return lax.dot_general(a, b, FIRST, preferred_element_type=F32)  12.5 us
    unnamed x60, local copies, waits for them, and re-layouts  11.8 us
    ppermute x10, starting transfers between devices, swap(): return lax.ppermute(values, 'seq', [(i, i ^ bit) for i in range(count)])  9.16 us
    pallas_call x1, Pallas kernels, per_device(): kernel_call(functools.partial(front_kernel, experts, capacity), (shape((c...  4.67 us
  transfers between devices with their start and end apart: 18, of which 6 were waited for; matrix products, arithmetic and copies ran while one was open for 24% of the time, Pallas kernels for 5%

commit v1 on v0

v1 whole, which is shorter than its diff:
```python
import functools

import jax
import jax.numpy as jnp
from jax import lax
from jax.experimental import pallas as pl
from jax.experimental.pallas import tpu as pltpu
from jax.sharding import PartitionSpec as P

KSIZE = 31
RIM = 16
LANES = 128
CHUNK = 256
NORM_EPS = 1e-05
F32 = jnp.float32
BF16 = jnp.bfloat16
LAST = (((1,), (1,)), ((), ()))
FIRST = (((0,), (0,)), ((), ()))
SMALL = 12 * 1024 * 1024
LARGE = 28 * 1024 * 1024


def dot(a, b):
    return jnp.dot(a, b, preferred_element_type=F32)


def dot_last(a, b):
    return lax.dot_general(a, b, LAST, preferred_element_type=F32)


def dot_first(a, b):
    return lax.dot_general(a, b, FIRST, preferred_element_type=F32)


def slope_of(values):
    logistic = jax.nn.sigmoid(values)
    return logistic * (1.0 + values * (1.0 - logistic))


class Staged:
    def __init__(self, source, held, semaphore):
        self.held, self.copy, self.waited = held, pltpu.make_async_copy(source, held, semaphore), False
        self.shape = held.shape
        self.copy.start()

    def wait(self):
        if not self.waited:
            self.copy.wait()
        self.waited = True

    def __getitem__(self, at):
        self.wait()
        return self.held[at]


def kernel_call(body, operands, outs, scratch=(), flops=0, moved=1 << 22, limit=SMALL, scalars=()):
    count, out_count = len(operands), len(outs)
    staged = [place for place in range(count) if place not in scalars]
    held = [pltpu.VMEM(operands[place].shape, operands[place].dtype) for place in staged]
    results = [pltpu.VMEM(out.shape, out.dtype) for out in outs]

    def kernel(*refs):
        ins, out_refs, rest = refs[0:count], refs[count : count + out_count], refs[count + out_count :]
        copies, made, rest = rest[0 : len(staged)], rest[len(staged) : len(staged) + out_count], rest[len(staged) + out_count :]
        in_semaphores, out_semaphores, rest = rest[0], rest[1], rest[2:]
        values = list(ins)
        for turn, place in enumerate(staged):
            values[place] = Staged(ins[place], copies[turn], in_semaphores.at[turn])
        writes = [
            pltpu.make_async_copy(buffer, out, out_semaphores.at[turn])
            for turn, (buffer, out) in enumerate(zip(made, out_refs))
        ]
        started = []

        def write(*turns):
            for turn in turns:
                writes[turn].start()
                started.append(turn)

        body(values, made, rest, write)
        for value in values:
            if isinstance(value, Staged):
                value.wait()
        write(*[turn for turn in range(out_count) if turn not in started])
        for copy in writes:
            copy.wait()

    return pl.pallas_call(
        kernel,
        out_shape=tuple(outs),
        in_specs=[pl.BlockSpec(memory_space=pltpu.SMEM if place in scalars else pl.ANY) for place in range(count)],
        out_specs=tuple(pl.BlockSpec(memory_space=pl.ANY) for _ in outs),
        scratch_shapes=held + results + [pltpu.SemaphoreType.DMA((len(staged),)), pltpu.SemaphoreType.DMA((out_count,))] + list(scratch),
        compiler_params=pltpu.CompilerParams(vmem_limit_bytes=limit),
        cost_estimate=pl.CostEstimate(flops=1, bytes_accessed=1, transcendentals=0),
    )(*operands)


def columns_of(ids):
    count = ids.shape[1]
    row = lax.broadcasted_iota(jnp.int32, (count, count), 0)
    col = lax.broadcasted_iota(jnp.int32, (count, count), 1)
    return dot_last((row == col).astype(BF16), ids.astype(F32).astype(BF16)).astype(jnp.int32)


def choices(ids, experts):
    lane = lax.broadcasted_iota(jnp.int32, (ids.shape[0], experts), 1)
    return (ids[:, 0:1] == lane).astype(F32), (ids[:, 1:2] == lane).astype(F32)


def placements(ids, chip, near, capacity):
    count = ids.shape[0]
    first, second = choices(ids ^ chip, near)
    named = (first + second).astype(BF16)
    row = lax.broadcasted_iota(jnp.int32, (count, count), 0)
    col = lax.broadcasted_iota(jnp.int32, (count, count), 1)
    before = dot((col < row).astype(BF16), named)
    start = lax.broadcasted_iota(jnp.int32, (count, near), 1).astype(F32) * capacity
    place = before + start + 1.0
    slot = lax.broadcasted_iota(jnp.int32, (count, near * capacity), 1)
    picks = []
    for chosen in (first, second):
        at = jnp.sum(chosen * place, axis=1, keepdims=True).astype(jnp.int32) - 1
        picks.append((slot == at).astype(BF16))
    return picks


def pack_kernel(near, capacity, ins, outs, scratch, write):
    chip, ids, far, rows, far_rows = ins
    count = rows.shape[0]
    blocks = ((ids[...], rows), (far_ids_of(far, count), far_rows))
    for block, (names, source) in enumerate(blocks):
        first, second = placements(columns_of(names), chip[0], near, capacity)
        packed = dot_first(first + second, source[0:count, :]).astype(BF16)
        for place, out in enumerate(outs):
            out[block * capacity : (block + 1) * capacity, :] = packed[place * capacity : (place + 1) * capacity]


def far_ids_of(far, count):
    return far[count : count + RIM, 0:count][0:2].astype(F32).astype(jnp.int32)


def block_rows(refs, block, capacity):
    return jnp.concatenate([ref[block * capacity : (block + 1) * capacity, :] for ref in refs], axis=0)


def shifted(pad_ref, lanes, count):
    for rest in range(8):
        block = pad_ref[pl.ds(rest, count + 24), lanes]
        for turn in range(4):
            offset = 8 * turn + rest
            if 1 <= offset <= KSIZE:
                yield offset, block[8 * turn : 8 * turn + count]


def fill_padded(pad_ref, left_ref, mid_ref, right_ref):
    count = mid_ref.shape[0]
    pad_ref[0:RIM, :] = left_ref[...].astype(F32)
    pad_ref[RIM : RIM + count, :] = mid_ref[...].astype(F32)
    pad_ref[RIM + count : 2 * RIM + count, :] = right_ref[...].astype(F32)


def lane_loop(width, body):
    @pl.loop(0, width // LANES)
    def _(step):
        body(pl.ds(pl.multiple_of(step * LANES, LANES), LANES))


def front_kernel(ins, outs, scratch, write):
    frames, left, right, taps, gain = ins
    conv_ref, normed_ref = outs
    pad_ref, taps32_ref, mixed_ref, square_ref = scratch
    count, width = frames.shape
    fill_padded(pad_ref, left, frames, right)
    taps32_ref[...] = taps[...].astype(F32)
    square_ref[...] = jnp.zeros_like(square_ref)

    def conv(lanes):
        total = jnp.zeros((count, LANES), F32)
        for offset, rows in shifted(pad_ref, lanes, count):
            total = total + taps32_ref[offset - 1 : offset, lanes] * rows
        conv_ref[:, lanes] = total
        mixed = pad_ref[RIM : RIM + count, lanes] + total * jax.nn.sigmoid(total)
        mixed_ref[:, lanes] = mixed
        square_ref[...] += mixed * mixed

    lane_loop(width, conv)
    write(0)
    mean = jnp.sum(square_ref[...], axis=1, keepdims=True) / width
    inverse = lax.rsqrt(mean + NORM_EPS)
    normed_ref[...] = (mixed_ref[...] * inverse * gain[...].astype(F32)).astype(BF16)


def result_kernel(near, capacity, ins, outs, scratch, write):
    chip, ids, upstream_near, normed_near, far, normed_far, router = ins[0:7]
    rows_refs = ins[7:]
    near_ref, far_ref, near_logits_ref, far_logits_ref, router_out_ref = outs
    count = upstream_near.shape[0]
    router_out = jnp.zeros(router_out_ref.shape, F32)
    blocks = ((ids[...], upstream_near, normed_near), (far_ids_of(far, count), far, normed_far))
    for block, (names, grad, normed) in reversed(list(enumerate(blocks))):
        names = columns_of(names)
        upstream = grad[0:count, :].astype(F32)
        normed = normed[...]
        gates = jax.nn.sigmoid(dot_last(normed, router[...]))
        rows = block_rows(rows_refs, block, capacity)
        added = jnp.zeros(upstream.shape, F32)
        grad_logits = jnp.zeros(gates.shape, F32)
        for pick, chosen in zip(placements(names, chip[0], near, capacity), choices(names, gates.shape[1])):
            result = dot(pick, rows)
            gate = jnp.sum(chosen * gates, axis=1, keepdims=True)
            added = added + gate * result
            grad_gate = jnp.sum(upstream * result, axis=1, keepdims=True)
            grad_logits = grad_logits + chosen * (grad_gate * gate * (1.0 - gate))
        grad_logits = grad_logits.astype(BF16)
        (near_ref, far_ref)[block][...] = added.astype((F32, BF16)[block])
        write(block)
        (near_logits_ref, far_logits_ref)[block][...] = grad_logits
        router_out = router_out + dot_first(grad_logits, normed)
    router_out_ref[...] = router_out


def back_kernel(near, capacity, ins, outs, scratch, write):
    chip, ids, logits_near, far, logits_far, router = ins[0:6]
    rows_refs = ins[6:]
    count = outs[0].shape[0]
    blocks = ((ids[...], logits_near), (far_ids_of(far, count), logits_far))
    for block, (names, logits) in reversed(list(enumerate(blocks))):
        first, second = placements(columns_of(names), chip[0], near, capacity)
        total = dot(first + second, block_rows(rows_refs, block, capacity))
        outs[block][...] = (total + dot(logits[...], router[...])).astype(outs[block].dtype)
        write(block)


def half_lanes(core, width):
    return pl.ds(pl.multiple_of(core * (width // 2), LANES), width // 2)


def final_kernel(ins, outs, scratch, write):
    core, frames, left, right, conv, grad, gain, near_sum, far_sum, router, near_back, far_back = ins
    out_ref, mixed_grad_ref, conv_grad_ref, head_ref, tail_ref, kept_ref, given_ref = outs
    pad_ref, local_ref = scratch
    count, width = frames.shape
    fill_padded(pad_ref, left, frames, right)
    conv_out = conv[...]
    logistic = jax.nn.sigmoid(conv_out)
    mixed = frames[...].astype(F32) + conv_out * logistic
    inverse = lax.rsqrt(jnp.sum(mixed * mixed, axis=1, keepdims=True) / width + NORM_EPS)
    out_ref[...] = (mixed + (near_sum[...] + far_sum[...].astype(F32))).astype(BF16)
    write(0)
    local_ref[KSIZE + 1 :, :] = router[...]
    grad_normed = near_back[...] + far_back[...].astype(F32)
    local_ref[KSIZE : KSIZE + 1, :] = jnp.sum(grad_normed * mixed * inverse, axis=0, keepdims=True)
    scaled = grad_normed * gain[...].astype(F32)
    mean = jnp.sum(scaled * mixed, axis=1, keepdims=True) / width
    mixed_grad = grad[...].astype(F32) + inverse * scaled - mixed * (inverse * inverse * inverse * mean)
    mixed_grad_ref[...] = mixed_grad
    conv_grad = (mixed_grad * (logistic * (1.0 + conv_out * (1.0 - logistic)))).astype(BF16)
    conv_grad_ref[...] = conv_grad
    head_ref[...] = conv_grad[0:RIM]
    tail_ref[...] = conv_grad[count - RIM : count]
    write(1, 2, 3, 4)

    def reduce(lanes):
        grad = conv_grad_ref[:, lanes].astype(F32)
        for offset, rows in shifted(pad_ref, lanes, count):
            local_ref[offset - 1 : offset, lanes] = jnp.sum(grad * rows, axis=0, keepdims=True)

    lane_loop(width, reduce)
    kept_ref[...] = local_ref[:, half_lanes(core[0], width)]
    given_ref[...] = local_ref[:, half_lanes(1 - core[0], width)]


def frames_kernel(ins, outs, scratch, write):
    mixed_grad, conv_grad, left, right, taps = ins
    (out_ref,), (pad_ref, taps32_ref) = outs, scratch
    count, width = mixed_grad.shape
    fill_padded(pad_ref, left, conv_grad, right)
    taps32_ref[...] = taps[...].astype(F32)
    mixed_grad.wait()

    def conv(lanes):
        total = mixed_grad[:, lanes]
        for offset, rows in shifted(pad_ref, lanes, count):
            total = total + taps32_ref[KSIZE - offset : KSIZE - offset + 1, lanes] * rows
        out_ref[:, lanes] = total.astype(BF16)

    lane_loop(width, conv)


def chunk_loop(width, body):
    @pl.loop(0, width // CHUNK)
    def _(step):
        body(pl.ds(pl.multiple_of(step * CHUNK, CHUNK), CHUNK))


def gather_rows(refs, rows_ref):
    each = refs[0].shape[0]
    for place, ref in enumerate(refs):
        rows_ref[place * each : (place + 1) * each, :] = ref[...]


def scatter_columns(refs, columns, values):
    each = refs[0].shape[0]
    for place, ref in enumerate(refs):
        ref[:, columns] = values[place * each : (place + 1) * each]


def forward_kernel(near, ins, outs, scratch, write):
    rows, (near_in, far_in, near_out, far_out) = ins[0:near], ins[near:]
    out_refs, (rows_ref, near_pre_ref, far_pre_ref, near_active_ref, far_active_ref) = outs[0:near], outs[near:]
    gather_rows(rows, rows_ref)
    write(near)
    for weight, pre, active in ((near_in, near_pre_ref, near_active_ref), (far_in, far_pre_ref, far_active_ref)):
        weight.wait()

        def inner(columns):
            values = dot(rows_ref[...], weight[:, columns])
            pre[:, columns] = values
            active[:, columns] = jax.nn.silu(values).astype(BF16)

        chunk_loop(weight.shape[1], inner)
    write(near + 1, near + 2, near + 3, near + 4)
    near_out.wait()
    far_out.wait()

    def outer(columns):
        total = dot(near_active_ref[...], near_out[:, columns])
        total = total + dot(far_active_ref[...], far_out[:, columns])
        scatter_columns(out_refs, columns, total.astype(BF16))

    chunk_loop(near_out.shape[1], outer)


def backward_kernel(near, ins, outs, scratch, write):
    grads, (rows, router, mine, near_out, far_out, near_pre, far_pre, near_in, far_in) = ins[0:near], ins[near:]
    out_refs, (near_grad_ref, far_grad_ref, grad_rows_ref) = outs[0:near], outs[near:]
    (grads_ref,) = scratch
    gather_rows(grads, grads_ref)
    logits = jnp.sum(dot_last(rows[...], router[...]) * mine[...], axis=1, keepdims=True)
    gate = jax.nn.sigmoid(logits)
    grad_rows_ref[...] = (gate * grads_ref[...].astype(F32)).astype(BF16)
    write(near + 2)
    for weight, pre, grad in ((near_out, near_pre, near_grad_ref), (far_out, far_pre, far_grad_ref)):
        weight.wait()
        pre.wait()

        def inner(columns):
            hidden = dot_last(grad_rows_ref[...], weight[columns, :])
            grad[:, columns] = (hidden * slope_of(pre[:, columns])).astype(BF16)

        chunk_loop(weight.shape[0], inner)
    write(near, near + 1)
    near_in.wait()
    far_in.wait()

    def outer(rows):
        total = dot_last(near_grad_ref[...], near_in[rows, :])
        total = total + dot_last(far_grad_ref[...], far_in[rows, :])
        scatter_columns(out_refs, rows, total.astype(BF16))

    chunk_loop(near_in.shape[0], outer)


def last_kernel(ins, outs, scratch, write):
    core, mine, other = ins
    taps_ref, gain_ref, router_ref = outs
    width = taps_ref.shape[1]
    for place, half in ((core[0], mine), (1 - core[0], other)):
        lanes = half_lanes(place, width)
        taps_ref[:, lanes] = half[0:KSIZE]
        gain_ref[:, lanes] = half[KSIZE : KSIZE + 1]
        router_ref[:, lanes] = half[KSIZE + 1 :]


def rims(head, tail, count):
    ends = count - 1
    left = lax.ppermute(tail, "seq", [(i, i + 1) for i in range(ends)])
    right = lax.ppermute(head, "seq", [(i + 1, i) for i in range(ends)])
    return left, right


def swap(values, count, bit):
    return lax.ppermute(values, "seq", [(i, i ^ bit) for i in range(count)])


def exchange(parts, devices):
    return [parts[0]] + [swap(part, devices, 2 * r) for r, part in enumerate(parts) if r]


def per_device(frames, conv_kernel, norm_gain, router, expert_in, expert_out, expert_ids, out_grad):
    count, width = frames.shape
    devices = lax.axis_size("seq")
    experts = devices // 2
    capacity = 8 * count // devices
    near = experts // 2
    slots = experts * capacity
    gain = norm_gain.reshape(1, width)
    taps = conv_kernel
    router = router.T
    ids = expert_ids.T
    shape = jax.ShapeDtypeStruct
    pad = pltpu.VMEM((count + 2 * RIM, width), F32)
    taps32 = pltpu.VMEM((KSIZE, width), F32)
    chip = lax.axis_index("seq") // 2
    chips = chip.reshape(1).astype(jnp.int32)
    mine = (jnp.arange(experts, dtype=jnp.int32) == chip).astype(F32).reshape(1, experts)
    cross = functools.partial(swap, count=devices, bit=devices // 2)

    named = jnp.pad(ids.astype(BF16), ((0, RIM - 2), (0, width - count)))
    far_grad = cross(jnp.concatenate([out_grad, named]))
    left, right = rims(frames[0:RIM], frames[count - RIM : count], devices)
    weight_in, weight_out = expert_in[0], expert_out[0]
    other_in = swap(weight_in, devices, 1)
    other_out = swap(weight_out, devices, 1)

    model32, model16 = shape((count, width), F32), shape((count, width), BF16)
    conv_out, normed = kernel_call(
        front_kernel,
        (frames, left, right, taps, gain),
        (model32, model16),
        (pad, taps32, pltpu.VMEM((count, width), F32), pltpu.VMEM((count, LANES), F32)),
    )
    far_normed = cross(normed)

    part = (shape((2 * capacity, width), BF16),) * near
    pack = functools.partial(pack_kernel, near, capacity)
    grads = exchange(
        kernel_call(pack, (chips, ids, far_grad, out_grad, far_grad), part, scalars=(0,)), devices
    )
    rows = exchange(
        kernel_call(pack, (chips, ids, far_grad, normed, far_normed), part, scalars=(0,)), devices
    )

    half = weight_in.shape[1]
    wide = shape((slots, half), F32)
    narrow = shape((slots, half), BF16)
    model = shape((slots, width), BF16)
    work = 8 * slots * width * half
    outs = kernel_call(
        functools.partial(forward_kernel, near),
        (*rows, weight_in, other_in, weight_out, other_out),
        part + (model, wide, wide, narrow, narrow),
        flops=work, moved=1 << 24, limit=LARGE,
    )
    parts_out, (all_rows, *pre_act), active = outs[0:near], outs[near : near + 3], outs[near + 3 :]
    results = exchange(parts_out, devices)
    outs = kernel_call(
        functools.partial(backward_kernel, near),
        (*grads, all_rows, router, mine, weight_out, other_out, *pre_act, weight_in, other_in),
        part + (narrow, narrow, model),
        (pltpu.VMEM((slots, width), BF16),),
        flops=work, moved=1 << 24, limit=LARGE,
    )
    results, all_rows, active, outs = lax.optimization_barrier((results, all_rows, active, outs))
    parts_in, pre_grad, grad_rows = outs[0:near], outs[near : near + 2], outs[near + 2]
    backs = exchange(parts_in, devices)
    far_rows, far_grads, far_active, far_pre = [
        swap(values, devices, 1) for values in (all_rows, grad_rows, active[1], pre_grad[1])
    ]
    expert_out_grad = (dot_first(active[0], grad_rows) + dot_first(far_active, far_grads)).astype(BF16)
    expert_in_grad = (dot_first(all_rows, pre_grad[0]) + dot_first(far_rows, far_pre)).astype(BF16)

    logits = shape((count, experts), BF16)
    near_sum, far_sum, near_logits, far_logits, router_local = kernel_call(
        functools.partial(result_kernel, near, capacity),
        (chips, ids, out_grad, normed, far_grad, far_normed, router, *results),
        (model32, model16, logits, logits, shape((experts, width), F32)),
        scalars=(0,),
    )
    far_sum = cross(far_sum)
    backs[1], far_sum = lax.optimization_barrier((backs[1], far_sum))
    near_back, far_back = kernel_call(
        functools.partial(back_kernel, near, capacity),
        (chips, ids, near_logits, far_grad, far_logits, router, *backs),
        (model32, model16),
        scalars=(0,),
    )
    far_back = cross(far_back)
    far_back, expert_in_grad, expert_out_grad = lax.optimization_barrier((far_back, expert_in_grad, expert_out_grad))

    rim = shape((RIM, width), BF16)
    lines = KSIZE + 1 + experts
    columns = shape((lines, width // 2), F32)
    core = (lax.axis_index("seq") % 2).reshape(1).astype(jnp.int32)
    block_out, mixed_grad, conv_grad, head, tail, kept, given = kernel_call(
        final_kernel,
        (core, frames, left, right, conv_out, out_grad, gain, near_sum, far_sum, router_local, near_back, far_back),
        (model16, model32, model16, rim, rim, columns, columns),
        (pad, pltpu.VMEM((lines, width), F32)),
        scalars=(0,),
    )
    grad_left, grad_right = rims(head, tail, devices)
    local = kept + swap(given, devices, 1)
    bit = 2
    while bit < devices:
        other = swap(local, devices, bit)
        if bit == 2:
            other, grad_left, grad_right = lax.optimization_barrier((other, grad_left, grad_right))
            (frames_grad,) = kernel_call(
                frames_kernel, (mixed_grad, conv_grad, grad_left, grad_right, taps), (model16,), (pad, taps32)
            )
        if bit == 4:
            other, frames_grad = lax.optimization_barrier((other, frames_grad))
        local = local + other
        bit *= 2
    kernel_grad, gain_grad, router_grad = kernel_call(
        last_kernel,
        (core, local, swap(local, devices, 1)),
        (shape((KSIZE, width), F32), shape((1, width), F32), shape((experts, width), F32)),
        scalars=(0,),
    )
    return (
        block_out,
        frames_grad,
        kernel_grad,
        gain_grad[0],
        router_grad.T,
        expert_in_grad[None],
        expert_out_grad[None],
    )


def solution(mesh):
    in_specs = (
        P(("groups", "seq"), None),
        P(),
        P(),
        P(),
        P("seq", None, None),
        P("seq", None, None),
        P(("groups", "seq"), None),
        P(("groups", "seq"), None),
    )
    out_specs = (
        P(("groups", "seq"), None),
        P(("groups", "seq"), None),
        P("groups", None),
        P("groups"),
        P("groups", None),
        P(("groups", "seq"), None, None),
        P(("groups", "seq"), None, None),
    )
    return jax.shard_map(
        per_device, mesh=mesh, in_specs=in_specs, out_specs=out_specs, check_vma=False
    )
```

time: 180 us -> 156 us (0.87)
  matrix products: 38.5 us -> 12.5 us
  Pallas kernels: 14.1 us -> 36.9 us
  waiting for transfers between devices: 73.2 us -> 50.6 us
  starting transfers between devices: 34.2 us -> 39.4 us
    all_to_all x4 -> x0, waiting for transfers between devices: 67.9 us -> none  [exchange(): lax.all_to_all(payload, 'seq', 0, 0, axis_index_groups=groups, tiled=True)]
    ppermute x10 -> x27, waiting for transfers between devices: 3.74 us -> 48.6 us  [swap(): return lax.ppermute(values, 'seq', [(i, i ^ bit) for i in range(count)])]
    dot_general x9 -> x0, matrix products: 26.1 us -> none  [the longest x5 13.6 us: dot(): return jnp.dot(a, b, preferred_element_type=F32)]
    ppermute x10 -> x27, starting transfers between devices: 9.16 us -> 32.7 us  [swap(): return lax.ppermute(values, 'seq', [(i, i ^ bit) for i in range(count)])]
    pallas_call x6 -> x10, Pallas kernels: 14.1 us -> 36.9 us  [kernel_call(): pl.pallas_call(kernel, out_shape=tuple(outs), in_specs=[pl.BlockSpec(memo...]
    all_to_all x4 -> x0, starting transfers between devices: 18.6 us -> none  [exchange(): lax.all_to_all(payload, 'seq', 0, 0, axis_index_groups=groups, tiled=True)]
    unnamed x60 -> x64, local copies, waits for them, and re-layouts: 11.8 us -> 11.9 us
  transfers between devices with their start and end apart: 18 -> 31, of which waited for: 6 -> 11; matrix products, arithmetic and copies ran while one was open for 24% -> 10% of each run, Pallas kernels for 5% -> 21%
where the time goes in v1:
time: 156 us
  waiting for transfers between devices  50.6 us (32%)
  starting transfers between devices  39.4 us (25%)
  Pallas kernels  36.9 us (24%)
  local copies, waits for them, and re-layouts  13.4 us (9%)
  matrix products  12.5 us (8%)
  other arithmetic  1.71 us (1%)
    ppermute x27, waiting for transfers between devices, swap(): return lax.ppermute(values, 'seq', [(i, i ^ bit) for i in range(count)])  48.6 us
    pallas_call x10, Pallas kernels, kernel_call(): pl.pallas_call(kernel, out_shape=tuple(outs), in_specs=[pl.BlockSpec(memo...  36.9 us
    ppermute x27, starting transfers between devices, swap(): return lax.ppermute(values, 'seq', [(i, i ^ bit) for i in range(count)])  32.7 us
    dot_general x4, matrix products, dot_first(): return lax.dot_general(a, b, FIRST, preferred_element_type=F32)  12.5 us
    unnamed x64, local copies, waits for them, and re-layouts  11.9 us
    ppermute x2, starting transfers between devices, rims(): left = lax.ppermute(tail, 'seq', [(i, i + 1) for i in range(ends)])  4.1 us
  transfers between devices with their start and end apart: 31, of which 11 were waited for; matrix products, arithmetic and copies ran while one was open for 10% of the time, Pallas kernels for 21%

profile of v1, /device:TPU:0, one launch (start us, length us, event | category | flops | bytes accessed | tf_op | source)
XLA Modules:
  0.0 155.8 jit_solution(2451845325650219532)
XLA Ops:
  2.1 2.3 %collective-permute-start = (bf16[16,1024]{1,0:T(8,128)(2,1)S(1)}, bf16[16,1024]{1,0:T(8,128)(2,1)S(1)}, u32[]{:S(2)}, u32[]{:S(2)}) collective-permute-start(bf16[16,1024]{1,0:T(8,128)(2,1)S(1)} %get-tuple-element.142), channel_id=1, source_target_pairs={{0,1},{1,2},{2,3},{3,4},{4,5},{5,6},{6,7},{7,8},{8,9},{9,10},{10,1... | collective-permute-start | bytes 98312 | tf_op jit(solution)/shard_map/ppermute | solution.py:378
  7.4 6.9 %collective-permute-start.2 = (bf16[144,1024]{1,0:T(8,128)(2,1)S(1)}, bf16[144,1024]{1,0:T(8,128)(2,1)S(1)}, u32[]{:S(2)}, u32[]{:S(2)}) collective-permute-start(bf16[144,1024]{1,0:T(8,128)(2,1)S(1)} %fusion.1), channel_id=1, source_target_pairs={{0,8},{1,9},{2,10},{3,11},{4,12},{5,13},{6,14},{7,15},{8,0},{9,1},... | collective-permute-start | bytes 884744 | tf_op jit(solution)/shard_map/ppermute | solution.py:384
  16.8 3.2 %shard_map.135 = (f32[128,1024]{1,0:T(8,128)S(1)}, bf16[128,1024]{1,0:T(8,128)(2,1)S(1)}) custom-call(bf16[128,1024]{1,0:T(8,128)(2,1)S(1)} %copy-done.6, bf16[16,1024]{1,0:T(8,128)(2,1)S(1)} %collective-permute-done.refs_1_.refs_2_, bf16[16,1024]{1,0:T(8,128)(2,1)S(1)} %collective-permute-done.1.refs_2_.refs_3_, bf16[31,1024]{1,0:T(8,128)(2,1)S(1)} %copy-done.18, ...), custom_call_target="tpu_custom_call" | custom-call | flops 1 | bytes 1 | tf_op jit(solution)/shard_map/pallas_call | solution.py:88
  20.9 17.4 %collective-permute-done.3.refs_4_.refs_5_ = bf16[128,1024]{1,0:T(8,128)(2,1)S(1)} collective-permute-done((bf16[128,1024]{1,0:T(8,128)(2,1)S(1)}, bf16[128,1024]{1,0:T(8,128)(2,1)S(1)}, u32[]{:S(2)}, u32[]{:S(2)}) %collective-permute-start.3) | collective-permute-done | bytes 262176 | tf_op jit(solution)/shard_map/ppermute | solution.py:384
  42.1 2.2 %collective-permute-start.6 = (bf16[128,1024]{1,0:T(8,128)(2,1)S(1)}, bf16[128,1024]{1,0:T(8,128)(2,1)S(1)}, u32[]{:S(2)}, u32[]{:S(2)}) collective-permute-start(bf16[128,1024]{1,0:T(8,128)(2,1)S(1)} %get-tuple-element.79), channel_id=1, source_target_pairs={{0,6},{1,7},{2,4},{3,5},{4,2},{5,3},{6,0},{7,1},{8,14},{9,15},{10,... | collective-permute-start | bytes 786440 | tf_op jit(solution)/shard_map/ppermute | solution.py:384
  51.3 5.8 %collective-permute-done.6.refs_3_ = bf16[128,1024]{1,0:T(8,128)(2,1)S(1)} collective-permute-done((bf16[128,1024]{1,0:T(8,128)(2,1)S(1)}, bf16[128,1024]{1,0:T(8,128)(2,1)S(1)}, u32[]{:S(2)}, u32[]{:S(2)}) %collective-permute-start.6) | collective-permute-done | bytes 262176 | tf_op jit(solution)/shard_map/ppermute | solution.py:384
  59.5 7.7 %shard_map.137 = (bf16[128,1024]{1,0:T(8,128)(2,1)S(1)}, bf16[128,1024]{1,0:T(8,128)(2,1)S(1)}, bf16[128,1024]{1,0:T(8,128)(2,1)S(1)}, bf16[128,1024]{1,0:T(8,12...) custom-call(bf16[128,1024]{1,0:T(8,128)(2,1)S(1)} %get-tuple-element, ...), custom_call_target="tpu_custom_call" | custom-call | flops 1 | bytes 1 | tf_op jit(solution)/shard_map/pallas_call | solution.py:88
  71.8 9.5 %shard_map.139 = (bf16[128,1024]{1,0:T(8,128)(2,1)S(1)}, bf16[128,1024]{1,0:T(8,128)(2,1)S(1)}, bf16[128,1024]{1,0:T(8,128)(2,1)S(1)}, bf16[128,1024]{1,0:T(8,12...) custom-call(bf16[128,1024]{1,0:T(8,128)(2,1)S(1)} %get-tuple-element.87.refs_0_, ...), custom_call_target="tpu_custom_call" | custom-call | flops 1 | bytes 1 | tf_op jit(solution)/shard_map/pallas_call | solution.py:88
  83.1 2.8 %shard_map.140 = (f32[128,1024]{1,0:T(8,128)S(1)}, bf16[128,1024]{1,0:T(8,128)(2,1)S(1)}, bf16[128,8]{1,0:T(8,128)(2,1)S(1)}, bf16[128,8]{1,0:T(8,128)(2,1)S(1)}, f32[8,1024]{1,0:T(8,128)S(1)}) custom-call(s32[1]{0:T(128)} %bitcast.1.refs_0_, s32[2,128]{1,0:T(2,128)S(1)} %bitcast.30, bf16[128,1024]{1,0:T(8,128)(2,1)S(1)} %copy-done.4, ...), custom_call_target="tpu_custom_call" | custom-call | flops 1 | bytes 1 | tf_op jit(solution)/shard_map/pallas_call | solution.py:88
  87.8 3.3 %collective-permute-start.16 = (bf16[128,1024]{1,0:T(8,128)(2,1)S(1)}, bf16[128,1024]{1,0:T(8,128)(2,1)S(1)}, u32[]{:S(2)}, u32[]{:S(2)}) collective-permute-start(bf16[128,1024]{1,0:T(8,128)(2,1)S(1)} %get-tuple-element.106), channel_id=1, source_target_pairs={{0,8},{1,9},{2,10},{3,11},{4,12},{5,13},{6,14},{7,15},{8,0},{9,1},... | collective-permute-start | bytes 786440 | tf_op jit(solution)/shard_map/ppermute | solution.py:384
  91.1 2.0 %collective-permute-start.18 = (bf16[128,1024]{1,0:T(8,128)(2,1)}, bf16[128,1024]{1,0:T(8,128)(2,1)S(1)}, u32[]{:S(2)}, u32[]{:S(2)}) collective-permute-start(bf16[128,1024]{1,0:T(8,128)(2,1)} %get-tuple-element.114), channel_id=1, source_target_pairs={{0,6},{1,7},{2,4},{3,5},{4,2},{5,3},{6,0},{7,1},{8,14},{9,15},{10,... | collective-permute-start | bytes 786440 | tf_op jit(solution)/shard_map/ppermute | solution.py:384
  93.2 9.9 %collective-permute-done.16.refs_8_ = bf16[128,1024]{1,0:T(8,128)(2,1)S(1)} collective-permute-done((bf16[128,1024]{1,0:T(8,128)(2,1)S(1)}, bf16[128,1024]{1,0:T(8,128)(2,1)S(1)}, u32[]{:S(2)}, u32[]{:S(2)}) %collective-permute-start.16) | collective-permute-done | bytes 262176 | tf_op jit(solution)/shard_map/ppermute | solution.py:384
  103.1 2.5 %collective-permute-done.17.refs_8_ = bf16[128,1024]{1,0:T(8,128)(2,1)S(1)} collective-permute-done((bf16[128,1024]{1,0:T(8,128)(2,1)S(1)}, bf16[128,1024]{1,0:T(8,128)(2,1)S(1)}, u32[]{:S(2)}, u32[]{:S(2)}) %collective-permute-start.17) | collective-permute-done | bytes 262176 | tf_op jit(solution)/shard_map/ppermute | solution.py:384
  105.6 3.4 %collective-permute-done.18.refs_9_ = bf16[128,1024]{1,0:T(8,128)(2,1)S(1)} collective-permute-done((bf16[128,1024]{1,0:T(8,128)(2,1)}, bf16[128,1024]{1,0:T(8,128)(2,1)S(1)}, u32[]{:S(2)}, u32[]{:S(2)}) %collective-permute-start.18) | collective-permute-done | bytes 262176 | tf_op jit(solution)/shard_map/ppermute | solution.py:384
  111.4 2.1 %shard_map.141 = (f32[128,1024]{1,0:T(8,128)S(1)}, bf16[128,1024]{1,0:T(8,128)(2,1)S(1)}) custom-call(s32[1]{0:T(128)} %bitcast.1.refs_0_, s32[2,128]{1,0:T(2,128)S(1)} %bitcast.31, bf16[128,8]{1,0:T(8,128)(2,1)S(1)} %copy-done.26, bf16[144,1024]{1,0:T(8,128)(2,1)S(1)} %collective-permute-done.2.refs_2_.refs_4_.refs_3_, bf16[128,8]{1,0:T(8,128)(2,1)S(1)} %copy-done.28, ...), custom_call_target="tpu_custom_call" | custom-call | flops 1 | bytes 1 | tf_op jit(solution)/shard_map/pallas_call | solution.py:88
  114.9 2.8 %fusion.3 = f32[1024,1024]{1,0:T(8,128)S(1)} fusion(bf16[512,1024]{1,0:T(8,128)(2,1)} %collective-permute-done.20, bf16[512,1024]{1,0:T(8,128)(2,1)} %collective-permute-done.21), kind=kOutput, calls=%fused_computation.8 | convolution fusion | flops 1073741824 | bytes 6291456 | tf_op jit(solution)/shard_map/dot_general | solution.py:32
  117.8 2.7 %add_convert_fusion.1 = bf16[1024,1024]{1,0:T(8,128)(2,1)} fusion(f32[1024,1024]{1,0:T(8,128)S(1)} %fusion.3, bf16[512,1024]{1,0:T(8,128)(2,1)S(1)} %get-tuple-element.117.refs_4_, bf16[512,1024]{1,0:T(8,128)(2,1)S(1)} %copy-done.15), kind=kOutput, calls=%fused_computation.1 | convolution fusion | flops 1075838976 | bytes 8388608 | tf_op jit(solution)/shard_map/dot_general | solution.py:32
  120.5 2.9 %fusion.4 = f32[1024,1024]{1,0:T(8,128)S(1)} fusion(bf16[512,1024]{1,0:T(8,128)(2,1)} %collective-permute-done.22, bf16[512,1024]{1,0:T(8,128)(2,1)} %collective-permute-done.23), kind=kOutput, calls=%fused_computation.9 | convolution fusion | flops 1073741824 | bytes 6291456 | tf_op jit(solution)/shard_map/dot_general | solution.py:32
  123.5 4.0 %add_convert_fusion = bf16[1024,1024]{1,0:T(8,128)(2,1)} fusion(f32[1024,1024]{1,0:T(8,128)S(1)} %fusion.4, bf16[512,1024]{1,0:T(8,128)(2,1)S(1)} %copy-done.13, bf16[512,1024]{1,0:T(8,128)(2,1)} %get-tuple-element.121), kind=kOutput, calls=%fused_computation | convolution fusion | flops 1075838976 | bytes 8388608 | tf_op jit(solution)/shard_map/dot_general | solution.py:32
  127.6 3.5 %shard_map.142 = (bf16[128,1024]{1,0:T(8,128)(2,1)}, f32[128,1024]{1,0:T(8,128)S(1)}, bf16[128,1024]{1,0:T(8,128)(2,1)S(1)}, bf16[16,1024]{1,0:T(8,128)(2,1)S(1)...) custom-call(s32[1]{0:T(128)} %bitcast.refs_0_, bf16[128,1024]{1,0:T(8,128)(2,1)S(1)} %copy-done.7, ...), custom_call_target="tpu_custom_call" | custom-call | flops 1 | bytes 1 | tf_op jit(solution)/shard_map/pallas_call | solution.py:88
  139.1 3.9 %collective-permute-start.28 = (f32[40,512]{1,0:T(8,128)S(1)}, f32[40,512]{1,0:T(8,128)S(1)}, u32[]{:S(2)}, u32[]{:S(2)}) collective-permute-start(f32[40,512]{1,0:T(8,128)S(1)} %add.29), channel_id=1, source_target_pairs={{0,4},{1,5},{2,6},{3,7},{4,0},{5,1},{6,2},{7,3},{8,12},{9,13},{10,... | collective-permute-start | bytes 245768 | tf_op jit(solution)/shard_map/ppermute | solution.py:384
  143.0 3.7 %shard_map.143 = bf16[128,1024]{1,0:T(8,128)(2,1)} custom-call(f32[128,1024]{1,0:T(8,128)S(1)} %get-tuple-element.130.refs_0_, bf16[128,1024]{1,0:T(8,128)(2,1)S(1)} %get-tuple-element.131.refs_1_, bf16[16,1024]{1,0:T(8,128)(2,1)S(1)} %collective-permute-done.26.refs_2_, bf16[16,1024]{1,0:T(8,128)(2,1)S(1)} %collective-permute-done.27.refs_3_, ...), custom_call_target="tpu_custom_call" | custom-call | flops 1 | bytes 1 | tf_op jit(solution)/shard_map/pallas_call | solution.py:88
  146.7 2.2 %collective-permute-start.29 = (f32[40,512]{1,0:T(8,128)S(1)}, f32[40,512]{1,0:T(8,128)S(1)}, u32[]{:S(2)}, u32[]{:S(2)}) collective-permute-start(f32[40,512]{1,0:T(8,128)S(1)} %add.30), channel_id=1, source_target_pairs={{0,8},{1,9},{2,10},{3,11},{4,12},{5,13},{6,14},{7,15},{8,0},{9,1},... | collective-permute-start | bytes 245768 | tf_op jit(solution)/shard_map/ppermute | solution.py:384
  148.9 4.5 %collective-permute-done.29 = f32[40,512]{1,0:T(8,128)S(1)} collective-permute-done((f32[40,512]{1,0:T(8,128)S(1)}, f32[40,512]{1,0:T(8,128)S(1)}, u32[]{:S(2)}, u32[]{:S(2)}) %collective-permute-start.29) | collective-permute-done | bytes 81952 | tf_op jit(solution)/shard_map/ppermute | solution.py:384
  (125 shorter events, 43.2 us)
Async XLA Ops:
  0.6 57.2 %collective-permute-start.7 = (bf16[1024,1024]{1,0:T(8,128)(2,1)}, bf16[1024,1024]{1,0:T(8,128)(2,1)}, u32[]{:S(2)}, u32[]{:S(2)}) collective-permute-start(bf16[1024,1024]{1,0:T(8,128)(2,1)} %bitcast.19), channel_id=1, source_target_pairs={{0,1},{1,0},{2,3},{3,2},{4,5},{5,4},{6,7},{7,6},{8,9},{9,8},{10,11... | collective-permute-start | bytes 6291464 | tf_op jit(solution)/shard_map/ppermute | solution.py:384
  1.2 56.7 %collective-permute-start.8 = (bf16[1024,1024]{1,0:T(8,128)(2,1)}, bf16[1024,1024]{1,0:T(8,128)(2,1)}, u32[]{:S(2)}, u32[]{:S(2)}) collective-permute-start(bf16[1024,1024]{1,0:T(8,128)(2,1)} %bitcast.22), channel_id=1, source_target_pairs={{0,1},{1,0},{2,3},{3,2},{4,5},{5,4},{6,7},{7,6},{8,9},{9,8},{10,11... | collective-permute-start | bytes 6291464 | tf_op jit(solution)/shard_map/ppermute | solution.py:384
  2.1 12.9 %collective-permute-start = (bf16[16,1024]{1,0:T(8,128)(2,1)S(1)}, bf16[16,1024]{1,0:T(8,128)(2,1)S(1)}, u32[]{:S(2)}, u32[]{:S(2)}) collective-permute-start(bf16[16,1024]{1,0:T(8,128)(2,1)S(1)} %get-tuple-element.142), channel_id=1, source_target_pairs={{0,1},{1,2},{2,3},{3,4},{4,5},{5,6},{6,7},{7,8},{8,9},{9,10},{10,1... | collective-permute-start | bytes 98312 | tf_op jit(solution)/shard_map/ppermute | solution.py:378
  4.4 10.6 %collective-permute-start.1 = (bf16[16,1024]{1,0:T(8,128)(2,1)S(1)}, bf16[16,1024]{1,0:T(8,128)(2,1)S(1)}, u32[]{:S(2)}, u32[]{:S(2)}) collective-permute-start(bf16[16,1024]{1,0:T(8,128)(2,1)S(1)} %get-tuple-element.141), channel_id=1, source_target_pairs={{1,0},{2,1},{3,2},{4,3},{5,4},{6,5},{7,6},{8,7},{9,8},{10,9},{11,1... | collective-permute-start | bytes 98312 | tf_op jit(solution)/shard_map/ppermute | solution.py:379
  7.4 30.9 %collective-permute-start.2 = (bf16[144,1024]{1,0:T(8,128)(2,1)S(1)}, bf16[144,1024]{1,0:T(8,128)(2,1)S(1)}, u32[]{:S(2)}, u32[]{:S(2)}) collective-permute-start(bf16[144,1024]{1,0:T(8,128)(2,1)S(1)} %fusion.1), channel_id=1, source_target_pairs={{0,8},{1,9},{2,10},{3,11},{4,12},{5,13},{6,14},{7,15},{8,0},{9,1},... | collective-permute-start | bytes 884744 | tf_op jit(solution)/shard_map/ppermute | solution.py:384
  20.8 17.4 %collective-permute-start.3 = (bf16[128,1024]{1,0:T(8,128)(2,1)S(1)}, bf16[128,1024]{1,0:T(8,128)(2,1)S(1)}, u32[]{:S(2)}, u32[]{:S(2)}) collective-permute-start(bf16[128,1024]{1,0:T(8,128)(2,1)S(1)} %get-tuple-element.75.refs_3_), channel_id=1, source_target_pairs={{0,8},{1,9},{2,10},{3,11},{4,12},{5,13},{6,14},{7,15},{8,0},{9,1},... | collective-permute-start | bytes 786440 | tf_op jit(solution)/shard_map/ppermute | solution.py:384
  40.7 8.9 %collective-permute-start.4 = (bf16[128,1024]{1,0:T(8,128)(2,1)S(1)}, bf16[128,1024]{1,0:T(8,128)(2,1)S(1)}, u32[]{:S(2)}, u32[]{:S(2)}) collective-permute-start(bf16[128,1024]{1,0:T(8,128)(2,1)S(1)} %get-tuple-element.77), channel_id=1, source_target_pairs={{0,2},{1,3},{2,0},{3,1},{4,6},{5,7},{6,4},{7,5},{8,10},{9,11},{10,... | collective-permute-start | bytes 786440 | tf_op jit(solution)/shard_map/ppermute | solution.py:384
  42.1 9.2 %collective-permute-start.5 = (bf16[128,1024]{1,0:T(8,128)(2,1)S(1)}, bf16[128,1024]{1,0:T(8,128)(2,1)S(1)}, u32[]{:S(2)}, u32[]{:S(2)}) collective-permute-start(bf16[128,1024]{1,0:T(8,128)(2,1)S(1)} %get-tuple-element.78), channel_id=1, source_target_pairs={{0,4},{1,5},{2,6},{3,7},{4,0},{5,1},{6,2},{7,3},{8,12},{9,13},{10,... | collective-permute-start | bytes 786440 | tf_op jit(solution)/shard_map/ppermute | solution.py:384
  42.1 15.0 %collective-permute-start.6 = (bf16[128,1024]{1,0:T(8,128)(2,1)S(1)}, bf16[128,1024]{1,0:T(8,128)(2,1)S(1)}, u32[]{:S(2)}, u32[]{:S(2)}) collective-permute-start(bf16[128,1024]{1,0:T(8,128)(2,1)S(1)} %get-tuple-element.79), channel_id=1, source_target_pairs={{0,6},{1,7},{2,4},{3,5},{4,2},{5,3},{6,0},{7,1},{8,14},{9,15},{10,... | collective-permute-start | bytes 786440 | tf_op jit(solution)/shard_map/ppermute | solution.py:384
  49.6 21.4 %collective-permute-start.12 = (bf16[128,1024]{1,0:T(8,128)(2,1)S(1)}, bf16[128,1024]{1,0:T(8,128)(2,1)S(1)}, u32[]{:S(2)}, u32[]{:S(2)}) collective-permute-start(bf16[128,1024]{1,0:T(8,128)(2,1)S(1)} %get-tuple-element.88), channel_id=1, source_target_pairs={{0,2},{1,3},{2,0},{3,1},{4,6},{5,7},{6,4},{7,5},{8,10},{9,11},{10,... | collective-permute-start | bytes 786440 | tf_op jit(solution)/shard_map/ppermute | solution.py:384
  51.3 20.5 %collective-permute-start.13 = (bf16[128,1024]{1,0:T(8,128)(2,1)S(1)}, bf16[128,1024]{1,0:T(8,128)(2,1)S(1)}, u32[]{:S(2)}, u32[]{:S(2)}) collective-permute-start(bf16[128,1024]{1,0:T(8,128)(2,1)S(1)} %get-tuple-element.89), channel_id=1, source_target_pairs={{0,4},{1,5},{2,6},{3,7},{4,0},{5,1},{6,2},{7,3},{8,12},{9,13},{10,... | collective-permute-start | bytes 786440 | tf_op jit(solution)/shard_map/ppermute | solution.py:384
  57.1 14.7 %collective-permute-start.14 = (bf16[128,1024]{1,0:T(8,128)(2,1)S(1)}, bf16[128,1024]{1,0:T(8,128)(2,1)S(1)}, u32[]{:S(2)}, u32[]{:S(2)}) collective-permute-start(bf16[128,1024]{1,0:T(8,128)(2,1)S(1)} %get-tuple-element.90), channel_id=1, source_target_pairs={{0,6},{1,7},{2,4},{3,5},{4,2},{5,3},{6,0},{7,1},{8,14},{9,15},{10,... | collective-permute-start | bytes 786440 | tf_op jit(solution)/shard_map/ppermute | solution.py:384
  68.3 13.1 %collective-permute-start.9 = (bf16[128,1024]{1,0:T(8,128)(2,1)S(1)}, bf16[128,1024]{1,0:T(8,128)(2,1)S(1)}, u32[]{:S(2)}, u32[]{:S(2)}) collective-permute-start(bf16[128,1024]{1,0:T(8,128)(2,1)S(1)} %get-tuple-element.81), channel_id=1, source_target_pairs={{0,2},{1,3},{2,0},{3,1},{4,6},{5,7},{6,4},{7,5},{8,10},{9,11},{10,... | collective-permute-start | bytes 786440 | tf_op jit(solution)/shard_map/ppermute | solution.py:384
  69.4 11.9 %collective-permute-start.10 = (bf16[128,1024]{1,0:T(8,128)(2,1)S(1)}, bf16[128,1024]{1,0:T(8,128)(2,1)S(1)}, u32[]{:S(2)}, u32[]{:S(2)}) collective-permute-start(bf16[128,1024]{1,0:T(8,128)(2,1)S(1)} %get-tuple-element.82), channel_id=1, source_target_pairs={{0,4},{1,5},{2,6},{3,7},{4,0},{5,1},{6,2},{7,3},{8,12},{9,13},{10,... | collective-permute-start | bytes 786440 | tf_op jit(solution)/shard_map/ppermute | solution.py:384
  71.0 10.4 %collective-permute-start.11 = (bf16[128,1024]{1,0:T(8,128)(2,1)S(1)}, bf16[128,1024]{1,0:T(8,128)(2,1)S(1)}, u32[]{:S(2)}, u32[]{:S(2)}) collective-permute-start(bf16[128,1024]{1,0:T(8,128)(2,1)S(1)} %get-tuple-element.83), channel_id=1, source_target_pairs={{0,6},{1,7},{2,4},{3,5},{4,2},{5,3},{6,0},{7,1},{8,14},{9,15},{10,... | collective-permute-start | bytes 786440 | tf_op jit(solution)/shard_map/ppermute | solution.py:384
  81.4 33.6 %collective-permute-start.20 = (bf16[512,1024]{1,0:T(8,128)(2,1)S(1)}, bf16[512,1024]{1,0:T(8,128)(2,1)}, u32[]{:S(2)}, u32[]{:S(2)}) collective-permute-start(bf16[512,1024]{1,0:T(8,128)(2,1)S(1)} %get-tuple-element.117.refs_4_), channel_id=1, source_target_pairs={{0,1},{1,0},{2,3},{3,2},{4,5},{5,4},{6,7},{7,6},{8,9},{9,8},{10,11... | collective-permute-start | bytes 3145736 | tf_op jit(solution)/shard_map/ppermute | solution.py:384
  81.4 33.5 %collective-permute-start.21 = (bf16[512,1024]{1,0:T(8,128)(2,1)}, bf16[512,1024]{1,0:T(8,128)(2,1)}, u32[]{:S(2)}, u32[]{:S(2)}) collective-permute-start(bf16[512,1024]{1,0:T(8,128)(2,1)} %get-tuple-element.119), channel_id=1, source_target_pairs={{0,1},{1,0},{2,3},{3,2},{4,5},{5,4},{6,7},{7,6},{8,9},{9,8},{10,11... | collective-permute-start | bytes 3145736 | tf_op jit(solution)/shard_map/ppermute | solution.py:384
  81.9 9.2 %collective-permute-start.15 = (bf16[128,1024]{1,0:T(8,128)(2,1)S(1)}, bf16[128,1024]{1,0:T(8,128)(2,1)S(1)}, u32[]{:S(2)}, u32[]{:S(2)}) collective-permute-start(bf16[128,1024]{1,0:T(8,128)(2,1)S(1)} %get-tuple-element.105), channel_id=1, source_target_pairs={{0,2},{1,3},{2,0},{3,1},{4,6},{5,7},{6,4},{7,5},{8,10},{9,11},{10,... | collective-permute-start | bytes 786440 | tf_op jit(solution)/shard_map/ppermute | solution.py:384
  87.8 15.3 %collective-permute-start.16 = (bf16[128,1024]{1,0:T(8,128)(2,1)S(1)}, bf16[128,1024]{1,0:T(8,128)(2,1)S(1)}, u32[]{:S(2)}, u32[]{:S(2)}) collective-permute-start(bf16[128,1024]{1,0:T(8,128)(2,1)S(1)} %get-tuple-element.106), channel_id=1, source_target_pairs={{0,8},{1,9},{2,10},{3,11},{4,12},{5,13},{6,14},{7,15},{8,0},{9,1},... | collective-permute-start | bytes 786440 | tf_op jit(solution)/shard_map/ppermute | solution.py:384
  91.1 14.4 %collective-permute-start.17 = (bf16[128,1024]{1,0:T(8,128)(2,1)S(1)}, bf16[128,1024]{1,0:T(8,128)(2,1)S(1)}, u32[]{:S(2)}, u32[]{:S(2)}) collective-permute-start(bf16[128,1024]{1,0:T(8,128)(2,1)S(1)} %get-tuple-element.113), channel_id=1, source_target_pairs={{0,4},{1,5},{2,6},{3,7},{4,0},{5,1},{6,2},{7,3},{8,12},{9,13},{10,... | collective-permute-start | bytes 786440 | tf_op jit(solution)/shard_map/ppermute | solution.py:384
  91.1 17.8 %collective-permute-start.18 = (bf16[128,1024]{1,0:T(8,128)(2,1)}, bf16[128,1024]{1,0:T(8,128)(2,1)S(1)}, u32[]{:S(2)}, u32[]{:S(2)}) collective-permute-start(bf16[128,1024]{1,0:T(8,128)(2,1)} %get-tuple-element.114), channel_id=1, source_target_pairs={{0,6},{1,7},{2,4},{3,5},{4,2},{5,3},{6,0},{7,1},{8,14},{9,15},{10,... | collective-permute-start | bytes 786440 | tf_op jit(solution)/shard_map/ppermute | solution.py:384
  103.1 17.4 %collective-permute-start.22 = (bf16[512,1024]{1,0:T(8,128)(2,1)}, bf16[512,1024]{1,0:T(8,128)(2,1)}, u32[]{:S(2)}, u32[]{:S(2)}) collective-permute-start(bf16[512,1024]{1,0:T(8,128)(2,1)} %get-tuple-element.122), channel_id=1, source_target_pairs={{0,1},{1,0},{2,3},{3,2},{4,5},{5,4},{6,7},{7,6},{8,9},{9,8},{10,11... | collective-permute-start | bytes 3145736 | tf_op jit(solution)/shard_map/ppermute | solution.py:384
  105.6 14.9 %collective-permute-start.23 = (bf16[512,1024]{1,0:T(8,128)(2,1)}, bf16[512,1024]{1,0:T(8,128)(2,1)}, u32[]{:S(2)}, u32[]{:S(2)}) collective-permute-start(bf16[512,1024]{1,0:T(8,128)(2,1)} %get-tuple-element.121), channel_id=1, source_target_pairs={{0,1},{1,0},{2,3},{3,2},{4,5},{5,4},{6,7},{7,6},{8,9},{9,8},{10,11... | collective-permute-start | bytes 3145736 | tf_op jit(solution)/shard_map/ppermute | solution.py:384
  113.6 14.0 %collective-permute-start.19 = (bf16[128,1024]{1,0:T(8,128)(2,1)S(1)}, bf16[128,1024]{1,0:T(8,128)(2,1)S(1)}, u32[]{:S(2)}, u32[]{:S(2)}) collective-permute-start(bf16[128,1024]{1,0:T(8,128)(2,1)S(1)} %get-tuple-element.116), channel_id=1, source_target_pairs={{0,8},{1,9},{2,10},{3,11},{4,12},{5,13},{6,14},{7,15},{8,0},{9,1},... | collective-permute-start | bytes 786440 | tf_op jit(solution)/shard_map/ppermute | solution.py:384
  (39 other events, 297.0 us)

commit v2 on v1

--- a/solution.py
+++ b/solution.py
@@ -17,7 +17,8 @@
 LAST = (((1,), (1,)), ((), ()))
 FIRST = (((0,), (0,)), ((), ()))
 SMALL = 12 * 1024 * 1024
-LARGE = 28 * 1024 * 1024
+LARGE = 60 * 1024 * 1024
+WEIGHT = 0.15 * 3.6e6
 
 
 def dot(a, b):
@@ -53,7 +54,7 @@
         return self.held[at]
 
 
-def kernel_call(body, operands, outs, scratch=(), flops=0, moved=1 << 22, limit=SMALL, scalars=()):
+def kernel_call(body, operands, outs, scratch=(), weight=0.0, limit=SMALL, scalars=()):
     count, out_count = len(operands), len(outs)
     staged = [place for place in range(count) if place not in scalars]
     held = [pltpu.VMEM(operands[place].shape, operands[place].dtype) for place in staged]
@@ -92,7 +93,7 @@
         out_specs=tuple(pl.BlockSpec(memory_space=pl.ANY) for _ in outs),
         scratch_shapes=held + results + [pltpu.SemaphoreType.DMA((len(staged),)), pltpu.SemaphoreType.DMA((out_count,))] + list(scratch),
         compiler_params=pltpu.CompilerParams(vmem_limit_bytes=limit),
-        cost_estimate=pl.CostEstimate(flops=1, bytes_accessed=1, transcendentals=0),
+        cost_estimate=pl.CostEstimate(flops=1, bytes_accessed=int(WEIGHT * weight) + 1, transcendentals=0),
     )(*operands)
 
 
@@ -126,9 +127,10 @@
 
 
 def pack_kernel(near, capacity, ins, outs, scratch, write):
-    chip, ids, far, rows, far_rows = ins
-    count = rows.shape[0]
-    blocks = ((ids[...], rows), (far_ids_of(far, count), far_rows))
+    chip, normed, far_normed = ins[0:3]
+    count = normed.shape[0] - RIM
+    rows, far_rows = ins[3:5] if len(ins) > 3 else (normed, far_normed)
+    blocks = ((ids_of(normed, count), rows), (ids_of(far_normed, count), far_rows))
     for block, (names, source) in enumerate(blocks):
         first, second = placements(columns_of(names), chip[0], near, capacity)
         packed = dot_first(first + second, source[0:count, :]).astype(BF16)
@@ -136,8 +138,8 @@
             out[block * capacity : (block + 1) * capacity, :] = packed[place * capacity : (place + 1) * capacity]
 
 
-def far_ids_of(far, count):
-    return far[count : count + RIM, 0:count][0:2].astype(F32).astype(jnp.int32)
+def ids_of(normed, count):
+    return normed[count : count + RIM, 0:count][0:2].astype(F32).astype(jnp.int32)
 
 
 def block_rows(refs, block, capacity):
@@ -166,9 +168,7 @@
         body(pl.ds(pl.multiple_of(step * LANES, LANES), LANES))
 
 
-def front_kernel(ins, outs, scratch, write):
-    frames, left, right, taps, gain = ins
-    conv_ref, normed_ref = outs
+def convolve_and_norm(frames, left, right, taps, gain, names, conv_ref, normed_ref, scratch):
     pad_ref, taps32_ref, mixed_ref, square_ref = scratch
     count, width = frames.shape
     fill_padded(pad_ref, left, frames, right)
@@ -179,29 +179,46 @@
         total = jnp.zeros((count, LANES), F32)
         for offset, rows in shifted(pad_ref, lanes, count):
             total = total + taps32_ref[offset - 1 : offset, lanes] * rows
-        conv_ref[:, lanes] = total
+        if conv_ref is not None:
+            conv_ref[:, lanes] = total
         mixed = pad_ref[RIM : RIM + count, lanes] + total * jax.nn.sigmoid(total)
         mixed_ref[:, lanes] = mixed
         square_ref[...] += mixed * mixed
 
     lane_loop(width, conv)
-    write(0)
     mean = jnp.sum(square_ref[...], axis=1, keepdims=True) / width
     inverse = lax.rsqrt(mean + NORM_EPS)
-    normed_ref[...] = (mixed_ref[...] * inverse * gain[...].astype(F32)).astype(BF16)
+    normed_ref[0:count, :] = (mixed_ref[...] * inverse * gain[...].astype(F32)).astype(BF16)
+    normed_ref[count : count + RIM, :] = names
+
+
+def front_kernel(ins, outs, scratch, write):
+    frames, left, right, taps, gain, names = ins
+    convolve_and_norm(frames, left, right, taps, gain, names[...], outs[0], outs[1], scratch)
+
+
+def far_front_kernel(near, capacity, ins, outs, scratch, write):
+    chip, frames, rims_and_names, taps, gain, normed = ins
+    far_normed, parts = outs[0], outs[1:]
+    left, right = rims_and_names[0:RIM, :], rims_and_names[RIM : 2 * RIM, :]
+    first, last = left.astype(F32)[0:1], right.astype(F32)[RIM - 1 : RIM]
+    names = jnp.concatenate([first, last, jnp.zeros((RIM - 2, frames.shape[1]), F32)], axis=0).astype(BF16)
+    convolve_and_norm(frames, left, right, taps, gain, names, None, far_normed, scratch)
+    write(0)
+    pack_kernel(near, capacity, (chip, normed, far_normed), parts, scratch, write)
 
 
 def result_kernel(near, capacity, ins, outs, scratch, write):
-    chip, ids, upstream_near, normed_near, far, normed_far, router = ins[0:7]
-    rows_refs = ins[7:]
+    chip, upstream_near, normed_near, upstream_far, normed_far, router = ins[0:6]
+    rows_refs = ins[6:]
     near_ref, far_ref, near_logits_ref, far_logits_ref, router_out_ref = outs
     count = upstream_near.shape[0]
     router_out = jnp.zeros(router_out_ref.shape, F32)
-    blocks = ((ids[...], upstream_near, normed_near), (far_ids_of(far, count), far, normed_far))
-    for block, (names, grad, normed) in reversed(list(enumerate(blocks))):
-        names = columns_of(names)
-        upstream = grad[0:count, :].astype(F32)
-        normed = normed[...]
+    blocks = ((upstream_near, normed_near), (upstream_far, normed_far))
+    for block, (grad, normed) in reversed(list(enumerate(blocks))):
+        names = columns_of(ids_of(normed, count))
+        upstream = grad[...].astype(F32)
+        normed = normed[0:count, :]
         gates = jax.nn.sigmoid(dot_last(normed, router[...]))
         rows = block_rows(rows_refs, block, capacity)
         added = jnp.zeros(upstream.shape, F32)
@@ -221,12 +238,12 @@
 
 
 def back_kernel(near, capacity, ins, outs, scratch, write):
-    chip, ids, logits_near, far, logits_far, router = ins[0:6]
+    chip, normed_near, logits_near, normed_far, logits_far, router = ins[0:6]
     rows_refs = ins[6:]
     count = outs[0].shape[0]
-    blocks = ((ids[...], logits_near), (far_ids_of(far, count), logits_far))
-    for block, (names, logits) in reversed(list(enumerate(blocks))):
-        first, second = placements(columns_of(names), chip[0], near, capacity)
+    blocks = ((normed_near, logits_near), (normed_far, logits_far))
+    for block, (normed, logits) in reversed(list(enumerate(blocks))):
+        first, second = placements(columns_of(ids_of(normed, count)), chip[0], near, capacity)
         total = dot(first + second, block_rows(rows_refs, block, capacity))
         outs[block][...] = (total + dot(logits[...], router[...])).astype(outs[block].dtype)
         write(block)
@@ -407,41 +424,53 @@
     mine = (jnp.arange(experts, dtype=jnp.int32) == chip).astype(F32).reshape(1, experts)
     cross = functools.partial(swap, count=devices, bit=devices // 2)
 
-    named = jnp.pad(ids.astype(BF16), ((0, RIM - 2), (0, width - count)))
-    far_grad = cross(jnp.concatenate([out_grad, named]))
-    left, right = rims(frames[0:RIM], frames[count - RIM : count], devices)
+    frames, head, tail = lax.optimization_barrier((frames, frames[0:RIM], frames[count - RIM : count]))
+    left, right = rims(head, tail, devices)
+    far_frames = cross(frames)
+    names = jnp.pad(ids.astype(BF16), ((0, RIM - 2), (0, width - count)))
     weight_in, weight_out = expert_in[0], expert_out[0]
     other_in = swap(weight_in, devices, 1)
     other_out = swap(weight_out, devices, 1)
+    left, right, other_in, other_out = lax.optimization_barrier((left, right, other_in, other_out))
 
     model32, model16 = shape((count, width), F32), shape((count, width), BF16)
+    named16 = shape((count + RIM, width), BF16)
+    front_scratch = (pad, taps32, pltpu.VMEM((count, width), F32), pltpu.VMEM((count, LANES), F32))
     conv_out, normed = kernel_call(
-        front_kernel,
-        (frames, left, right, taps, gain),
-        (model32, model16),
-        (pad, taps32, pltpu.VMEM((count, width), F32), pltpu.VMEM((count, LANES), F32)),
-    )
-    far_normed = cross(normed)
-
+        front_kernel, (frames, left, right, taps, gain, names), (model32, named16), front_scratch, weight=3.3
+    )
+    far_rims = cross(jnp.concatenate([names[0:1], left[1:], right[: RIM - 1], names[1:2]]))
+    far_rims, far_frames, out_grad = lax.optimization_barrier((far_rims, far_frames, out_grad))
+    far_grad = cross(out_grad)
     part = (shape((2 * capacity, width), BF16),) * near
-    pack = functools.partial(pack_kernel, near, capacity)
-    grads = exchange(
-        kernel_call(pack, (chips, ids, far_grad, out_grad, far_grad), part, scalars=(0,)), devices
-    )
-    rows = exchange(
-        kernel_call(pack, (chips, ids, far_grad, normed, far_normed), part, scalars=(0,)), devices
-    )
+    far_normed, *parts = kernel_call(
+        functools.partial(far_front_kernel, near, capacity),
+        (chips, far_frames, far_rims, taps, gain, normed),
+        (named16, *part),
+        front_scratch,
+        weight=0.0,
+        scalars=(0,),
+    )
+    rows = exchange(parts, devices)
+    parts = kernel_call(
+        functools.partial(pack_kernel, near, capacity),
+        (chips, normed, far_normed, out_grad, far_grad),
+        part,
+        weight=0.0,
+        scalars=(0,),
+    )
+    rows[0:3], parts = lax.optimization_barrier((rows[0:3], parts))
+    grads = exchange(parts, devices)
 
     half = weight_in.shape[1]
     wide = shape((slots, half), F32)
     narrow = shape((slots, half), BF16)
     model = shape((slots, width), BF16)
-    work = 8 * slots * width * half
     outs = kernel_call(
         functools.partial(forward_kernel, near),
         (*rows, weight_in, other_in, weight_out, other_out),
         part + (model, wide, wide, narrow, narrow),
-        flops=work, moved=1 << 24, limit=LARGE,
+        weight=0.0, limit=LARGE,
     )
     parts_out, (all_rows, *pre_act), active = outs[0:near], outs[near : near + 3], outs[near + 3 :]
     results = exchange(parts_out, devices)
@@ -450,33 +479,36 @@
         (*grads, all_rows, router, mine, weight_out, other_out, *pre_act, weight_in, other_in),
         part + (narrow, narrow, model),
         (pltpu.VMEM((slots, width), BF16),),
-        flops=work, moved=1 << 24, limit=LARGE,
-    )
-    results, all_rows, active, outs = lax.optimization_barrier((results, all_rows, active, outs))
+        weight=0.0, limit=LARGE,
+    )
+    results, outs, all_rows, active = lax.optimization_barrier((results, outs, all_rows, active))
     parts_in, pre_grad, grad_rows = outs[0:near], outs[near : near + 2], outs[near + 2]
     backs = exchange(parts_in, devices)
-    far_rows, far_grads, far_active, far_pre = [
-        swap(values, devices, 1) for values in (all_rows, grad_rows, active[1], pre_grad[1])
+    logits = shape((count, experts), BF16)
+    near_sum, far_sum, near_logits, far_logits, router_local = kernel_call(
+        functools.partial(result_kernel, near, capacity),
+        (chips, out_grad, normed, far_grad, far_normed, router, *results),
+        (model32, model16, logits, logits, shape((experts, width), F32)),
+        weight=0.0,
+        scalars=(0,),
+    )
+    far_sum = cross(far_sum)
+    near_back, far_back = kernel_call(
+        functools.partial(back_kernel, near, capacity),
+        (chips, normed, near_logits, far_normed, far_logits, router, *backs),
+        (model32, model16),
+        weight=0.0,
+        scalars=(0,),
+    )
+    far_back, far_sum, all_rows, active, grad_rows, pre_grad = lax.optimization_barrier(
+        (far_back, far_sum, all_rows, active, grad_rows, pre_grad)
+    )
+    far_back = cross(far_back)
+    far_rows, far_active, far_grads, far_pre = [
+        swap(values, devices, 1) for values in (all_rows, active[1], grad_rows, pre_grad[1])
     ]
     expert_out_grad = (dot_first(active[0], grad_rows) + dot_first(far_active, far_grads)).astype(BF16)
     expert_in_grad = (dot_first(all_rows, pre_grad[0]) + dot_first(far_rows, far_pre)).astype(BF16)
-
-    logits = shape((count, experts), BF16)
-    near_sum, far_sum, near_logits, far_logits, router_local = kernel_call(
-        functools.partial(result_kernel, near, capacity),
-        (chips, ids, out_grad, normed, far_grad, far_normed, router, *results),
-        (model32, model16, logits, logits, shape((experts, width), F32)),
-        scalars=(0,),
-    )
-    far_sum = cross(far_sum)
-    backs[1], far_sum = lax.optimization_barrier((backs[1], far_sum))
-    near_back, far_back = kernel_call(
-        functools.partial(back_kernel, near, capacity),
-        (chips, ids, near_logits, far_grad, far_logits, router, *backs),
-        (model32, model16),
-        scalars=(0,),
-    )
-    far_back = cross(far_back)
     far_back, expert_in_grad, expert_out_grad = lax.optimization_barrier((far_back, expert_in_grad, expert_out_grad))
 
     rim = shape((RIM, width), BF16)
@@ -488,6 +520,7 @@
         (core, frames, left, right, conv_out, out_grad, gain, near_sum, far_sum, router_local, near_back, far_back),
         (model16, model32, model16, rim, rim, columns, columns),
         (pad, pltpu.VMEM((lines, width), F32)),
+        weight=0.0,
         scalars=(0,),
     )
     grad_left, grad_right = rims(head, tail, devices)
@@ -495,12 +528,12 @@
     bit = 2
     while bit < devices:
         other = swap(local, devices, bit)
-        if bit == 2:
+        if bit == devices // 4:
             other, grad_left, grad_right = lax.optimization_barrier((other, grad_left, grad_right))
             (frames_grad,) = kernel_call(
-                frames_kernel, (mixed_grad, conv_grad, grad_left, grad_right, taps), (model16,), (pad, taps32)
+                frames_kernel, (mixed_grad, conv_grad, grad_left, grad_right, taps), (model16,), (pad, taps32), weight=0.0
             )
-        if bit == 4:
+        if 2 * bit == devices:
             other, frames_grad = lax.optimization_barrier((other, frames_grad))
         local = local + other
         bit *= 2
@@ -508,6 +541,7 @@
         last_kernel,
         (core, local, swap(local, devices, 1)),
         (shape((KSIZE, width), F32), shape((1, width), F32), shape((experts, width), F32)),
+        weight=0.0,
         scalars=(0,),
     )
     return (

time: 156 us -> 146 us (0.936)
  waiting for transfers between devices: 50.6 us -> 33.2 us
  Pallas kernels: 36.9 us -> 44.6 us
  starting transfers between devices: 39.4 us -> 43.9 us
  local copies, waits for them, and re-layouts: 13.4 us -> 10.2 us
  matrix products: 12.5 us -> 10.9 us
    ppermute x27 -> x28, waiting for transfers between devices: 48.6 us -> 29.9 us  [swap(): return lax.ppermute(values, 'seq', [(i, i ^ bit) for i in range(count)])]
    pallas_call x10, Pallas kernels: 36.9 us -> 44.6 us  [kernel_call(): pl.pallas_call(kernel, out_shape=tuple(outs), in_specs=[pl.BlockSpec(memo...]
    ppermute x27 -> x28, starting transfers between devices: 32.7 us -> 37.7 us  [swap(): return lax.ppermute(values, 'seq', [(i, i ^ bit) for i in range(count)])]
    unnamed x64 -> x48, local copies, waits for them, and re-layouts: 11.9 us -> 8.68 us
    dot_general x4, matrix products: 12.5 us -> 10.9 us  [dot_first(): return lax.dot_general(a, b, FIRST, preferred_element_type=F32)]
  transfers between devices with their start and end apart: 31 -> 32, of which waited for: 11 -> 12; matrix products, arithmetic and copies ran while one was open for 10% -> 9% of each run, Pallas kernels for 21% -> 28%
where the time goes in v2:
time: 146 us; the launch traced here: 145 us
  Pallas kernels  44.6 us (31%)
  starting transfers between devices  43.9 us (30%)
  waiting for transfers between devices  33.2 us (23%)
  matrix products  10.9 us (7%)
  local copies, waits for them, and re-layouts  10.2 us (7%)
    pallas_call x10, Pallas kernels, kernel_call(): pl.pallas_call(kernel, out_shape=tuple(outs), in_specs=[pl.BlockSpec(memo...  44.6 us
    ppermute x28, starting transfers between devices, swap(): return lax.ppermute(values, 'seq', [(i, i ^ bit) for i in range(count)])  37.7 us
    ppermute x28, waiting for transfers between devices, swap(): return lax.ppermute(values, 'seq', [(i, i ^ bit) for i in range(count)])  29.9 us
    dot_general x4, matrix products, dot_first(): return lax.dot_general(a, b, FIRST, preferred_element_type=F32)  10.9 us
    unnamed x48, local copies, waits for them, and re-layouts  8.68 us
    ppermute x2, starting transfers between devices, rims(): left = lax.ppermute(tail, 'seq', [(i, i + 1) for i in range(ends)])  3.61 us
    ppermute x2, waiting for transfers between devices, rims(): right = lax.ppermute(head, 'seq', [(i + 1, i) for i in range(ends)])  3.29 us
  transfers between devices with their start and end apart: 32, of which 12 were waited for; matrix products, arithmetic and copies ran while one was open for 9% of the time, Pallas kernels for 28%

profile of v2, /device:TPU:0, one launch (start us, length us, event | category | flops | bytes accessed | tf_op | source)
XLA Modules:
  0.0 145.3 jit_solution(4427480889650276927)
XLA Ops:
  2.0 2.3 %collective-permute-start = (bf16[16,1024]{1,0:T(8,128)(2,1)S(1)}, bf16[16,1024]{1,0:T(8,128)(2,1)S(1)}, u32[]{:S(2)}, u32[]{:S(2)}) collective-permute-start(bf16[16,1024]{1,0:T(8,128)(2,1)S(1)} %get-tuple-element.99), channel_id=1, source_target_pairs={{0,1},{1,2},{2,3},{3,4},{4,5},{5,6},{6,7},{7,8},{8,9},{9,10},{10,1... | collective-permute-start | bytes 98312 | tf_op jit(solution)/shard_map/ppermute | solution.py:395
  5.6 6.9 %collective-permute-start.5 = (bf16[128,1024]{1,0:T(8,128)(2,1)}, bf16[128,1024]{1,0:T(8,128)(2,1)S(1)}, u32[]{:S(2)}, u32[]{:S(2)}) collective-permute-start(bf16[128,1024]{1,0:T(8,128)(2,1)} %refs_1_.1), channel_id=1, source_target_pairs={{0,8},{1,9},{2,10},{3,11},{4,12},{5,13},{6,14},{7,15},{8,0},{9,1},... | collective-permute-start | bytes 786440 | tf_op jit(solution)/shard_map/ppermute | solution.py:401
  15.3 7.0 %collective-permute-start.4 = (bf16[32,1024]{1,0:T(8,128)(2,1)S(1)}, bf16[32,1024]{1,0:T(8,128)(2,1)S(1)}, u32[]{:S(2)}, u32[]{:S(2)}) collective-permute-start(bf16[32,1024]{1,0:T(8,128)(2,1)S(1)} %pad_maximum_fusion), channel_id=1, source_target_pairs={{0,8},{1,9},{2,10},{3,11},{4,12},{5,13},{6,14},{7,15},{8,0},{9,1},... | collective-permute-start | bytes 196616 | tf_op jit(solution)/shard_map/ppermute | solution.py:401
  24.8 3.3 %shard_map.135 = (f32[128,1024]{1,0:T(8,128)S(1)}, bf16[144,1024]{1,0:T(8,128)(2,1)S(1)}) custom-call(bf16[128,1024]{1,0:T(8,128)(2,1)S(1)} %copy-done.2, bf16[16,1024]{1,0:T(8,128)(2,1)S(1)} %collective-permute-done.refs_1_.refs_2_, bf16[16,1024]{1,0:T(8,128)(2,1)S(1)} %collective-permute-done.1.refs_2_.refs_3_, bf16[31,1024]{1,0:T(8,128)(2,1)S(1)} %copy-done.4, ...), custom_call_target="tpu_custom_call" | custom-call | flops 1 | bytes 1782001 | tf_op jit(solution)/shard_map/pallas_call | solution.py:89
  29.1 4.9 %shard_map.136 = (bf16[144,1024]{1,0:T(8,128)(2,1)S(1)}, bf16[128,1024]{1,0:T(8,128)(2,1)S(1)}, bf16[128,1024]{1,0:T(8,128)(2,1)S(1)}, bf16[128,1024]{1,0:T(8,128)(2,1)S(1)}, bf16[128,1024]{1,0:T(8,128)(2,1)S(1)}) custom-call(s32[1]{0:T(128)} %bitcast.4.refs_0_, bf16[128,1024]{1,0:T(8,128)(2,1)S(1)} %collective-permute-done.5.refs_1_, ...), custom_call_target="tpu_custom_call" | custom-call | flops 1 | bytes 1 | tf_op jit(solution)/shard_map/pallas_call | solution.py:89
  34.7 3.1 %collective-permute-start.8 = (bf16[128,1024]{1,0:T(8,128)(2,1)S(1)}, bf16[128,1024]{1,0:T(8,128)(2,1)S(1)}, u32[]{:S(2)}, u32[]{:S(2)}) collective-permute-start(bf16[128,1024]{1,0:T(8,128)(2,1)S(1)} %get-tuple-element.111), channel_id=1, source_target_pairs={{0,4},{1,5},{2,6},{3,7},{4,0},{5,1},{6,2},{7,3},{8,12},{9,13},{10,... | collective-permute-start | bytes 786440 | tf_op jit(solution)/shard_map/ppermute | solution.py:401
  43.5 2.6 %collective-permute-done.8.refs_2_ = bf16[128,1024]{1,0:T(8,128)(2,1)S(1)} collective-permute-done((bf16[128,1024]{1,0:T(8,128)(2,1)S(1)}, bf16[128,1024]{1,0:T(8,128)(2,1)S(1)}, u32[]{:S(2)}, u32[]{:S(2)}) %collective-permute-start.8) | collective-permute-done | bytes 262176 | tf_op jit(solution)/shard_map/ppermute | solution.py:401
  49.6 2.7 %collective-permute-done.9.refs_3_ = bf16[128,1024]{1,0:T(8,128)(2,1)S(1)} collective-permute-done((bf16[128,1024]{1,0:T(8,128)(2,1)S(1)}, bf16[128,1024]{1,0:T(8,128)(2,1)S(1)}, u32[]{:S(2)}, u32[]{:S(2)}) %collective-permute-start.9) | collective-permute-done | bytes 262176 | tf_op jit(solution)/shard_map/ppermute | solution.py:401
  53.0 9.6 %shard_map.138 = (bf16[128,1024]{1,0:T(8,128)(2,1)}, bf16[128,1024]{1,0:T(8,128)(2,1)}, bf16[128,1024]{1,0:T(8,128)(2,1)}, bf16[128,1024]{1,0:T(8,128)(2,1)}, bf...) custom-call(bf16[128,1024]{1,0:T(8,128)(2,1)} %copy-done.10, ...), custom_call_target="tpu_custom_call" | custom-call | flops 1 | bytes 1 | tf_op jit(solution)/shard_map/pallas_call | solution.py:89
  67.5 11.9 %shard_map.139 = (bf16[128,1024]{1,0:T(8,128)(2,1)}, bf16[128,1024]{1,0:T(8,128)(2,1)}, bf16[128,1024]{1,0:T(8,128)(2,1)}, bf16[128,1024]{1,0:T(8,128)(2,1)}, bf...) custom-call(bf16[128,1024]{1,0:T(8,128)(2,1)} %copy-done.7, ...), custom_call_target="tpu_custom_call" | custom-call | flops 1 | bytes 1 | tf_op jit(solution)/shard_map/pallas_call | solution.py:89
  83.0 2.8 %shard_map.140 = (f32[128,1024]{1,0:T(8,128)S(1)}, bf16[128,1024]{1,0:T(8,128)(2,1)S(1)}, bf16[128,8]{1,0:T(8,128)(2,1)S(1)}, bf16[128,8]{1,0:T(8,128)(2,1)S(1)}, f32[8,1024]{1,0:T(8,128)S(1)}) custom-call(s32[1]{0:T(128)} %bitcast.4.refs_0_, bf16[128,1024]{1,0:T(8,128)(2,1)S(1)} %copy-done.1, ...), custom_call_target="tpu_custom_call" | custom-call | flops 1 | bytes 1 | tf_op jit(solution)/shard_map/pallas_call | solution.py:89
  88.0 7.4 %collective-permute-done.17.refs_8_ = bf16[128,1024]{1,0:T(8,128)(2,1)S(1)} collective-permute-done((bf16[128,1024]{1,0:T(8,128)(2,1)}, bf16[128,1024]{1,0:T(8,128)(2,1)S(1)}, u32[]{:S(2)}, u32[]{:S(2)}) %collective-permute-start.17) | collective-permute-done | bytes 262176 | tf_op jit(solution)/shard_map/ppermute | solution.py:401
  95.4 3.9 %collective-permute-done.18.refs_9_ = bf16[128,1024]{1,0:T(8,128)(2,1)S(1)} collective-permute-done((bf16[128,1024]{1,0:T(8,128)(2,1)}, bf16[128,1024]{1,0:T(8,128)(2,1)S(1)}, u32[]{:S(2)}, u32[]{:S(2)}) %collective-permute-start.18) | collective-permute-done | bytes 262176 | tf_op jit(solution)/shard_map/ppermute | solution.py:401
  100.2 2.2 %shard_map.141 = (f32[128,1024]{1,0:T(8,128)S(1)}, bf16[128,1024]{1,0:T(8,128)(2,1)S(1)}) custom-call(s32[1]{0:T(128)} %bitcast.4.refs_0_, bf16[144,1024]{1,0:T(8,128)(2,1)S(1)} %get-tuple-element.105.refs_5_.refs_1_.refs_2_, bf16[128,8]{1,0:T(8,128)(2,1)S(1)} %get-tuple-element.147.refs_2_, ...), custom_call_target="tpu_custom_call" | custom-call | flops 1 | bytes 1 | tf_op jit(solution)/shard_map/pallas_call | solution.py:89
  105.5 3.0 %collective-permute-done.24 = bf16[512,1024]{1,0:T(8,128)(2,1)} collective-permute-done((bf16[512,1024]{1,0:T(8,128)(2,1)}, bf16[512,1024]{1,0:T(8,128)(2,1)}, u32[]{:S(2)}, u32[]{:S(2)}) %collective-permute-start.24) | collective-permute-done | bytes 1048608 | tf_op jit(solution)/shard_map/ppermute | solution.py:401
  108.5 2.8 %fusion.2 = f32[1024,1024]{1,0:T(8,128)S(1)} fusion(bf16[512,1024]{1,0:T(8,128)(2,1)} %collective-permute-done.23, bf16[512,1024]{1,0:T(8,128)(2,1)} %collective-permute-done.24), kind=kOutput, calls=%fused_computation.9 | convolution fusion | flops 1073741824 | bytes 6291456 | tf_op jit(solution)/shard_map/dot_general | solution.py:33
  111.4 2.7 %add_convert_fusion = bf16[1024,1024]{1,0:T(8,128)(2,1)} fusion(f32[1024,1024]{1,0:T(8,128)S(1)} %fusion.2, bf16[512,1024]{1,0:T(8,128)(2,1)S(1)} %copy-done.15, bf16[512,1024]{1,0:T(8,128)(2,1)S(1)} %copy-done.17), kind=kOutput, calls=%fused_computation | convolution fusion | flops 1075838976 | bytes 8388608 | tf_op jit(solution)/shard_map/dot_general | solution.py:33
  114.1 2.7 %fusion.1 = f32[1024,1024]{1,0:T(8,128)S(1)} fusion(bf16[512,1024]{1,0:T(8,128)(2,1)S(1)} %collective-permute-done.21, bf16[512,1024]{1,0:T(8,128)(2,1)} %collective-permute-done.22), kind=kOutput, calls=%fused_computation.8 | convolution fusion | flops 1073741824 | bytes 6291456 | tf_op jit(solution)/shard_map/dot_general | solution.py:33
  116.8 2.7 %add_convert_fusion.1 = bf16[1024,1024]{1,0:T(8,128)(2,1)} fusion(f32[1024,1024]{1,0:T(8,128)S(1)} %fusion.1, bf16[512,1024]{1,0:T(8,128)(2,1)S(1)} %copy-done.14, bf16[512,1024]{1,0:T(8,128)(2,1)S(1)} %copy-done.16), kind=kOutput, calls=%fused_computation.1 | convolution fusion | flops 1075838976 | bytes 8388608 | tf_op jit(solution)/shard_map/dot_general | solution.py:33
  119.5 3.4 %shard_map.142 = (bf16[128,1024]{1,0:T(8,128)(2,1)}, f32[128,1024]{1,0:T(8,128)S(1)}, bf16[128,1024]{1,0:T(8,128)(2,1)S(1)}, bf16[16,1024]{1,0:T(8,128)(2,1)S(1)...) custom-call(s32[1]{0:T(128)} %bitcast.refs_0_, bf16[128,1024]{1,0:T(8,128)(2,1)S(1)} %copy-done.3, ...), custom_call_target="tpu_custom_call" | custom-call | flops 1 | bytes 1 | tf_op jit(solution)/shard_map/pallas_call | solution.py:89
  125.6 3.2 %collective-permute-done.26 = f32[40,512]{1,0:T(8,128)S(1)} collective-permute-done((f32[40,512]{1,0:T(8,128)S(1)}, f32[40,512]{1,0:T(8,128)S(1)}, u32[]{:S(2)}, u32[]{:S(2)}) %collective-permute-start.26) | collective-permute-done | bytes 81952 | tf_op jit(solution)/shard_map/ppermute | solution.py:401
  131.6 3.3 %collective-permute-done.29.refs_3_ = bf16[16,1024]{1,0:T(8,128)(2,1)S(1)} collective-permute-done((bf16[16,1024]{1,0:T(8,128)(2,1)S(1)}, bf16[16,1024]{1,0:T(8,128)(2,1)S(1)}, u32[]{:S(2)}, u32[]{:S(2)}) %collective-permute-start.29) | collective-permute-done | bytes 32800 | tf_op jit(solution)/shard_map/ppermute | solution.py:396
  134.9 4.3 %collective-permute-start.30 = (f32[40,512]{1,0:T(8,128)S(1)}, f32[40,512]{1,0:T(8,128)S(1)}, u32[]{:S(2)}, u32[]{:S(2)}) collective-permute-start(f32[40,512]{1,0:T(8,128)S(1)} %add.30), channel_id=1, source_target_pairs={{0,8},{1,9},{2,10},{3,11},{4,12},{5,13},{6,14},{7,15},{8,0},{9,1},... | collective-permute-start | bytes 245768 | tf_op jit(solution)/shard_map/ppermute | solution.py:401
  139.1 3.7 %shard_map.143 = bf16[128,1024]{1,0:T(8,128)(2,1)} custom-call(f32[128,1024]{1,0:T(8,128)S(1)} %get-tuple-element.178.refs_0_, bf16[128,1024]{1,0:T(8,128)(2,1)S(1)} %get-tuple-element.179.refs_1_, bf16[16,1024]{1,0:T(8,128)(2,1)S(1)} %collective-permute-done.28.refs_2_, bf16[16,1024]{1,0:T(8,128)(2,1)S(1)} %collective-permute-done.29.refs_3_, ...), custom_call_target="tpu_custom_call" | custom-call | flops 1 | bytes 1 | tf_op jit(solution)/shard_map/pallas_call | solution.py:89
  (114 shorter events, 41.6 us)
Async XLA Ops:
  0.6 12.6 %collective-permute-start.2 = (bf16[1024,1024]{1,0:T(8,128)(2,1)}, bf16[1024,1024]{1,0:T(8,128)(2,1)S(1)}, u32[]{:S(2)}, u32[]{:S(2)}) collective-permute-start(bf16[1024,1024]{1,0:T(8,128)(2,1)} %bitcast.24), channel_id=1, source_target_pairs={{0,1},{1,0},{2,3},{3,2},{4,5},{5,4},{6,7},{7,6},{8,9},{9,8},{10,11... | collective-permute-start | bytes 6291464 | tf_op jit(solution)/shard_map/ppermute | solution.py:401
  1.1 12.1 %collective-permute-start.3 = (bf16[1024,1024]{1,0:T(8,128)(2,1)}, bf16[1024,1024]{1,0:T(8,128)(2,1)S(1)}, u32[]{:S(2)}, u32[]{:S(2)}) collective-permute-start(bf16[1024,1024]{1,0:T(8,128)(2,1)} %bitcast.27), channel_id=1, source_target_pairs={{0,1},{1,0},{2,3},{3,2},{4,5},{5,4},{6,7},{7,6},{8,9},{9,8},{10,11... | collective-permute-start | bytes 6291464 | tf_op jit(solution)/shard_map/ppermute | solution.py:401
  2.0 11.2 %collective-permute-start = (bf16[16,1024]{1,0:T(8,128)(2,1)S(1)}, bf16[16,1024]{1,0:T(8,128)(2,1)S(1)}, u32[]{:S(2)}, u32[]{:S(2)}) collective-permute-start(bf16[16,1024]{1,0:T(8,128)(2,1)S(1)} %get-tuple-element.99), channel_id=1, source_target_pairs={{0,1},{1,2},{2,3},{3,4},{4,5},{5,6},{6,7},{7,8},{8,9},{9,10},{10,1... | collective-permute-start | bytes 98312 | tf_op jit(solution)/shard_map/ppermute | solution.py:395
  4.3 8.9 %collective-permute-start.1 = (bf16[16,1024]{1,0:T(8,128)(2,1)S(1)}, bf16[16,1024]{1,0:T(8,128)(2,1)S(1)}, u32[]{:S(2)}, u32[]{:S(2)}) collective-permute-start(bf16[16,1024]{1,0:T(8,128)(2,1)S(1)} %get-tuple-element.100), channel_id=1, source_target_pairs={{1,0},{2,1},{3,2},{4,3},{5,4},{6,5},{7,6},{8,7},{9,8},{10,9},{11,1... | collective-permute-start | bytes 98312 | tf_op jit(solution)/shard_map/ppermute | solution.py:396
  5.6 22.5 %collective-permute-start.5 = (bf16[128,1024]{1,0:T(8,128)(2,1)}, bf16[128,1024]{1,0:T(8,128)(2,1)S(1)}, u32[]{:S(2)}, u32[]{:S(2)}) collective-permute-start(bf16[128,1024]{1,0:T(8,128)(2,1)} %refs_1_.1), channel_id=1, source_target_pairs={{0,8},{1,9},{2,10},{3,11},{4,12},{5,13},{6,14},{7,15},{8,0},{9,1},... | collective-permute-start | bytes 786440 | tf_op jit(solution)/shard_map/ppermute | solution.py:401
  15.3 12.8 %collective-permute-start.4 = (bf16[32,1024]{1,0:T(8,128)(2,1)S(1)}, bf16[32,1024]{1,0:T(8,128)(2,1)S(1)}, u32[]{:S(2)}, u32[]{:S(2)}) collective-permute-start(bf16[32,1024]{1,0:T(8,128)(2,1)S(1)} %pad_maximum_fusion), channel_id=1, source_target_pairs={{0,8},{1,9},{2,10},{3,11},{4,12},{5,13},{6,14},{7,15},{8,0},{9,1},... | collective-permute-start | bytes 196616 | tf_op jit(solution)/shard_map/ppermute | solution.py:401
  28.1 12.6 %collective-permute-start.6 = (bf16[128,1024]{1,0:T(8,128)(2,1)}, bf16[128,1024]{1,0:T(8,128)(2,1)S(1)}, u32[]{:S(2)}, u32[]{:S(2)}) collective-permute-start(bf16[128,1024]{1,0:T(8,128)(2,1)} %refs_5_), channel_id=1, source_target_pairs={{0,8},{1,9},{2,10},{3,11},{4,12},{5,13},{6,14},{7,15},{8,0},{9,1},... | collective-permute-start | bytes 786440 | tf_op jit(solution)/shard_map/ppermute | solution.py:401
  34.7 8.8 %collective-permute-start.7 = (bf16[128,1024]{1,0:T(8,128)(2,1)S(1)}, bf16[128,1024]{1,0:T(8,128)(2,1)S(1)}, u32[]{:S(2)}, u32[]{:S(2)}) collective-permute-start(bf16[128,1024]{1,0:T(8,128)(2,1)S(1)} %get-tuple-element.110), channel_id=1, source_target_pairs={{0,2},{1,3},{2,0},{3,1},{4,6},{5,7},{6,4},{7,5},{8,10},{9,11},{10,... | collective-permute-start | bytes 786440 | tf_op jit(solution)/shard_map/ppermute | solution.py:401
  34.7 11.4 %collective-permute-start.8 = (bf16[128,1024]{1,0:T(8,128)(2,1)S(1)}, bf16[128,1024]{1,0:T(8,128)(2,1)S(1)}, u32[]{:S(2)}, u32[]{:S(2)}) collective-permute-start(bf16[128,1024]{1,0:T(8,128)(2,1)S(1)} %get-tuple-element.111), channel_id=1, source_target_pairs={{0,4},{1,5},{2,6},{3,7},{4,0},{5,1},{6,2},{7,3},{8,12},{9,13},{10,... | collective-permute-start | bytes 786440 | tf_op jit(solution)/shard_map/ppermute | solution.py:401
  37.8 14.4 %collective-permute-start.9 = (bf16[128,1024]{1,0:T(8,128)(2,1)S(1)}, bf16[128,1024]{1,0:T(8,128)(2,1)S(1)}, u32[]{:S(2)}, u32[]{:S(2)}) collective-permute-start(bf16[128,1024]{1,0:T(8,128)(2,1)S(1)} %get-tuple-element.119), channel_id=1, source_target_pairs={{0,6},{1,7},{2,4},{3,5},{4,2},{5,3},{6,0},{7,1},{8,14},{9,15},{10,... | collective-permute-start | bytes 786440 | tf_op jit(solution)/shard_map/ppermute | solution.py:401
  46.1 18.0 %collective-permute-start.13 = (bf16[128,1024]{1,0:T(8,128)(2,1)S(1)}, bf16[128,1024]{1,0:T(8,128)(2,1)S(1)}, u32[]{:S(2)}, u32[]{:S(2)}) collective-permute-start(bf16[128,1024]{1,0:T(8,128)(2,1)S(1)} %get-tuple-element.127), channel_id=1, source_target_pairs={{0,2},{1,3},{2,0},{3,1},{4,6},{5,7},{6,4},{7,5},{8,10},{9,11},{10,... | collective-permute-start | bytes 786440 | tf_op jit(solution)/shard_map/ppermute | solution.py:401
  47.1 19.6 %collective-permute-start.14 = (bf16[128,1024]{1,0:T(8,128)(2,1)S(1)}, bf16[128,1024]{1,0:T(8,128)(2,1)S(1)}, u32[]{:S(2)}, u32[]{:S(2)}) collective-permute-start(bf16[128,1024]{1,0:T(8,128)(2,1)S(1)} %get-tuple-element.128), channel_id=1, source_target_pairs={{0,4},{1,5},{2,6},{3,7},{4,0},{5,1},{6,2},{7,3},{8,12},{9,13},{10,... | collective-permute-start | bytes 786440 | tf_op jit(solution)/shard_map/ppermute | solution.py:401
  48.5 18.2 %collective-permute-start.15 = (bf16[128,1024]{1,0:T(8,128)(2,1)S(1)}, bf16[128,1024]{1,0:T(8,128)(2,1)S(1)}, u32[]{:S(2)}, u32[]{:S(2)}) collective-permute-start(bf16[128,1024]{1,0:T(8,128)(2,1)S(1)} %get-tuple-element.129), channel_id=1, source_target_pairs={{0,6},{1,7},{2,4},{3,5},{4,2},{5,3},{6,0},{7,1},{8,14},{9,15},{10,... | collective-permute-start | bytes 786440 | tf_op jit(solution)/shard_map/ppermute | solution.py:401
  62.6 16.7 %collective-permute-start.10 = (bf16[128,1024]{1,0:T(8,128)(2,1)}, bf16[128,1024]{1,0:T(8,128)(2,1)S(1)}, u32[]{:S(2)}, u32[]{:S(2)}) collective-permute-start(bf16[128,1024]{1,0:T(8,128)(2,1)} %get-tuple-element.123), channel_id=1, source_target_pairs={{0,2},{1,3},{2,0},{3,1},{4,6},{5,7},{6,4},{7,5},{8,10},{9,11},{10,... | collective-permute-start | bytes 786440 | tf_op jit(solution)/shard_map/ppermute | solution.py:401
  63.7 15.7 %collective-permute-start.11 = (bf16[128,1024]{1,0:T(8,128)(2,1)}, bf16[128,1024]{1,0:T(8,128)(2,1)S(1)}, u32[]{:S(2)}, u32[]{:S(2)}) collective-permute-start(bf16[128,1024]{1,0:T(8,128)(2,1)} %get-tuple-element.124), channel_id=1, source_target_pairs={{0,4},{1,5},{2,6},{3,7},{4,0},{5,1},{6,2},{7,3},{8,12},{9,13},{10,... | collective-permute-start | bytes 786440 | tf_op jit(solution)/shard_map/ppermute | solution.py:401
  64.1 15.3 %collective-permute-start.12 = (bf16[128,1024]{1,0:T(8,128)(2,1)}, bf16[128,1024]{1,0:T(8,128)(2,1)S(1)}, u32[]{:S(2)}, u32[]{:S(2)}) collective-permute-start(bf16[128,1024]{1,0:T(8,128)(2,1)} %get-tuple-element.125), channel_id=1, source_target_pairs={{0,6},{1,7},{2,4},{3,5},{4,2},{5,3},{6,0},{7,1},{8,14},{9,15},{10,... | collective-permute-start | bytes 786440 | tf_op jit(solution)/shard_map/ppermute | solution.py:401
  79.4 8.6 %collective-permute-start.16 = (bf16[128,1024]{1,0:T(8,128)(2,1)}, bf16[128,1024]{1,0:T(8,128)(2,1)S(1)}, u32[]{:S(2)}, u32[]{:S(2)}) collective-permute-start(bf16[128,1024]{1,0:T(8,128)(2,1)} %get-tuple-element.150), channel_id=1, source_target_pairs={{0,2},{1,3},{2,0},{3,1},{4,6},{5,7},{6,4},{7,5},{8,10},{9,11},{10,... | collective-permute-start | bytes 786440 | tf_op jit(solution)/shard_map/ppermute | solution.py:401
  80.4 15.0 %collective-permute-start.17 = (bf16[128,1024]{1,0:T(8,128)(2,1)}, bf16[128,1024]{1,0:T(8,128)(2,1)S(1)}, u32[]{:S(2)}, u32[]{:S(2)}) collective-permute-start(bf16[128,1024]{1,0:T(8,128)(2,1)} %get-tuple-element.151), channel_id=1, source_target_pairs={{0,4},{1,5},{2,6},{3,7},{4,0},{5,1},{6,2},{7,3},{8,12},{9,13},{10,... | collective-permute-start | bytes 786440 | tf_op jit(solution)/shard_map/ppermute | solution.py:401
  80.9 18.4 %collective-permute-start.18 = (bf16[128,1024]{1,0:T(8,128)(2,1)}, bf16[128,1024]{1,0:T(8,128)(2,1)S(1)}, u32[]{:S(2)}, u32[]{:S(2)}) collective-permute-start(bf16[128,1024]{1,0:T(8,128)(2,1)} %get-tuple-element.152), channel_id=1, source_target_pairs={{0,6},{1,7},{2,4},{3,5},{4,2},{5,3},{6,0},{7,1},{8,14},{9,15},{10,... | collective-permute-start | bytes 786440 | tf_op jit(solution)/shard_map/ppermute | solution.py:401
  85.8 16.6 %collective-permute-start.19 = (bf16[128,1024]{1,0:T(8,128)(2,1)S(1)}, bf16[128,1024]{1,0:T(8,128)(2,1)S(1)}, u32[]{:S(2)}, u32[]{:S(2)}) collective-permute-start(bf16[128,1024]{1,0:T(8,128)(2,1)S(1)} %get-tuple-element.154), channel_id=1, source_target_pairs={{0,8},{1,9},{2,10},{3,11},{4,12},{5,13},{6,14},{7,15},{8,0},{9,1},... | collective-permute-start | bytes 786440 | tf_op jit(solution)/shard_map/ppermute | solution.py:401
  103.0 11.0 %collective-permute-start.22 = (bf16[512,1024]{1,0:T(8,128)(2,1)}, bf16[512,1024]{1,0:T(8,128)(2,1)}, u32[]{:S(2)}, u32[]{:S(2)}) collective-permute-start(bf16[512,1024]{1,0:T(8,128)(2,1)} %get-tuple-element.167), channel_id=1, source_target_pairs={{0,1},{1,0},{2,3},{3,2},{4,5},{5,4},{6,7},{7,6},{8,9},{9,8},{10,11... | collective-permute-start | bytes 3145736 | tf_op jit(solution)/shard_map/ppermute | solution.py:401
  103.1 11.0 %collective-permute-start.21 = (bf16[512,1024]{1,0:T(8,128)(2,1)}, bf16[512,1024]{1,0:T(8,128)(2,1)S(1)}, u32[]{:S(2)}, u32[]{:S(2)}) collective-permute-start(bf16[512,1024]{1,0:T(8,128)(2,1)} %get-tuple-element.165.refs_4_), channel_id=1, source_target_pairs={{0,1},{1,0},{2,3},{3,2},{4,5},{5,4},{6,7},{7,6},{8,9},{9,8},{10,11... | collective-permute-start | bytes 3145736 | tf_op jit(solution)/shard_map/ppermute | solution.py:401
  103.5 15.9 %collective-permute-start.20 = (bf16[128,1024]{1,0:T(8,128)(2,1)S(1)}, bf16[128,1024]{1,0:T(8,128)(2,1)S(1)}, u32[]{:S(2)}, u32[]{:S(2)}) collective-permute-start(bf16[128,1024]{1,0:T(8,128)(2,1)S(1)} %get-tuple-element.164), channel_id=1, source_target_pairs={{0,8},{1,9},{2,10},{3,11},{4,12},{5,13},{6,14},{7,15},{8,0},{9,1},... | collective-permute-start | bytes 786440 | tf_op jit(solution)/shard_map/ppermute | solution.py:401
  134.9 8.0 %collective-permute-start.30 = (f32[40,512]{1,0:T(8,128)S(1)}, f32[40,512]{1,0:T(8,128)S(1)}, u32[]{:S(2)}, u32[]{:S(2)}) collective-permute-start(f32[40,512]{1,0:T(8,128)S(1)} %add.30), channel_id=1, source_target_pairs={{0,8},{1,9},{2,10},{3,11},{4,12},{5,13},{6,14},{7,15},{8,0},{9,1},... | collective-permute-start | bytes 245768 | tf_op jit(solution)/shard_map/ppermute | solution.py:401
  (32 other events, 169.6 us)

commit v3 on v2

--- a/solution.py
+++ b/solution.py
@@ -40,11 +40,16 @@
 
 class Staged:
     def __init__(self, source, held, semaphore):
-        self.held, self.copy, self.waited = held, pltpu.make_async_copy(source, held, semaphore), False
-        self.shape = held.shape
-        self.copy.start()
+        self.held, self.copy = held, pltpu.make_async_copy(source, held, semaphore)
+        self.shape, self.started, self.waited = held.shape, False, False
+
+    def start(self):
+        if not self.started:
+            self.copy.start()
+        self.started = True
 
     def wait(self):
+        self.start()
         if not self.waited:
             self.copy.wait()
         self.waited = True
@@ -54,7 +59,7 @@
         return self.held[at]
 
 
-def kernel_call(body, operands, outs, scratch=(), weight=0.0, limit=SMALL, scalars=()):
+def kernel_call(body, operands, outs, scratch=(), weight=0.0, limit=SMALL, scalars=(), first=None):
     count, out_count = len(operands), len(outs)
     staged = [place for place in range(count) if place not in scalars]
     held = [pltpu.VMEM(operands[place].shape, operands[place].dtype) for place in staged]
@@ -67,6 +72,8 @@
         values = list(ins)
         for turn, place in enumerate(staged):
             values[place] = Staged(ins[place], copies[turn], in_semaphores.at[turn])
+            if first is None or place < first:
+                values[place].start()
         writes = [
             pltpu.make_async_copy(buffer, out, out_semaphores.at[turn])
             for turn, (buffer, out) in enumerate(zip(made, out_refs))
@@ -155,11 +162,12 @@
                 yield offset, block[8 * turn : 8 * turn + count]
 
 
-def fill_padded(pad_ref, left_ref, mid_ref, right_ref):
-    count = mid_ref.shape[0]
-    pad_ref[0:RIM, :] = left_ref[...].astype(F32)
-    pad_ref[RIM : RIM + count, :] = mid_ref[...].astype(F32)
-    pad_ref[RIM + count : 2 * RIM + count, :] = right_ref[...].astype(F32)
+def fill_padded(pad_ref, core, twin, mid, other):
+    count = mid.shape[0]
+    after = RIM + count
+    pad_ref[pl.ds(pl.multiple_of((1 - core) * after, 8), RIM), :] = twin[...].astype(F32)
+    pad_ref[RIM:after, :] = mid[...].astype(F32)
+    pad_ref[pl.ds(pl.multiple_of(core * after, 8), RIM), :] = other[...].astype(F32)
 
 
 def lane_loop(width, body):
@@ -168,10 +176,10 @@
         body(pl.ds(pl.multiple_of(step * LANES, LANES), LANES))
 
 
-def convolve_and_norm(frames, left, right, taps, gain, names, conv_ref, normed_ref, scratch):
+def convolve_and_norm(core, frames, twin, other, taps, gain, names, conv_ref, normed_ref, scratch):
     pad_ref, taps32_ref, mixed_ref, square_ref = scratch
     count, width = frames.shape
-    fill_padded(pad_ref, left, frames, right)
+    fill_padded(pad_ref, core, twin, frames, other)
     taps32_ref[...] = taps[...].astype(F32)
     square_ref[...] = jnp.zeros_like(square_ref)
 
@@ -193,17 +201,19 @@
 
 
 def front_kernel(ins, outs, scratch, write):
-    frames, left, right, taps, gain, names = ins
-    convolve_and_norm(frames, left, right, taps, gain, names[...], outs[0], outs[1], scratch)
+    core, frames, twin, other, taps, gain, names = ins
+    convolve_and_norm(core[0], frames, twin, other, taps, gain, names[...], outs[0], outs[1], scratch)
 
 
 def far_front_kernel(near, capacity, ins, outs, scratch, write):
-    chip, frames, rims_and_names, taps, gain, normed = ins
+    chip, core, frames, rims_and_names, taps, gain, normed = ins
     far_normed, parts = outs[0], outs[1:]
-    left, right = rims_and_names[0:RIM, :], rims_and_names[RIM : 2 * RIM, :]
-    first, last = left.astype(F32)[0:1], right.astype(F32)[RIM - 1 : RIM]
+    twin, other = rims_and_names[0:RIM, :], rims_and_names[RIM : 2 * RIM, :]
+    even = core[0] == 0
+    first = jnp.where(even, twin.astype(F32)[RIM - 1 : RIM], twin.astype(F32)[0:1])
+    last = jnp.where(even, other.astype(F32)[0:1], other.astype(F32)[RIM - 1 : RIM])
     names = jnp.concatenate([first, last, jnp.zeros((RIM - 2, frames.shape[1]), F32)], axis=0).astype(BF16)
-    convolve_and_norm(frames, left, right, taps, gain, names, None, far_normed, scratch)
+    convolve_and_norm(core[0], frames, twin, other, taps, gain, names, None, far_normed, scratch)
     write(0)
     pack_kernel(near, capacity, (chip, normed, far_normed), parts, scratch, write)
 
@@ -254,11 +264,11 @@
 
 
 def final_kernel(ins, outs, scratch, write):
-    core, frames, left, right, conv, grad, gain, near_sum, far_sum, router, near_back, far_back = ins
-    out_ref, mixed_grad_ref, conv_grad_ref, head_ref, tail_ref, kept_ref, given_ref = outs
+    core, frames, twin, other, conv, grad, gain, near_sum, far_sum, router, near_back, far_back = ins
+    out_ref, mixed_grad_ref, conv_grad_ref, twin_ref, other_ref, kept_ref, given_ref = outs
     pad_ref, local_ref = scratch
     count, width = frames.shape
-    fill_padded(pad_ref, left, frames, right)
+    fill_padded(pad_ref, core[0], twin, frames, other)
     conv_out = conv[...]
     logistic = jax.nn.sigmoid(conv_out)
     mixed = frames[...].astype(F32) + conv_out * logistic
@@ -274,8 +284,8 @@
     mixed_grad_ref[...] = mixed_grad
     conv_grad = (mixed_grad * (logistic * (1.0 + conv_out * (1.0 - logistic)))).astype(BF16)
     conv_grad_ref[...] = conv_grad
-    head_ref[...] = conv_grad[0:RIM]
-    tail_ref[...] = conv_grad[count - RIM : count]
+    twin_ref[...] = jnp.where(core[0] == 0, conv_grad[count - RIM : count], conv_grad[0:RIM])
+    other_ref[...] = jnp.where(core[0] == 0, conv_grad[0:RIM], conv_grad[count - RIM : count])
     write(1, 2, 3, 4)
 
     def reduce(lanes):
@@ -289,10 +299,10 @@
 
 
 def frames_kernel(ins, outs, scratch, write):
-    mixed_grad, conv_grad, left, right, taps = ins
+    core, mixed_grad, conv_grad, twin, other, taps = ins
     (out_ref,), (pad_ref, taps32_ref) = outs, scratch
     count, width = mixed_grad.shape
-    fill_padded(pad_ref, left, conv_grad, right)
+    fill_padded(pad_ref, core[0], twin, conv_grad, other)
     taps32_ref[...] = taps[...].astype(F32)
     mixed_grad.wait()
 
@@ -305,10 +315,8 @@
     lane_loop(width, conv)
 
 
-def chunk_loop(width, body):
-    @pl.loop(0, width // CHUNK)
-    def _(step):
-        body(pl.ds(pl.multiple_of(step * CHUNK, CHUNK), CHUNK))
+def chunks(width):
+    return [slice(start, start + CHUNK) for start in range(0, width, CHUNK)]
 
 
 def gather_rows(refs, rows_ref):
@@ -325,58 +333,74 @@
 
 def forward_kernel(near, ins, outs, scratch, write):
     rows, (near_in, far_in, near_out, far_out) = ins[0:near], ins[near:]
-    out_refs, (rows_ref, near_pre_ref, far_pre_ref, near_active_ref, far_active_ref) = outs[0:near], outs[near:]
+    out_refs, (rows_ref, near_slope, far_slope, near_active, far_active) = outs[0:near], outs[near:]
     gather_rows(rows, rows_ref)
+    near_in.wait()
+    near_out.start()
+    far_out.start()
     write(near)
-    for weight, pre, active in ((near_in, near_pre_ref, near_active_ref), (far_in, far_pre_ref, far_active_ref)):
+    for weight, slope, active in ((near_in, near_slope, near_active), (far_in, far_slope, far_active)):
         weight.wait()
-
-        def inner(columns):
+        for columns in chunks(weight.shape[1]):
             values = dot(rows_ref[...], weight[:, columns])
-            pre[:, columns] = values
-            active[:, columns] = jax.nn.silu(values).astype(BF16)
-
-        chunk_loop(weight.shape[1], inner)
+            logistic = jax.nn.sigmoid(values)
+            active[:, columns] = (values * logistic).astype(BF16)
+            slope[:, columns] = (logistic * (1.0 + values * (1.0 - logistic))).astype(BF16)
     write(near + 1, near + 2, near + 3, near + 4)
     near_out.wait()
     far_out.wait()
-
-    def outer(columns):
-        total = dot(near_active_ref[...], near_out[:, columns])
-        total = total + dot(far_active_ref[...], far_out[:, columns])
+    for columns in chunks(near_out.shape[1]):
+        total = dot(near_active[...], near_out[:, columns])
+        total = total + dot(far_active[...], far_out[:, columns])
         scatter_columns(out_refs, columns, total.astype(BF16))
 
-    chunk_loop(near_out.shape[1], outer)
-
 
 def backward_kernel(near, ins, outs, scratch, write):
-    grads, (rows, router, mine, near_out, far_out, near_pre, far_pre, near_in, far_in) = ins[0:near], ins[near:]
-    out_refs, (near_grad_ref, far_grad_ref, grad_rows_ref) = outs[0:near], outs[near:]
+    chip, grads, rest = ins[0], ins[1 : near + 1], ins[near + 1 :]
+    rows, router, near_out, far_out, near_slope, far_slope, near_in, far_in, far_active = rest
+    out_refs, (near_grad, sent) = outs[0:near], outs[near:]
     (grads_ref,) = scratch
+    count = rows.shape[0]
+    rows_part, active_part, grads_part, pre_part = (slice(turn * count, (turn + 1) * count) for turn in range(4))
     gather_rows(grads, grads_ref)
-    logits = jnp.sum(dot_last(rows[...], router[...]) * mine[...], axis=1, keepdims=True)
-    gate = jax.nn.sigmoid(logits)
-    grad_rows_ref[...] = (gate * grads_ref[...].astype(F32)).astype(BF16)
-    write(near + 2)
-    for weight, pre, grad in ((near_out, near_pre, near_grad_ref), (far_out, far_pre, far_grad_ref)):
+    logits = dot_last(rows[...], router[...])
+    mine = lax.broadcasted_iota(jnp.int32, logits.shape, 1) == chip[0]
+    gate = jax.nn.sigmoid(jnp.sum(jnp.where(mine, logits, 0.0), axis=1, keepdims=True))
+    sent[grads_part, :] = (gate * grads_ref[...].astype(F32)).astype(BF16)
+    for later in (far_out, near_slope, far_slope, near_in, far_in, far_active):
+        later.start()
+    for weight, slope, grad, part in ((near_out, near_slope, near_grad, slice(None)), (far_out, far_slope, sent, pre_part)):
         weight.wait()
-        pre.wait()
-
-        def inner(columns):
-            hidden = dot_last(grad_rows_ref[...], weight[columns, :])
-            grad[:, columns] = (hidden * slope_of(pre[:, columns])).astype(BF16)
-
-        chunk_loop(weight.shape[0], inner)
-    write(near, near + 1)
+        slope.wait()
+        for columns in chunks(weight.shape[0]):
+            hidden = dot_last(sent[grads_part, :], weight[columns, :])
+            grad[part, columns] = (hidden * slope[:, columns].astype(F32)).astype(BF16)
+    write(near)
+    sent[rows_part, :] = rows[...]
+    sent[active_part, :] = far_active[...]
+    write(near + 1)
     near_in.wait()
     far_in.wait()
-
-    def outer(rows):
-        total = dot_last(near_grad_ref[...], near_in[rows, :])
-        total = total + dot_last(far_grad_ref[...], far_in[rows, :])
-        scatter_columns(out_refs, rows, total.astype(BF16))
-
-    chunk_loop(near_in.shape[0], outer)
+    for columns in chunks(near_in.shape[0]):
+        total = dot_last(near_grad[...], near_in[columns, :])
+        total = total + dot_last(sent[pre_part, :], far_in[columns, :])
+        scatter_columns(out_refs, columns, total.astype(BF16))
+
+
+def weights_kernel(ins, outs, scratch, write):
+    near_active, near_grad, near_part, far_part = ins
+    in_grad, out_grad = outs
+    count, width = near_active.shape
+    rows_part, active_part, grads_part, pre_part = (slice(turn * count, (turn + 1) * count) for turn in range(4))
+    for ref in ins:
+        ref.wait()
+    for columns in chunks(width):
+        total = dot_first(near_active[:, columns], near_part[grads_part, :])
+        out_grad[columns, :] = (total + dot_first(far_part[active_part, columns], far_part[grads_part, :])).astype(BF16)
+    write(1)
+    for columns in chunks(width):
+        total = dot_first(near_part[rows_part, columns], near_grad[...])
+        in_grad[columns, :] = (total + dot_first(far_part[rows_part, columns], far_part[pre_part, :])).astype(BF16)
 
 
 def last_kernel(ins, outs, scratch, write):
@@ -390,11 +414,9 @@
         router_ref[:, lanes] = half[KSIZE + 1 :]
 
 
-def rims(head, tail, count):
-    ends = count - 1
-    left = lax.ppermute(tail, "seq", [(i, i + 1) for i in range(ends)])
-    right = lax.ppermute(head, "seq", [(i + 1, i) for i in range(ends)])
-    return left, right
+def pair_up(values, count):
+    pairs = [(i, i + 1) for i in range(1, count - 1, 2)]
+    return lax.ppermute(values, "seq", pairs + [(j, i) for i, j in pairs])
 
 
 def swap(values, count, bit):
@@ -421,35 +443,45 @@
     taps32 = pltpu.VMEM((KSIZE, width), F32)
     chip = lax.axis_index("seq") // 2
     chips = chip.reshape(1).astype(jnp.int32)
-    mine = (jnp.arange(experts, dtype=jnp.int32) == chip).astype(F32).reshape(1, experts)
     cross = functools.partial(swap, count=devices, bit=devices // 2)
 
-    frames, head, tail = lax.optimization_barrier((frames, frames[0:RIM], frames[count - RIM : count]))
-    left, right = rims(head, tail, devices)
+    core = lax.axis_index("seq") % 2
+    cores = core.reshape(1).astype(jnp.int32)
+    ends = (frames[count - RIM : count], frames[0:RIM])
+    frames, to_twin, to_other = lax.optimization_barrier(
+        (frames, jnp.where(core == 0, *ends), jnp.where(core == 0, *ends[::-1]))
+    )
+    twin, other = swap(to_twin, devices, 1), pair_up(to_other, devices)
     far_frames = cross(frames)
     names = jnp.pad(ids.astype(BF16), ((0, RIM - 2), (0, width - count)))
     weight_in, weight_out = expert_in[0], expert_out[0]
     other_in = swap(weight_in, devices, 1)
     other_out = swap(weight_out, devices, 1)
-    left, right, other_in, other_out = lax.optimization_barrier((left, right, other_in, other_out))
+    twin, other, other_in, other_out = lax.optimization_barrier((twin, other, other_in, other_out))
 
     model32, model16 = shape((count, width), F32), shape((count, width), BF16)
     named16 = shape((count + RIM, width), BF16)
     front_scratch = (pad, taps32, pltpu.VMEM((count, width), F32), pltpu.VMEM((count, LANES), F32))
     conv_out, normed = kernel_call(
-        front_kernel, (frames, left, right, taps, gain, names), (model32, named16), front_scratch, weight=3.3
-    )
-    far_rims = cross(jnp.concatenate([names[0:1], left[1:], right[: RIM - 1], names[1:2]]))
+        front_kernel,
+        (cores, frames, twin, other, taps, gain, names),
+        (model32, named16),
+        front_scratch,
+        weight=3.3,
+        scalars=(0,),
+    )
+    even = jnp.concatenate([twin[: RIM - 1], names[0:1], names[1:2], other[1:]])
+    odd = jnp.concatenate([names[0:1], twin[1:], other[: RIM - 1], names[1:2]])
+    far_rims = cross(jnp.where(core == 0, even, odd))
     far_rims, far_frames, out_grad = lax.optimization_barrier((far_rims, far_frames, out_grad))
     far_grad = cross(out_grad)
     part = (shape((2 * capacity, width), BF16),) * near
     far_normed, *parts = kernel_call(
         functools.partial(far_front_kernel, near, capacity),
-        (chips, far_frames, far_rims, taps, gain, normed),
+        (chips, cores, far_frames, far_rims, taps, gain, normed),
         (named16, *part),
         front_scratch,
-        weight=0.0,
-        scalars=(0,),
+        scalars=(0, 1),
     )
     rows = exchange(parts, devices)
     parts = kernel_call(
@@ -462,28 +494,29 @@
     rows[0:3], parts = lax.optimization_barrier((rows[0:3], parts))
     grads = exchange(parts, devices)
 
-    half = weight_in.shape[1]
-    wide = shape((slots, half), F32)
-    narrow = shape((slots, half), BF16)
-    model = shape((slots, width), BF16)
+    narrow = shape((slots, weight_in.shape[1]), BF16)
     outs = kernel_call(
         functools.partial(forward_kernel, near),
         (*rows, weight_in, other_in, weight_out, other_out),
-        part + (model, wide, wide, narrow, narrow),
-        weight=0.0, limit=LARGE,
-    )
-    parts_out, (all_rows, *pre_act), active = outs[0:near], outs[near : near + 3], outs[near + 3 :]
+        part + (shape((slots, width), BF16), narrow, narrow, narrow, narrow),
+        limit=LARGE,
+        first=near + 2,
+    )
+    parts_out, (all_rows, *slopes), (near_active, far_active) = outs[0:near], outs[near : near + 3], outs[near + 3 :]
     results = exchange(parts_out, devices)
     outs = kernel_call(
         functools.partial(backward_kernel, near),
-        (*grads, all_rows, router, mine, weight_out, other_out, *pre_act, weight_in, other_in),
-        part + (narrow, narrow, model),
+        (chips, *grads, all_rows, router, weight_out, other_out, *slopes, weight_in, other_in, far_active),
+        part + (narrow, shape((4 * slots, width), BF16)),
         (pltpu.VMEM((slots, width), BF16),),
-        weight=0.0, limit=LARGE,
-    )
-    results, outs, all_rows, active = lax.optimization_barrier((results, outs, all_rows, active))
-    parts_in, pre_grad, grad_rows = outs[0:near], outs[near : near + 2], outs[near + 2]
+        limit=LARGE,
+        first=near + 4,
+        scalars=(0,),
+    )
+    results, outs = lax.optimization_barrier((results, outs))
+    parts_in, near_grad, sent = outs[0:near], outs[near], outs[near + 1]
     backs = exchange(parts_in, devices)
+
     logits = shape((count, experts), BF16)
     near_sum, far_sum, near_logits, far_logits, router_local = kernel_call(
         functools.partial(result_kernel, near, capacity),
@@ -500,46 +533,47 @@
         weight=0.0,
         scalars=(0,),
     )
-    far_back, far_sum, all_rows, active, grad_rows, pre_grad = lax.optimization_barrier(
-        (far_back, far_sum, all_rows, active, grad_rows, pre_grad)
-    )
+    far_back, far_sum = lax.optimization_barrier((far_back, far_sum))
     far_back = cross(far_back)
-    far_rows, far_active, far_grads, far_pre = [
-        swap(values, devices, 1) for values in (all_rows, active[1], grad_rows, pre_grad[1])
-    ]
-    expert_out_grad = (dot_first(active[0], grad_rows) + dot_first(far_active, far_grads)).astype(BF16)
-    expert_in_grad = (dot_first(all_rows, pre_grad[0]) + dot_first(far_rows, far_pre)).astype(BF16)
+    grad = shape(weight_in.shape, BF16)
+    expert_in_grad, expert_out_grad = kernel_call(
+        weights_kernel, (near_active, near_grad, sent, swap(sent, devices, 1)), (grad, grad), limit=LARGE
+    )
     far_back, expert_in_grad, expert_out_grad = lax.optimization_barrier((far_back, expert_in_grad, expert_out_grad))
 
     rim = shape((RIM, width), BF16)
     lines = KSIZE + 1 + experts
     columns = shape((lines, width // 2), F32)
-    core = (lax.axis_index("seq") % 2).reshape(1).astype(jnp.int32)
-    block_out, mixed_grad, conv_grad, head, tail, kept, given = kernel_call(
+    block_out, mixed_grad, conv_grad, to_twin, to_other, kept, given = kernel_call(
         final_kernel,
-        (core, frames, left, right, conv_out, out_grad, gain, near_sum, far_sum, router_local, near_back, far_back),
+        (cores, frames, twin, other, conv_out, out_grad, gain, near_sum, far_sum, router_local, near_back, far_back),
         (model16, model32, model16, rim, rim, columns, columns),
         (pad, pltpu.VMEM((lines, width), F32)),
         weight=0.0,
         scalars=(0,),
     )
-    grad_left, grad_right = rims(head, tail, devices)
+    grad_twin, grad_other = swap(to_twin, devices, 1), pair_up(to_other, devices)
     local = kept + swap(given, devices, 1)
     bit = 2
     while bit < devices:
-        other = swap(local, devices, bit)
-        if bit == devices // 4:
-            other, grad_left, grad_right = lax.optimization_barrier((other, grad_left, grad_right))
+        last = 4 * bit > devices
+        others = [swap(local, devices, step) for step in ((bit,) if last else (bit, 2 * bit, 3 * bit))]
+        if bit == 2:
+            others, grad_twin, grad_other = lax.optimization_barrier((others, grad_twin, grad_other))
             (frames_grad,) = kernel_call(
-                frames_kernel, (mixed_grad, conv_grad, grad_left, grad_right, taps), (model16,), (pad, taps32), weight=0.0
+                frames_kernel,
+                (cores, mixed_grad, conv_grad, grad_twin, grad_other, taps),
+                (model16,),
+                (pad, taps32),
+                scalars=(0,),
             )
-        if 2 * bit == devices:
-            other, frames_grad = lax.optimization_barrier((other, frames_grad))
-        local = local + other
-        bit *= 2
+        bit *= 2 if last else 4
+        if bit == devices:
+            others, frames_grad = lax.optimization_barrier((others, frames_grad))
+        local = local + others[0] if last else (local + others[0]) + (others[1] + others[2])
     kernel_grad, gain_grad, router_grad = kernel_call(
         last_kernel,
-        (core, local, swap(local, devices, 1)),
+        (cores, local, swap(local, devices, 1)),
         (shape((KSIZE, width), F32), shape((1, width), F32), shape((experts, width), F32)),
         weight=0.0,
         scalars=(0,),

time: 146 us -> 136 us (0.932)
  matrix products: 10.9 us -> 0 us
  Pallas kernels: 44.6 us -> 51.7 us
  starting transfers between devices: 43.9 us -> 36.9 us
  waiting for transfers between devices: 33.2 us -> 34.9 us
    dot_general x4 -> x0, matrix products: 10.9 us -> none  [dot_first(): return lax.dot_general(a, b, FIRST, preferred_element_type=F32)]
    pallas_call x10 -> x11, Pallas kernels: 44.6 us -> 51.7 us  [kernel_call(): pl.pallas_call(kernel, out_shape=tuple(outs), in_specs=[pl.BlockSpec(memo...]
    ppermute x28, waiting for transfers between devices: 29.9 us -> 34.9 us  [swap(): return lax.ppermute(values, 'seq', [(i, i ^ bit) for i in range(count)])]
    ppermute x4 -> x2, starting transfers between devices: 6.2 us -> 1.3 us  [pair_up(): return lax.ppermute(values, 'seq', pairs + [(j, i) for i, j in pairs])]
    ppermute x4 -> x2, waiting for transfers between devices: 3.29 us -> 0.01 us  [pair_up(): return lax.ppermute(values, 'seq', pairs + [(j, i) for i, j in pairs])]
    ppermute x28, starting transfers between devices: 37.7 us -> 35.6 us  [swap(): return lax.ppermute(values, 'seq', [(i, i ^ bit) for i in range(count)])]
    unnamed x48 -> x38, local copies, waits for them, and re-layouts: 8.68 us -> 8.37 us
  transfers between devices with their start and end apart: 32 -> 30, of which waited for: 12 -> 16; matrix products, arithmetic and copies ran while one was open for 9% -> 2% of each run, Pallas kernels for 28% -> 35%
where the time goes in v3:
time: 136 us; the launch traced here: 135 us
  Pallas kernels  51.7 us (38%)
  starting transfers between devices  36.9 us (27%)
  waiting for transfers between devices  34.9 us (26%)
  local copies, waits for them, and re-layouts  9.1 us (7%)
  other arithmetic  1.57 us (1%)
    pallas_call x11, Pallas kernels, kernel_call(): pl.pallas_call(kernel, out_shape=tuple(outs), in_specs=[pl.BlockSpec(memo...  51.7 us
    ppermute x28, starting transfers between devices, swap(): return lax.ppermute(values, 'seq', [(i, i ^ bit) for i in range(count)])  35.6 us
    ppermute x28, waiting for transfers between devices, swap(): return lax.ppermute(values, 'seq', [(i, i ^ bit) for i in range(count)])  34.9 us
    unnamed x38, local copies, waits for them, and re-layouts  8.37 us
  transfers between devices with their start and end apart: 30, of which 16 were waited for; matrix products, arithmetic and copies ran while one was open for 2% of the time, Pallas kernels for 35%

profile of v3, /device:TPU:0, one launch (start us, length us, event | category | flops | bytes accessed | tf_op | source)
XLA Modules:
  0.0 135.3 jit_solution(9624347330781930036)
XLA Ops:
  3.2 6.4 %collective-permute-start.5 = (bf16[128,1024]{1,0:T(8,128)(2,1)}, bf16[128,1024]{1,0:T(8,128)(2,1)S(1)}, u32[]{:S(2)}, u32[]{:S(2)}) collective-permute-start(bf16[128,1024]{1,0:T(8,128)(2,1)} %refs_1_.2), channel_id=1, source_target_pairs={{0,8},{1,9},{2,10},{3,11},{4,12},{5,13},{6,14},{7,15},{8,0},{9,1},... | collective-permute-start | bytes 786440 | tf_op jit(solution)/shard_map/ppermute | solution.py:423
  11.7 2.1 %collective-permute-start.4 = (bf16[32,1024]{1,0:T(8,128)(2,1)S(1)}, bf16[32,1024]{1,0:T(8,128)(2,1)S(1)}, u32[]{:S(2)}, u32[]{:S(2)}) collective-permute-start(bf16[32,1024]{1,0:T(8,128)(2,1)S(1)} %maximum_select_fusion), channel_id=1, source_target_pairs={{0,8},{1,9},{2,10},{3,11},{4,12},{5,13},{6,14},{7,15},{8,0},{9,1},... | collective-permute-start | bytes 196616 | tf_op jit(solution)/shard_map/ppermute | solution.py:423
  16.3 3.3 %shard_map.135 = (f32[128,1024]{1,0:T(8,128)S(1)}, bf16[144,1024]{1,0:T(8,128)(2,1)S(1)}) custom-call(s32[1]{0:T(128)} %bitcast.refs_0_.refs_1_, bf16[128,1024]{1,0:T(8,128)(2,1)S(1)} %copy-done.2, bf16[16,1024]{1,0:T(8,128)(2,1)S(1)} %collective-permute-done.refs_2_, bf16[16,1024]{1,0:T(8,128)(2,1)S(1)} %collective-permute-done.1.refs_3_, ...), custom_call_target="tpu_custom_call" | custom-call | flops 1 | bytes 1782001 | tf_op jit(solution)/shard_map/pallas_call | solution.py:96
  19.6 4.7 %collective-permute-done.5.refs_2_ = bf16[128,1024]{1,0:T(8,128)(2,1)S(1)} collective-permute-done((bf16[128,1024]{1,0:T(8,128)(2,1)}, bf16[128,1024]{1,0:T(8,128)(2,1)S(1)}, u32[]{:S(2)}, u32[]{:S(2)}) %collective-permute-start.5) | collective-permute-done | bytes 262176 | tf_op jit(solution)/shard_map/ppermute | solution.py:423
  26.1 4.9 %shard_map.136 = (bf16[144,1024]{1,0:T(8,128)(2,1)S(1)}, bf16[128,1024]{1,0:T(8,128)(2,1)S(1)}, bf16[128,1024]{1,0:T(8,128)(2,1)S(1)}, bf16[128,1024]{1,0:T(8,128)(2,1)S(1)}, bf16[128,1024]{1,0:T(8,128)(2,1)S(1)}) custom-call(s32[1]{0:T(128)} %bitcast.4.refs_0_, s32[1]{0:T(128)} %bitcast.refs_0_.refs_1_, ...), custom_call_target="tpu_custom_call" | custom-call | flops 1 | bytes 1 | tf_op jit(solution)/shard_map/pallas_call | solution.py:96
  32.1 3.4 %collective-permute-start.8 = (bf16[128,1024]{1,0:T(8,128)(2,1)S(1)}, bf16[128,1024]{1,0:T(8,128)(2,1)S(1)}, u32[]{:S(2)}, u32[]{:S(2)}) collective-permute-start(bf16[128,1024]{1,0:T(8,128)(2,1)S(1)} %get-tuple-element.104), channel_id=1, source_target_pairs={{0,4},{1,5},{2,6},{3,7},{4,0},{5,1},{6,2},{7,3},{8,12},{9,13},{10,... | collective-permute-start | bytes 786440 | tf_op jit(solution)/shard_map/ppermute | solution.py:423
  36.9 3.0 %collective-permute-done.6.refs_4_.refs_3_ = bf16[128,1024]{1,0:T(8,128)(2,1)S(1)} collective-permute-done((bf16[128,1024]{1,0:T(8,128)(2,1)}, bf16[128,1024]{1,0:T(8,128)(2,1)S(1)}, u32[]{:S(2)}, u32[]{:S(2)}) %collective-permute-start.6) | collective-permute-done | bytes 262176 | tf_op jit(solution)/shard_map/ppermute | solution.py:423
  40.9 2.0 %shard_map.137 = (bf16[128,1024]{1,0:T(8,128)(2,1)S(1)}, bf16[128,1024]{1,0:T(8,128)(2,1)S(1)}, bf16[128,1024]{1,0:T(8,128)(2,1)S(1)}, bf16[128,1024]{1,0:T(8,128)(2,1)S(1)}) custom-call(s32[1]{0:T(128)} %bitcast.4.refs_0_, bf16[144,1024]{1,0:T(8,128)(2,1)S(1)} %get-tuple-element.98.refs_6_.refs_1_.refs_2_, ...), custom_call_target="tpu_custom_call" | custom-call | flops 1 | bytes 1 | tf_op jit(solution)/shard_map/pallas_call | solution.py:96
  42.9 2.7 %collective-permute-done.8.refs_2_ = bf16[128,1024]{1,0:T(8,128)(2,1)S(1)} collective-permute-done((bf16[128,1024]{1,0:T(8,128)(2,1)S(1)}, bf16[128,1024]{1,0:T(8,128)(2,1)S(1)}, u32[]{:S(2)}, u32[]{:S(2)}) %collective-permute-start.8) | collective-permute-done | bytes 262176 | tf_op jit(solution)/shard_map/ppermute | solution.py:423
  46.8 2.3 %collective-permute-start.15 = (bf16[128,1024]{1,0:T(8,128)(2,1)S(1)}, bf16[128,1024]{1,0:T(8,128)(2,1)S(1)}, u32[]{:S(2)}, u32[]{:S(2)}) collective-permute-start(bf16[128,1024]{1,0:T(8,128)(2,1)S(1)} %get-tuple-element.122), channel_id=1, source_target_pairs={{0,6},{1,7},{2,4},{3,5},{4,2},{5,3},{6,0},{7,1},{8,14},{9,15},{10,... | collective-permute-start | bytes 786440 | tf_op jit(solution)/shard_map/ppermute | solution.py:423
  49.0 8.6 %shard_map.138 = (bf16[128,1024]{1,0:T(8,128)(2,1)}, bf16[128,1024]{1,0:T(8,128)(2,1)}, bf16[128,1024]{1,0:T(8,128)(2,1)}, bf16[128,1024]{1,0:T(8,128)(2,1)}, bf...) custom-call(bf16[128,1024]{1,0:T(8,128)(2,1)} %copy-done.10, ...), custom_call_target="tpu_custom_call" | custom-call | flops 1 | bytes 1 | tf_op jit(solution)/shard_map/pallas_call | solution.py:96
  57.6 3.8 %collective-permute-start.10 = (bf16[128,1024]{1,0:T(8,128)(2,1)}, bf16[128,1024]{1,0:T(8,128)(2,1)S(1)}, u32[]{:S(2)}, u32[]{:S(2)}) collective-permute-start(bf16[128,1024]{1,0:T(8,128)(2,1)} %get-tuple-element.116), channel_id=1, source_target_pairs={{0,2},{1,3},{2,0},{3,1},{4,6},{5,7},{6,4},{7,5},{8,10},{9,11},{10,... | collective-permute-start | bytes 786440 | tf_op jit(solution)/shard_map/ppermute | solution.py:423
  63.8 9.8 %shard_map.139 = (bf16[128,1024]{1,0:T(8,128)(2,1)}, bf16[128,1024]{1,0:T(8,128)(2,1)}, bf16[128,1024]{1,0:T(8,128)(2,1)}, bf16[128,1024]{1,0:T(8,128)(2,1)}, bf...) custom-call(s32[1]{0:T(128)} %bitcast.4.refs_0_, bf16[128,1024]{1,0:T(8,128)(2,1)} %copy-done.9, ...), custom_call_target="tpu_custom_call" | custom-call | flops 1 | bytes 1 | tf_op jit(solution)/shard_map/pallas_call | solution.py:96
  78.4 2.8 %shard_map.140 = (f32[128,1024]{1,0:T(8,128)S(1)}, bf16[128,1024]{1,0:T(8,128)(2,1)S(1)}, bf16[128,8]{1,0:T(8,128)(2,1)S(1)}, bf16[128,8]{1,0:T(8,128)(2,1)S(1)}, f32[8,1024]{1,0:T(8,128)S(1)}) custom-call(s32[1]{0:T(128)} %bitcast.4.refs_0_, bf16[128,1024]{1,0:T(8,128)(2,1)S(1)} %copy-done.1, ...), custom_call_target="tpu_custom_call" | custom-call | flops 1 | bytes 1 | tf_op jit(solution)/shard_map/pallas_call | solution.py:96
  81.3 2.5 %collective-permute-done.16.refs_7_ = bf16[128,1024]{1,0:T(8,128)(2,1)S(1)} collective-permute-done((bf16[128,1024]{1,0:T(8,128)(2,1)}, bf16[128,1024]{1,0:T(8,128)(2,1)S(1)}, u32[]{:S(2)}, u32[]{:S(2)}) %collective-permute-start.16) | collective-permute-done | bytes 262176 | tf_op jit(solution)/shard_map/ppermute | solution.py:423
  83.8 7.7 %collective-permute-done.17.refs_8_ = bf16[128,1024]{1,0:T(8,128)(2,1)S(1)} collective-permute-done((bf16[128,1024]{1,0:T(8,128)(2,1)}, bf16[128,1024]{1,0:T(8,128)(2,1)S(1)}, u32[]{:S(2)}, u32[]{:S(2)}) %collective-permute-start.17) | collective-permute-done | bytes 262176 | tf_op jit(solution)/shard_map/ppermute | solution.py:423
  91.5 3.7 %collective-permute-done.18.refs_9_ = bf16[128,1024]{1,0:T(8,128)(2,1)S(1)} collective-permute-done((bf16[128,1024]{1,0:T(8,128)(2,1)}, bf16[128,1024]{1,0:T(8,128)(2,1)S(1)}, u32[]{:S(2)}, u32[]{:S(2)}) %collective-permute-start.18) | collective-permute-done | bytes 262176 | tf_op jit(solution)/shard_map/ppermute | solution.py:423
  95.2 2.3 %shard_map.141 = (f32[128,1024]{1,0:T(8,128)S(1)}, bf16[128,1024]{1,0:T(8,128)(2,1)S(1)}) custom-call(s32[1]{0:T(128)} %bitcast.4.refs_0_, bf16[144,1024]{1,0:T(8,128)(2,1)S(1)} %get-tuple-element.98.refs_6_.refs_1_.refs_2_, bf16[128,8]{1,0:T(8,128)(2,1)S(1)} %get-tuple-element.138.refs_2_, bf16[144,1024]{1,0:T(8,128)(2,1)S(1)} %get-tuple-element.101.refs_2_.refs_4_.refs_3_, ...), custom_call_target="tpu_custom_call" | custom-call | flops 1 | bytes 1 | tf_op jit(solution)/shard_map/pallas_call | solution.py:96
  98.2 2.0 %copy-done.13 = bf16[2048,1024]{1,0:T(8,128)(2,1)} copy-done((bf16[2048,1024]{1,0:T(8,128)(2,1)}, bf16[2048,1024]{1,0:T(8,128)(2,1)S(1)}, u32[]{:S(2)}) %copy-start.13) | copy-done | bytes 4194328
  100.2 10.0 %shard_map.142 = (bf16[1024,1024]{1,0:T(8,128)(2,1)}, bf16[1024,1024]{1,0:T(8,128)(2,1)}) custom-call(bf16[512,1024]{1,0:T(8,128)(2,1)} %get-tuple-element.150.refs_0_, bf16[512,1024]{1,0:T(8,128)(2,1)} %get-tuple-element.151.refs_1_, bf16[2048,1024]{1,0:T(8,128)(2,1)} %get-tuple-element.152.refs_2_, bf16[2048,1024]{1,0:T(8,128)(2,1)} %copy-done.13), custom_call_target="tpu_custom_call" | custom-call | flops 1 | bytes 1 | tf_op jit(solution)/shard_map/pallas_call | solution.py:96
  111.7 3.4 %shard_map.143 = (bf16[128,1024]{1,0:T(8,128)(2,1)}, f32[128,1024]{1,0:T(8,128)S(1)}, bf16[128,1024]{1,0:T(8,128)(2,1)S(1)}, bf16[16,1024]{1,0:T(8,128)(2,1)S(1)...) custom-call(s32[1]{0:T(128)} %bitcast.refs_0_.refs_1_, ...), custom_call_target="tpu_custom_call" | custom-call | flops 1 | bytes 1 | tf_op jit(solution)/shard_map/pallas_call | solution.py:96
  116.5 1.9 %collective-permute-start.25 = (f32[40,512]{1,0:T(8,128)S(1)}, f32[40,512]{1,0:T(8,128)S(1)}, u32[]{:S(2)}, u32[]{:S(2)}) collective-permute-start(f32[40,512]{1,0:T(8,128)S(1)} %add.23), channel_id=1, source_target_pairs={{0,6},{1,7},{2,4},{3,5},{4,2},{5,3},{6,0},{7,1},{8,14},{9,15},{10,... | collective-permute-start | bytes 245768 | tf_op jit(solution)/shard_map/ppermute | solution.py:423
  123.9 4.0 %collective-permute-start.28 = (f32[40,512]{1,0:T(8,128)S(1)}, f32[40,512]{1,0:T(8,128)S(1)}, u32[]{:S(2)}, u32[]{:S(2)}) collective-permute-start(f32[40,512]{1,0:T(8,128)S(1)} %add_add_fusion), channel_id=1, source_target_pairs={{0,8},{1,9},{2,10},{3,11},{4,12},{5,13},{6,14},{7,15},{8,0},{9,1},... | collective-permute-start | bytes 245768 | tf_op jit(solution)/shard_map/ppermute | solution.py:423
  127.9 3.7 %shard_map.144 = bf16[128,1024]{1,0:T(8,128)(2,1)} custom-call(s32[1]{0:T(128)} %bitcast.refs_0_.refs_1_, f32[128,1024]{1,0:T(8,128)S(1)} %get-tuple-element.164.refs_1_, bf16[128,1024]{1,0:T(8,128)(2,1)S(1)} %get-tuple-element.165.refs_2_, bf16[16,1024]{1,0:T(8,128)(2,1)S(1)} %collective-permute-done.26.refs_3_, ...), custom_call_target="tpu_custom_call" | custom-call | flops 1 | bytes 1 | tf_op jit(solution)/shard_map/pallas_call | solution.py:96
  (96 shorter events, 33.3 us)
Async XLA Ops:
  0.6 9.7 %collective-permute-start.2 = (bf16[1024,1024]{1,0:T(8,128)(2,1)}, bf16[1024,1024]{1,0:T(8,128)(2,1)S(1)}, u32[]{:S(2)}, u32[]{:S(2)}) collective-permute-start(bf16[1024,1024]{1,0:T(8,128)(2,1)} %bitcast.14), channel_id=1, source_target_pairs={{0,1},{1,0},{2,3},{3,2},{4,5},{5,4},{6,7},{7,6},{8,9},{9,8},{10,11... | collective-permute-start | bytes 6291464 | tf_op jit(solution)/shard_map/ppermute | solution.py:423
  1.1 9.2 %collective-permute-start.3 = (bf16[1024,1024]{1,0:T(8,128)(2,1)}, bf16[1024,1024]{1,0:T(8,128)(2,1)}, u32[]{:S(2)}, u32[]{:S(2)}) collective-permute-start(bf16[1024,1024]{1,0:T(8,128)(2,1)} %bitcast.17), channel_id=1, source_target_pairs={{0,1},{1,0},{2,3},{3,2},{4,5},{5,4},{6,7},{7,6},{8,9},{9,8},{10,11... | collective-permute-start | bytes 6291464 | tf_op jit(solution)/shard_map/ppermute | solution.py:423
  2.0 8.3 %collective-permute-start = (bf16[16,1024]{1,0:T(8,128)(2,1)S(1)}, bf16[16,1024]{1,0:T(8,128)(2,1)S(1)}, u32[]{:S(2)}, u32[]{:S(2)}) collective-permute-start(bf16[16,1024]{1,0:T(8,128)(2,1)S(1)} %get-tuple-element.92), channel_id=1, source_target_pairs={{0,1},{1,0},{2,3},{3,2},{4,5},{5,4},{6,7},{7,6},{8,9},{9,8},{10,11... | collective-permute-start | bytes 98312 | tf_op jit(solution)/shard_map/ppermute | solution.py:423
  2.5 7.8 %collective-permute-start.1 = (bf16[16,1024]{1,0:T(8,128)(2,1)S(1)}, bf16[16,1024]{1,0:T(8,128)(2,1)S(1)}, u32[]{:S(2)}, u32[]{:S(2)}) collective-permute-start(bf16[16,1024]{1,0:T(8,128)(2,1)S(1)} %get-tuple-element.93), channel_id=1, source_target_pairs={{1,2},{3,4},{5,6},{7,8},{9,10},{11,12},{13,14},{2,1},{4,3},{6,5},{... | collective-permute-start | bytes 98312 | tf_op jit(solution)/shard_map/ppermute | solution.py:419
  3.2 21.2 %collective-permute-start.5 = (bf16[128,1024]{1,0:T(8,128)(2,1)}, bf16[128,1024]{1,0:T(8,128)(2,1)S(1)}, u32[]{:S(2)}, u32[]{:S(2)}) collective-permute-start(bf16[128,1024]{1,0:T(8,128)(2,1)} %refs_1_.2), channel_id=1, source_target_pairs={{0,8},{1,9},{2,10},{3,11},{4,12},{5,13},{6,14},{7,15},{8,0},{9,1},... | collective-permute-start | bytes 786440 | tf_op jit(solution)/shard_map/ppermute | solution.py:423
  11.7 13.6 %collective-permute-start.4 = (bf16[32,1024]{1,0:T(8,128)(2,1)S(1)}, bf16[32,1024]{1,0:T(8,128)(2,1)S(1)}, u32[]{:S(2)}, u32[]{:S(2)}) collective-permute-start(bf16[32,1024]{1,0:T(8,128)(2,1)S(1)} %maximum_select_fusion), channel_id=1, source_target_pairs={{0,8},{1,9},{2,10},{3,11},{4,12},{5,13},{6,14},{7,15},{8,0},{9,1},... | collective-permute-start | bytes 196616 | tf_op jit(solution)/shard_map/ppermute | solution.py:423
  25.3 14.7 %collective-permute-start.6 = (bf16[128,1024]{1,0:T(8,128)(2,1)}, bf16[128,1024]{1,0:T(8,128)(2,1)S(1)}, u32[]{:S(2)}, u32[]{:S(2)}) collective-permute-start(bf16[128,1024]{1,0:T(8,128)(2,1)} %refs_5_.1), channel_id=1, source_target_pairs={{0,8},{1,9},{2,10},{3,11},{4,12},{5,13},{6,14},{7,15},{8,0},{9,1},... | collective-permute-start | bytes 786440 | tf_op jit(solution)/shard_map/ppermute | solution.py:423
  31.8 11.1 %collective-permute-start.7 = (bf16[128,1024]{1,0:T(8,128)(2,1)S(1)}, bf16[128,1024]{1,0:T(8,128)(2,1)S(1)}, u32[]{:S(2)}, u32[]{:S(2)}) collective-permute-start(bf16[128,1024]{1,0:T(8,128)(2,1)S(1)} %get-tuple-element.103), channel_id=1, source_target_pairs={{0,2},{1,3},{2,0},{3,1},{4,6},{5,7},{6,4},{7,5},{8,10},{9,11},{10,... | collective-permute-start | bytes 786440 | tf_op jit(solution)/shard_map/ppermute | solution.py:423
  32.1 13.4 %collective-permute-start.8 = (bf16[128,1024]{1,0:T(8,128)(2,1)S(1)}, bf16[128,1024]{1,0:T(8,128)(2,1)S(1)}, u32[]{:S(2)}, u32[]{:S(2)}) collective-permute-start(bf16[128,1024]{1,0:T(8,128)(2,1)S(1)} %get-tuple-element.104), channel_id=1, source_target_pairs={{0,4},{1,5},{2,6},{3,7},{4,0},{5,1},{6,2},{7,3},{8,12},{9,13},{10,... | collective-permute-start | bytes 786440 | tf_op jit(solution)/shard_map/ppermute | solution.py:423
  35.5 13.6 %collective-permute-start.9 = (bf16[128,1024]{1,0:T(8,128)(2,1)S(1)}, bf16[128,1024]{1,0:T(8,128)(2,1)}, u32[]{:S(2)}, u32[]{:S(2)}) collective-permute-start(bf16[128,1024]{1,0:T(8,128)(2,1)S(1)} %get-tuple-element.112), channel_id=1, source_target_pairs={{0,6},{1,7},{2,4},{3,5},{4,2},{5,3},{6,0},{7,1},{8,14},{9,15},{10,... | collective-permute-start | bytes 786440 | tf_op jit(solution)/shard_map/ppermute | solution.py:423
  45.5 15.9 %collective-permute-start.13 = (bf16[128,1024]{1,0:T(8,128)(2,1)S(1)}, bf16[128,1024]{1,0:T(8,128)(2,1)S(1)}, u32[]{:S(2)}, u32[]{:S(2)}) collective-permute-start(bf16[128,1024]{1,0:T(8,128)(2,1)S(1)} %get-tuple-element.120), channel_id=1, source_target_pairs={{0,2},{1,3},{2,0},{3,1},{4,6},{5,7},{6,4},{7,5},{8,10},{9,11},{10,... | collective-permute-start | bytes 786440 | tf_op jit(solution)/shard_map/ppermute | solution.py:423
  45.5 17.4 %collective-permute-start.14 = (bf16[128,1024]{1,0:T(8,128)(2,1)S(1)}, bf16[128,1024]{1,0:T(8,128)(2,1)S(1)}, u32[]{:S(2)}, u32[]{:S(2)}) collective-permute-start(bf16[128,1024]{1,0:T(8,128)(2,1)S(1)} %get-tuple-element.121), channel_id=1, source_target_pairs={{0,4},{1,5},{2,6},{3,7},{4,0},{5,1},{6,2},{7,3},{8,12},{9,13},{10,... | collective-permute-start | bytes 786440 | tf_op jit(solution)/shard_map/ppermute | solution.py:423
  46.8 16.2 %collective-permute-start.15 = (bf16[128,1024]{1,0:T(8,128)(2,1)S(1)}, bf16[128,1024]{1,0:T(8,128)(2,1)S(1)}, u32[]{:S(2)}, u32[]{:S(2)}) collective-permute-start(bf16[128,1024]{1,0:T(8,128)(2,1)S(1)} %get-tuple-element.122), channel_id=1, source_target_pairs={{0,6},{1,7},{2,4},{3,5},{4,2},{5,3},{6,0},{7,1},{8,14},{9,15},{10,... | collective-permute-start | bytes 786440 | tf_op jit(solution)/shard_map/ppermute | solution.py:423
  57.6 16.0 %collective-permute-start.10 = (bf16[128,1024]{1,0:T(8,128)(2,1)}, bf16[128,1024]{1,0:T(8,128)(2,1)S(1)}, u32[]{:S(2)}, u32[]{:S(2)}) collective-permute-start(bf16[128,1024]{1,0:T(8,128)(2,1)} %get-tuple-element.116), channel_id=1, source_target_pairs={{0,2},{1,3},{2,0},{3,1},{4,6},{5,7},{6,4},{7,5},{8,10},{9,11},{10,... | collective-permute-start | bytes 786440 | tf_op jit(solution)/shard_map/ppermute | solution.py:423
  61.4 12.2 %collective-permute-start.11 = (bf16[128,1024]{1,0:T(8,128)(2,1)}, bf16[128,1024]{1,0:T(8,128)(2,1)S(1)}, u32[]{:S(2)}, u32[]{:S(2)}) collective-permute-start(bf16[128,1024]{1,0:T(8,128)(2,1)} %get-tuple-element.117), channel_id=1, source_target_pairs={{0,4},{1,5},{2,6},{3,7},{4,0},{5,1},{6,2},{7,3},{8,12},{9,13},{10,... | collective-permute-start | bytes 786440 | tf_op jit(solution)/shard_map/ppermute | solution.py:423
  61.4 13.5 %collective-permute-start.12 = (bf16[128,1024]{1,0:T(8,128)(2,1)}, bf16[128,1024]{1,0:T(8,128)(2,1)S(1)}, u32[]{:S(2)}, u32[]{:S(2)}) collective-permute-start(bf16[128,1024]{1,0:T(8,128)(2,1)} %get-tuple-element.118), channel_id=1, source_target_pairs={{0,6},{1,7},{2,4},{3,5},{4,2},{5,3},{6,0},{7,1},{8,14},{9,15},{10,... | collective-permute-start | bytes 786440 | tf_op jit(solution)/shard_map/ppermute | solution.py:423
  74.9 23.3 %collective-permute-start.21 = (bf16[2048,1024]{1,0:T(8,128)(2,1)}, bf16[2048,1024]{1,0:T(8,128)(2,1)S(1)}, u32[]{:S(2)}, u32[]{:S(2)}) collective-permute-start(bf16[2048,1024]{1,0:T(8,128)(2,1)} %get-tuple-element.152.refs_2_), channel_id=1, source_target_pairs={{0,1},{1,0},{2,3},{3,2},{4,5},{5,4},{6,7},{7,6},{8,9},{9,8},{10,11... | collective-permute-start | bytes 12582920 | tf_op jit(solution)/shard_map/ppermute | solution.py:423
  74.9 8.9 %collective-permute-start.16 = (bf16[128,1024]{1,0:T(8,128)(2,1)}, bf16[128,1024]{1,0:T(8,128)(2,1)S(1)}, u32[]{:S(2)}, u32[]{:S(2)}) collective-permute-start(bf16[128,1024]{1,0:T(8,128)(2,1)} %get-tuple-element.141), channel_id=1, source_target_pairs={{0,2},{1,3},{2,0},{3,1},{4,6},{5,7},{6,4},{7,5},{8,10},{9,11},{10,... | collective-permute-start | bytes 786440 | tf_op jit(solution)/shard_map/ppermute | solution.py:423
  76.6 15.0 %collective-permute-start.17 = (bf16[128,1024]{1,0:T(8,128)(2,1)}, bf16[128,1024]{1,0:T(8,128)(2,1)S(1)}, u32[]{:S(2)}, u32[]{:S(2)}) collective-permute-start(bf16[128,1024]{1,0:T(8,128)(2,1)} %get-tuple-element.142), channel_id=1, source_target_pairs={{0,4},{1,5},{2,6},{3,7},{4,0},{5,1},{6,2},{7,3},{8,12},{9,13},{10,... | collective-permute-start | bytes 786440 | tf_op jit(solution)/shard_map/ppermute | solution.py:423
  76.9 18.3 %collective-permute-start.18 = (bf16[128,1024]{1,0:T(8,128)(2,1)}, bf16[128,1024]{1,0:T(8,128)(2,1)S(1)}, u32[]{:S(2)}, u32[]{:S(2)}) collective-permute-start(bf16[128,1024]{1,0:T(8,128)(2,1)} %get-tuple-element.143), channel_id=1, source_target_pairs={{0,6},{1,7},{2,4},{3,5},{4,2},{5,3},{6,0},{7,1},{8,14},{9,15},{10,... | collective-permute-start | bytes 786440 | tf_op jit(solution)/shard_map/ppermute | solution.py:423
  81.2 16.2 %collective-permute-start.19 = (bf16[128,1024]{1,0:T(8,128)(2,1)S(1)}, bf16[128,1024]{1,0:T(8,128)(2,1)S(1)}, u32[]{:S(2)}, u32[]{:S(2)}) collective-permute-start(bf16[128,1024]{1,0:T(8,128)(2,1)S(1)} %get-tuple-element.145), channel_id=1, source_target_pairs={{0,8},{1,9},{2,10},{3,11},{4,12},{5,13},{6,14},{7,15},{8,0},{9,1},... | collective-permute-start | bytes 786440 | tf_op jit(solution)/shard_map/ppermute | solution.py:423
  97.5 14.2 %collective-permute-start.20 = (bf16[128,1024]{1,0:T(8,128)(2,1)S(1)}, bf16[128,1024]{1,0:T(8,128)(2,1)S(1)}, u32[]{:S(2)}, u32[]{:S(2)}) collective-permute-start(bf16[128,1024]{1,0:T(8,128)(2,1)S(1)} %get-tuple-element.149), channel_id=1, source_target_pairs={{0,8},{1,9},{2,10},{3,11},{4,12},{5,13},{6,14},{7,15},{8,0},{9,1},... | collective-permute-start | bytes 786440 | tf_op jit(solution)/shard_map/ppermute | solution.py:423
  116.5 6.3 %collective-permute-start.25 = (f32[40,512]{1,0:T(8,128)S(1)}, f32[40,512]{1,0:T(8,128)S(1)}, u32[]{:S(2)}, u32[]{:S(2)}) collective-permute-start(f32[40,512]{1,0:T(8,128)S(1)} %add.23), channel_id=1, source_target_pairs={{0,6},{1,7},{2,4},{3,5},{4,2},{5,3},{6,0},{7,1},{8,14},{9,15},{10,... | collective-permute-start | bytes 245768 | tf_op jit(solution)/shard_map/ppermute | solution.py:423
  123.9 9.0 %collective-permute-start.28 = (f32[40,512]{1,0:T(8,128)S(1)}, f32[40,512]{1,0:T(8,128)S(1)}, u32[]{:S(2)}, u32[]{:S(2)}) collective-permute-start(f32[40,512]{1,0:T(8,128)S(1)} %add_add_fusion), channel_id=1, source_target_pairs={{0,8},{1,9},{2,10},{3,11},{4,12},{5,13},{6,14},{7,15},{8,0},{9,1},... | collective-permute-start | bytes 245768 | tf_op jit(solution)/shard_map/ppermute | solution.py:423
  (25 other events, 144.7 us)

commit v4 on v3

--- a/solution.py
+++ b/solution.py
@@ -18,6 +18,8 @@
 FIRST = (((0,), (0,)), ((), ()))
 SMALL = 12 * 1024 * 1024
 LARGE = 60 * 1024 * 1024
+WEIGHTS = 24 * 1024 * 1024
+FRONT = 3.3
 WEIGHT = 0.15 * 3.6e6
 
 
@@ -57,6 +59,14 @@
     def __getitem__(self, at):
         self.wait()
         return self.held[at]
+
+
+class Rows:
+    def __init__(self, array, start, size):
+        self.array, self.start, self.shape, self.dtype = array, start, (size, array.shape[1]), array.dtype
+
+    def of(self, ref):
+        return ref.at[pl.ds(self.start, self.shape[0])]
 
 
 def kernel_call(body, operands, outs, scratch=(), weight=0.0, limit=SMALL, scalars=(), first=None):
@@ -71,7 +81,8 @@
         in_semaphores, out_semaphores, rest = rest[0], rest[1], rest[2:]
         values = list(ins)
         for turn, place in enumerate(staged):
-            values[place] = Staged(ins[place], copies[turn], in_semaphores.at[turn])
+            source = operands[place].of(ins[place]) if isinstance(operands[place], Rows) else ins[place]
+            values[place] = Staged(source, copies[turn], in_semaphores.at[turn])
             if first is None or place < first:
                 values[place].start()
         writes = [
@@ -101,7 +112,7 @@
         scratch_shapes=held + results + [pltpu.SemaphoreType.DMA((len(staged),)), pltpu.SemaphoreType.DMA((out_count,))] + list(scratch),
         compiler_params=pltpu.CompilerParams(vmem_limit_bytes=limit),
         cost_estimate=pl.CostEstimate(flops=1, bytes_accessed=int(WEIGHT * weight) + 1, transcendentals=0),
-    )(*operands)
+    )(*[each.array if isinstance(each, Rows) else each for each in operands])
 
 
 def columns_of(ids):
@@ -134,23 +145,30 @@
 
 
 def pack_kernel(near, capacity, ins, outs, scratch, write):
-    chip, normed, far_normed = ins[0:3]
-    count = normed.shape[0] - RIM
-    rows, far_rows = ins[3:5] if len(ins) > 3 else (normed, far_normed)
-    blocks = ((ids_of(normed, count), rows), (ids_of(far_normed, count), far_rows))
-    for block, (names, source) in enumerate(blocks):
-        first, second = placements(columns_of(names), chip[0], near, capacity)
-        packed = dot_first(first + second, source[0:count, :]).astype(BF16)
+    chip, names, rows = ins
+    count = rows.shape[0]
+    first, second = placements(columns_of(ids_of(names[...], count)), chip[0], near, capacity)
+    packed = dot_first(first + second, rows[...]).astype(BF16)
+    for place, out in enumerate(outs):
+        out[...] = packed[place * capacity : (place + 1) * capacity]
+
+
+def pack_both_kernel(near, capacity, ins, outs, scratch, write):
+    chip, names, rows, far_names, far_rows = ins
+    for block, (these, source) in enumerate(((names, rows), (far_names, far_rows))):
+        count = source.shape[0]
+        first, second = placements(columns_of(ids_of(these[...], count)), chip[0], near, capacity)
+        packed = dot_first(first + second, source[...]).astype(BF16)
         for place, out in enumerate(outs):
             out[block * capacity : (block + 1) * capacity, :] = packed[place * capacity : (place + 1) * capacity]
 
 
-def ids_of(normed, count):
-    return normed[count : count + RIM, 0:count][0:2].astype(F32).astype(jnp.int32)
-
-
-def block_rows(refs, block, capacity):
-    return jnp.concatenate([ref[block * capacity : (block + 1) * capacity, :] for ref in refs], axis=0)
+def ids_of(names, count):
+    return names[:, 0:count][0:2].astype(F32).astype(jnp.int32)
+
+
+def all_of(refs):
+    return jnp.concatenate([ref[...] for ref in refs], axis=0)
 
 
 def shifted(pad_ref, lanes, count):
@@ -176,7 +194,7 @@
         body(pl.ds(pl.multiple_of(step * LANES, LANES), LANES))
 
 
-def convolve_and_norm(core, frames, twin, other, taps, gain, names, conv_ref, normed_ref, scratch):
+def convolve_and_norm(core, frames, twin, other, taps, gain, conv_ref, normed_ref, scratch):
     pad_ref, taps32_ref, mixed_ref, square_ref = scratch
     count, width = frames.shape
     fill_padded(pad_ref, core, twin, frames, other)
@@ -196,67 +214,53 @@
     lane_loop(width, conv)
     mean = jnp.sum(square_ref[...], axis=1, keepdims=True) / width
     inverse = lax.rsqrt(mean + NORM_EPS)
-    normed_ref[0:count, :] = (mixed_ref[...] * inverse * gain[...].astype(F32)).astype(BF16)
-    normed_ref[count : count + RIM, :] = names
-
-
-def front_kernel(ins, outs, scratch, write):
-    core, frames, twin, other, taps, gain, names = ins
-    convolve_and_norm(core[0], frames, twin, other, taps, gain, names[...], outs[0], outs[1], scratch)
+    normed_ref[...] = (mixed_ref[...] * inverse * gain[...].astype(F32)).astype(BF16)
+
+
+def front_kernel(near, capacity, ins, outs, scratch, write):
+    chip, core, frames, twin, other, taps, gain, names = ins
+    conv, normed, parts = outs[0], outs[1], outs[2:]
+    convolve_and_norm(core[0], frames, twin, other, taps, gain, conv, normed, scratch)
+    write(0, 1)
+    pack_kernel(near, capacity, (chip, names, normed), parts, scratch, write)
 
 
 def far_front_kernel(near, capacity, ins, outs, scratch, write):
-    chip, core, frames, rims_and_names, taps, gain, normed = ins
-    far_normed, parts = outs[0], outs[1:]
+    chip, core, frames, rims_and_names, taps, gain = ins
+    names, normed, parts = outs[0], outs[1], outs[2:]
     twin, other = rims_and_names[0:RIM, :], rims_and_names[RIM : 2 * RIM, :]
     even = core[0] == 0
     first = jnp.where(even, twin.astype(F32)[RIM - 1 : RIM], twin.astype(F32)[0:1])
     last = jnp.where(even, other.astype(F32)[0:1], other.astype(F32)[RIM - 1 : RIM])
-    names = jnp.concatenate([first, last, jnp.zeros((RIM - 2, frames.shape[1]), F32)], axis=0).astype(BF16)
-    convolve_and_norm(core[0], frames, twin, other, taps, gain, names, None, far_normed, scratch)
-    write(0)
-    pack_kernel(near, capacity, (chip, normed, far_normed), parts, scratch, write)
+    names[...] = jnp.concatenate([first, last, jnp.zeros((RIM - 2, frames.shape[1]), F32)], axis=0).astype(BF16)
+    convolve_and_norm(core[0], frames, twin, other, taps, gain, None, normed, scratch)
+    write(0, 1)
+    pack_kernel(near, capacity, (chip, names, normed), parts, scratch, write)
 
 
 def result_kernel(near, capacity, ins, outs, scratch, write):
-    chip, upstream_near, normed_near, upstream_far, normed_far, router = ins[0:6]
-    rows_refs = ins[6:]
-    near_ref, far_ref, near_logits_ref, far_logits_ref, router_out_ref = outs
-    count = upstream_near.shape[0]
-    router_out = jnp.zeros(router_out_ref.shape, F32)
-    blocks = ((upstream_near, normed_near), (upstream_far, normed_far))
-    for block, (grad, normed) in reversed(list(enumerate(blocks))):
-        names = columns_of(ids_of(normed, count))
-        upstream = grad[...].astype(F32)
-        normed = normed[0:count, :]
-        gates = jax.nn.sigmoid(dot_last(normed, router[...]))
-        rows = block_rows(rows_refs, block, capacity)
-        added = jnp.zeros(upstream.shape, F32)
-        grad_logits = jnp.zeros(gates.shape, F32)
-        for pick, chosen in zip(placements(names, chip[0], near, capacity), choices(names, gates.shape[1])):
-            result = dot(pick, rows)
-            gate = jnp.sum(chosen * gates, axis=1, keepdims=True)
-            added = added + gate * result
-            grad_gate = jnp.sum(upstream * result, axis=1, keepdims=True)
-            grad_logits = grad_logits + chosen * (grad_gate * gate * (1.0 - gate))
-        grad_logits = grad_logits.astype(BF16)
-        (near_ref, far_ref)[block][...] = added.astype((F32, BF16)[block])
+    chip, router, blocks, rows_refs = ins[0], ins[1], (ins[2:4], ins[4:6]), ins[6:]
+    for block, (names, normed) in reversed(list(enumerate(blocks))):
+        ids = columns_of(ids_of(names[...], normed.shape[0]))
+        gates = jax.nn.sigmoid(dot_last(normed[...], router[...]))
+        rows = jnp.concatenate([ref[block * capacity : (block + 1) * capacity, :] for ref in rows_refs], axis=0)
+        added = jnp.zeros(outs[block].shape, F32)
+        for pick, chosen in zip(placements(ids, chip[0], near, capacity), choices(ids, gates.shape[1])):
+            added = added + jnp.sum(chosen * gates, axis=1, keepdims=True) * dot(pick, rows)
+        outs[block][...] = added.astype(outs[block].dtype)
         write(block)
-        (near_logits_ref, far_logits_ref)[block][...] = grad_logits
-        router_out = router_out + dot_first(grad_logits, normed)
-    router_out_ref[...] = router_out
+
+
+def block_kernel(ins, outs, scratch, write):
+    near_sum, mixed, far_sum = ins
+    outs[0][...] = (mixed[...] + (near_sum[...] + far_sum[...].astype(F32))).astype(BF16)
 
 
 def back_kernel(near, capacity, ins, outs, scratch, write):
-    chip, normed_near, logits_near, normed_far, logits_far, router = ins[0:6]
-    rows_refs = ins[6:]
+    chip, names, rows_refs = ins[0], ins[1], ins[2:]
     count = outs[0].shape[0]
-    blocks = ((normed_near, logits_near), (normed_far, logits_far))
-    for block, (normed, logits) in reversed(list(enumerate(blocks))):
-        first, second = placements(columns_of(ids_of(normed, count)), chip[0], near, capacity)
-        total = dot(first + second, block_rows(rows_refs, block, capacity))
-        outs[block][...] = (total + dot(logits[...], router[...])).astype(outs[block].dtype)
-        write(block)
+    first, second = placements(columns_of(ids_of(names[...], count)), chip[0], near, capacity)
+    outs[0][...] = dot(first + second, all_of(rows_refs)).astype(outs[0].dtype)
 
 
 def half_lanes(core, width):
@@ -264,8 +268,8 @@
 
 
 def final_kernel(ins, outs, scratch, write):
-    core, frames, twin, other, conv, grad, gain, near_sum, far_sum, router, near_back, far_back = ins
-    out_ref, mixed_grad_ref, conv_grad_ref, twin_ref, other_ref, kept_ref, given_ref = outs
+    core, frames, twin, other, conv, grad, gain, router, near_back, far_back = ins
+    mixed_ref, mixed_grad_ref, conv_grad_ref, twin_ref, other_ref, kept_ref, given_ref = outs
     pad_ref, local_ref = scratch
     count, width = frames.shape
     fill_padded(pad_ref, core[0], twin, frames, other)
@@ -273,9 +277,9 @@
     logistic = jax.nn.sigmoid(conv_out)
     mixed = frames[...].astype(F32) + conv_out * logistic
     inverse = lax.rsqrt(jnp.sum(mixed * mixed, axis=1, keepdims=True) / width + NORM_EPS)
-    out_ref[...] = (mixed + (near_sum[...] + far_sum[...].astype(F32))).astype(BF16)
+    local_ref[KSIZE + 1 :, :] = router[...]
+    mixed_ref[...] = mixed
     write(0)
-    local_ref[KSIZE + 1 :, :] = router[...]
     grad_normed = near_back[...] + far_back[...].astype(F32)
     local_ref[KSIZE : KSIZE + 1, :] = jnp.sum(grad_normed * mixed * inverse, axis=0, keepdims=True)
     scaled = grad_normed * gain[...].astype(F32)
@@ -325,14 +329,28 @@
         rows_ref[place * each : (place + 1) * each, :] = ref[...]
 
 
+def gather_pairs(refs, rows_ref):
+    each = refs[0].shape[0] // 2
+    for place, ref in enumerate(refs):
+        for block, start in enumerate((place * each, (len(refs) + place) * each)):
+            rows_ref[start : start + each, :] = ref[block * each : (block + 1) * each, :]
+
+
 def scatter_columns(refs, columns, values):
     each = refs[0].shape[0]
     for place, ref in enumerate(refs):
         ref[:, columns] = values[place * each : (place + 1) * each]
 
 
+def scatter_pairs(refs, columns, values):
+    each = refs[0].shape[0] // 2
+    for place, ref in enumerate(refs):
+        for block, start in enumerate((place * each, (len(refs) + place) * each)):
+            ref[block * each : (block + 1) * each, columns] = values[start : start + each]
+
+
 def forward_kernel(near, ins, outs, scratch, write):
-    rows, (near_in, far_in, near_out, far_out) = ins[0:near], ins[near:]
+    rows, (near_in, far_in, near_out, far_out) = ins[0 : 2 * near], ins[2 * near :]
     out_refs, (rows_ref, near_slope, far_slope, near_active, far_active) = outs[0:near], outs[near:]
     gather_rows(rows, rows_ref)
     near_in.wait()
@@ -352,38 +370,47 @@
     for columns in chunks(near_out.shape[1]):
         total = dot(near_active[...], near_out[:, columns])
         total = total + dot(far_active[...], far_out[:, columns])
-        scatter_columns(out_refs, columns, total.astype(BF16))
+        scatter_pairs(out_refs, columns, total.astype(BF16))
 
 
 def backward_kernel(near, ins, outs, scratch, write):
     chip, grads, rest = ins[0], ins[1 : near + 1], ins[near + 1 :]
-    rows, router, near_out, far_out, near_slope, far_slope, near_in, far_in, far_active = rest
-    out_refs, (near_grad, sent) = outs[0:near], outs[near:]
-    (grads_ref,) = scratch
+    rows, router, near_out, far_out, near_slope, far_slope, near_active, far_active, near_in, far_in = rest
+    out_refs, (near_grad, sent, router_out) = outs[0 : 2 * near], outs[2 * near :]
+    grads_ref, dots_ref = scratch
     count = rows.shape[0]
     rows_part, active_part, grads_part, pre_part = (slice(turn * count, (turn + 1) * count) for turn in range(4))
-    gather_rows(grads, grads_ref)
+    gather_pairs(grads, grads_ref)
     logits = dot_last(rows[...], router[...])
     mine = lax.broadcasted_iota(jnp.int32, logits.shape, 1) == chip[0]
     gate = jax.nn.sigmoid(jnp.sum(jnp.where(mine, logits, 0.0), axis=1, keepdims=True))
     sent[grads_part, :] = (gate * grads_ref[...].astype(F32)).astype(BF16)
-    for later in (far_out, near_slope, far_slope, near_in, far_in, far_active):
+    for later in rest[3:]:
         later.start()
-    for weight, slope, grad, part in ((near_out, near_slope, near_grad, slice(None)), (far_out, far_slope, sent, pre_part)):
-        weight.wait()
-        slope.wait()
+    dots_ref[...] = jnp.zeros_like(dots_ref)
+    for weight, slope, active, grad, part in (
+        (near_out, near_slope, near_active, near_grad, slice(None)),
+        (far_out, far_slope, far_active, sent, pre_part),
+    ):
+        for ref in (weight, slope, active):
+            ref.wait()
         for columns in chunks(weight.shape[0]):
             hidden = dot_last(sent[grads_part, :], weight[columns, :])
+            dots_ref[...] += hidden * active[:, columns].astype(F32)
             grad[part, columns] = (hidden * slope[:, columns].astype(F32)).astype(BF16)
-    write(near)
+    write(2 * near)
     sent[rows_part, :] = rows[...]
     sent[active_part, :] = far_active[...]
-    write(near + 1)
+    write(2 * near + 1)
+    chosen = jnp.sum(dots_ref[...], axis=1, keepdims=True) * (1.0 - gate)
+    grad_logits = jnp.where(mine, chosen, 0.0).astype(BF16)
+    router_out[...] = dot_first(grad_logits, rows[...])
     near_in.wait()
     far_in.wait()
     for columns in chunks(near_in.shape[0]):
         total = dot_last(near_grad[...], near_in[columns, :])
         total = total + dot_last(sent[pre_part, :], far_in[columns, :])
+        total = total + dot(grad_logits, router[:, columns])
         scatter_columns(out_refs, columns, total.astype(BF16))
 
 
@@ -460,94 +487,97 @@
     twin, other, other_in, other_out = lax.optimization_barrier((twin, other, other_in, other_out))
 
     model32, model16 = shape((count, width), F32), shape((count, width), BF16)
-    named16 = shape((count + RIM, width), BF16)
-    front_scratch = (pad, taps32, pltpu.VMEM((count, width), F32), pltpu.VMEM((count, LANES), F32))
-    conv_out, normed = kernel_call(
-        front_kernel,
-        (cores, frames, twin, other, taps, gain, names),
-        (model32, named16),
-        front_scratch,
-        weight=3.3,
-        scalars=(0,),
-    )
+    part = (shape((capacity, width), BF16),) * near
+    pair = (shape((2 * capacity, width), BF16),) * near
     even = jnp.concatenate([twin[: RIM - 1], names[0:1], names[1:2], other[1:]])
     odd = jnp.concatenate([names[0:1], twin[1:], other[: RIM - 1], names[1:2]])
     far_rims = cross(jnp.where(core == 0, even, odd))
+    front_scratch = (pad, taps32, pltpu.VMEM((count, width), F32), pltpu.VMEM((count, LANES), F32))
+    conv_out, normed, *parts = kernel_call(
+        functools.partial(front_kernel, near, capacity),
+        (chips, cores, frames, twin, other, taps, gain, names),
+        (model32, model16, *part),
+        front_scratch,
+        weight=FRONT,
+        scalars=(0, 1),
+    )
+    rows = exchange(parts, devices)
     far_rims, far_frames, out_grad = lax.optimization_barrier((far_rims, far_frames, out_grad))
     far_grad = cross(out_grad)
-    part = (shape((2 * capacity, width), BF16),) * near
-    far_normed, *parts = kernel_call(
+    far_names, far_normed, *parts = kernel_call(
         functools.partial(far_front_kernel, near, capacity),
-        (chips, cores, far_frames, far_rims, taps, gain, normed),
-        (named16, *part),
+        (chips, cores, far_frames, far_rims, taps, gain),
+        (shape((RIM, width), BF16), model16, *part),
         front_scratch,
+        limit=LARGE,
         scalars=(0, 1),
     )
-    rows = exchange(parts, devices)
+    rows, parts = lax.optimization_barrier((rows, parts))
+    far_rows = exchange(parts, devices)
     parts = kernel_call(
-        functools.partial(pack_kernel, near, capacity),
-        (chips, normed, far_normed, out_grad, far_grad),
-        part,
-        weight=0.0,
+        functools.partial(pack_both_kernel, near, capacity),
+        (chips, names, out_grad, far_names, far_grad),
+        pair,
         scalars=(0,),
     )
-    rows[0:3], parts = lax.optimization_barrier((rows[0:3], parts))
-    grads = exchange(parts, devices)
+    far_rows, parts = lax.optimization_barrier((far_rows, parts))
+    rows, grads = rows + far_rows, exchange(parts, devices)
 
     narrow = shape((slots, weight_in.shape[1]), BF16)
     outs = kernel_call(
         functools.partial(forward_kernel, near),
         (*rows, weight_in, other_in, weight_out, other_out),
-        part + (shape((slots, width), BF16), narrow, narrow, narrow, narrow),
+        pair + (shape((slots, width), BF16), narrow, narrow, narrow, narrow),
         limit=LARGE,
-        first=near + 2,
-    )
-    parts_out, (all_rows, *slopes), (near_active, far_active) = outs[0:near], outs[near : near + 3], outs[near + 3 :]
-    results = exchange(parts_out, devices)
+        first=2 * near + 2,
+    )
+    parts, all_rows, slopes, (near_active, far_active) = outs[0:near], outs[near], outs[near + 1 : near + 3], outs[near + 3 :]
+    results = exchange(parts, devices)
     outs = kernel_call(
         functools.partial(backward_kernel, near),
-        (chips, *grads, all_rows, router, weight_out, other_out, *slopes, weight_in, other_in, far_active),
-        part + (narrow, shape((4 * slots, width), BF16)),
-        (pltpu.VMEM((slots, width), BF16),),
+        (chips, *grads, all_rows, router, weight_out, other_out, *slopes, near_active, far_active, weight_in, other_in),
+        2 * part + (narrow, shape((4 * slots, width), BF16), shape((experts, width), F32)),
+        (pltpu.VMEM((slots, width), BF16), pltpu.VMEM((slots, CHUNK), F32)),
         limit=LARGE,
         first=near + 4,
         scalars=(0,),
     )
     results, outs = lax.optimization_barrier((results, outs))
-    parts_in, near_grad, sent = outs[0:near], outs[near], outs[near + 1]
-    backs = exchange(parts_in, devices)
-
-    logits = shape((count, experts), BF16)
-    near_sum, far_sum, near_logits, far_logits, router_local = kernel_call(
+    own_in, far_in, (near_grad, sent, router_local) = outs[0:near], outs[near : 2 * near], outs[2 * near :]
+    backs = exchange(far_in, devices)
+    near_sum, far_sum = kernel_call(
         functools.partial(result_kernel, near, capacity),
-        (chips, out_grad, normed, far_grad, far_normed, router, *results),
-        (model32, model16, logits, logits, shape((experts, width), F32)),
-        weight=0.0,
+        (chips, router, names, normed, far_names, far_normed, *results),
+        (model32, model16),
+        weight=2.4,
         scalars=(0,),
     )
-    far_sum = cross(far_sum)
-    near_back, far_back = kernel_call(
-        functools.partial(back_kernel, near, capacity),
-        (chips, normed, near_logits, far_normed, far_logits, router, *backs),
-        (model32, model16),
-        weight=0.0,
-        scalars=(0,),
-    )
-    far_back, far_sum = lax.optimization_barrier((far_back, far_sum))
+    backs, near_sum, far_sum = lax.optimization_barrier((backs, near_sum, far_sum))
+    (far_back,) = kernel_call(
+        functools.partial(back_kernel, near, capacity), (chips, far_names, *backs), (model16,), scalars=(0,)
+    )
+    far_back, own_in, far_sum = lax.optimization_barrier((far_back, own_in, far_sum))
     far_back = cross(far_back)
     grad = shape(weight_in.shape, BF16)
     expert_in_grad, expert_out_grad = kernel_call(
-        weights_kernel, (near_active, near_grad, sent, swap(sent, devices, 1)), (grad, grad), limit=LARGE
+        weights_kernel, (near_active, near_grad, sent, swap(sent, devices, 1)), (grad, grad), limit=WEIGHTS
+    )
+    backs, expert_in_grad, expert_out_grad = lax.optimization_barrier(
+        (exchange(own_in, devices), expert_in_grad, expert_out_grad)
+    )
+    (near_back,) = kernel_call(
+        functools.partial(back_kernel, near, capacity), (chips, names, *backs), (model32,), scalars=(0,)
     )
     far_back, expert_in_grad, expert_out_grad = lax.optimization_barrier((far_back, expert_in_grad, expert_out_grad))
+    far_sum = cross(far_sum)
 
     rim = shape((RIM, width), BF16)
     lines = KSIZE + 1 + experts
     columns = shape((lines, width // 2), F32)
-    block_out, mixed_grad, conv_grad, to_twin, to_other, kept, given = kernel_call(
+    mixed, mixed_grad, conv_grad, to_twin, to_other, kept, given = kernel_call(
         final_kernel,
-        (cores, frames, twin, other, conv_out, out_grad, gain, near_sum, far_sum, router_local, near_back, far_back),
-        (model16, model32, model16, rim, rim, columns, columns),
+        (cores, frames, twin, other, conv_out, out_grad, gain, router_local, near_back, far_back),
+        (model32, model32, model16, rim, rim, columns, columns),
         (pad, pltpu.VMEM((lines, width), F32)),
         weight=0.0,
         scalars=(0,),
@@ -559,7 +589,8 @@
         last = 4 * bit > devices
         others = [swap(local, devices, step) for step in ((bit,) if last else (bit, 2 * bit, 3 * bit))]
         if bit == 2:
-            others, grad_twin, grad_other = lax.optimization_barrier((others, grad_twin, grad_other))
+            others, grad_twin, grad_other, far_sum = lax.optimization_barrier((others, grad_twin, grad_other, far_sum))
+            (block_out,) = kernel_call(block_kernel, (near_sum, mixed, far_sum), (model16,))
             (frames_grad,) = kernel_call(
                 frames_kernel,
                 (cores, mixed_grad, conv_grad, grad_twin, grad_other, taps),
@@ -569,7 +600,7 @@
             )
         bit *= 2 if last else 4
         if bit == devices:
-            others, frames_grad = lax.optimization_barrier((others, frames_grad))
+            others, frames_grad, block_out = lax.optimization_barrier((others, frames_grad, block_out))
         local = local + others[0] if last else (local + others[0]) + (others[1] + others[2])
     kernel_grad, gain_grad, router_grad = kernel_call(
         last_kernel,

time: 136 us -> 129 us (0.949)
  waiting for transfers between devices: 34.9 us -> 17.8 us
  starting transfers between devices: 36.9 us -> 45.4 us
  Pallas kernels: 51.7 us -> 53.4 us
    ppermute x28 -> x34, waiting for transfers between devices: 34.9 us -> 17.8 us  [swap(): return lax.ppermute(values, 'seq', [(i, i ^ bit) for i in range(count)])]
    ppermute x28 -> x34, starting transfers between devices: 35.6 us -> 44.1 us  [swap(): return lax.ppermute(values, 'seq', [(i, i ^ bit) for i in range(count)])]
    pallas_call x11 -> x13, Pallas kernels: 51.7 us -> 53.4 us  [kernel_call(): pl.pallas_call(kernel, out_shape=tuple(outs), in_specs=[pl.BlockSpec(memo...]
    unnamed x38 -> x64, local copies, waits for them, and re-layouts: 8.37 us -> 8.78 us
  transfers between devices with their start and end apart: 30 -> 36, of which waited for: 16 -> 13; matrix products, arithmetic and copies ran while one was open for 2% -> 2% of each run, Pallas kernels for 35% -> 41%
where the time goes in v4:
time: 129 us
  Pallas kernels  53.4 us (41%)
  starting transfers between devices  45.4 us (35%)
  waiting for transfers between devices  17.8 us (14%)
  local copies, waits for them, and re-layouts  9.51 us (7%)
  other arithmetic  1.57 us (1%)
  between operations  1.3 us (1%)
    pallas_call x13, Pallas kernels, kernel_call(): pl.pallas_call(kernel, out_shape=tuple(outs), in_specs=[pl.BlockSpec(memo...  53.4 us
    ppermute x34, starting transfers between devices, swap(): return lax.ppermute(values, 'seq', [(i, i ^ bit) for i in range(count)])  44.1 us
    ppermute x34, waiting for transfers between devices, swap(): return lax.ppermute(values, 'seq', [(i, i ^ bit) for i in range(count)])  17.8 us
    unnamed x64, local copies, waits for them, and re-layouts  8.78 us
  transfers between devices with their start and end apart: 36, of which 13 were waited for; matrix products, arithmetic and copies ran while one was open for 2% of the time, Pallas kernels for 41%

profile of v4, /device:TPU:0, one launch (start us, length us, event | category | flops | bytes accessed | tf_op | source)
XLA Modules:
  0.0 129.0 jit_solution(16273566603453888766)
XLA Ops:
  3.2 6.4 %collective-permute-start.5 = (bf16[128,1024]{1,0:T(8,128)(2,1)}, bf16[128,1024]{1,0:T(8,128)(2,1)S(1)}, u32[]{:S(2)}, u32[]{:S(2)}) collective-permute-start(bf16[128,1024]{1,0:T(8,128)(2,1)} %refs_1_), channel_id=1, source_target_pairs={{0,8},{1,9},{2,10},{3,11},{4,12},{5,13},{6,14},{7,15},{8,0},{9,1},... | collective-permute-start | bytes 786440 | tf_op jit(solution)/shard_map/ppermute | solution.py:450
  10.4 2.1 %collective-permute-start.4 = (bf16[32,1024]{1,0:T(8,128)(2,1)S(1)}, bf16[32,1024]{1,0:T(8,128)(2,1)S(1)}, u32[]{:S(2)}, u32[]{:S(2)}) collective-permute-start(bf16[32,1024]{1,0:T(8,128)(2,1)S(1)} %maximum_select_fusion), channel_id=1, source_target_pairs={{0,8},{1,9},{2,10},{3,11},{4,12},{5,13},{6,14},{7,15},{8,0},{9,1},... | collective-permute-start | bytes 196616 | tf_op jit(solution)/shard_map/ppermute | solution.py:450
  15.0 4.8 %shard_map.135 = (f32[128,1024]{1,0:T(8,128)S(1)}, bf16[128,1024]{1,0:T(8,128)(2,1)S(1)}, bf16[64,1024]{1,0:T(8,128)(2,1)S(1)}, bf16[64,1024]{1,0:T(8,128)(2,1)S...) custom-call(s32[1]{0:T(128)} %bitcast.3.refs_0_, s32[1]{0:T(128)} %bitcast.refs_1_.refs_0_, ...), custom_call_target="tpu_custom_call" | custom-call | flops 1 | bytes 1782001 | tf_op jit(solution)/shard_map/pallas_call | solution.py:107
  21.9 2.2 %collective-permute-start.7 = (bf16[64,1024]{1,0:T(8,128)(2,1)S(1)}, bf16[64,1024]{1,0:T(8,128)(2,1)S(1)}, u32[]{:S(2)}, u32[]{:S(2)}) collective-permute-start(bf16[64,1024]{1,0:T(8,128)(2,1)S(1)} %get-tuple-element.137), channel_id=1, source_target_pairs={{0,4},{1,5},{2,6},{3,7},{4,0},{5,1},{6,2},{7,3},{8,12},{9,13},{10,... | collective-permute-start | bytes 393224 | tf_op jit(solution)/shard_map/ppermute | solution.py:450
  26.8 5.6 %shard_map.136 = (bf16[16,1024]{1,0:T(8,128)(2,1)}, bf16[128,1024]{1,0:T(8,128)(2,1)}, bf16[64,1024]{1,0:T(8,128)(2,1)}, bf16[64,1024]{1,0:T(8,128)(2,1)}, bf16[...) custom-call(s32[1]{0:T(128)} %bitcast.3.refs_0_, s32[1]{0:T(128)} %bitcast.refs_1_.refs_0_, bf16[128,1024]{1,0:T(8,128)(2,1)} %copy-done.24, ...), custom_call_target="tpu_custom_call" | custom-call | flops 1 | bytes 1 | tf_op jit(solution)/shard_map/pallas_call | solution.py:107
  33.0 2.0 %collective-permute-start.9 = (bf16[64,1024]{1,0:T(8,128)(2,1)}, bf16[64,1024]{1,0:T(8,128)(2,1)S(1)}, u32[]{:S(2)}, u32[]{:S(2)}) collective-permute-start(bf16[64,1024]{1,0:T(8,128)(2,1)} %get-tuple-element.150), channel_id=1, source_target_pairs={{0,2},{1,3},{2,0},{3,1},{4,6},{5,7},{6,4},{7,5},{8,10},{9,11},{10,... | collective-permute-start | bytes 393224 | tf_op jit(solution)/shard_map/ppermute | solution.py:450
  36.5 3.5 %collective-permute-done.12.refs_4_ = bf16[128,1024]{1,0:T(8,128)(2,1)S(1)} collective-permute-done((bf16[128,1024]{1,0:T(8,128)(2,1)}, bf16[128,1024]{1,0:T(8,128)(2,1)S(1)}, u32[]{:S(2)}, u32[]{:S(2)}) %collective-permute-start.12) | collective-permute-done | bytes 262176 | tf_op jit(solution)/shard_map/ppermute | solution.py:450
  41.7 2.0 %shard_map.137 = (bf16[128,1024]{1,0:T(8,128)(2,1)S(1)}, bf16[128,1024]{1,0:T(8,128)(2,1)S(1)}, bf16[128,1024]{1,0:T(8,128)(2,1)S(1)}, bf16[128,1024]{1,0:T(8,128)(2,1)S(1)}) custom-call(s32[1]{0:T(128)} %bitcast.3.refs_0_, bf16[16,1024]{1,0:T(8,128)(2,1)S(1)} %pad.4.refs_7_.refs_1_.refs_2_, bf16[128,1024]{1,0:T(8,128)(2,1)S(1)} %copy-done.5, ...), custom_call_target="tpu_custom_call" | custom-call | flops 1 | bytes 1 | tf_op jit(solution)/shard_map/pallas_call | solution.py:107
  47.0 2.2 %collective-permute-start.18 = (bf16[128,1024]{1,0:T(8,128)(2,1)S(1)}, bf16[128,1024]{1,0:T(8,128)(2,1)S(1)}, u32[]{:S(2)}, u32[]{:S(2)}) collective-permute-start(bf16[128,1024]{1,0:T(8,128)(2,1)S(1)} %get-tuple-element.171), channel_id=1, source_target_pairs={{0,6},{1,7},{2,4},{3,5},{4,2},{5,3},{6,0},{7,1},{8,14},{9,15},{10,... | collective-permute-start | bytes 786440 | tf_op jit(solution)/shard_map/ppermute | solution.py:450
  49.2 8.7 %shard_map.138 = (bf16[128,1024]{1,0:T(8,128)(2,1)}, bf16[128,1024]{1,0:T(8,128)(2,1)}, bf16[128,1024]{1,0:T(8,128)(2,1)}, bf16[128,1024]{1,0:T(8,128)(2,1)}, bf...) custom-call(bf16[64,1024]{1,0:T(8,128)(2,1)} %copy-done.13, ...), custom_call_target="tpu_custom_call" | custom-call | flops 1 | bytes 1 | tf_op jit(solution)/shard_map/pallas_call | solution.py:107
  59.2 2.2 %collective-permute-start.15 = (bf16[128,1024]{1,0:T(8,128)(2,1)}, bf16[128,1024]{1,0:T(8,128)(2,1)S(1)}, u32[]{:S(2)}, u32[]{:S(2)}) collective-permute-start(bf16[128,1024]{1,0:T(8,128)(2,1)} %get-tuple-element.167), channel_id=1, source_target_pairs={{0,6},{1,7},{2,4},{3,5},{4,2},{5,3},{6,0},{7,1},{8,14},{9,15},{10,... | collective-permute-start | bytes 786440 | tf_op jit(solution)/shard_map/ppermute | solution.py:450
  62.3 11.3 %shard_map.139 = (bf16[64,1024]{1,0:T(8,128)(2,1)}, bf16[64,1024]{1,0:T(8,128)(2,1)}, bf16[64,1024]{1,0:T(8,128)(2,1)}, bf16[64,1024]{1,0:T(8,128)(2,1)}, bf16[6...) custom-call(s32[1]{0:T(128)} %bitcast.3.refs_0_, ...), custom_call_target="tpu_custom_call" | custom-call | flops 1 | bytes 1 | tf_op jit(solution)/shard_map/pallas_call | solution.py:107
  75.1 2.2 %collective-permute-start.21 = (bf16[64,1024]{1,0:T(8,128)(2,1)}, bf16[64,1024]{1,0:T(8,128)(2,1)S(1)}, u32[]{:S(2)}, u32[]{:S(2)}) collective-permute-start(bf16[64,1024]{1,0:T(8,128)(2,1)} %get-tuple-element.192), channel_id=1, source_target_pairs={{0,6},{1,7},{2,4},{3,5},{4,2},{5,3},{6,0},{7,1},{8,14},{9,15},{10,... | collective-permute-start | bytes 393224 | tf_op jit(solution)/shard_map/ppermute | solution.py:450
  77.3 2.2 %shard_map.140 = (f32[128,1024]{1,0:T(8,128)S(1)}, bf16[128,1024]{1,0:T(8,128)(2,1)S(1)}) custom-call(s32[1]{0:T(128)} %bitcast.3.refs_0_, bf16[8,1024]{1,0:T(8,128)(2,1)S(1)} %bitcast.12, bf16[16,1024]{1,0:T(8,128)(2,1)S(1)} %pad.4.refs_7_.refs_1_.refs_2_, bf16[128,1024]{1,0:T(8,128)(2,1)S(1)} %get-tuple-element.193.refs_3_, ...), custom_call_target="tpu_custom_call" | custom-call | flops 1 | bytes 1296001 | tf_op jit(solution)/shard_map/pallas_call | solution.py:107
  79.8 1.8 %collective-permute-done.20.refs_4_ = bf16[64,1024]{1,0:T(8,128)(2,1)S(1)} collective-permute-done((bf16[64,1024]{1,0:T(8,128)(2,1)}, bf16[64,1024]{1,0:T(8,128)(2,1)S(1)}, u32[]{:S(2)}, u32[]{:S(2)}) %collective-permute-start.20) | collective-permute-done | bytes 131104 | tf_op jit(solution)/shard_map/ppermute | solution.py:450
  81.6 2.2 %collective-permute-done.21.refs_5_ = bf16[64,1024]{1,0:T(8,128)(2,1)S(1)} collective-permute-done((bf16[64,1024]{1,0:T(8,128)(2,1)}, bf16[64,1024]{1,0:T(8,128)(2,1)S(1)}, u32[]{:S(2)}, u32[]{:S(2)}) %collective-permute-start.21) | collective-permute-done | bytes 131104 | tf_op jit(solution)/shard_map/ppermute | solution.py:450
  84.7 1.7 %shard_map.141 = bf16[128,1024]{1,0:T(8,128)(2,1)S(1)} custom-call(s32[1]{0:T(128)} %bitcast.3.refs_0_, bf16[16,1024]{1,0:T(8,128)(2,1)S(1)} %copy-done.9, bf16[64,1024]{1,0:T(8,128)(2,1)S(1)} %copy-done.14, bf16[64,1024]{1,0:T(8,128)(2,1)S(1)} %collective-permute-done.19.refs_3_, bf16[64,1024]{1,0:T(8,128)(2,1)S(1)} %collective-permute-done.20.refs_4_, ...), custom_call_target="tpu_custom_call" | custom-call | flops 1 | bytes 1 | tf_op jit(solution)/shard_map/pallas_call | solution.py:107
  93.0 2.2 %copy-done.1 = bf16[2048,1024]{1,0:T(8,128)(2,1)S(1)} copy-done((bf16[2048,1024]{1,0:T(8,128)(2,1)S(1)}, bf16[2048,1024]{1,0:T(8,128)(2,1)}, u32[]{:S(2)}) %copy-start.1) | copy-done | bytes 4194328
  95.2 6.6 %shard_map.142 = (bf16[1024,1024]{1,0:T(8,128)(2,1)}, bf16[1024,1024]{1,0:T(8,128)(2,1)}) custom-call(bf16[512,1024]{1,0:T(8,128)(2,1)S(1)} %copy-done, bf16[512,1024]{1,0:T(8,128)(2,1)S(1)} %copy-done.4, bf16[2048,1024]{1,0:T(8,128)(2,1)S(1)} %copy-done.1, bf16[2048,1024]{1,0:T(8,128)(2,1)S(1)} %collective-permute-done.25.refs_3_), custom_call_target="tpu_custom_call" | custom-call | flops 1 | bytes 1 | tf_op jit(solution)/shard_map/pallas_call | solution.py:107
  104.4 3.4 %shard_map.144 = (f32[128,1024]{1,0:T(8,128)S(1)}, f32[128,1024]{1,0:T(8,128)S(1)}, bf16[128,1024]{1,0:T(8,128)(2,1)S(1)}, bf16[16,1024]{1,0:T(8,128)(2,1)S(1)},...) custom-call(s32[1]{0:T(128)} %bitcast.refs_1_.refs_0_, ...), custom_call_target="tpu_custom_call" | custom-call | flops 1 | bytes 1 | tf_op jit(solution)/shard_map/pallas_call | solution.py:107
  110.1 4.2 %collective-permute-start.29 = (f32[40,512]{1,0:T(8,128)S(1)}, f32[40,512]{1,0:T(8,128)S(1)}, u32[]{:S(2)}, u32[]{:S(2)}) collective-permute-start(f32[40,512]{1,0:T(8,128)S(1)} %add.23), channel_id=1, source_target_pairs={{0,4},{1,5},{2,6},{3,7},{4,0},{5,1},{6,2},{7,3},{8,12},{9,13},{10,... | collective-permute-start | bytes 245768 | tf_op jit(solution)/shard_map/ppermute | solution.py:450
  115.5 3.0 %collective-permute-done.29 = f32[40,512]{1,0:T(8,128)S(1)} collective-permute-done((f32[40,512]{1,0:T(8,128)S(1)}, f32[40,512]{1,0:T(8,128)S(1)}, u32[]{:S(2)}, u32[]{:S(2)}) %collective-permute-start.29) | collective-permute-done | bytes 81952 | tf_op jit(solution)/shard_map/ppermute | solution.py:450
  118.8 2.2 %collective-permute-start.34 = (f32[40,512]{1,0:T(8,128)S(1)}, f32[40,512]{1,0:T(8,128)S(1)}, u32[]{:S(2)}, u32[]{:S(2)}) collective-permute-start(f32[40,512]{1,0:T(8,128)S(1)} %add_add_fusion), channel_id=1, source_target_pairs={{0,8},{1,9},{2,10},{3,11},{4,12},{5,13},{6,14},{7,15},{8,0},{9,1},... | collective-permute-start | bytes 245768 | tf_op jit(solution)/shard_map/ppermute | solution.py:450
  121.9 3.7 %shard_map.145 = bf16[128,1024]{1,0:T(8,128)(2,1)} custom-call(s32[1]{0:T(128)} %bitcast.refs_1_.refs_0_, f32[128,1024]{1,0:T(8,128)S(1)} %get-tuple-element.234.refs_1_, bf16[128,1024]{1,0:T(8,128)(2,1)S(1)} %get-tuple-element.235.refs_2_, bf16[16,1024]{1,0:T(8,128)(2,1)S(1)} %collective-permute-done.31.refs_3_, ...), custom_call_target="tpu_custom_call" | custom-call | flops 1 | bytes 1 | tf_op jit(solution)/shard_map/pallas_call | solution.py:107
  (136 shorter events, 39.5 us)
Async XLA Ops:
  0.6 9.7 %collective-permute-start.2 = (bf16[1024,1024]{1,0:T(8,128)(2,1)}, bf16[1024,1024]{1,0:T(8,128)(2,1)S(1)}, u32[]{:S(2)}, u32[]{:S(2)}) collective-permute-start(bf16[1024,1024]{1,0:T(8,128)(2,1)} %bitcast.13), channel_id=1, source_target_pairs={{0,1},{1,0},{2,3},{3,2},{4,5},{5,4},{6,7},{7,6},{8,9},{9,8},{10,11... | collective-permute-start | bytes 6291464 | tf_op jit(solution)/shard_map/ppermute | solution.py:450
  1.1 9.2 %collective-permute-start.3 = (bf16[1024,1024]{1,0:T(8,128)(2,1)}, bf16[1024,1024]{1,0:T(8,128)(2,1)}, u32[]{:S(2)}, u32[]{:S(2)}) collective-permute-start(bf16[1024,1024]{1,0:T(8,128)(2,1)} %bitcast.16), channel_id=1, source_target_pairs={{0,1},{1,0},{2,3},{3,2},{4,5},{5,4},{6,7},{7,6},{8,9},{9,8},{10,11... | collective-permute-start | bytes 6291464 | tf_op jit(solution)/shard_map/ppermute | solution.py:450
  3.2 22.4 %collective-permute-start.5 = (bf16[128,1024]{1,0:T(8,128)(2,1)}, bf16[128,1024]{1,0:T(8,128)(2,1)S(1)}, u32[]{:S(2)}, u32[]{:S(2)}) collective-permute-start(bf16[128,1024]{1,0:T(8,128)(2,1)} %refs_1_), channel_id=1, source_target_pairs={{0,8},{1,9},{2,10},{3,11},{4,12},{5,13},{6,14},{7,15},{8,0},{9,1},... | collective-permute-start | bytes 786440 | tf_op jit(solution)/shard_map/ppermute | solution.py:450
  10.4 15.1 %collective-permute-start.4 = (bf16[32,1024]{1,0:T(8,128)(2,1)S(1)}, bf16[32,1024]{1,0:T(8,128)(2,1)S(1)}, u32[]{:S(2)}, u32[]{:S(2)}) collective-permute-start(bf16[32,1024]{1,0:T(8,128)(2,1)S(1)} %maximum_select_fusion), channel_id=1, source_target_pairs={{0,8},{1,9},{2,10},{3,11},{4,12},{5,13},{6,14},{7,15},{8,0},{9,1},... | collective-permute-start | bytes 196616 | tf_op jit(solution)/shard_map/ppermute | solution.py:450
  20.5 11.9 %collective-permute-start.6 = (bf16[64,1024]{1,0:T(8,128)(2,1)S(1)}, bf16[64,1024]{1,0:T(8,128)(2,1)S(1)}, u32[]{:S(2)}, u32[]{:S(2)}) collective-permute-start(bf16[64,1024]{1,0:T(8,128)(2,1)S(1)} %get-tuple-element.136), channel_id=1, source_target_pairs={{0,2},{1,3},{2,0},{3,1},{4,6},{5,7},{6,4},{7,5},{8,10},{9,11},{10,... | collective-permute-start | bytes 393224 | tf_op jit(solution)/shard_map/ppermute | solution.py:450
  21.9 10.5 %collective-permute-start.7 = (bf16[64,1024]{1,0:T(8,128)(2,1)S(1)}, bf16[64,1024]{1,0:T(8,128)(2,1)S(1)}, u32[]{:S(2)}, u32[]{:S(2)}) collective-permute-start(bf16[64,1024]{1,0:T(8,128)(2,1)S(1)} %get-tuple-element.137), channel_id=1, source_target_pairs={{0,4},{1,5},{2,6},{3,7},{4,0},{5,1},{6,2},{7,3},{8,12},{9,13},{10,... | collective-permute-start | bytes 393224 | tf_op jit(solution)/shard_map/ppermute | solution.py:450
  24.1 9.0 %collective-permute-start.8 = (bf16[64,1024]{1,0:T(8,128)(2,1)S(1)}, bf16[64,1024]{1,0:T(8,128)(2,1)S(1)}, u32[]{:S(2)}, u32[]{:S(2)}) collective-permute-start(bf16[64,1024]{1,0:T(8,128)(2,1)S(1)} %get-tuple-element.138), channel_id=1, source_target_pairs={{0,6},{1,7},{2,4},{3,5},{4,2},{5,3},{6,0},{7,1},{8,14},{9,15},{10,... | collective-permute-start | bytes 393224 | tf_op jit(solution)/shard_map/ppermute | solution.py:450
  25.5 14.5 %collective-permute-start.12 = (bf16[128,1024]{1,0:T(8,128)(2,1)}, bf16[128,1024]{1,0:T(8,128)(2,1)S(1)}, u32[]{:S(2)}, u32[]{:S(2)}) collective-permute-start(bf16[128,1024]{1,0:T(8,128)(2,1)} %refs_5_.3), channel_id=1, source_target_pairs={{0,8},{1,9},{2,10},{3,11},{4,12},{5,13},{6,14},{7,15},{8,0},{9,1},... | collective-permute-start | bytes 786440 | tf_op jit(solution)/shard_map/ppermute | solution.py:450
  33.0 11.4 %collective-permute-start.9 = (bf16[64,1024]{1,0:T(8,128)(2,1)}, bf16[64,1024]{1,0:T(8,128)(2,1)S(1)}, u32[]{:S(2)}, u32[]{:S(2)}) collective-permute-start(bf16[64,1024]{1,0:T(8,128)(2,1)} %get-tuple-element.150), channel_id=1, source_target_pairs={{0,2},{1,3},{2,0},{3,1},{4,6},{5,7},{6,4},{7,5},{8,10},{9,11},{10,... | collective-permute-start | bytes 393224 | tf_op jit(solution)/shard_map/ppermute | solution.py:450
  35.0 9.4 %collective-permute-start.10 = (bf16[64,1024]{1,0:T(8,128)(2,1)}, bf16[64,1024]{1,0:T(8,128)(2,1)S(1)}, u32[]{:S(2)}, u32[]{:S(2)}) collective-permute-start(bf16[64,1024]{1,0:T(8,128)(2,1)} %get-tuple-element.151), channel_id=1, source_target_pairs={{0,4},{1,5},{2,6},{3,7},{4,0},{5,1},{6,2},{7,3},{8,12},{9,13},{10,... | collective-permute-start | bytes 393224 | tf_op jit(solution)/shard_map/ppermute | solution.py:450
  35.0 10.7 %collective-permute-start.11 = (bf16[64,1024]{1,0:T(8,128)(2,1)}, bf16[64,1024]{1,0:T(8,128)(2,1)S(1)}, u32[]{:S(2)}, u32[]{:S(2)}) collective-permute-start(bf16[64,1024]{1,0:T(8,128)(2,1)} %get-tuple-element.152), channel_id=1, source_target_pairs={{0,6},{1,7},{2,4},{3,5},{4,2},{5,3},{6,0},{7,1},{8,14},{9,15},{10,... | collective-permute-start | bytes 393224 | tf_op jit(solution)/shard_map/ppermute | solution.py:450
  45.7 13.5 %collective-permute-start.16 = (bf16[128,1024]{1,0:T(8,128)(2,1)S(1)}, bf16[128,1024]{1,0:T(8,128)(2,1)S(1)}, u32[]{:S(2)}, u32[]{:S(2)}) collective-permute-start(bf16[128,1024]{1,0:T(8,128)(2,1)S(1)} %get-tuple-element.169), channel_id=1, source_target_pairs={{0,2},{1,3},{2,0},{3,1},{4,6},{5,7},{6,4},{7,5},{8,10},{9,11},{10,... | collective-permute-start | bytes 786440 | tf_op jit(solution)/shard_map/ppermute | solution.py:450
  47.0 14.5 %collective-permute-start.17 = (bf16[128,1024]{1,0:T(8,128)(2,1)S(1)}, bf16[128,1024]{1,0:T(8,128)(2,1)S(1)}, u32[]{:S(2)}, u32[]{:S(2)}) collective-permute-start(bf16[128,1024]{1,0:T(8,128)(2,1)S(1)} %get-tuple-element.170), channel_id=1, source_target_pairs={{0,4},{1,5},{2,6},{3,7},{4,0},{5,1},{6,2},{7,3},{8,12},{9,13},{10,... | collective-permute-start | bytes 786440 | tf_op jit(solution)/shard_map/ppermute | solution.py:450
  47.0 14.5 %collective-permute-start.18 = (bf16[128,1024]{1,0:T(8,128)(2,1)S(1)}, bf16[128,1024]{1,0:T(8,128)(2,1)S(1)}, u32[]{:S(2)}, u32[]{:S(2)}) collective-permute-start(bf16[128,1024]{1,0:T(8,128)(2,1)S(1)} %get-tuple-element.171), channel_id=1, source_target_pairs={{0,6},{1,7},{2,4},{3,5},{4,2},{5,3},{6,0},{7,1},{8,14},{9,15},{10,... | collective-permute-start | bytes 786440 | tf_op jit(solution)/shard_map/ppermute | solution.py:450
  57.9 15.7 %collective-permute-start.13 = (bf16[128,1024]{1,0:T(8,128)(2,1)}, bf16[128,1024]{1,0:T(8,128)(2,1)S(1)}, u32[]{:S(2)}, u32[]{:S(2)}) collective-permute-start(bf16[128,1024]{1,0:T(8,128)(2,1)} %get-tuple-element.165), channel_id=1, source_target_pairs={{0,2},{1,3},{2,0},{3,1},{4,6},{5,7},{6,4},{7,5},{8,10},{9,11},{10,... | collective-permute-start | bytes 786440 | tf_op jit(solution)/shard_map/ppermute | solution.py:450
  59.2 14.4 %collective-permute-start.14 = (bf16[128,1024]{1,0:T(8,128)(2,1)}, bf16[128,1024]{1,0:T(8,128)(2,1)S(1)}, u32[]{:S(2)}, u32[]{:S(2)}) collective-permute-start(bf16[128,1024]{1,0:T(8,128)(2,1)} %get-tuple-element.166), channel_id=1, source_target_pairs={{0,4},{1,5},{2,6},{3,7},{4,0},{5,1},{6,2},{7,3},{8,12},{9,13},{10,... | collective-permute-start | bytes 786440 | tf_op jit(solution)/shard_map/ppermute | solution.py:450
  59.2 14.4 %collective-permute-start.15 = (bf16[128,1024]{1,0:T(8,128)(2,1)}, bf16[128,1024]{1,0:T(8,128)(2,1)S(1)}, u32[]{:S(2)}, u32[]{:S(2)}) collective-permute-start(bf16[128,1024]{1,0:T(8,128)(2,1)} %get-tuple-element.167), channel_id=1, source_target_pairs={{0,6},{1,7},{2,4},{3,5},{4,2},{5,3},{6,0},{7,1},{8,14},{9,15},{10,... | collective-permute-start | bytes 786440 | tf_op jit(solution)/shard_map/ppermute | solution.py:450
  73.6 17.8 %collective-permute-start.25 = (bf16[2048,1024]{1,0:T(8,128)(2,1)}, bf16[2048,1024]{1,0:T(8,128)(2,1)S(1)}, u32[]{:S(2)}, u32[]{:S(2)}) collective-permute-start(bf16[2048,1024]{1,0:T(8,128)(2,1)} %get-tuple-element.215.refs_2_), channel_id=1, source_target_pairs={{0,1},{1,0},{2,3},{3,2},{4,5},{5,4},{6,7},{7,6},{8,9},{9,8},{10,11... | collective-permute-start | bytes 12582920 | tf_op jit(solution)/shard_map/ppermute | solution.py:450
  75.1 8.7 %collective-permute-start.21 = (bf16[64,1024]{1,0:T(8,128)(2,1)}, bf16[64,1024]{1,0:T(8,128)(2,1)S(1)}, u32[]{:S(2)}, u32[]{:S(2)}) collective-permute-start(bf16[64,1024]{1,0:T(8,128)(2,1)} %get-tuple-element.192), channel_id=1, source_target_pairs={{0,6},{1,7},{2,4},{3,5},{4,2},{5,3},{6,0},{7,1},{8,14},{9,15},{10,... | collective-permute-start | bytes 393224 | tf_op jit(solution)/shard_map/ppermute | solution.py:450
  86.5 17.8 %collective-permute-start.26 = (bf16[128,1024]{1,0:T(8,128)(2,1)S(1)}, bf16[128,1024]{1,0:T(8,128)(2,1)S(1)}, u32[]{:S(2)}, u32[]{:S(2)}) collective-permute-start(bf16[128,1024]{1,0:T(8,128)(2,1)S(1)} %shard_map.141), channel_id=1, source_target_pairs={{0,8},{1,9},{2,10},{3,11},{4,12},{5,13},{6,14},{7,15},{8,0},{9,1},... | collective-permute-start | bytes 786440 | tf_op jit(solution)/shard_map/ppermute | solution.py:450
  87.9 13.9 %collective-permute-start.22 = (bf16[64,1024]{1,0:T(8,128)(2,1)}, bf16[64,1024]{1,0:T(8,128)(2,1)S(1)}, u32[]{:S(2)}, u32[]{:S(2)}) collective-permute-start(bf16[64,1024]{1,0:T(8,128)(2,1)} %get-tuple-element.211), channel_id=1, source_target_pairs={{0,2},{1,3},{2,0},{3,1},{4,6},{5,7},{6,4},{7,5},{8,10},{9,11},{10,... | collective-permute-start | bytes 393224 | tf_op jit(solution)/shard_map/ppermute | solution.py:450
  89.6 12.2 %collective-permute-start.23 = (bf16[64,1024]{1,0:T(8,128)(2,1)}, bf16[64,1024]{1,0:T(8,128)(2,1)S(1)}, u32[]{:S(2)}, u32[]{:S(2)}) collective-permute-start(bf16[64,1024]{1,0:T(8,128)(2,1)} %get-tuple-element.212), channel_id=1, source_target_pairs={{0,4},{1,5},{2,6},{3,7},{4,0},{5,1},{6,2},{7,3},{8,12},{9,13},{10,... | collective-permute-start | bytes 393224 | tf_op jit(solution)/shard_map/ppermute | solution.py:450
  91.4 11.4 %collective-permute-start.24 = (bf16[64,1024]{1,0:T(8,128)(2,1)}, bf16[64,1024]{1,0:T(8,128)(2,1)S(1)}, u32[]{:S(2)}, u32[]{:S(2)}) collective-permute-start(bf16[64,1024]{1,0:T(8,128)(2,1)} %get-tuple-element.213), channel_id=1, source_target_pairs={{0,6},{1,7},{2,4},{3,5},{4,2},{5,3},{6,0},{7,1},{8,14},{9,15},{10,... | collective-permute-start | bytes 393224 | tf_op jit(solution)/shard_map/ppermute | solution.py:450
  91.4 22.9 %collective-permute-start.33 = (bf16[128,1024]{1,0:T(8,128)(2,1)S(1)}, bf16[128,1024]{1,0:T(8,128)(2,1)S(1)}, u32[]{:S(2)}, u32[]{:S(2)}) collective-permute-start(bf16[128,1024]{1,0:T(8,128)(2,1)S(1)} %get-tuple-element.230), channel_id=1, source_target_pairs={{0,8},{1,9},{2,10},{3,11},{4,12},{5,13},{6,14},{7,15},{8,0},{9,1},... | collective-permute-start | bytes 786440 | tf_op jit(solution)/shard_map/ppermute | solution.py:450
  (44 other events, 330.8 us)

commit v5 on v4

--- a/solution.py
+++ b/solution.py
@@ -350,42 +350,48 @@
 
 
 def forward_kernel(near, ins, outs, scratch, write):
-    rows, (near_in, far_in, near_out, far_out) = ins[0 : 2 * near], ins[2 * near :]
-    out_refs, (rows_ref, near_slope, far_slope, near_active, far_active) = outs[0:near], outs[near:]
-    gather_rows(rows, rows_ref)
+    chip, rows, (router, near_in, far_in, near_out, far_out) = ins[0], ins[1 : 2 * near + 1], ins[2 * near + 1 :]
+    out_refs, (sent, near_slope, far_slope, near_active, gate_ref) = outs[0:near], outs[near:]
+    count = near_slope.shape[0]
+    rows_part, active_part = slice(0, count), slice(count, 2 * count)
+    gather_rows(rows, sent)
+    logits = dot_last(sent[rows_part, :], router[...])
+    mine = lax.broadcasted_iota(jnp.int32, logits.shape, 1) == chip[0]
+    gate_ref[...] = jax.nn.sigmoid(jnp.sum(jnp.where(mine, logits, 0.0), axis=1, keepdims=True))
     near_in.wait()
     near_out.start()
     far_out.start()
-    write(near)
-    for weight, slope, active in ((near_in, near_slope, near_active), (far_in, far_slope, far_active)):
+    for weight, slope, active, part in (
+        (near_in, near_slope, near_active, slice(None)),
+        (far_in, far_slope, sent, active_part),
+    ):
         weight.wait()
         for columns in chunks(weight.shape[1]):
-            values = dot(rows_ref[...], weight[:, columns])
+            values = dot(sent[rows_part, :], weight[:, columns])
             logistic = jax.nn.sigmoid(values)
-            active[:, columns] = (values * logistic).astype(BF16)
+            active[part, columns] = (values * logistic).astype(BF16)
             slope[:, columns] = (logistic * (1.0 + values * (1.0 - logistic))).astype(BF16)
-    write(near + 1, near + 2, near + 3, near + 4)
+    write(near, near + 1, near + 2, near + 3, near + 4)
     near_out.wait()
     far_out.wait()
     for columns in chunks(near_out.shape[1]):
         total = dot(near_active[...], near_out[:, columns])
-        total = total + dot(far_active[...], far_out[:, columns])
+        total = total + dot(sent[active_part, :], far_out[:, columns])
         scatter_pairs(out_refs, columns, total.astype(BF16))
 
 
 def backward_kernel(near, ins, outs, scratch, write):
     chip, grads, rest = ins[0], ins[1 : near + 1], ins[near + 1 :]
-    rows, router, near_out, far_out, near_slope, far_slope, near_active, far_active, near_in, far_in = rest
+    gate_ref, near_out, near_slope, near_active, far_out, far_slope, far_active, near_in, far_in, router, rows = rest
     out_refs, (near_grad, sent, router_out) = outs[0 : 2 * near], outs[2 * near :]
     grads_ref, dots_ref = scratch
     count = rows.shape[0]
-    rows_part, active_part, grads_part, pre_part = (slice(turn * count, (turn + 1) * count) for turn in range(4))
+    grads_part, pre_part = slice(0, count), slice(count, 2 * count)
     gather_pairs(grads, grads_ref)
-    logits = dot_last(rows[...], router[...])
-    mine = lax.broadcasted_iota(jnp.int32, logits.shape, 1) == chip[0]
-    gate = jax.nn.sigmoid(jnp.sum(jnp.where(mine, logits, 0.0), axis=1, keepdims=True))
+    gate = gate_ref[...]
     sent[grads_part, :] = (gate * grads_ref[...].astype(F32)).astype(BF16)
-    for later in rest[3:]:
+    near_out.wait()
+    for later in rest[2:]:
         later.start()
     dots_ref[...] = jnp.zeros_like(dots_ref)
     for weight, slope, active, grad, part in (
@@ -396,38 +402,38 @@
             ref.wait()
         for columns in chunks(weight.shape[0]):
             hidden = dot_last(sent[grads_part, :], weight[columns, :])
-            dots_ref[...] += hidden * active[:, columns].astype(F32)
+            product = hidden * active[:, columns].astype(F32)
+            dots_ref[...] += sum(product[:, at : at + LANES] for at in range(0, CHUNK, LANES))
             grad[part, columns] = (hidden * slope[:, columns].astype(F32)).astype(BF16)
-    write(2 * near)
-    sent[rows_part, :] = rows[...]
-    sent[active_part, :] = far_active[...]
-    write(2 * near + 1)
-    chosen = jnp.sum(dots_ref[...], axis=1, keepdims=True) * (1.0 - gate)
-    grad_logits = jnp.where(mine, chosen, 0.0).astype(BF16)
-    router_out[...] = dot_first(grad_logits, rows[...])
+    write(2 * near, 2 * near + 1)
+    chosen = (jnp.sum(dots_ref[...], axis=1, keepdims=True) * (1.0 - gate)).astype(BF16)
+    experts = router.shape[0]
+    mine = lax.broadcasted_iota(jnp.int32, (count, experts), 1) == chip[0]
+    router_out[...] = dot_first(jnp.where(mine, chosen.astype(F32), 0.0).astype(BF16), rows[...])
+    own = lax.broadcasted_iota(jnp.int32, router.shape, 0) == chip[0]
+    router_row = jnp.sum(jnp.where(own, router[...].astype(F32), 0.0), axis=0, keepdims=True)
+    chosen = chosen.astype(F32)
     near_in.wait()
     far_in.wait()
     for columns in chunks(near_in.shape[0]):
         total = dot_last(near_grad[...], near_in[columns, :])
         total = total + dot_last(sent[pre_part, :], far_in[columns, :])
-        total = total + dot(grad_logits, router[:, columns])
+        total = total + chosen * router_row[:, columns]
         scatter_columns(out_refs, columns, total.astype(BF16))
 
 
 def weights_kernel(ins, outs, scratch, write):
-    near_active, near_grad, near_part, far_part = ins
+    near_active, near_grads, far_active, far_grads, near_rows, near_grad, far_rows, far_grad = ins
     in_grad, out_grad = outs
-    count, width = near_active.shape
-    rows_part, active_part, grads_part, pre_part = (slice(turn * count, (turn + 1) * count) for turn in range(4))
-    for ref in ins:
-        ref.wait()
-    for columns in chunks(width):
-        total = dot_first(near_active[:, columns], near_part[grads_part, :])
-        out_grad[columns, :] = (total + dot_first(far_part[active_part, columns], far_part[grads_part, :])).astype(BF16)
-    write(1)
-    for columns in chunks(width):
-        total = dot_first(near_part[rows_part, columns], near_grad[...])
-        in_grad[columns, :] = (total + dot_first(far_part[rows_part, columns], far_part[pre_part, :])).astype(BF16)
+    for turn, (a, b, c, d) in ((1, ins[0:4]), (0, ins[4:8])):
+        for ref in (a, b, c, d):
+            ref.wait()
+        for ref in ins[4:8]:
+            ref.start()
+        for columns in chunks(a.shape[1]):
+            total = dot_first(a[:, columns], b[...]) + dot_first(c[:, columns], d[...])
+            outs[turn][columns, :] = total.astype(BF16)
+        write(turn)
 
 
 def last_kernel(ins, outs, scratch, write):
@@ -499,6 +505,7 @@
         (model32, model16, *part),
         front_scratch,
         weight=FRONT,
+        limit=LARGE,
         scalars=(0, 1),
     )
     rows = exchange(parts, devices)
@@ -518,32 +525,35 @@
         functools.partial(pack_both_kernel, near, capacity),
         (chips, names, out_grad, far_names, far_grad),
         pair,
+        limit=LARGE,
         scalars=(0,),
     )
     far_rows, parts = lax.optimization_barrier((far_rows, parts))
     rows, grads = rows + far_rows, exchange(parts, devices)
 
     narrow = shape((slots, weight_in.shape[1]), BF16)
-    outs = kernel_call(
+    *parts, sent, near_slope, far_slope, near_active, gate = kernel_call(
         functools.partial(forward_kernel, near),
-        (*rows, weight_in, other_in, weight_out, other_out),
-        pair + (shape((slots, width), BF16), narrow, narrow, narrow, narrow),
+        (chips, *rows, router, weight_in, other_in, weight_out, other_out),
+        pair + (shape((2 * slots, width), BF16), narrow, narrow, narrow, shape((slots, 1), F32)),
         limit=LARGE,
-        first=2 * near + 2,
-    )
-    parts, all_rows, slopes, (near_active, far_active) = outs[0:near], outs[near], outs[near + 1 : near + 3], outs[near + 3 :]
+        first=2 * near + 4,
+        scalars=(0,),
+    )
     results = exchange(parts, devices)
+    all_rows, far_active = Rows(sent, 0, slots), Rows(sent, slots, slots)
     outs = kernel_call(
         functools.partial(backward_kernel, near),
-        (chips, *grads, all_rows, router, weight_out, other_out, *slopes, near_active, far_active, weight_in, other_in),
-        2 * part + (narrow, shape((4 * slots, width), BF16), shape((experts, width), F32)),
-        (pltpu.VMEM((slots, width), BF16), pltpu.VMEM((slots, CHUNK), F32)),
+        (chips, *grads, gate, weight_out, near_slope, near_active, other_out, far_slope, far_active)
+        + (weight_in, other_in, router, all_rows),
+        2 * part + (narrow, shape((2 * slots, width), BF16), shape((experts, width), F32)),
+        (pltpu.VMEM((slots, width), BF16), pltpu.VMEM((slots, LANES), F32)),
         limit=LARGE,
-        first=near + 4,
+        first=near + 3,
         scalars=(0,),
     )
-    results, outs = lax.optimization_barrier((results, outs))
-    own_in, far_in, (near_grad, sent, router_local) = outs[0:near], outs[near : 2 * near], outs[2 * near :]
+    results, outs, sent = lax.optimization_barrier((results, outs, sent))
+    own_in, far_in, (near_grad, sent_grads, router_local) = outs[0:near], outs[near : 2 * near], outs[2 * near :]
     backs = exchange(far_in, devices)
     near_sum, far_sum = kernel_call(
         functools.partial(result_kernel, near, capacity),
@@ -552,18 +562,27 @@
         weight=2.4,
         scalars=(0,),
     )
+    come, come_grads = swap(sent, devices, 1), swap(sent_grads, devices, 1)
+    backs[1], own_in, come, come_grads = lax.optimization_barrier((backs[1], own_in, come, come_grads))
+    own_backs = exchange(own_in, devices)
     backs, near_sum, far_sum = lax.optimization_barrier((backs, near_sum, far_sum))
     (far_back,) = kernel_call(
         functools.partial(back_kernel, near, capacity), (chips, far_names, *backs), (model16,), scalars=(0,)
     )
-    far_back, own_in, far_sum = lax.optimization_barrier((far_back, own_in, far_sum))
+    far_back, far_sum = lax.optimization_barrier((far_back, far_sum))
     far_back = cross(far_back)
     grad = shape(weight_in.shape, BF16)
+    first, second = (functools.partial(Rows, start=start, size=slots) for start in (0, slots))
     expert_in_grad, expert_out_grad = kernel_call(
-        weights_kernel, (near_active, near_grad, sent, swap(sent, devices, 1)), (grad, grad), limit=WEIGHTS
+        weights_kernel,
+        (near_active, first(sent_grads), second(come), first(come_grads))
+        + (first(sent), near_grad, first(come), second(come_grads)),
+        (grad, grad),
+        limit=WEIGHTS,
+        first=4,
     )
     backs, expert_in_grad, expert_out_grad = lax.optimization_barrier(
-        (exchange(own_in, devices), expert_in_grad, expert_out_grad)
+        (own_backs, expert_in_grad, expert_out_grad)
     )
     (near_back,) = kernel_call(
         functools.partial(back_kernel, near, capacity), (chips, names, *backs), (model32,), scalars=(0,)
@@ -600,7 +619,7 @@
             )
         bit *= 2 if last else 4
         if bit == devices:
-            others, frames_grad, block_out = lax.optimization_barrier((others, frames_grad, block_out))
+            others, frames_grad = lax.optimization_barrier((others, frames_grad))
         local = local + others[0] if last else (local + others[0]) + (others[1] + others[2])
     kernel_grad, gain_grad, router_grad = kernel_call(
         last_kernel,

time: 129 us -> 126 us (0.977)
  local copies, waits for them, and re-layouts: 9.51 us -> 6.66 us
  waiting for transfers between devices: 17.8 us -> 15.6 us
  Pallas kernels: 53.4 us -> 55 us
    unnamed x64 -> x68, local copies, waits for them, and re-layouts: 8.78 us -> 4.73 us
    ppermute x34 -> x35, waiting for transfers between devices: 17.8 us -> 15.6 us  [swap(): return lax.ppermute(values, 'seq', [(i, i ^ bit) for i in range(count)])]
    pallas_call x13, Pallas kernels: 53.4 us -> 55 us  [kernel_call(): pl.pallas_call(kernel, out_shape=tuple(outs), in_specs=[pl.BlockSpec(memo...]
    ppermute x34 -> x35, starting transfers between devices: 44.1 us -> 43.5 us  [swap(): return lax.ppermute(values, 'seq', [(i, i ^ bit) for i in range(count)])]
  transfers between devices with their start and end apart: 36 -> 37, of which waited for: 13 -> 14; matrix products, arithmetic and copies ran while one was open for 2% -> 3% of each run, Pallas kernels for 41% -> 42%
where the time goes in v5:
time: 126 us; the launch traced here: 125 us
  Pallas kernels  55 us (44%)
  starting transfers between devices  44.8 us (36%)
  waiting for transfers between devices  15.6 us (12%)
  local copies, waits for them, and re-layouts  6.66 us (5%)
  other arithmetic  1.57 us (1%)
  between operations  1.39 us (1%)
    pallas_call x13, Pallas kernels, kernel_call(): pl.pallas_call(kernel, out_shape=tuple(outs), in_specs=[pl.BlockSpec(memo...  55 us
    ppermute x35, starting transfers between devices, swap(): return lax.ppermute(values, 'seq', [(i, i ^ bit) for i in range(count)])  43.5 us
    ppermute x35, waiting for transfers between devices, swap(): return lax.ppermute(values, 'seq', [(i, i ^ bit) for i in range(count)])  15.6 us
    unnamed x68, local copies, waits for them, and re-layouts  4.73 us
  transfers between devices with their start and end apart: 37, of which 14 were waited for; matrix products, arithmetic and copies ran while one was open for 3% of the time, Pallas kernels for 42%

profile of v5, /device:TPU:0, one launch (start us, length us, event | category | flops | bytes accessed | tf_op | source)
XLA Modules:
  0.0 125.1 jit_solution(10820346630369029664)
XLA Ops:
  3.2 6.4 %collective-permute-start.8 = (bf16[128,1024]{1,0:T(8,128)(2,1)}, bf16[128,1024]{1,0:T(8,128)(2,1)S(1)}, u32[]{:S(2)}, u32[]{:S(2)}) collective-permute-start(bf16[128,1024]{1,0:T(8,128)(2,1)} %refs_1_), channel_id=1, source_target_pairs={{0,8},{1,9},{2,10},{3,11},{4,12},{5,13},{6,14},{7,15},{8,0},{9,1},... | collective-permute-start | bytes 786440 | tf_op jit(solution)/shard_map/ppermute | solution.py:456
  10.4 2.1 %collective-permute-start.7 = (bf16[32,1024]{1,0:T(8,128)(2,1)S(1)}, bf16[32,1024]{1,0:T(8,128)(2,1)S(1)}, u32[]{:S(2)}, u32[]{:S(2)}) collective-permute-start(bf16[32,1024]{1,0:T(8,128)(2,1)S(1)} %maximum_select_fusion), channel_id=1, source_target_pairs={{0,8},{1,9},{2,10},{3,11},{4,12},{5,13},{6,14},{7,15},{8,0},{9,1},... | collective-permute-start | bytes 196616 | tf_op jit(solution)/shard_map/ppermute | solution.py:456
  14.4 5.5 %shard_map.135 = (f32[128,1024]{1,0:T(8,128)}, bf16[128,1024]{1,0:T(8,128)(2,1)}, bf16[64,1024]{1,0:T(8,128)(2,1)}, bf16[64,1024]{1,0:T(8,128)(2,1)}, bf16[64,10...) custom-call(s32[1]{0:T(128)} %bitcast.refs_0_, s32[1]{0:T(128)} %bitcast.1.refs_1_.refs_0_, bf16[128,1024]{1,0:T(8,128)(2,1)} %refs_1_, ...), custom_call_target="tpu_custom_call" | custom-call | flops 1 | bytes 1782001 | tf_op jit(solution)/shard_map/pallas_call | solution.py:107
  21.5 2.2 %collective-permute-start.5 = (bf16[64,1024]{1,0:T(8,128)(2,1)}, bf16[64,1024]{1,0:T(8,128)(2,1)S(1)}, u32[]{:S(2)}, u32[]{:S(2)}) collective-permute-start(bf16[64,1024]{1,0:T(8,128)(2,1)} %get-tuple-element.138), channel_id=1, source_target_pairs={{0,4},{1,5},{2,6},{3,7},{4,0},{5,1},{6,2},{7,3},{8,12},{9,13},{10,... | collective-permute-start | bytes 393224 | tf_op jit(solution)/shard_map/ppermute | solution.py:456
  26.0 5.8 %shard_map.136 = (bf16[16,1024]{1,0:T(8,128)(2,1)}, bf16[128,1024]{1,0:T(8,128)(2,1)}, bf16[64,1024]{1,0:T(8,128)(2,1)}, bf16[64,1024]{1,0:T(8,128)(2,1)}, bf16[...) custom-call(s32[1]{0:T(128)} %bitcast.refs_0_, s32[1]{0:T(128)} %bitcast.1.refs_1_.refs_0_, bf16[128,1024]{1,0:T(8,128)(2,1)} %copy-done.25, ...), custom_call_target="tpu_custom_call" | custom-call | flops 1 | bytes 1 | tf_op jit(solution)/shard_map/pallas_call | solution.py:107
  36.5 3.5 %collective-permute-done.12.refs_4_ = bf16[128,1024]{1,0:T(8,128)(2,1)S(1)} collective-permute-done((bf16[128,1024]{1,0:T(8,128)(2,1)}, bf16[128,1024]{1,0:T(8,128)(2,1)S(1)}, u32[]{:S(2)}, u32[]{:S(2)}) %collective-permute-start.12) | collective-permute-done | bytes 262176 | tf_op jit(solution)/shard_map/ppermute | solution.py:456
  40.7 3.3 %shard_map.137 = (bf16[128,1024]{1,0:T(8,128)(2,1)}, bf16[128,1024]{1,0:T(8,128)(2,1)}, bf16[128,1024]{1,0:T(8,128)(2,1)}, bf16[128,1024]{1,0:T(8,128)(2,1)}) custom-call(s32[1]{0:T(128)} %bitcast.refs_0_, bf16[16,1024]{1,0:T(8,128)(2,1)} %pad.4.refs_7_.refs_1_.refs_2_, bf16[128,1024]{1,0:T(8,128)(2,1)} %refs_5_.3, ...), custom_call_target="tpu_custom_call" | custom-call | flops 1 | bytes 1 | tf_op jit(solution)/shard_map/pallas_call | solution.py:107
  44.1 1.8 %collective-permute-done.11.refs_8_ = bf16[64,1024]{1,0:T(8,128)(2,1)S(1)} collective-permute-done((bf16[64,1024]{1,0:T(8,128)(2,1)}, bf16[64,1024]{1,0:T(8,128)(2,1)S(1)}, u32[]{:S(2)}, u32[]{:S(2)}) %collective-permute-start.11) | collective-permute-done | bytes 131104 | tf_op jit(solution)/shard_map/ppermute | solution.py:456
  47.0 2.4 %collective-permute-start.18 = (bf16[128,1024]{1,0:T(8,128)(2,1)}, bf16[128,1024]{1,0:T(8,128)(2,1)S(1)}, u32[]{:S(2)}, u32[]{:S(2)}) collective-permute-start(bf16[128,1024]{1,0:T(8,128)(2,1)} %get-tuple-element.173), channel_id=1, source_target_pairs={{0,6},{1,7},{2,4},{3,5},{4,2},{5,3},{6,0},{7,1},{8,14},{9,15},{10,... | collective-permute-start | bytes 786440 | tf_op jit(solution)/shard_map/ppermute | solution.py:456
  49.4 8.7 %shard_map.138 = (bf16[128,1024]{1,0:T(8,128)(2,1)}, bf16[128,1024]{1,0:T(8,128)(2,1)}, bf16[128,1024]{1,0:T(8,128)(2,1)}, bf16[128,1024]{1,0:T(8,128)(2,1)}, bf...) custom-call(s32[1]{0:T(128)} %bitcast.refs_0_, ...), custom_call_target="tpu_custom_call" | custom-call | flops 1 | bytes 1 | tf_op jit(solution)/shard_map/pallas_call | solution.py:107
  59.2 2.4 %collective-permute-start.15 = (bf16[128,1024]{1,0:T(8,128)(2,1)}, bf16[128,1024]{1,0:T(8,128)(2,1)S(1)}, u32[]{:S(2)}, u32[]{:S(2)}) collective-permute-start(bf16[128,1024]{1,0:T(8,128)(2,1)} %get-tuple-element.169), channel_id=1, source_target_pairs={{0,6},{1,7},{2,4},{3,5},{4,2},{5,3},{6,0},{7,1},{8,14},{9,15},{10,... | collective-permute-start | bytes 786440 | tf_op jit(solution)/shard_map/ppermute | solution.py:456
  62.5 10.6 %shard_map.139 = (bf16[64,1024]{1,0:T(8,128)(2,1)}, bf16[64,1024]{1,0:T(8,128)(2,1)}, bf16[64,1024]{1,0:T(8,128)(2,1)}, bf16[64,1024]{1,0:T(8,128)(2,1)}, bf16[6...) custom-call(s32[1]{0:T(128)} %bitcast.refs_0_, ...), custom_call_target="tpu_custom_call" | custom-call | flops 1 | bytes 1 | tf_op jit(solution)/shard_map/pallas_call | solution.py:107
  74.9 2.4 %collective-permute-start.23 = (bf16[64,1024]{1,0:T(8,128)(2,1)}, bf16[64,1024]{1,0:T(8,128)(2,1)S(1)}, u32[]{:S(2)}, u32[]{:S(2)}) collective-permute-start(bf16[64,1024]{1,0:T(8,128)(2,1)} %get-tuple-element.200), channel_id=1, source_target_pairs={{0,6},{1,7},{2,4},{3,5},{4,2},{5,3},{6,0},{7,1},{8,14},{9,15},{10,... | collective-permute-start | bytes 393224 | tf_op jit(solution)/shard_map/ppermute | solution.py:456
  77.3 2.5 %shard_map.140 = (f32[128,1024]{1,0:T(8,128)S(1)}, bf16[128,1024]{1,0:T(8,128)(2,1)S(1)}) custom-call(s32[1]{0:T(128)} %bitcast.refs_0_, bf16[8,1024]{1,0:T(8,128)(2,1)S(1)} %bitcast.13, bf16[16,1024]{1,0:T(8,128)(2,1)S(1)} %copy-done.6, bf16[128,1024]{1,0:T(8,128)(2,1)S(1)} %copy-done.14, bf16[16,1024]{1,0:T(8,128)(2,1)S(1)} %copy-done.13, ...), custom_call_target="tpu_custom_call" | custom-call | flops 1 | bytes 1296001 | tf_op jit(solution)/shard_map/pallas_call | solution.py:107
  81.4 2.0 %collective-permute-done.23.refs_5_ = bf16[64,1024]{1,0:T(8,128)(2,1)S(1)} collective-permute-done((bf16[64,1024]{1,0:T(8,128)(2,1)}, bf16[64,1024]{1,0:T(8,128)(2,1)S(1)}, u32[]{:S(2)}, u32[]{:S(2)}) %collective-permute-start.23) | collective-permute-done | bytes 131104 | tf_op jit(solution)/shard_map/ppermute | solution.py:456
  84.4 1.5 %shard_map.143 = bf16[128,1024]{1,0:T(8,128)(2,1)S(1)} custom-call(s32[1]{0:T(128)} %bitcast.refs_0_, bf16[16,1024]{1,0:T(8,128)(2,1)S(1)} %copy-done.13, bf16[64,1024]{1,0:T(8,128)(2,1)S(1)} %copy-done.18, bf16[64,1024]{1,0:T(8,128)(2,1)S(1)} %collective-permute-done.19.refs_3_, bf16[64,1024]{1,0:T(8,128)(2,1)S(1)} %collective-permute-done.22.refs_4_, ...), custom_call_target="tpu_custom_call" | custom-call | flops 1 | bytes 1 | tf_op jit(solution)/shard_map/pallas_call | solution.py:107
  87.0 1.7 %collective-permute-start.24 = (bf16[64,1024]{1,0:T(8,128)(2,1)}, bf16[64,1024]{1,0:T(8,128)(2,1)S(1)}, u32[]{:S(2)}, u32[]{:S(2)}) collective-permute-start(bf16[64,1024]{1,0:T(8,128)(2,1)} %get-tuple-element.213), channel_id=1, source_target_pairs={{0,2},{1,3},{2,0},{3,1},{4,6},{5,7},{6,4},{7,5},{8,10},{9,11},{10,... | collective-permute-start | bytes 393224 | tf_op jit(solution)/shard_map/ppermute | solution.py:456
  88.7 1.7 %collective-permute-start.25 = (bf16[64,1024]{1,0:T(8,128)(2,1)}, bf16[64,1024]{1,0:T(8,128)(2,1)S(1)}, u32[]{:S(2)}, u32[]{:S(2)}) collective-permute-start(bf16[64,1024]{1,0:T(8,128)(2,1)} %get-tuple-element.214), channel_id=1, source_target_pairs={{0,4},{1,5},{2,6},{3,7},{4,0},{5,1},{6,2},{7,3},{8,12},{9,13},{10,... | collective-permute-start | bytes 393224 | tf_op jit(solution)/shard_map/ppermute | solution.py:456
  90.5 1.9 %collective-permute-start.34 = (bf16[128,1024]{1,0:T(8,128)(2,1)S(1)}, bf16[128,1024]{1,0:T(8,128)(2,1)S(1)}, u32[]{:S(2)}, u32[]{:S(2)}) collective-permute-start(bf16[128,1024]{1,0:T(8,128)(2,1)S(1)} %get-tuple-element.239), channel_id=1, source_target_pairs={{0,8},{1,9},{2,10},{3,11},{4,12},{5,13},{6,14},{7,15},{8,0},{9,1},... | collective-permute-start | bytes 786440 | tf_op jit(solution)/shard_map/ppermute | solution.py:456
  92.4 1.6 %copy-done.2 = bf16[1024,1024]{1,0:T(8,128)(2,1)S(1)} copy-done((bf16[1024,1024]{1,0:T(8,128)(2,1)S(1)}, bf16[1024,1024]{1,0:T(8,128)(2,1)}, u32[]{:S(2)}) %copy-start.2) | copy-done | bytes 2097176
  94.0 6.7 %shard_map.141 = (bf16[1024,1024]{1,0:T(8,128)(2,1)}, bf16[1024,1024]{1,0:T(8,128)(2,1)}) custom-call(bf16[512,1024]{1,0:T(8,128)(2,1)S(1)} %copy-done.1, bf16[1024,1024]{1,0:T(8,128)(2,1)S(1)} %copy-done.2, bf16[1024,1024]{1,0:T(8,128)(2,1)S(1)} %collective-permute-done.20.refs_2_.refs_6_, bf16[1024,1024]{1,0:T(8,128)(2,1)S(1)} %collective-permute-done.21.refs_3_.refs_7_, ...), custom_call_target="tpu_custom_call" | custom-call | flops 1 | bytes 1 | tf_op jit(solution)/shard_map/pallas_call | solution.py:107
  103.3 3.4 %shard_map.144 = (f32[128,1024]{1,0:T(8,128)S(1)}, f32[128,1024]{1,0:T(8,128)S(1)}, bf16[128,1024]{1,0:T(8,128)(2,1)S(1)}, bf16[16,1024]{1,0:T(8,128)(2,1)S(1)},...) custom-call(s32[1]{0:T(128)} %bitcast.1.refs_1_.refs_0_, ...), custom_call_target="tpu_custom_call" | custom-call | flops 1 | bytes 1 | tf_op jit(solution)/shard_map/pallas_call | solution.py:107
  115.3 3.6 %collective-permute-start.35 = (f32[40,512]{1,0:T(8,128)S(1)}, f32[40,512]{1,0:T(8,128)S(1)}, u32[]{:S(2)}, u32[]{:S(2)}) collective-permute-start(f32[40,512]{1,0:T(8,128)S(1)} %add_add_fusion), channel_id=1, source_target_pairs={{0,8},{1,9},{2,10},{3,11},{4,12},{5,13},{6,14},{7,15},{8,0},{9,1},... | collective-permute-start | bytes 245768 | tf_op jit(solution)/shard_map/ppermute | solution.py:456
  118.9 3.7 %shard_map.146 = bf16[128,1024]{1,0:T(8,128)(2,1)} custom-call(s32[1]{0:T(128)} %bitcast.1.refs_1_.refs_0_, f32[128,1024]{1,0:T(8,128)S(1)} %get-tuple-element.244.refs_1_, bf16[128,1024]{1,0:T(8,128)(2,1)S(1)} %get-tuple-element.245.refs_2_, bf16[16,1024]{1,0:T(8,128)(2,1)S(1)} %collective-permute-done.32.refs_3_, ...), custom_call_target="tpu_custom_call" | custom-call | flops 1 | bytes 1 | tf_op jit(solution)/shard_map/pallas_call | solution.py:107
  (142 shorter events, 36.1 us)
Async XLA Ops:
  0.6 9.7 %collective-permute-start.2 = (bf16[1024,1024]{1,0:T(8,128)(2,1)}, bf16[1024,1024]{1,0:T(8,128)(2,1)}, u32[]{:S(2)}, u32[]{:S(2)}) collective-permute-start(bf16[1024,1024]{1,0:T(8,128)(2,1)} %bitcast.14), channel_id=1, source_target_pairs={{0,1},{1,0},{2,3},{3,2},{4,5},{5,4},{6,7},{7,6},{8,9},{9,8},{10,11... | collective-permute-start | bytes 6291464 | tf_op jit(solution)/shard_map/ppermute | solution.py:456
  1.1 9.2 %collective-permute-start.3 = (bf16[1024,1024]{1,0:T(8,128)(2,1)}, bf16[1024,1024]{1,0:T(8,128)(2,1)}, u32[]{:S(2)}, u32[]{:S(2)}) collective-permute-start(bf16[1024,1024]{1,0:T(8,128)(2,1)} %bitcast.17), channel_id=1, source_target_pairs={{0,1},{1,0},{2,3},{3,2},{4,5},{5,4},{6,7},{7,6},{8,9},{9,8},{10,11... | collective-permute-start | bytes 6291464 | tf_op jit(solution)/shard_map/ppermute | solution.py:456
  2.0 8.3 %collective-permute-start = (bf16[16,1024]{1,0:T(8,128)(2,1)S(1)}, bf16[16,1024]{1,0:T(8,128)(2,1)S(1)}, u32[]{:S(2)}, u32[]{:S(2)}) collective-permute-start(bf16[16,1024]{1,0:T(8,128)(2,1)S(1)} %get-tuple-element.132), channel_id=1, source_target_pairs={{0,1},{1,0},{2,3},{3,2},{4,5},{5,4},{6,7},{7,6},{8,9},{9,8},{10,11... | collective-permute-start | bytes 98312 | tf_op jit(solution)/shard_map/ppermute | solution.py:456
  3.2 21.9 %collective-permute-start.8 = (bf16[128,1024]{1,0:T(8,128)(2,1)}, bf16[128,1024]{1,0:T(8,128)(2,1)S(1)}, u32[]{:S(2)}, u32[]{:S(2)}) collective-permute-start(bf16[128,1024]{1,0:T(8,128)(2,1)} %refs_1_), channel_id=1, source_target_pairs={{0,8},{1,9},{2,10},{3,11},{4,12},{5,13},{6,14},{7,15},{8,0},{9,1},... | collective-permute-start | bytes 786440 | tf_op jit(solution)/shard_map/ppermute | solution.py:456
  10.4 14.9 %collective-permute-start.7 = (bf16[32,1024]{1,0:T(8,128)(2,1)S(1)}, bf16[32,1024]{1,0:T(8,128)(2,1)S(1)}, u32[]{:S(2)}, u32[]{:S(2)}) collective-permute-start(bf16[32,1024]{1,0:T(8,128)(2,1)S(1)} %maximum_select_fusion), channel_id=1, source_target_pairs={{0,8},{1,9},{2,10},{3,11},{4,12},{5,13},{6,14},{7,15},{8,0},{9,1},... | collective-permute-start | bytes 196616 | tf_op jit(solution)/shard_map/ppermute | solution.py:456
  20.0 11.8 %collective-permute-start.4 = (bf16[64,1024]{1,0:T(8,128)(2,1)}, bf16[64,1024]{1,0:T(8,128)(2,1)S(1)}, u32[]{:S(2)}, u32[]{:S(2)}) collective-permute-start(bf16[64,1024]{1,0:T(8,128)(2,1)} %get-tuple-element.137), channel_id=1, source_target_pairs={{0,2},{1,3},{2,0},{3,1},{4,6},{5,7},{6,4},{7,5},{8,10},{9,11},{10,... | collective-permute-start | bytes 393224 | tf_op jit(solution)/shard_map/ppermute | solution.py:456
  21.5 10.3 %collective-permute-start.5 = (bf16[64,1024]{1,0:T(8,128)(2,1)}, bf16[64,1024]{1,0:T(8,128)(2,1)S(1)}, u32[]{:S(2)}, u32[]{:S(2)}) collective-permute-start(bf16[64,1024]{1,0:T(8,128)(2,1)} %get-tuple-element.138), channel_id=1, source_target_pairs={{0,4},{1,5},{2,6},{3,7},{4,0},{5,1},{6,2},{7,3},{8,12},{9,13},{10,... | collective-permute-start | bytes 393224 | tf_op jit(solution)/shard_map/ppermute | solution.py:456
  23.7 8.9 %collective-permute-start.6 = (bf16[64,1024]{1,0:T(8,128)(2,1)}, bf16[64,1024]{1,0:T(8,128)(2,1)S(1)}, u32[]{:S(2)}, u32[]{:S(2)}) collective-permute-start(bf16[64,1024]{1,0:T(8,128)(2,1)} %get-tuple-element.139), channel_id=1, source_target_pairs={{0,6},{1,7},{2,4},{3,5},{4,2},{5,3},{6,0},{7,1},{8,14},{9,15},{10,... | collective-permute-start | bytes 393224 | tf_op jit(solution)/shard_map/ppermute | solution.py:456
  25.4 14.6 %collective-permute-start.12 = (bf16[128,1024]{1,0:T(8,128)(2,1)}, bf16[128,1024]{1,0:T(8,128)(2,1)S(1)}, u32[]{:S(2)}, u32[]{:S(2)}) collective-permute-start(bf16[128,1024]{1,0:T(8,128)(2,1)} %refs_5_.3), channel_id=1, source_target_pairs={{0,8},{1,9},{2,10},{3,11},{4,12},{5,13},{6,14},{7,15},{8,0},{9,1},... | collective-permute-start | bytes 786440 | tf_op jit(solution)/shard_map/ppermute | solution.py:456
  32.6 11.4 %collective-permute-start.9 = (bf16[64,1024]{1,0:T(8,128)(2,1)}, bf16[64,1024]{1,0:T(8,128)(2,1)S(1)}, u32[]{:S(2)}, u32[]{:S(2)}) collective-permute-start(bf16[64,1024]{1,0:T(8,128)(2,1)} %get-tuple-element.151), channel_id=1, source_target_pairs={{0,2},{1,3},{2,0},{3,1},{4,6},{5,7},{6,4},{7,5},{8,10},{9,11},{10,... | collective-permute-start | bytes 393224 | tf_op jit(solution)/shard_map/ppermute | solution.py:456
  33.6 10.4 %collective-permute-start.10 = (bf16[64,1024]{1,0:T(8,128)(2,1)}, bf16[64,1024]{1,0:T(8,128)(2,1)S(1)}, u32[]{:S(2)}, u32[]{:S(2)}) collective-permute-start(bf16[64,1024]{1,0:T(8,128)(2,1)} %get-tuple-element.152), channel_id=1, source_target_pairs={{0,4},{1,5},{2,6},{3,7},{4,0},{5,1},{6,2},{7,3},{8,12},{9,13},{10,... | collective-permute-start | bytes 393224 | tf_op jit(solution)/shard_map/ppermute | solution.py:456
  35.1 10.8 %collective-permute-start.11 = (bf16[64,1024]{1,0:T(8,128)(2,1)}, bf16[64,1024]{1,0:T(8,128)(2,1)S(1)}, u32[]{:S(2)}, u32[]{:S(2)}) collective-permute-start(bf16[64,1024]{1,0:T(8,128)(2,1)} %get-tuple-element.153), channel_id=1, source_target_pairs={{0,6},{1,7},{2,4},{3,5},{4,2},{5,3},{6,0},{7,1},{8,14},{9,15},{10,... | collective-permute-start | bytes 393224 | tf_op jit(solution)/shard_map/ppermute | solution.py:456
  45.9 13.3 %collective-permute-start.16 = (bf16[128,1024]{1,0:T(8,128)(2,1)}, bf16[128,1024]{1,0:T(8,128)(2,1)S(1)}, u32[]{:S(2)}, u32[]{:S(2)}) collective-permute-start(bf16[128,1024]{1,0:T(8,128)(2,1)} %get-tuple-element.171), channel_id=1, source_target_pairs={{0,2},{1,3},{2,0},{3,1},{4,6},{5,7},{6,4},{7,5},{8,10},{9,11},{10,... | collective-permute-start | bytes 786440 | tf_op jit(solution)/shard_map/ppermute | solution.py:456
  47.0 14.7 %collective-permute-start.17 = (bf16[128,1024]{1,0:T(8,128)(2,1)}, bf16[128,1024]{1,0:T(8,128)(2,1)S(1)}, u32[]{:S(2)}, u32[]{:S(2)}) collective-permute-start(bf16[128,1024]{1,0:T(8,128)(2,1)} %get-tuple-element.172), channel_id=1, source_target_pairs={{0,4},{1,5},{2,6},{3,7},{4,0},{5,1},{6,2},{7,3},{8,12},{9,13},{10,... | collective-permute-start | bytes 786440 | tf_op jit(solution)/shard_map/ppermute | solution.py:456
  47.0 14.7 %collective-permute-start.18 = (bf16[128,1024]{1,0:T(8,128)(2,1)}, bf16[128,1024]{1,0:T(8,128)(2,1)S(1)}, u32[]{:S(2)}, u32[]{:S(2)}) collective-permute-start(bf16[128,1024]{1,0:T(8,128)(2,1)} %get-tuple-element.173), channel_id=1, source_target_pairs={{0,6},{1,7},{2,4},{3,5},{4,2},{5,3},{6,0},{7,1},{8,14},{9,15},{10,... | collective-permute-start | bytes 786440 | tf_op jit(solution)/shard_map/ppermute | solution.py:456
  58.1 15.0 %collective-permute-start.13 = (bf16[128,1024]{1,0:T(8,128)(2,1)}, bf16[128,1024]{1,0:T(8,128)(2,1)S(1)}, u32[]{:S(2)}, u32[]{:S(2)}) collective-permute-start(bf16[128,1024]{1,0:T(8,128)(2,1)} %get-tuple-element.167), channel_id=1, source_target_pairs={{0,2},{1,3},{2,0},{3,1},{4,6},{5,7},{6,4},{7,5},{8,10},{9,11},{10,... | collective-permute-start | bytes 786440 | tf_op jit(solution)/shard_map/ppermute | solution.py:456
  59.2 13.9 %collective-permute-start.14 = (bf16[128,1024]{1,0:T(8,128)(2,1)}, bf16[128,1024]{1,0:T(8,128)(2,1)S(1)}, u32[]{:S(2)}, u32[]{:S(2)}) collective-permute-start(bf16[128,1024]{1,0:T(8,128)(2,1)} %get-tuple-element.168), channel_id=1, source_target_pairs={{0,4},{1,5},{2,6},{3,7},{4,0},{5,1},{6,2},{7,3},{8,12},{9,13},{10,... | collective-permute-start | bytes 786440 | tf_op jit(solution)/shard_map/ppermute | solution.py:456
  59.2 13.9 %collective-permute-start.15 = (bf16[128,1024]{1,0:T(8,128)(2,1)}, bf16[128,1024]{1,0:T(8,128)(2,1)S(1)}, u32[]{:S(2)}, u32[]{:S(2)}) collective-permute-start(bf16[128,1024]{1,0:T(8,128)(2,1)} %get-tuple-element.169), channel_id=1, source_target_pairs={{0,6},{1,7},{2,4},{3,5},{4,2},{5,3},{6,0},{7,1},{8,14},{9,15},{10,... | collective-permute-start | bytes 786440 | tf_op jit(solution)/shard_map/ppermute | solution.py:456
  74.9 8.6 %collective-permute-start.23 = (bf16[64,1024]{1,0:T(8,128)(2,1)}, bf16[64,1024]{1,0:T(8,128)(2,1)S(1)}, u32[]{:S(2)}, u32[]{:S(2)}) collective-permute-start(bf16[64,1024]{1,0:T(8,128)(2,1)} %get-tuple-element.200), channel_id=1, source_target_pairs={{0,6},{1,7},{2,4},{3,5},{4,2},{5,3},{6,0},{7,1},{8,14},{9,15},{10,... | collective-permute-start | bytes 393224 | tf_op jit(solution)/shard_map/ppermute | solution.py:456
  85.9 17.3 %collective-permute-start.27 = (bf16[128,1024]{1,0:T(8,128)(2,1)S(1)}, bf16[128,1024]{1,0:T(8,128)(2,1)S(1)}, u32[]{:S(2)}, u32[]{:S(2)}) collective-permute-start(bf16[128,1024]{1,0:T(8,128)(2,1)S(1)} %shard_map.143), channel_id=1, source_target_pairs={{0,8},{1,9},{2,10},{3,11},{4,12},{5,13},{6,14},{7,15},{8,0},{9,1},... | collective-permute-start | bytes 786440 | tf_op jit(solution)/shard_map/ppermute | solution.py:456
  87.0 13.7 %collective-permute-start.24 = (bf16[64,1024]{1,0:T(8,128)(2,1)}, bf16[64,1024]{1,0:T(8,128)(2,1)S(1)}, u32[]{:S(2)}, u32[]{:S(2)}) collective-permute-start(bf16[64,1024]{1,0:T(8,128)(2,1)} %get-tuple-element.213), channel_id=1, source_target_pairs={{0,2},{1,3},{2,0},{3,1},{4,6},{5,7},{6,4},{7,5},{8,10},{9,11},{10,... | collective-permute-start | bytes 393224 | tf_op jit(solution)/shard_map/ppermute | solution.py:456
  88.7 12.1 %collective-permute-start.25 = (bf16[64,1024]{1,0:T(8,128)(2,1)}, bf16[64,1024]{1,0:T(8,128)(2,1)S(1)}, u32[]{:S(2)}, u32[]{:S(2)}) collective-permute-start(bf16[64,1024]{1,0:T(8,128)(2,1)} %get-tuple-element.214), channel_id=1, source_target_pairs={{0,4},{1,5},{2,6},{3,7},{4,0},{5,1},{6,2},{7,3},{8,12},{9,13},{10,... | collective-permute-start | bytes 393224 | tf_op jit(solution)/shard_map/ppermute | solution.py:456
  90.4 11.3 %collective-permute-start.26 = (bf16[64,1024]{1,0:T(8,128)(2,1)}, bf16[64,1024]{1,0:T(8,128)(2,1)S(1)}, u32[]{:S(2)}, u32[]{:S(2)}) collective-permute-start(bf16[64,1024]{1,0:T(8,128)(2,1)} %get-tuple-element.215), channel_id=1, source_target_pairs={{0,6},{1,7},{2,4},{3,5},{4,2},{5,3},{6,0},{7,1},{8,14},{9,15},{10,... | collective-permute-start | bytes 393224 | tf_op jit(solution)/shard_map/ppermute | solution.py:456
  90.5 21.1 %collective-permute-start.34 = (bf16[128,1024]{1,0:T(8,128)(2,1)S(1)}, bf16[128,1024]{1,0:T(8,128)(2,1)S(1)}, u32[]{:S(2)}, u32[]{:S(2)}) collective-permute-start(bf16[128,1024]{1,0:T(8,128)(2,1)S(1)} %get-tuple-element.239), channel_id=1, source_target_pairs={{0,8},{1,9},{2,10},{3,11},{4,12},{5,13},{6,14},{7,15},{8,0},{9,1},... | collective-permute-start | bytes 786440 | tf_op jit(solution)/shard_map/ppermute | solution.py:456
  (47 other events, 424.2 us)

commit v6 on v5

--- a/solution.py
+++ b/solution.py
@@ -144,21 +144,24 @@
     return picks
 
 
-def pack_kernel(near, capacity, ins, outs, scratch, write):
-    chip, names, rows = ins
-    count = rows.shape[0]
-    first, second = placements(columns_of(ids_of(names[...], count)), chip[0], near, capacity)
-    packed = dot_first(first + second, rows[...]).astype(BF16)
+def picks_of(names, count, chip, near, capacity):
+    first, second = placements(columns_of(ids_of(names, count)), chip[0], near, capacity)
+    return first + second
+
+
+def pack_rows(picks, rows, outs):
+    capacity = outs[0].shape[0]
+    packed = dot_first(picks, rows).astype(BF16)
     for place, out in enumerate(outs):
         out[...] = packed[place * capacity : (place + 1) * capacity]
 
 
 def pack_both_kernel(near, capacity, ins, outs, scratch, write):
     chip, names, rows, far_names, far_rows = ins
-    for block, (these, source) in enumerate(((names, rows), (far_names, far_rows))):
-        count = source.shape[0]
-        first, second = placements(columns_of(ids_of(these[...], count)), chip[0], near, capacity)
-        packed = dot_first(first + second, source[...]).astype(BF16)
+    count = rows.shape[0]
+    picks = [picks_of(these[...], count, chip, near, capacity) for these in (names, far_names)]
+    for block, source in enumerate((rows, far_rows)):
+        packed = dot_first(picks[block], source[...]).astype(BF16)
         for place, out in enumerate(outs):
             out[block * capacity : (block + 1) * capacity, :] = packed[place * capacity : (place + 1) * capacity]
 
@@ -220,9 +223,11 @@
 def front_kernel(near, capacity, ins, outs, scratch, write):
     chip, core, frames, twin, other, taps, gain, names = ins
     conv, normed, parts = outs[0], outs[1], outs[2:]
+    picks_ref, scratch = scratch[0], scratch[1:]
+    picks_ref[...] = picks_of(names[...], frames.shape[0], chip, near, capacity)
     convolve_and_norm(core[0], frames, twin, other, taps, gain, conv, normed, scratch)
     write(0, 1)
-    pack_kernel(near, capacity, (chip, names, normed), parts, scratch, write)
+    pack_rows(picks_ref[...], normed[...], parts)
 
 
 def far_front_kernel(near, capacity, ins, outs, scratch, write):
@@ -233,9 +238,11 @@
     first = jnp.where(even, twin.astype(F32)[RIM - 1 : RIM], twin.astype(F32)[0:1])
     last = jnp.where(even, other.astype(F32)[0:1], other.astype(F32)[RIM - 1 : RIM])
     names[...] = jnp.concatenate([first, last, jnp.zeros((RIM - 2, frames.shape[1]), F32)], axis=0).astype(BF16)
+    picks_ref, scratch = scratch[0], scratch[1:]
+    picks_ref[...] = picks_of(names[...], frames.shape[0], chip, near, capacity)
     convolve_and_norm(core[0], frames, twin, other, taps, gain, None, normed, scratch)
     write(0, 1)
-    pack_kernel(near, capacity, (chip, names, normed), parts, scratch, write)
+    pack_rows(picks_ref[...], normed[...], parts)
 
 
 def result_kernel(near, capacity, ins, outs, scratch, write):
@@ -498,7 +505,8 @@
     even = jnp.concatenate([twin[: RIM - 1], names[0:1], names[1:2], other[1:]])
     odd = jnp.concatenate([names[0:1], twin[1:], other[: RIM - 1], names[1:2]])
     far_rims = cross(jnp.where(core == 0, even, odd))
-    front_scratch = (pad, taps32, pltpu.VMEM((count, width), F32), pltpu.VMEM((count, LANES), F32))
+    front_scratch = (pltpu.VMEM((count, near * capacity), BF16), pad, taps32)
+    front_scratch += (pltpu.VMEM((count, width), F32), pltpu.VMEM((count, LANES), F32))
     conv_out, normed, *parts = kernel_call(
         functools.partial(front_kernel, near, capacity),
         (chips, cores, frames, twin, other, taps, gain, names),
@@ -537,7 +545,6 @@
         (chips, *rows, router, weight_in, other_in, weight_out, other_out),
         pair + (shape((2 * slots, width), BF16), narrow, narrow, narrow, shape((slots, 1), F32)),
         limit=LARGE,
-        first=2 * near + 4,
         scalars=(0,),
     )
     results = exchange(parts, devices)
@@ -549,7 +556,6 @@
         2 * part + (narrow, shape((2 * slots, width), BF16), shape((experts, width), F32)),
         (pltpu.VMEM((slots, width), BF16), pltpu.VMEM((slots, LANES), F32)),
         limit=LARGE,
-        first=near + 3,
         scalars=(0,),
     )
     results, outs, sent = lax.optimization_barrier((results, outs, sent))
@@ -579,7 +585,6 @@
         + (first(sent), near_grad, first(come), second(come_grads)),
         (grad, grad),
         limit=WEIGHTS,
-        first=4,
     )
     backs, expert_in_grad, expert_out_grad = lax.optimization_barrier(
         (own_backs, expert_in_grad, expert_out_grad)

time: 126 us -> 125 us (level)
  transfers between devices with their start and end apart: 37 -> 37, of which waited for: 14 -> 16; matrix products, arithmetic and copies ran while one was open for 3% -> 3% of each run, Pallas kernels for 42% -> 42%
where the time goes in v6:
time: 125 us; the launch traced here: 124 us
  Pallas kernels  54 us (43%)
  starting transfers between devices  44.9 us (36%)
  waiting for transfers between devices  15.8 us (13%)
  local copies, waits for them, and re-layouts  6.66 us (5%)
  other arithmetic  1.57 us (1%)
  between operations  1.36 us (1%)
    pallas_call x13, Pallas kernels, kernel_call(): pl.pallas_call(kernel, out_shape=tuple(outs), in_specs=[pl.BlockSpec(memo...  54 us
    ppermute x35, starting transfers between devices, swap(): return lax.ppermute(values, 'seq', [(i, i ^ bit) for i in range(count)])  43.6 us
    ppermute x35, waiting for transfers between devices, swap(): return lax.ppermute(values, 'seq', [(i, i ^ bit) for i in range(count)])  15.8 us
    unnamed x68, local copies, waits for them, and re-layouts  4.73 us
  transfers between devices with their start and end apart: 37, of which 16 were waited for; matrix products, arithmetic and copies ran while one was open for 3% of the time, Pallas kernels for 42%

profile of v6, /device:TPU:0, one launch (start us, length us, event | category | flops | bytes accessed | tf_op | source)
XLA Modules:
  0.0 124.3 jit_solution(11302879471896130277)
XLA Ops:
  3.2 6.4 %collective-permute-start.8 = (bf16[128,1024]{1,0:T(8,128)(2,1)}, bf16[128,1024]{1,0:T(8,128)(2,1)S(1)}, u32[]{:S(2)}, u32[]{:S(2)}) collective-permute-start(bf16[128,1024]{1,0:T(8,128)(2,1)} %refs_1_), channel_id=1, source_target_pairs={{0,8},{1,9},{2,10},{3,11},{4,12},{5,13},{6,14},{7,15},{8,0},{9,1},... | collective-permute-start | bytes 786440 | tf_op jit(solution)/shard_map/ppermute | solution.py:463
  10.4 2.1 %collective-permute-start.7 = (bf16[32,1024]{1,0:T(8,128)(2,1)S(1)}, bf16[32,1024]{1,0:T(8,128)(2,1)S(1)}, u32[]{:S(2)}, u32[]{:S(2)}) collective-permute-start(bf16[32,1024]{1,0:T(8,128)(2,1)S(1)} %maximum_select_fusion), channel_id=1, source_target_pairs={{0,8},{1,9},{2,10},{3,11},{4,12},{5,13},{6,14},{7,15},{8,0},{9,1},... | collective-permute-start | bytes 196616 | tf_op jit(solution)/shard_map/ppermute | solution.py:463
  14.4 5.5 %shard_map.135 = (f32[128,1024]{1,0:T(8,128)}, bf16[128,1024]{1,0:T(8,128)(2,1)}, bf16[64,1024]{1,0:T(8,128)(2,1)}, bf16[64,1024]{1,0:T(8,128)(2,1)}, bf16[64,10...) custom-call(s32[1]{0:T(128)} %bitcast.refs_0_, s32[1]{0:T(128)} %bitcast.1.refs_1_.refs_0_, bf16[128,1024]{1,0:T(8,128)(2,1)} %refs_1_, ...), custom_call_target="tpu_custom_call" | custom-call | flops 1 | bytes 1782001 | tf_op jit(solution)/shard_map/pallas_call | solution.py:107
  21.4 2.2 %collective-permute-start.5 = (bf16[64,1024]{1,0:T(8,128)(2,1)}, bf16[64,1024]{1,0:T(8,128)(2,1)S(1)}, u32[]{:S(2)}, u32[]{:S(2)}) collective-permute-start(bf16[64,1024]{1,0:T(8,128)(2,1)} %get-tuple-element.138), channel_id=1, source_target_pairs={{0,4},{1,5},{2,6},{3,7},{4,0},{5,1},{6,2},{7,3},{8,12},{9,13},{10,... | collective-permute-start | bytes 393224 | tf_op jit(solution)/shard_map/ppermute | solution.py:463
  26.0 5.8 %shard_map.136 = (bf16[16,1024]{1,0:T(8,128)(2,1)}, bf16[128,1024]{1,0:T(8,128)(2,1)}, bf16[64,1024]{1,0:T(8,128)(2,1)}, bf16[64,1024]{1,0:T(8,128)(2,1)}, bf16[...) custom-call(s32[1]{0:T(128)} %bitcast.refs_0_, s32[1]{0:T(128)} %bitcast.1.refs_1_.refs_0_, bf16[128,1024]{1,0:T(8,128)(2,1)} %copy-done.25, ...), custom_call_target="tpu_custom_call" | custom-call | flops 1 | bytes 1 | tf_op jit(solution)/shard_map/pallas_call | solution.py:107
  36.5 3.5 %collective-permute-done.12.refs_4_ = bf16[128,1024]{1,0:T(8,128)(2,1)S(1)} collective-permute-done((bf16[128,1024]{1,0:T(8,128)(2,1)}, bf16[128,1024]{1,0:T(8,128)(2,1)S(1)}, u32[]{:S(2)}, u32[]{:S(2)}) %collective-permute-start.12) | collective-permute-done | bytes 262176 | tf_op jit(solution)/shard_map/ppermute | solution.py:463
  40.7 3.4 %shard_map.137 = (bf16[128,1024]{1,0:T(8,128)(2,1)}, bf16[128,1024]{1,0:T(8,128)(2,1)}, bf16[128,1024]{1,0:T(8,128)(2,1)}, bf16[128,1024]{1,0:T(8,128)(2,1)}) custom-call(s32[1]{0:T(128)} %bitcast.refs_0_, bf16[16,1024]{1,0:T(8,128)(2,1)} %pad.4.refs_7_.refs_1_.refs_2_, bf16[128,1024]{1,0:T(8,128)(2,1)} %refs_5_.3, ...), custom_call_target="tpu_custom_call" | custom-call | flops 1 | bytes 1 | tf_op jit(solution)/shard_map/pallas_call | solution.py:107
  44.1 1.8 %collective-permute-done.11.refs_8_ = bf16[64,1024]{1,0:T(8,128)(2,1)S(1)} collective-permute-done((bf16[64,1024]{1,0:T(8,128)(2,1)}, bf16[64,1024]{1,0:T(8,128)(2,1)S(1)}, u32[]{:S(2)}, u32[]{:S(2)}) %collective-permute-start.11) | collective-permute-done | bytes 131104 | tf_op jit(solution)/shard_map/ppermute | solution.py:463
  47.0 2.4 %collective-permute-start.18 = (bf16[128,1024]{1,0:T(8,128)(2,1)}, bf16[128,1024]{1,0:T(8,128)(2,1)S(1)}, u32[]{:S(2)}, u32[]{:S(2)}) collective-permute-start(bf16[128,1024]{1,0:T(8,128)(2,1)} %get-tuple-element.173), channel_id=1, source_target_pairs={{0,6},{1,7},{2,4},{3,5},{4,2},{5,3},{6,0},{7,1},{8,14},{9,15},{10,... | collective-permute-start | bytes 786440 | tf_op jit(solution)/shard_map/ppermute | solution.py:463
  49.4 8.7 %shard_map.138 = (bf16[128,1024]{1,0:T(8,128)(2,1)}, bf16[128,1024]{1,0:T(8,128)(2,1)}, bf16[128,1024]{1,0:T(8,128)(2,1)}, bf16[128,1024]{1,0:T(8,128)(2,1)}, bf...) custom-call(s32[1]{0:T(128)} %bitcast.refs_0_, ...), custom_call_target="tpu_custom_call" | custom-call | flops 1 | bytes 1 | tf_op jit(solution)/shard_map/pallas_call | solution.py:107
  59.2 2.4 %collective-permute-start.15 = (bf16[128,1024]{1,0:T(8,128)(2,1)}, bf16[128,1024]{1,0:T(8,128)(2,1)S(1)}, u32[]{:S(2)}, u32[]{:S(2)}) collective-permute-start(bf16[128,1024]{1,0:T(8,128)(2,1)} %get-tuple-element.169), channel_id=1, source_target_pairs={{0,6},{1,7},{2,4},{3,5},{4,2},{5,3},{6,0},{7,1},{8,14},{9,15},{10,... | collective-permute-start | bytes 786440 | tf_op jit(solution)/shard_map/ppermute | solution.py:463
  62.5 9.5 %shard_map.139 = (bf16[64,1024]{1,0:T(8,128)(2,1)}, bf16[64,1024]{1,0:T(8,128)(2,1)}, bf16[64,1024]{1,0:T(8,128)(2,1)}, bf16[64,1024]{1,0:T(8,128)(2,1)}, bf16[6...) custom-call(s32[1]{0:T(128)} %bitcast.refs_0_, ...), custom_call_target="tpu_custom_call" | custom-call | flops 1 | bytes 1 | tf_op jit(solution)/shard_map/pallas_call | solution.py:107
  74.4 2.2 %collective-permute-start.23 = (bf16[64,1024]{1,0:T(8,128)(2,1)}, bf16[64,1024]{1,0:T(8,128)(2,1)S(1)}, u32[]{:S(2)}, u32[]{:S(2)}) collective-permute-start(bf16[64,1024]{1,0:T(8,128)(2,1)} %get-tuple-element.200), channel_id=1, source_target_pairs={{0,6},{1,7},{2,4},{3,5},{4,2},{5,3},{6,0},{7,1},{8,14},{9,15},{10,... | collective-permute-start | bytes 393224 | tf_op jit(solution)/shard_map/ppermute | solution.py:463
  76.6 2.4 %shard_map.140 = (f32[128,1024]{1,0:T(8,128)S(1)}, bf16[128,1024]{1,0:T(8,128)(2,1)S(1)}) custom-call(s32[1]{0:T(128)} %bitcast.refs_0_, bf16[8,1024]{1,0:T(8,128)(2,1)S(1)} %bitcast.13, bf16[16,1024]{1,0:T(8,128)(2,1)S(1)} %copy-done.6, bf16[128,1024]{1,0:T(8,128)(2,1)S(1)} %copy-done.14, bf16[16,1024]{1,0:T(8,128)(2,1)S(1)} %copy-done.13, ...), custom_call_target="tpu_custom_call" | custom-call | flops 1 | bytes 1296001 | tf_op jit(solution)/shard_map/pallas_call | solution.py:107
  80.7 1.9 %collective-permute-done.23.refs_5_ = bf16[64,1024]{1,0:T(8,128)(2,1)S(1)} collective-permute-done((bf16[64,1024]{1,0:T(8,128)(2,1)}, bf16[64,1024]{1,0:T(8,128)(2,1)S(1)}, u32[]{:S(2)}, u32[]{:S(2)}) %collective-permute-start.23) | collective-permute-done | bytes 131104 | tf_op jit(solution)/shard_map/ppermute | solution.py:463
  83.6 1.5 %shard_map.143 = bf16[128,1024]{1,0:T(8,128)(2,1)S(1)} custom-call(s32[1]{0:T(128)} %bitcast.refs_0_, bf16[16,1024]{1,0:T(8,128)(2,1)S(1)} %copy-done.13, bf16[64,1024]{1,0:T(8,128)(2,1)S(1)} %copy-done.18, bf16[64,1024]{1,0:T(8,128)(2,1)S(1)} %collective-permute-done.19.refs_3_, bf16[64,1024]{1,0:T(8,128)(2,1)S(1)} %collective-permute-done.22.refs_4_, ...), custom_call_target="tpu_custom_call" | custom-call | flops 1 | bytes 1 | tf_op jit(solution)/shard_map/pallas_call | solution.py:107
  87.9 1.7 %collective-permute-start.25 = (bf16[64,1024]{1,0:T(8,128)(2,1)}, bf16[64,1024]{1,0:T(8,128)(2,1)S(1)}, u32[]{:S(2)}, u32[]{:S(2)}) collective-permute-start(bf16[64,1024]{1,0:T(8,128)(2,1)} %get-tuple-element.214), channel_id=1, source_target_pairs={{0,4},{1,5},{2,6},{3,7},{4,0},{5,1},{6,2},{7,3},{8,12},{9,13},{10,... | collective-permute-start | bytes 393224 | tf_op jit(solution)/shard_map/ppermute | solution.py:463
  90.0 1.7 %collective-permute-start.34 = (bf16[128,1024]{1,0:T(8,128)(2,1)S(1)}, bf16[128,1024]{1,0:T(8,128)(2,1)S(1)}, u32[]{:S(2)}, u32[]{:S(2)}) collective-permute-start(bf16[128,1024]{1,0:T(8,128)(2,1)S(1)} %get-tuple-element.239), channel_id=1, source_target_pairs={{0,8},{1,9},{2,10},{3,11},{4,12},{5,13},{6,14},{7,15},{8,0},{9,1},... | collective-permute-start | bytes 786440 | tf_op jit(solution)/shard_map/ppermute | solution.py:463
  91.7 1.6 %copy-done.2 = bf16[1024,1024]{1,0:T(8,128)(2,1)S(1)} copy-done((bf16[1024,1024]{1,0:T(8,128)(2,1)S(1)}, bf16[1024,1024]{1,0:T(8,128)(2,1)}, u32[]{:S(2)}) %copy-start.2) | copy-done | bytes 2097176
  93.3 6.7 %shard_map.141 = (bf16[1024,1024]{1,0:T(8,128)(2,1)}, bf16[1024,1024]{1,0:T(8,128)(2,1)}) custom-call(bf16[512,1024]{1,0:T(8,128)(2,1)S(1)} %copy-done.1, bf16[1024,1024]{1,0:T(8,128)(2,1)S(1)} %copy-done.2, bf16[1024,1024]{1,0:T(8,128)(2,1)S(1)} %collective-permute-done.20.refs_2_.refs_6_, bf16[1024,1024]{1,0:T(8,128)(2,1)S(1)} %collective-permute-done.21.refs_3_.refs_7_, ...), custom_call_target="tpu_custom_call" | custom-call | flops 1 | bytes 1 | tf_op jit(solution)/shard_map/pallas_call | solution.py:107
  102.4 3.4 %shard_map.144 = (f32[128,1024]{1,0:T(8,128)S(1)}, f32[128,1024]{1,0:T(8,128)S(1)}, bf16[128,1024]{1,0:T(8,128)(2,1)S(1)}, bf16[16,1024]{1,0:T(8,128)(2,1)S(1)},...) custom-call(s32[1]{0:T(128)} %bitcast.1.refs_1_.refs_0_, ...), custom_call_target="tpu_custom_call" | custom-call | flops 1 | bytes 1 | tf_op jit(solution)/shard_map/pallas_call | solution.py:107
  109.0 1.7 %collective-permute-start.29 = (f32[40,512]{1,0:T(8,128)S(1)}, f32[40,512]{1,0:T(8,128)S(1)}, u32[]{:S(2)}, u32[]{:S(2)}) collective-permute-start(f32[40,512]{1,0:T(8,128)S(1)} %add.23), channel_id=1, source_target_pairs={{0,2},{1,3},{2,0},{3,1},{4,6},{5,7},{6,4},{7,5},{8,10},{9,11},{10,... | collective-permute-start | bytes 245768 | tf_op jit(solution)/shard_map/ppermute | solution.py:463
  114.4 3.8 %collective-permute-start.35 = (f32[40,512]{1,0:T(8,128)S(1)}, f32[40,512]{1,0:T(8,128)S(1)}, u32[]{:S(2)}, u32[]{:S(2)}) collective-permute-start(f32[40,512]{1,0:T(8,128)S(1)} %add_add_fusion), channel_id=1, source_target_pairs={{0,8},{1,9},{2,10},{3,11},{4,12},{5,13},{6,14},{7,15},{8,0},{9,1},... | collective-permute-start | bytes 245768 | tf_op jit(solution)/shard_map/ppermute | solution.py:463
  118.2 3.7 %shard_map.146 = bf16[128,1024]{1,0:T(8,128)(2,1)} custom-call(s32[1]{0:T(128)} %bitcast.1.refs_1_.refs_0_, f32[128,1024]{1,0:T(8,128)S(1)} %get-tuple-element.244.refs_1_, bf16[128,1024]{1,0:T(8,128)(2,1)S(1)} %get-tuple-element.245.refs_2_, bf16[16,1024]{1,0:T(8,128)(2,1)S(1)} %collective-permute-done.32.refs_3_, ...), custom_call_target="tpu_custom_call" | custom-call | flops 1 | bytes 1 | tf_op jit(solution)/shard_map/pallas_call | solution.py:107
  (142 shorter events, 36.8 us)
Async XLA Ops:
  0.6 9.7 %collective-permute-start.2 = (bf16[1024,1024]{1,0:T(8,128)(2,1)}, bf16[1024,1024]{1,0:T(8,128)(2,1)}, u32[]{:S(2)}, u32[]{:S(2)}) collective-permute-start(bf16[1024,1024]{1,0:T(8,128)(2,1)} %bitcast.14), channel_id=1, source_target_pairs={{0,1},{1,0},{2,3},{3,2},{4,5},{5,4},{6,7},{7,6},{8,9},{9,8},{10,11... | collective-permute-start | bytes 6291464 | tf_op jit(solution)/shard_map/ppermute | solution.py:463
  1.1 9.2 %collective-permute-start.3 = (bf16[1024,1024]{1,0:T(8,128)(2,1)}, bf16[1024,1024]{1,0:T(8,128)(2,1)}, u32[]{:S(2)}, u32[]{:S(2)}) collective-permute-start(bf16[1024,1024]{1,0:T(8,128)(2,1)} %bitcast.17), channel_id=1, source_target_pairs={{0,1},{1,0},{2,3},{3,2},{4,5},{5,4},{6,7},{7,6},{8,9},{9,8},{10,11... | collective-permute-start | bytes 6291464 | tf_op jit(solution)/shard_map/ppermute | solution.py:463
  2.0 8.3 %collective-permute-start = (bf16[16,1024]{1,0:T(8,128)(2,1)S(1)}, bf16[16,1024]{1,0:T(8,128)(2,1)S(1)}, u32[]{:S(2)}, u32[]{:S(2)}) collective-permute-start(bf16[16,1024]{1,0:T(8,128)(2,1)S(1)} %get-tuple-element.132), channel_id=1, source_target_pairs={{0,1},{1,0},{2,3},{3,2},{4,5},{5,4},{6,7},{7,6},{8,9},{9,8},{10,11... | collective-permute-start | bytes 98312 | tf_op jit(solution)/shard_map/ppermute | solution.py:463
  3.2 21.9 %collective-permute-start.8 = (bf16[128,1024]{1,0:T(8,128)(2,1)}, bf16[128,1024]{1,0:T(8,128)(2,1)S(1)}, u32[]{:S(2)}, u32[]{:S(2)}) collective-permute-start(bf16[128,1024]{1,0:T(8,128)(2,1)} %refs_1_), channel_id=1, source_target_pairs={{0,8},{1,9},{2,10},{3,11},{4,12},{5,13},{6,14},{7,15},{8,0},{9,1},... | collective-permute-start | bytes 786440 | tf_op jit(solution)/shard_map/ppermute | solution.py:463
  10.4 14.9 %collective-permute-start.7 = (bf16[32,1024]{1,0:T(8,128)(2,1)S(1)}, bf16[32,1024]{1,0:T(8,128)(2,1)S(1)}, u32[]{:S(2)}, u32[]{:S(2)}) collective-permute-start(bf16[32,1024]{1,0:T(8,128)(2,1)S(1)} %maximum_select_fusion), channel_id=1, source_target_pairs={{0,8},{1,9},{2,10},{3,11},{4,12},{5,13},{6,14},{7,15},{8,0},{9,1},... | collective-permute-start | bytes 196616 | tf_op jit(solution)/shard_map/ppermute | solution.py:463
  19.9 11.9 %collective-permute-start.4 = (bf16[64,1024]{1,0:T(8,128)(2,1)}, bf16[64,1024]{1,0:T(8,128)(2,1)S(1)}, u32[]{:S(2)}, u32[]{:S(2)}) collective-permute-start(bf16[64,1024]{1,0:T(8,128)(2,1)} %get-tuple-element.137), channel_id=1, source_target_pairs={{0,2},{1,3},{2,0},{3,1},{4,6},{5,7},{6,4},{7,5},{8,10},{9,11},{10,... | collective-permute-start | bytes 393224 | tf_op jit(solution)/shard_map/ppermute | solution.py:463
  21.4 10.4 %collective-permute-start.5 = (bf16[64,1024]{1,0:T(8,128)(2,1)}, bf16[64,1024]{1,0:T(8,128)(2,1)S(1)}, u32[]{:S(2)}, u32[]{:S(2)}) collective-permute-start(bf16[64,1024]{1,0:T(8,128)(2,1)} %get-tuple-element.138), channel_id=1, source_target_pairs={{0,4},{1,5},{2,6},{3,7},{4,0},{5,1},{6,2},{7,3},{8,12},{9,13},{10,... | collective-permute-start | bytes 393224 | tf_op jit(solution)/shard_map/ppermute | solution.py:463
  23.7 8.9 %collective-permute-start.6 = (bf16[64,1024]{1,0:T(8,128)(2,1)}, bf16[64,1024]{1,0:T(8,128)(2,1)S(1)}, u32[]{:S(2)}, u32[]{:S(2)}) collective-permute-start(bf16[64,1024]{1,0:T(8,128)(2,1)} %get-tuple-element.139), channel_id=1, source_target_pairs={{0,6},{1,7},{2,4},{3,5},{4,2},{5,3},{6,0},{7,1},{8,14},{9,15},{10,... | collective-permute-start | bytes 393224 | tf_op jit(solution)/shard_map/ppermute | solution.py:463
  25.4 14.6 %collective-permute-start.12 = (bf16[128,1024]{1,0:T(8,128)(2,1)}, bf16[128,1024]{1,0:T(8,128)(2,1)S(1)}, u32[]{:S(2)}, u32[]{:S(2)}) collective-permute-start(bf16[128,1024]{1,0:T(8,128)(2,1)} %refs_5_.3), channel_id=1, source_target_pairs={{0,8},{1,9},{2,10},{3,11},{4,12},{5,13},{6,14},{7,15},{8,0},{9,1},... | collective-permute-start | bytes 786440 | tf_op jit(solution)/shard_map/ppermute | solution.py:463
  32.6 11.5 %collective-permute-start.9 = (bf16[64,1024]{1,0:T(8,128)(2,1)}, bf16[64,1024]{1,0:T(8,128)(2,1)S(1)}, u32[]{:S(2)}, u32[]{:S(2)}) collective-permute-start(bf16[64,1024]{1,0:T(8,128)(2,1)} %get-tuple-element.151), channel_id=1, source_target_pairs={{0,2},{1,3},{2,0},{3,1},{4,6},{5,7},{6,4},{7,5},{8,10},{9,11},{10,... | collective-permute-start | bytes 393224 | tf_op jit(solution)/shard_map/ppermute | solution.py:463
  33.6 10.6 %collective-permute-start.10 = (bf16[64,1024]{1,0:T(8,128)(2,1)}, bf16[64,1024]{1,0:T(8,128)(2,1)S(1)}, u32[]{:S(2)}, u32[]{:S(2)}) collective-permute-start(bf16[64,1024]{1,0:T(8,128)(2,1)} %get-tuple-element.152), channel_id=1, source_target_pairs={{0,4},{1,5},{2,6},{3,7},{4,0},{5,1},{6,2},{7,3},{8,12},{9,13},{10,... | collective-permute-start | bytes 393224 | tf_op jit(solution)/shard_map/ppermute | solution.py:463
  35.1 10.8 %collective-permute-start.11 = (bf16[64,1024]{1,0:T(8,128)(2,1)}, bf16[64,1024]{1,0:T(8,128)(2,1)S(1)}, u32[]{:S(2)}, u32[]{:S(2)}) collective-permute-start(bf16[64,1024]{1,0:T(8,128)(2,1)} %get-tuple-element.153), channel_id=1, source_target_pairs={{0,6},{1,7},{2,4},{3,5},{4,2},{5,3},{6,0},{7,1},{8,14},{9,15},{10,... | collective-permute-start | bytes 393224 | tf_op jit(solution)/shard_map/ppermute | solution.py:463
  45.9 13.3 %collective-permute-start.16 = (bf16[128,1024]{1,0:T(8,128)(2,1)}, bf16[128,1024]{1,0:T(8,128)(2,1)S(1)}, u32[]{:S(2)}, u32[]{:S(2)}) collective-permute-start(bf16[128,1024]{1,0:T(8,128)(2,1)} %get-tuple-element.171), channel_id=1, source_target_pairs={{0,2},{1,3},{2,0},{3,1},{4,6},{5,7},{6,4},{7,5},{8,10},{9,11},{10,... | collective-permute-start | bytes 786440 | tf_op jit(solution)/shard_map/ppermute | solution.py:463
  47.0 14.7 %collective-permute-start.17 = (bf16[128,1024]{1,0:T(8,128)(2,1)}, bf16[128,1024]{1,0:T(8,128)(2,1)S(1)}, u32[]{:S(2)}, u32[]{:S(2)}) collective-permute-start(bf16[128,1024]{1,0:T(8,128)(2,1)} %get-tuple-element.172), channel_id=1, source_target_pairs={{0,4},{1,5},{2,6},{3,7},{4,0},{5,1},{6,2},{7,3},{8,12},{9,13},{10,... | collective-permute-start | bytes 786440 | tf_op jit(solution)/shard_map/ppermute | solution.py:463
  47.0 14.7 %collective-permute-start.18 = (bf16[128,1024]{1,0:T(8,128)(2,1)}, bf16[128,1024]{1,0:T(8,128)(2,1)S(1)}, u32[]{:S(2)}, u32[]{:S(2)}) collective-permute-start(bf16[128,1024]{1,0:T(8,128)(2,1)} %get-tuple-element.173), channel_id=1, source_target_pairs={{0,6},{1,7},{2,4},{3,5},{4,2},{5,3},{6,0},{7,1},{8,14},{9,15},{10,... | collective-permute-start | bytes 786440 | tf_op jit(solution)/shard_map/ppermute | solution.py:463
  58.1 14.0 %collective-permute-start.13 = (bf16[128,1024]{1,0:T(8,128)(2,1)}, bf16[128,1024]{1,0:T(8,128)(2,1)S(1)}, u32[]{:S(2)}, u32[]{:S(2)}) collective-permute-start(bf16[128,1024]{1,0:T(8,128)(2,1)} %get-tuple-element.167), channel_id=1, source_target_pairs={{0,2},{1,3},{2,0},{3,1},{4,6},{5,7},{6,4},{7,5},{8,10},{9,11},{10,... | collective-permute-start | bytes 786440 | tf_op jit(solution)/shard_map/ppermute | solution.py:463
  59.2 12.9 %collective-permute-start.14 = (bf16[128,1024]{1,0:T(8,128)(2,1)}, bf16[128,1024]{1,0:T(8,128)(2,1)S(1)}, u32[]{:S(2)}, u32[]{:S(2)}) collective-permute-start(bf16[128,1024]{1,0:T(8,128)(2,1)} %get-tuple-element.168), channel_id=1, source_target_pairs={{0,4},{1,5},{2,6},{3,7},{4,0},{5,1},{6,2},{7,3},{8,12},{9,13},{10,... | collective-permute-start | bytes 786440 | tf_op jit(solution)/shard_map/ppermute | solution.py:463
  59.2 13.3 %collective-permute-start.15 = (bf16[128,1024]{1,0:T(8,128)(2,1)}, bf16[128,1024]{1,0:T(8,128)(2,1)S(1)}, u32[]{:S(2)}, u32[]{:S(2)}) collective-permute-start(bf16[128,1024]{1,0:T(8,128)(2,1)} %get-tuple-element.169), channel_id=1, source_target_pairs={{0,6},{1,7},{2,4},{3,5},{4,2},{5,3},{6,0},{7,1},{8,14},{9,15},{10,... | collective-permute-start | bytes 786440 | tf_op jit(solution)/shard_map/ppermute | solution.py:463
  74.4 8.3 %collective-permute-start.23 = (bf16[64,1024]{1,0:T(8,128)(2,1)}, bf16[64,1024]{1,0:T(8,128)(2,1)S(1)}, u32[]{:S(2)}, u32[]{:S(2)}) collective-permute-start(bf16[64,1024]{1,0:T(8,128)(2,1)} %get-tuple-element.200), channel_id=1, source_target_pairs={{0,6},{1,7},{2,4},{3,5},{4,2},{5,3},{6,0},{7,1},{8,14},{9,15},{10,... | collective-permute-start | bytes 393224 | tf_op jit(solution)/shard_map/ppermute | solution.py:463
  85.2 17.2 %collective-permute-start.27 = (bf16[128,1024]{1,0:T(8,128)(2,1)S(1)}, bf16[128,1024]{1,0:T(8,128)(2,1)S(1)}, u32[]{:S(2)}, u32[]{:S(2)}) collective-permute-start(bf16[128,1024]{1,0:T(8,128)(2,1)S(1)} %shard_map.143), channel_id=1, source_target_pairs={{0,8},{1,9},{2,10},{3,11},{4,12},{5,13},{6,14},{7,15},{8,0},{9,1},... | collective-permute-start | bytes 786440 | tf_op jit(solution)/shard_map/ppermute | solution.py:463
  86.5 13.5 %collective-permute-start.24 = (bf16[64,1024]{1,0:T(8,128)(2,1)}, bf16[64,1024]{1,0:T(8,128)(2,1)S(1)}, u32[]{:S(2)}, u32[]{:S(2)}) collective-permute-start(bf16[64,1024]{1,0:T(8,128)(2,1)} %get-tuple-element.213), channel_id=1, source_target_pairs={{0,2},{1,3},{2,0},{3,1},{4,6},{5,7},{6,4},{7,5},{8,10},{9,11},{10,... | collective-permute-start | bytes 393224 | tf_op jit(solution)/shard_map/ppermute | solution.py:463
  87.9 12.1 %collective-permute-start.25 = (bf16[64,1024]{1,0:T(8,128)(2,1)}, bf16[64,1024]{1,0:T(8,128)(2,1)S(1)}, u32[]{:S(2)}, u32[]{:S(2)}) collective-permute-start(bf16[64,1024]{1,0:T(8,128)(2,1)} %get-tuple-element.214), channel_id=1, source_target_pairs={{0,4},{1,5},{2,6},{3,7},{4,0},{5,1},{6,2},{7,3},{8,12},{9,13},{10,... | collective-permute-start | bytes 393224 | tf_op jit(solution)/shard_map/ppermute | solution.py:463
  89.7 11.1 %collective-permute-start.26 = (bf16[64,1024]{1,0:T(8,128)(2,1)}, bf16[64,1024]{1,0:T(8,128)(2,1)S(1)}, u32[]{:S(2)}, u32[]{:S(2)}) collective-permute-start(bf16[64,1024]{1,0:T(8,128)(2,1)} %get-tuple-element.215), channel_id=1, source_target_pairs={{0,6},{1,7},{2,4},{3,5},{4,2},{5,3},{6,0},{7,1},{8,14},{9,15},{10,... | collective-permute-start | bytes 393224 | tf_op jit(solution)/shard_map/ppermute | solution.py:463
  90.0 20.7 %collective-permute-start.34 = (bf16[128,1024]{1,0:T(8,128)(2,1)S(1)}, bf16[128,1024]{1,0:T(8,128)(2,1)S(1)}, u32[]{:S(2)}, u32[]{:S(2)}) collective-permute-start(bf16[128,1024]{1,0:T(8,128)(2,1)S(1)} %get-tuple-element.239), channel_id=1, source_target_pairs={{0,8},{1,9},{2,10},{3,11},{4,12},{5,13},{6,14},{7,15},{8,0},{9,1},... | collective-permute-start | bytes 786440 | tf_op jit(solution)/shard_map/ppermute | solution.py:463
  (47 other events, 419.2 us)

commit v7 on v6

--- a/solution.py
+++ b/solution.py
@@ -217,7 +217,7 @@
     lane_loop(width, conv)
     mean = jnp.sum(square_ref[...], axis=1, keepdims=True) / width
     inverse = lax.rsqrt(mean + NORM_EPS)
-    normed_ref[...] = (mixed_ref[...] * inverse * gain[...].astype(F32)).astype(BF16)
+    normed_ref[...] = (mixed_ref[...] * inverse * gain[...].astype(F32)[0:1]).astype(BF16)
 
 
 def front_kernel(near, capacity, ins, outs, scratch, write):
@@ -289,7 +289,7 @@
     write(0)
     grad_normed = near_back[...] + far_back[...].astype(F32)
     local_ref[KSIZE : KSIZE + 1, :] = jnp.sum(grad_normed * mixed * inverse, axis=0, keepdims=True)
-    scaled = grad_normed * gain[...].astype(F32)
+    scaled = grad_normed * gain[...].astype(F32)[0:1]
     mean = jnp.sum(scaled * mixed, axis=1, keepdims=True) / width
     mixed_grad = grad[...].astype(F32) + inverse * scaled - mixed * (inverse * inverse * inverse * mean)
     mixed_grad_ref[...] = mixed_grad
@@ -364,7 +364,8 @@
     gather_rows(rows, sent)
     logits = dot_last(sent[rows_part, :], router[...])
     mine = lax.broadcasted_iota(jnp.int32, logits.shape, 1) == chip[0]
-    gate_ref[...] = jax.nn.sigmoid(jnp.sum(jnp.where(mine, logits, 0.0), axis=1, keepdims=True))
+    gate = jax.nn.sigmoid(jnp.sum(jnp.where(mine, logits, 0.0), axis=1, keepdims=True))
+    gate_ref[...] = jnp.broadcast_to(gate, gate_ref.shape)
     near_in.wait()
     near_out.start()
     far_out.start()
@@ -395,7 +396,7 @@
     count = rows.shape[0]
     grads_part, pre_part = slice(0, count), slice(count, 2 * count)
     gather_pairs(grads, grads_ref)
-    gate = gate_ref[...]
+    gate = gate_ref[...][:, 0:1]
     sent[grads_part, :] = (gate * grads_ref[...].astype(F32)).astype(BF16)
     near_out.wait()
     for later in rest[2:]:
@@ -414,7 +415,7 @@
             grad[part, columns] = (hidden * slope[:, columns].astype(F32)).astype(BF16)
     write(2 * near, 2 * near + 1)
     chosen = (jnp.sum(dots_ref[...], axis=1, keepdims=True) * (1.0 - gate)).astype(BF16)
-    experts = router.shape[0]
+    experts = router_out.shape[0]
     mine = lax.broadcasted_iota(jnp.int32, (count, experts), 1) == chip[0]
     router_out[...] = dot_first(jnp.where(mine, chosen.astype(F32), 0.0).astype(BF16), rows[...])
     own = lax.broadcasted_iota(jnp.int32, router.shape, 0) == chip[0]
@@ -474,13 +475,20 @@
     capacity = 8 * count // devices
     near = experts // 2
     slots = experts * capacity
-    gain = norm_gain.reshape(1, width)
-    taps = conv_kernel
-    router = router.T
+    gain_at, router_at, router_rows = 2 * RIM, 3 * RIM, -(-experts // RIM) * RIM
+    params = jnp.concatenate(
+        [
+            jnp.pad(conv_kernel, ((0, gain_at - KSIZE), (0, 0))),
+            jnp.pad(norm_gain.reshape(1, width), ((0, RIM - 1), (0, 0))),
+            jnp.pad(router.T, ((0, router_rows - experts), (0, 0))),
+        ]
+    )
+    taps, gain = Rows(params, 0, gain_at), Rows(params, gain_at, RIM)
+    router = Rows(params, router_at, router_rows)
     ids = expert_ids.T
     shape = jax.ShapeDtypeStruct
     pad = pltpu.VMEM((count + 2 * RIM, width), F32)
-    taps32 = pltpu.VMEM((KSIZE, width), F32)
+    taps32 = pltpu.VMEM((KSIZE + 1, width), F32)
     chip = lax.axis_index("seq") // 2
     chips = chip.reshape(1).astype(jnp.int32)
     cross = functools.partial(swap, count=devices, bit=devices // 2)
@@ -543,7 +551,7 @@
     *parts, sent, near_slope, far_slope, near_active, gate = kernel_call(
         functools.partial(forward_kernel, near),
         (chips, *rows, router, weight_in, other_in, weight_out, other_out),
-        pair + (shape((2 * slots, width), BF16), narrow, narrow, narrow, shape((slots, 1), F32)),
+        pair + (shape((2 * slots, width), BF16), narrow, narrow, narrow, shape((slots, LANES), F32)),
         limit=LARGE,
         scalars=(0,),
     )

time: 125 us -> 125 us (level)
  other arithmetic: 1.57 us -> 3.1 us
  starting transfers between devices: 44.9 us -> 43.6 us
    concatenate x0 -> x1, other arithmetic: none -> 1.52 us  [per_device(): jnp.concatenate([jnp.pad(conv_kernel, ((0, gain_at - KSIZE), (0, 0))), jn...]
    ppermute x35, starting transfers between devices: 43.6 us -> 42.3 us  [swap(): return lax.ppermute(values, 'seq', [(i, i ^ bit) for i in range(count)])]
    unnamed x68 -> x64, local copies, waits for them, and re-layouts: 4.73 us -> 4.68 us
  transfers between devices with their start and end apart: 37 -> 37, of which waited for: 16 -> 16; matrix products, arithmetic and copies ran while one was open for 3% -> 4% of each run, Pallas kernels for 42% -> 42%
where the time goes in v7:
time: 125 us; the launch traced here: 124 us
  Pallas kernels  54.2 us (43%)
  starting transfers between devices  43.6 us (35%)
  waiting for transfers between devices  16 us (13%)
  local copies, waits for them, and re-layouts  6.03 us (5%)
  other arithmetic  3.1 us (2%)
  between operations  1.34 us (1%)
    pallas_call x13, Pallas kernels, kernel_call(): pl.pallas_call(kernel, out_shape=tuple(outs), in_specs=[pl.BlockSpec(memo...  54.2 us
    ppermute x35, starting transfers between devices, swap(): return lax.ppermute(values, 'seq', [(i, i ^ bit) for i in range(count)])  42.3 us
    ppermute x35, waiting for transfers between devices, swap(): return lax.ppermute(values, 'seq', [(i, i ^ bit) for i in range(count)])  16 us
    unnamed x64, local copies, waits for them, and re-layouts  4.68 us
  transfers between devices with their start and end apart: 37, of which 16 were waited for; matrix products, arithmetic and copies ran while one was open for 4% of the time, Pallas kernels for 42%

profile of v7, /device:TPU:0, one launch (start us, length us, event | category | flops | bytes accessed | tf_op | source)
XLA Modules:
  0.0 124.2 jit_solution(11881349948894883984)
XLA Ops:
  3.2 6.4 %collective-permute-start.8 = (bf16[128,1024]{1,0:T(8,128)(2,1)}, bf16[128,1024]{1,0:T(8,128)(2,1)S(1)}, u32[]{:S(2)}, u32[]{:S(2)}) collective-permute-start(bf16[128,1024]{1,0:T(8,128)(2,1)} %refs_1_), channel_id=1, source_target_pairs={{0,8},{1,9},{2,10},{3,11},{4,12},{5,13},{6,14},{7,15},{8,0},{9,1},... | collective-permute-start | bytes 786440 | tf_op jit(solution)/shard_map/ppermute | solution.py:464
  14.0 5.5 %shard_map.135 = (f32[128,1024]{1,0:T(8,128)}, bf16[128,1024]{1,0:T(8,128)(2,1)}, bf16[64,1024]{1,0:T(8,128)(2,1)}, bf16[64,1024]{1,0:T(8,128)(2,1)}, bf16[64,10...) custom-call(s32[1]{0:T(128)} %bitcast.refs_0_, s32[1]{0:T(128)} %bitcast.1.refs_1_.refs_0_, bf16[128,1024]{1,0:T(8,128)(2,1)} %refs_1_, ...), custom_call_target="tpu_custom_call" | custom-call | flops 1 | bytes 1782001 | tf_op jit(solution)/shard_map/pallas_call | solution.py:107
  21.1 2.2 %collective-permute-start.5 = (bf16[64,1024]{1,0:T(8,128)(2,1)}, bf16[64,1024]{1,0:T(8,128)(2,1)S(1)}, u32[]{:S(2)}, u32[]{:S(2)}) collective-permute-start(bf16[64,1024]{1,0:T(8,128)(2,1)} %get-tuple-element.138), channel_id=1, source_target_pairs={{0,4},{1,5},{2,6},{3,7},{4,0},{5,1},{6,2},{7,3},{8,12},{9,13},{10,... | collective-permute-start | bytes 393224 | tf_op jit(solution)/shard_map/ppermute | solution.py:464
  26.0 5.8 %shard_map.136 = (bf16[16,1024]{1,0:T(8,128)(2,1)}, bf16[128,1024]{1,0:T(8,128)(2,1)}, bf16[64,1024]{1,0:T(8,128)(2,1)}, bf16[64,1024]{1,0:T(8,128)(2,1)}, bf16[...) custom-call(s32[1]{0:T(128)} %bitcast.refs_0_, s32[1]{0:T(128)} %bitcast.1.refs_1_.refs_0_, bf16[128,1024]{1,0:T(8,128)(2,1)} %copy-done.23, ...), custom_call_target="tpu_custom_call" | custom-call | flops 1 | bytes 1 | tf_op jit(solution)/shard_map/pallas_call | solution.py:107
  32.7 1.7 %collective-permute-start.9 = (bf16[64,1024]{1,0:T(8,128)(2,1)}, bf16[64,1024]{1,0:T(8,128)(2,1)S(1)}, u32[]{:S(2)}, u32[]{:S(2)}) collective-permute-start(bf16[64,1024]{1,0:T(8,128)(2,1)} %get-tuple-element.151), channel_id=1, source_target_pairs={{0,2},{1,3},{2,0},{3,1},{4,6},{5,7},{6,4},{7,5},{8,10},{9,11},{10,... | collective-permute-start | bytes 393224 | tf_op jit(solution)/shard_map/ppermute | solution.py:464
  36.5 3.5 %collective-permute-done.12.refs_4_ = bf16[128,1024]{1,0:T(8,128)(2,1)S(1)} collective-permute-done((bf16[128,1024]{1,0:T(8,128)(2,1)}, bf16[128,1024]{1,0:T(8,128)(2,1)S(1)}, u32[]{:S(2)}, u32[]{:S(2)}) %collective-permute-start.12) | collective-permute-done | bytes 262176 | tf_op jit(solution)/shard_map/ppermute | solution.py:464
  40.7 3.4 %shard_map.137 = (bf16[128,1024]{1,0:T(8,128)(2,1)}, bf16[128,1024]{1,0:T(8,128)(2,1)}, bf16[128,1024]{1,0:T(8,128)(2,1)}, bf16[128,1024]{1,0:T(8,128)(2,1)}) custom-call(s32[1]{0:T(128)} %bitcast.refs_0_, bf16[16,1024]{1,0:T(8,128)(2,1)} %pad.19.refs_7_.refs_1_.refs_2_, bf16[128,1024]{1,0:T(8,128)(2,1)} %refs_5_, ...), custom_call_target="tpu_custom_call" | custom-call | flops 1 | bytes 1 | tf_op jit(solution)/shard_map/pallas_call | solution.py:107
  44.1 1.7 %collective-permute-done.11.refs_8_ = bf16[64,1024]{1,0:T(8,128)(2,1)S(1)} collective-permute-done((bf16[64,1024]{1,0:T(8,128)(2,1)}, bf16[64,1024]{1,0:T(8,128)(2,1)S(1)}, u32[]{:S(2)}, u32[]{:S(2)}) %collective-permute-start.11) | collective-permute-done | bytes 131104 | tf_op jit(solution)/shard_map/ppermute | solution.py:464
  47.0 2.3 %collective-permute-start.18 = (bf16[128,1024]{1,0:T(8,128)(2,1)}, bf16[128,1024]{1,0:T(8,128)(2,1)S(1)}, u32[]{:S(2)}, u32[]{:S(2)}) collective-permute-start(bf16[128,1024]{1,0:T(8,128)(2,1)} %get-tuple-element.173), channel_id=1, source_target_pairs={{0,6},{1,7},{2,4},{3,5},{4,2},{5,3},{6,0},{7,1},{8,14},{9,15},{10,... | collective-permute-start | bytes 786440 | tf_op jit(solution)/shard_map/ppermute | solution.py:464
  49.3 8.7 %shard_map.138 = (bf16[128,1024]{1,0:T(8,128)(2,1)}, bf16[128,1024]{1,0:T(8,128)(2,1)}, bf16[128,1024]{1,0:T(8,128)(2,1)}, bf16[128,1024]{1,0:T(8,128)(2,1)}, bf...) custom-call(s32[1]{0:T(128)} %bitcast.refs_0_, ...), custom_call_target="tpu_custom_call" | custom-call | flops 1 | bytes 1 | tf_op jit(solution)/shard_map/pallas_call | solution.py:107
  59.2 2.3 %collective-permute-start.15 = (bf16[128,1024]{1,0:T(8,128)(2,1)}, bf16[128,1024]{1,0:T(8,128)(2,1)S(1)}, u32[]{:S(2)}, u32[]{:S(2)}) collective-permute-start(bf16[128,1024]{1,0:T(8,128)(2,1)} %get-tuple-element.169), channel_id=1, source_target_pairs={{0,6},{1,7},{2,4},{3,5},{4,2},{5,3},{6,0},{7,1},{8,14},{9,15},{10,... | collective-permute-start | bytes 786440 | tf_op jit(solution)/shard_map/ppermute | solution.py:464
  62.4 9.6 %shard_map.139 = (bf16[64,1024]{1,0:T(8,128)(2,1)}, bf16[64,1024]{1,0:T(8,128)(2,1)}, bf16[64,1024]{1,0:T(8,128)(2,1)}, bf16[64,1024]{1,0:T(8,128)(2,1)}, bf16[6...) custom-call(s32[1]{0:T(128)} %bitcast.refs_0_, ...), custom_call_target="tpu_custom_call" | custom-call | flops 1 | bytes 1 | tf_op jit(solution)/shard_map/pallas_call | solution.py:107
  74.4 2.0 %collective-permute-start.23 = (bf16[64,1024]{1,0:T(8,128)(2,1)}, bf16[64,1024]{1,0:T(8,128)(2,1)S(1)}, u32[]{:S(2)}, u32[]{:S(2)}) collective-permute-start(bf16[64,1024]{1,0:T(8,128)(2,1)} %get-tuple-element.200), channel_id=1, source_target_pairs={{0,6},{1,7},{2,4},{3,5},{4,2},{5,3},{6,0},{7,1},{8,14},{9,15},{10,... | collective-permute-start | bytes 393224 | tf_op jit(solution)/shard_map/ppermute | solution.py:464
  76.5 2.5 %shard_map.140 = (f32[128,1024]{1,0:T(8,128)S(1)}, bf16[128,1024]{1,0:T(8,128)(2,1)S(1)}) custom-call(s32[1]{0:T(128)} %bitcast.refs_0_, bf16[64,1024]{1,0:T(8,128)(2,1)S(1)} %copy-done.1, bf16[16,1024]{1,0:T(8,128)(2,1)S(1)} %copy-done.7, bf16[128,1024]{1,0:T(8,128)(2,1)S(1)} %copy-done.14, bf16[16,1024]{1,0:T(8,128)(2,1)S(1)} %copy-done.13, ...), custom_call_target="tpu_custom_call" | custom-call | flops 1 | bytes 1296001 | tf_op jit(solution)/shard_map/pallas_call | solution.py:107
  80.8 1.8 %collective-permute-done.23.refs_5_ = bf16[64,1024]{1,0:T(8,128)(2,1)S(1)} collective-permute-done((bf16[64,1024]{1,0:T(8,128)(2,1)}, bf16[64,1024]{1,0:T(8,128)(2,1)S(1)}, u32[]{:S(2)}, u32[]{:S(2)}) %collective-permute-start.23) | collective-permute-done | bytes 131104 | tf_op jit(solution)/shard_map/ppermute | solution.py:464
  83.5 1.5 %shard_map.143 = bf16[128,1024]{1,0:T(8,128)(2,1)S(1)} custom-call(s32[1]{0:T(128)} %bitcast.refs_0_, bf16[16,1024]{1,0:T(8,128)(2,1)S(1)} %copy-done.13, bf16[64,1024]{1,0:T(8,128)(2,1)S(1)} %copy-done.17, bf16[64,1024]{1,0:T(8,128)(2,1)S(1)} %collective-permute-done.19.refs_3_, bf16[64,1024]{1,0:T(8,128)(2,1)S(1)} %collective-permute-done.22.refs_4_, ...), custom_call_target="tpu_custom_call" | custom-call | flops 1 | bytes 1 | tf_op jit(solution)/shard_map/pallas_call | solution.py:107
  87.7 1.7 %collective-permute-start.25 = (bf16[64,1024]{1,0:T(8,128)(2,1)}, bf16[64,1024]{1,0:T(8,128)(2,1)S(1)}, u32[]{:S(2)}, u32[]{:S(2)}) collective-permute-start(bf16[64,1024]{1,0:T(8,128)(2,1)} %get-tuple-element.214), channel_id=1, source_target_pairs={{0,4},{1,5},{2,6},{3,7},{4,0},{5,1},{6,2},{7,3},{8,12},{9,13},{10,... | collective-permute-start | bytes 393224 | tf_op jit(solution)/shard_map/ppermute | solution.py:464
  89.8 1.8 %collective-permute-start.34 = (bf16[128,1024]{1,0:T(8,128)(2,1)S(1)}, bf16[128,1024]{1,0:T(8,128)(2,1)S(1)}, u32[]{:S(2)}, u32[]{:S(2)}) collective-permute-start(bf16[128,1024]{1,0:T(8,128)(2,1)S(1)} %get-tuple-element.239), channel_id=1, source_target_pairs={{0,8},{1,9},{2,10},{3,11},{4,12},{5,13},{6,14},{7,15},{8,0},{9,1},... | collective-permute-start | bytes 786440 | tf_op jit(solution)/shard_map/ppermute | solution.py:464
  91.6 1.6 %copy-done.3 = bf16[1024,1024]{1,0:T(8,128)(2,1)S(1)} copy-done((bf16[1024,1024]{1,0:T(8,128)(2,1)S(1)}, bf16[1024,1024]{1,0:T(8,128)(2,1)}, u32[]{:S(2)}) %copy-start.3) | copy-done | bytes 2097176
  93.1 6.7 %shard_map.141 = (bf16[1024,1024]{1,0:T(8,128)(2,1)}, bf16[1024,1024]{1,0:T(8,128)(2,1)}) custom-call(bf16[512,1024]{1,0:T(8,128)(2,1)S(1)} %copy-done.2, bf16[1024,1024]{1,0:T(8,128)(2,1)S(1)} %copy-done.3, bf16[1024,1024]{1,0:T(8,128)(2,1)S(1)} %collective-permute-done.20.refs_2_.refs_6_, bf16[1024,1024]{1,0:T(8,128)(2,1)S(1)} %collective-permute-done.21.refs_3_.refs_7_, ...), custom_call_target="tpu_custom_call" | custom-call | flops 1 | bytes 1 | tf_op jit(solution)/shard_map/pallas_call | solution.py:107
  102.2 3.4 %shard_map.144 = (f32[128,1024]{1,0:T(8,128)S(1)}, f32[128,1024]{1,0:T(8,128)S(1)}, bf16[128,1024]{1,0:T(8,128)(2,1)S(1)}, bf16[16,1024]{1,0:T(8,128)(2,1)S(1)},...) custom-call(s32[1]{0:T(128)} %bitcast.1.refs_1_.refs_0_, ...), custom_call_target="tpu_custom_call" | custom-call | flops 1 | bytes 1 | tf_op jit(solution)/shard_map/pallas_call | solution.py:107
  106.9 1.5 %collective-permute-start.31 = (f32[40,512]{1,0:T(8,128)S(1)}, f32[40,512]{1,0:T(8,128)S(1)}, u32[]{:S(2)}, u32[]{:S(2)}) collective-permute-start(f32[40,512]{1,0:T(8,128)S(1)} %add.29), channel_id=1, source_target_pairs={{0,6},{1,7},{2,4},{3,5},{4,2},{5,3},{6,0},{7,1},{8,14},{9,15},{10,... | collective-permute-start | bytes 245768 | tf_op jit(solution)/shard_map/ppermute | solution.py:464
  114.2 3.9 %collective-permute-start.35 = (f32[40,512]{1,0:T(8,128)S(1)}, f32[40,512]{1,0:T(8,128)S(1)}, u32[]{:S(2)}, u32[]{:S(2)}) collective-permute-start(f32[40,512]{1,0:T(8,128)S(1)} %add_add_fusion), channel_id=1, source_target_pairs={{0,8},{1,9},{2,10},{3,11},{4,12},{5,13},{6,14},{7,15},{8,0},{9,1},... | collective-permute-start | bytes 245768 | tf_op jit(solution)/shard_map/ppermute | solution.py:464
  118.1 3.7 %shard_map.146 = bf16[128,1024]{1,0:T(8,128)(2,1)} custom-call(s32[1]{0:T(128)} %bitcast.1.refs_1_.refs_0_, f32[128,1024]{1,0:T(8,128)S(1)} %get-tuple-element.244.refs_1_, bf16[128,1024]{1,0:T(8,128)(2,1)S(1)} %get-tuple-element.245.refs_2_, bf16[16,1024]{1,0:T(8,128)(2,1)S(1)} %collective-permute-done.32.refs_3_, ...), custom_call_target="tpu_custom_call" | custom-call | flops 1 | bytes 1 | tf_op jit(solution)/shard_map/pallas_call | solution.py:107
  (139 shorter events, 37.6 us)
Async XLA Ops:
  0.6 11.0 %collective-permute-start.2 = (bf16[1024,1024]{1,0:T(8,128)(2,1)}, bf16[1024,1024]{1,0:T(8,128)(2,1)}, u32[]{:S(2)}, u32[]{:S(2)}) collective-permute-start(bf16[1024,1024]{1,0:T(8,128)(2,1)} %bitcast.11), channel_id=1, source_target_pairs={{0,1},{1,0},{2,3},{3,2},{4,5},{5,4},{6,7},{7,6},{8,9},{9,8},{10,11... | collective-permute-start | bytes 6291464 | tf_op jit(solution)/shard_map/ppermute | solution.py:464
  1.1 10.5 %collective-permute-start.3 = (bf16[1024,1024]{1,0:T(8,128)(2,1)}, bf16[1024,1024]{1,0:T(8,128)(2,1)}, u32[]{:S(2)}, u32[]{:S(2)}) collective-permute-start(bf16[1024,1024]{1,0:T(8,128)(2,1)} %bitcast.14), channel_id=1, source_target_pairs={{0,1},{1,0},{2,3},{3,2},{4,5},{5,4},{6,7},{7,6},{8,9},{9,8},{10,11... | collective-permute-start | bytes 6291464 | tf_op jit(solution)/shard_map/ppermute | solution.py:464
  2.0 9.6 %collective-permute-start = (bf16[16,1024]{1,0:T(8,128)(2,1)S(1)}, bf16[16,1024]{1,0:T(8,128)(2,1)S(1)}, u32[]{:S(2)}, u32[]{:S(2)}) collective-permute-start(bf16[16,1024]{1,0:T(8,128)(2,1)S(1)} %get-tuple-element.132), channel_id=1, source_target_pairs={{0,1},{1,0},{2,3},{3,2},{4,5},{5,4},{6,7},{7,6},{8,9},{9,8},{10,11... | collective-permute-start | bytes 98312 | tf_op jit(solution)/shard_map/ppermute | solution.py:464
  2.5 9.1 %collective-permute-start.1 = (bf16[16,1024]{1,0:T(8,128)(2,1)S(1)}, bf16[16,1024]{1,0:T(8,128)(2,1)S(1)}, u32[]{:S(2)}, u32[]{:S(2)}) collective-permute-start(bf16[16,1024]{1,0:T(8,128)(2,1)S(1)} %get-tuple-element.133), channel_id=1, source_target_pairs={{1,2},{3,4},{5,6},{7,8},{9,10},{11,12},{13,14},{2,1},{4,3},{6,5},{... | collective-permute-start | bytes 98312 | tf_op jit(solution)/shard_map/ppermute | solution.py:460
  3.2 21.5 %collective-permute-start.8 = (bf16[128,1024]{1,0:T(8,128)(2,1)}, bf16[128,1024]{1,0:T(8,128)(2,1)S(1)}, u32[]{:S(2)}, u32[]{:S(2)}) collective-permute-start(bf16[128,1024]{1,0:T(8,128)(2,1)} %refs_1_), channel_id=1, source_target_pairs={{0,8},{1,9},{2,10},{3,11},{4,12},{5,13},{6,14},{7,15},{8,0},{9,1},... | collective-permute-start | bytes 786440 | tf_op jit(solution)/shard_map/ppermute | solution.py:464
  11.7 13.7 %collective-permute-start.7 = (bf16[32,1024]{1,0:T(8,128)(2,1)S(1)}, bf16[32,1024]{1,0:T(8,128)(2,1)S(1)}, u32[]{:S(2)}, u32[]{:S(2)}) collective-permute-start(bf16[32,1024]{1,0:T(8,128)(2,1)S(1)} %maximum_select_fusion), channel_id=1, source_target_pairs={{0,8},{1,9},{2,10},{3,11},{4,12},{5,13},{6,14},{7,15},{8,0},{9,1},... | collective-permute-start | bytes 196616 | tf_op jit(solution)/shard_map/ppermute | solution.py:464
  19.6 12.2 %collective-permute-start.4 = (bf16[64,1024]{1,0:T(8,128)(2,1)}, bf16[64,1024]{1,0:T(8,128)(2,1)S(1)}, u32[]{:S(2)}, u32[]{:S(2)}) collective-permute-start(bf16[64,1024]{1,0:T(8,128)(2,1)} %get-tuple-element.137), channel_id=1, source_target_pairs={{0,2},{1,3},{2,0},{3,1},{4,6},{5,7},{6,4},{7,5},{8,10},{9,11},{10,... | collective-permute-start | bytes 393224 | tf_op jit(solution)/shard_map/ppermute | solution.py:464
  21.1 10.7 %collective-permute-start.5 = (bf16[64,1024]{1,0:T(8,128)(2,1)}, bf16[64,1024]{1,0:T(8,128)(2,1)S(1)}, u32[]{:S(2)}, u32[]{:S(2)}) collective-permute-start(bf16[64,1024]{1,0:T(8,128)(2,1)} %get-tuple-element.138), channel_id=1, source_target_pairs={{0,4},{1,5},{2,6},{3,7},{4,0},{5,1},{6,2},{7,3},{8,12},{9,13},{10,... | collective-permute-start | bytes 393224 | tf_op jit(solution)/shard_map/ppermute | solution.py:464
  23.3 9.4 %collective-permute-start.6 = (bf16[64,1024]{1,0:T(8,128)(2,1)}, bf16[64,1024]{1,0:T(8,128)(2,1)S(1)}, u32[]{:S(2)}, u32[]{:S(2)}) collective-permute-start(bf16[64,1024]{1,0:T(8,128)(2,1)} %get-tuple-element.139), channel_id=1, source_target_pairs={{0,6},{1,7},{2,4},{3,5},{4,2},{5,3},{6,0},{7,1},{8,14},{9,15},{10,... | collective-permute-start | bytes 393224 | tf_op jit(solution)/shard_map/ppermute | solution.py:464
  25.4 14.6 %collective-permute-start.12 = (bf16[128,1024]{1,0:T(8,128)(2,1)}, bf16[128,1024]{1,0:T(8,128)(2,1)S(1)}, u32[]{:S(2)}, u32[]{:S(2)}) collective-permute-start(bf16[128,1024]{1,0:T(8,128)(2,1)} %refs_5_), channel_id=1, source_target_pairs={{0,8},{1,9},{2,10},{3,11},{4,12},{5,13},{6,14},{7,15},{8,0},{9,1},... | collective-permute-start | bytes 786440 | tf_op jit(solution)/shard_map/ppermute | solution.py:464
  32.7 11.4 %collective-permute-start.9 = (bf16[64,1024]{1,0:T(8,128)(2,1)}, bf16[64,1024]{1,0:T(8,128)(2,1)S(1)}, u32[]{:S(2)}, u32[]{:S(2)}) collective-permute-start(bf16[64,1024]{1,0:T(8,128)(2,1)} %get-tuple-element.151), channel_id=1, source_target_pairs={{0,2},{1,3},{2,0},{3,1},{4,6},{5,7},{6,4},{7,5},{8,10},{9,11},{10,... | collective-permute-start | bytes 393224 | tf_op jit(solution)/shard_map/ppermute | solution.py:464
  34.4 9.7 %collective-permute-start.10 = (bf16[64,1024]{1,0:T(8,128)(2,1)}, bf16[64,1024]{1,0:T(8,128)(2,1)S(1)}, u32[]{:S(2)}, u32[]{:S(2)}) collective-permute-start(bf16[64,1024]{1,0:T(8,128)(2,1)} %get-tuple-element.152), channel_id=1, source_target_pairs={{0,4},{1,5},{2,6},{3,7},{4,0},{5,1},{6,2},{7,3},{8,12},{9,13},{10,... | collective-permute-start | bytes 393224 | tf_op jit(solution)/shard_map/ppermute | solution.py:464
  35.1 10.7 %collective-permute-start.11 = (bf16[64,1024]{1,0:T(8,128)(2,1)}, bf16[64,1024]{1,0:T(8,128)(2,1)S(1)}, u32[]{:S(2)}, u32[]{:S(2)}) collective-permute-start(bf16[64,1024]{1,0:T(8,128)(2,1)} %get-tuple-element.153), channel_id=1, source_target_pairs={{0,6},{1,7},{2,4},{3,5},{4,2},{5,3},{6,0},{7,1},{8,14},{9,15},{10,... | collective-permute-start | bytes 393224 | tf_op jit(solution)/shard_map/ppermute | solution.py:464
  45.8 13.4 %collective-permute-start.16 = (bf16[128,1024]{1,0:T(8,128)(2,1)}, bf16[128,1024]{1,0:T(8,128)(2,1)S(1)}, u32[]{:S(2)}, u32[]{:S(2)}) collective-permute-start(bf16[128,1024]{1,0:T(8,128)(2,1)} %get-tuple-element.171), channel_id=1, source_target_pairs={{0,2},{1,3},{2,0},{3,1},{4,6},{5,7},{6,4},{7,5},{8,10},{9,11},{10,... | collective-permute-start | bytes 786440 | tf_op jit(solution)/shard_map/ppermute | solution.py:464
  47.0 14.6 %collective-permute-start.17 = (bf16[128,1024]{1,0:T(8,128)(2,1)}, bf16[128,1024]{1,0:T(8,128)(2,1)S(1)}, u32[]{:S(2)}, u32[]{:S(2)}) collective-permute-start(bf16[128,1024]{1,0:T(8,128)(2,1)} %get-tuple-element.172), channel_id=1, source_target_pairs={{0,4},{1,5},{2,6},{3,7},{4,0},{5,1},{6,2},{7,3},{8,12},{9,13},{10,... | collective-permute-start | bytes 786440 | tf_op jit(solution)/shard_map/ppermute | solution.py:464
  47.0 14.6 %collective-permute-start.18 = (bf16[128,1024]{1,0:T(8,128)(2,1)}, bf16[128,1024]{1,0:T(8,128)(2,1)S(1)}, u32[]{:S(2)}, u32[]{:S(2)}) collective-permute-start(bf16[128,1024]{1,0:T(8,128)(2,1)} %get-tuple-element.173), channel_id=1, source_target_pairs={{0,6},{1,7},{2,4},{3,5},{4,2},{5,3},{6,0},{7,1},{8,14},{9,15},{10,... | collective-permute-start | bytes 786440 | tf_op jit(solution)/shard_map/ppermute | solution.py:464
  58.0 14.1 %collective-permute-start.13 = (bf16[128,1024]{1,0:T(8,128)(2,1)}, bf16[128,1024]{1,0:T(8,128)(2,1)S(1)}, u32[]{:S(2)}, u32[]{:S(2)}) collective-permute-start(bf16[128,1024]{1,0:T(8,128)(2,1)} %get-tuple-element.167), channel_id=1, source_target_pairs={{0,2},{1,3},{2,0},{3,1},{4,6},{5,7},{6,4},{7,5},{8,10},{9,11},{10,... | collective-permute-start | bytes 786440 | tf_op jit(solution)/shard_map/ppermute | solution.py:464
  59.2 12.8 %collective-permute-start.14 = (bf16[128,1024]{1,0:T(8,128)(2,1)}, bf16[128,1024]{1,0:T(8,128)(2,1)S(1)}, u32[]{:S(2)}, u32[]{:S(2)}) collective-permute-start(bf16[128,1024]{1,0:T(8,128)(2,1)} %get-tuple-element.168), channel_id=1, source_target_pairs={{0,4},{1,5},{2,6},{3,7},{4,0},{5,1},{6,2},{7,3},{8,12},{9,13},{10,... | collective-permute-start | bytes 786440 | tf_op jit(solution)/shard_map/ppermute | solution.py:464
  59.2 13.2 %collective-permute-start.15 = (bf16[128,1024]{1,0:T(8,128)(2,1)}, bf16[128,1024]{1,0:T(8,128)(2,1)S(1)}, u32[]{:S(2)}, u32[]{:S(2)}) collective-permute-start(bf16[128,1024]{1,0:T(8,128)(2,1)} %get-tuple-element.169), channel_id=1, source_target_pairs={{0,6},{1,7},{2,4},{3,5},{4,2},{5,3},{6,0},{7,1},{8,14},{9,15},{10,... | collective-permute-start | bytes 786440 | tf_op jit(solution)/shard_map/ppermute | solution.py:464
  85.1 17.1 %collective-permute-start.27 = (bf16[128,1024]{1,0:T(8,128)(2,1)S(1)}, bf16[128,1024]{1,0:T(8,128)(2,1)S(1)}, u32[]{:S(2)}, u32[]{:S(2)}) collective-permute-start(bf16[128,1024]{1,0:T(8,128)(2,1)S(1)} %shard_map.143), channel_id=1, source_target_pairs={{0,8},{1,9},{2,10},{3,11},{4,12},{5,13},{6,14},{7,15},{8,0},{9,1},... | collective-permute-start | bytes 786440 | tf_op jit(solution)/shard_map/ppermute | solution.py:464
  86.3 13.6 %collective-permute-start.24 = (bf16[64,1024]{1,0:T(8,128)(2,1)}, bf16[64,1024]{1,0:T(8,128)(2,1)S(1)}, u32[]{:S(2)}, u32[]{:S(2)}) collective-permute-start(bf16[64,1024]{1,0:T(8,128)(2,1)} %get-tuple-element.213), channel_id=1, source_target_pairs={{0,2},{1,3},{2,0},{3,1},{4,6},{5,7},{6,4},{7,5},{8,10},{9,11},{10,... | collective-permute-start | bytes 393224 | tf_op jit(solution)/shard_map/ppermute | solution.py:464
  87.7 12.1 %collective-permute-start.25 = (bf16[64,1024]{1,0:T(8,128)(2,1)}, bf16[64,1024]{1,0:T(8,128)(2,1)S(1)}, u32[]{:S(2)}, u32[]{:S(2)}) collective-permute-start(bf16[64,1024]{1,0:T(8,128)(2,1)} %get-tuple-element.214), channel_id=1, source_target_pairs={{0,4},{1,5},{2,6},{3,7},{4,0},{5,1},{6,2},{7,3},{8,12},{9,13},{10,... | collective-permute-start | bytes 393224 | tf_op jit(solution)/shard_map/ppermute | solution.py:464
  89.5 11.1 %collective-permute-start.26 = (bf16[64,1024]{1,0:T(8,128)(2,1)}, bf16[64,1024]{1,0:T(8,128)(2,1)S(1)}, u32[]{:S(2)}, u32[]{:S(2)}) collective-permute-start(bf16[64,1024]{1,0:T(8,128)(2,1)} %get-tuple-element.215), channel_id=1, source_target_pairs={{0,6},{1,7},{2,4},{3,5},{4,2},{5,3},{6,0},{7,1},{8,14},{9,15},{10,... | collective-permute-start | bytes 393224 | tf_op jit(solution)/shard_map/ppermute | solution.py:464
  89.8 20.7 %collective-permute-start.34 = (bf16[128,1024]{1,0:T(8,128)(2,1)S(1)}, bf16[128,1024]{1,0:T(8,128)(2,1)S(1)}, u32[]{:S(2)}, u32[]{:S(2)}) collective-permute-start(bf16[128,1024]{1,0:T(8,128)(2,1)S(1)} %get-tuple-element.239), channel_id=1, source_target_pairs={{0,8},{1,9},{2,10},{3,11},{4,12},{5,13},{6,14},{7,15},{8,0},{9,1},... | collective-permute-start | bytes 786440 | tf_op jit(solution)/shard_map/ppermute | solution.py:464
  (45 other events, 387.0 us)

commit v8 on v7

--- a/solution.py
+++ b/solution.py
@@ -583,7 +583,6 @@
     (far_back,) = kernel_call(
         functools.partial(back_kernel, near, capacity), (chips, far_names, *backs), (model16,), scalars=(0,)
     )
-    far_back, far_sum = lax.optimization_barrier((far_back, far_sum))
     far_back = cross(far_back)
     grad = shape(weight_in.shape, BF16)
     first, second = (functools.partial(Rows, start=start, size=slots) for start in (0, slots))
@@ -592,6 +591,7 @@
         (near_active, first(sent_grads), second(come), first(come_grads))
         + (first(sent), near_grad, first(come), second(come_grads)),
         (grad, grad),
+        weight=4.0,
         limit=WEIGHTS,
     )
     backs, expert_in_grad, expert_out_grad = lax.optimization_barrier(

time: 125 us -> 125 us (level)
  no operation moved by 1% of the time
where the time goes in v8:
time: 125 us; the launch traced here: 124 us
  Pallas kernels  54.2 us (43%)
  starting transfers between devices  43.6 us (35%)
  waiting for transfers between devices  16 us (13%)
  local copies, waits for them, and re-layouts  6.03 us (5%)
  other arithmetic  3.1 us (2%)
  between operations  1.34 us (1%)
    pallas_call x13, Pallas kernels, kernel_call(): pl.pallas_call(kernel, out_shape=tuple(outs), in_specs=[pl.BlockSpec(memo...  54.2 us
    ppermute x35, starting transfers between devices, swap(): return lax.ppermute(values, 'seq', [(i, i ^ bit) for i in range(count)])  42.3 us
    ppermute x35, waiting for transfers between devices, swap(): return lax.ppermute(values, 'seq', [(i, i ^ bit) for i in range(count)])  16 us
    unnamed x64, local copies, waits for them, and re-layouts  4.68 us
  transfers between devices with their start and end apart: 37, of which 16 were waited for; matrix products, arithmetic and copies ran while one was open for 4% of the time, Pallas kernels for 42%

profile of v8, /device:TPU:0, one launch (start us, length us, event | category | flops | bytes accessed | tf_op | source)
XLA Modules:
  0.0 124.2 jit_solution(11881349948894883984)
XLA Ops:
  3.2 6.4 %collective-permute-start.8 = (bf16[128,1024]{1,0:T(8,128)(2,1)}, bf16[128,1024]{1,0:T(8,128)(2,1)S(1)}, u32[]{:S(2)}, u32[]{:S(2)}) collective-permute-start(bf16[128,1024]{1,0:T(8,128)(2,1)} %refs_1_), channel_id=1, source_target_pairs={{0,8},{1,9},{2,10},{3,11},{4,12},{5,13},{6,14},{7,15},{8,0},{9,1},... | collective-permute-start | bytes 786440 | tf_op jit(solution)/shard_map/ppermute | solution.py:464
  14.0 5.5 %shard_map.135 = (f32[128,1024]{1,0:T(8,128)}, bf16[128,1024]{1,0:T(8,128)(2,1)}, bf16[64,1024]{1,0:T(8,128)(2,1)}, bf16[64,1024]{1,0:T(8,128)(2,1)}, bf16[64,10...) custom-call(s32[1]{0:T(128)} %bitcast.refs_0_, s32[1]{0:T(128)} %bitcast.1.refs_1_.refs_0_, bf16[128,1024]{1,0:T(8,128)(2,1)} %refs_1_, ...), custom_call_target="tpu_custom_call" | custom-call | flops 1 | bytes 1782001 | tf_op jit(solution)/shard_map/pallas_call | solution.py:107
  21.1 2.2 %collective-permute-start.5 = (bf16[64,1024]{1,0:T(8,128)(2,1)}, bf16[64,1024]{1,0:T(8,128)(2,1)S(1)}, u32[]{:S(2)}, u32[]{:S(2)}) collective-permute-start(bf16[64,1024]{1,0:T(8,128)(2,1)} %get-tuple-element.136), channel_id=1, source_target_pairs={{0,4},{1,5},{2,6},{3,7},{4,0},{5,1},{6,2},{7,3},{8,12},{9,13},{10,... | collective-permute-start | bytes 393224 | tf_op jit(solution)/shard_map/ppermute | solution.py:464
  26.0 5.8 %shard_map.136 = (bf16[16,1024]{1,0:T(8,128)(2,1)}, bf16[128,1024]{1,0:T(8,128)(2,1)}, bf16[64,1024]{1,0:T(8,128)(2,1)}, bf16[64,1024]{1,0:T(8,128)(2,1)}, bf16[...) custom-call(s32[1]{0:T(128)} %bitcast.refs_0_, s32[1]{0:T(128)} %bitcast.1.refs_1_.refs_0_, bf16[128,1024]{1,0:T(8,128)(2,1)} %copy-done.23, ...), custom_call_target="tpu_custom_call" | custom-call | flops 1 | bytes 1 | tf_op jit(solution)/shard_map/pallas_call | solution.py:107
  32.7 1.7 %collective-permute-start.9 = (bf16[64,1024]{1,0:T(8,128)(2,1)}, bf16[64,1024]{1,0:T(8,128)(2,1)S(1)}, u32[]{:S(2)}, u32[]{:S(2)}) collective-permute-start(bf16[64,1024]{1,0:T(8,128)(2,1)} %get-tuple-element.149), channel_id=1, source_target_pairs={{0,2},{1,3},{2,0},{3,1},{4,6},{5,7},{6,4},{7,5},{8,10},{9,11},{10,... | collective-permute-start | bytes 393224 | tf_op jit(solution)/shard_map/ppermute | solution.py:464
  36.5 3.5 %collective-permute-done.12.refs_4_ = bf16[128,1024]{1,0:T(8,128)(2,1)S(1)} collective-permute-done((bf16[128,1024]{1,0:T(8,128)(2,1)}, bf16[128,1024]{1,0:T(8,128)(2,1)S(1)}, u32[]{:S(2)}, u32[]{:S(2)}) %collective-permute-start.12) | collective-permute-done | bytes 262176 | tf_op jit(solution)/shard_map/ppermute | solution.py:464
  40.7 3.4 %shard_map.137 = (bf16[128,1024]{1,0:T(8,128)(2,1)}, bf16[128,1024]{1,0:T(8,128)(2,1)}, bf16[128,1024]{1,0:T(8,128)(2,1)}, bf16[128,1024]{1,0:T(8,128)(2,1)}) custom-call(s32[1]{0:T(128)} %bitcast.refs_0_, bf16[16,1024]{1,0:T(8,128)(2,1)} %pad.19.refs_7_.refs_1_.refs_2_, bf16[128,1024]{1,0:T(8,128)(2,1)} %refs_5_, ...), custom_call_target="tpu_custom_call" | custom-call | flops 1 | bytes 1 | tf_op jit(solution)/shard_map/pallas_call | solution.py:107
  44.1 1.7 %collective-permute-done.11.refs_8_ = bf16[64,1024]{1,0:T(8,128)(2,1)S(1)} collective-permute-done((bf16[64,1024]{1,0:T(8,128)(2,1)}, bf16[64,1024]{1,0:T(8,128)(2,1)S(1)}, u32[]{:S(2)}, u32[]{:S(2)}) %collective-permute-start.11) | collective-permute-done | bytes 131104 | tf_op jit(solution)/shard_map/ppermute | solution.py:464
  47.0 2.3 %collective-permute-start.18 = (bf16[128,1024]{1,0:T(8,128)(2,1)}, bf16[128,1024]{1,0:T(8,128)(2,1)S(1)}, u32[]{:S(2)}, u32[]{:S(2)}) collective-permute-start(bf16[128,1024]{1,0:T(8,128)(2,1)} %get-tuple-element.171), channel_id=1, source_target_pairs={{0,6},{1,7},{2,4},{3,5},{4,2},{5,3},{6,0},{7,1},{8,14},{9,15},{10,... | collective-permute-start | bytes 786440 | tf_op jit(solution)/shard_map/ppermute | solution.py:464
  49.3 8.7 %shard_map.138 = (bf16[128,1024]{1,0:T(8,128)(2,1)}, bf16[128,1024]{1,0:T(8,128)(2,1)}, bf16[128,1024]{1,0:T(8,128)(2,1)}, bf16[128,1024]{1,0:T(8,128)(2,1)}, bf...) custom-call(s32[1]{0:T(128)} %bitcast.refs_0_, ...), custom_call_target="tpu_custom_call" | custom-call | flops 1 | bytes 1 | tf_op jit(solution)/shard_map/pallas_call | solution.py:107
  59.2 2.3 %collective-permute-start.15 = (bf16[128,1024]{1,0:T(8,128)(2,1)}, bf16[128,1024]{1,0:T(8,128)(2,1)S(1)}, u32[]{:S(2)}, u32[]{:S(2)}) collective-permute-start(bf16[128,1024]{1,0:T(8,128)(2,1)} %get-tuple-element.167), channel_id=1, source_target_pairs={{0,6},{1,7},{2,4},{3,5},{4,2},{5,3},{6,0},{7,1},{8,14},{9,15},{10,... | collective-permute-start | bytes 786440 | tf_op jit(solution)/shard_map/ppermute | solution.py:464
  62.4 9.6 %shard_map.139 = (bf16[64,1024]{1,0:T(8,128)(2,1)}, bf16[64,1024]{1,0:T(8,128)(2,1)}, bf16[64,1024]{1,0:T(8,128)(2,1)}, bf16[64,1024]{1,0:T(8,128)(2,1)}, bf16[6...) custom-call(s32[1]{0:T(128)} %bitcast.refs_0_, ...), custom_call_target="tpu_custom_call" | custom-call | flops 1 | bytes 1 | tf_op jit(solution)/shard_map/pallas_call | solution.py:107
  74.4 2.0 %collective-permute-start.23 = (bf16[64,1024]{1,0:T(8,128)(2,1)}, bf16[64,1024]{1,0:T(8,128)(2,1)S(1)}, u32[]{:S(2)}, u32[]{:S(2)}) collective-permute-start(bf16[64,1024]{1,0:T(8,128)(2,1)} %get-tuple-element.198), channel_id=1, source_target_pairs={{0,6},{1,7},{2,4},{3,5},{4,2},{5,3},{6,0},{7,1},{8,14},{9,15},{10,... | collective-permute-start | bytes 393224 | tf_op jit(solution)/shard_map/ppermute | solution.py:464
  76.5 2.5 %shard_map.140 = (f32[128,1024]{1,0:T(8,128)S(1)}, bf16[128,1024]{1,0:T(8,128)(2,1)S(1)}) custom-call(s32[1]{0:T(128)} %bitcast.refs_0_, bf16[64,1024]{1,0:T(8,128)(2,1)S(1)} %copy-done.1, bf16[16,1024]{1,0:T(8,128)(2,1)S(1)} %copy-done.7, bf16[128,1024]{1,0:T(8,128)(2,1)S(1)} %copy-done.14, bf16[16,1024]{1,0:T(8,128)(2,1)S(1)} %copy-done.13, ...), custom_call_target="tpu_custom_call" | custom-call | flops 1 | bytes 1296001 | tf_op jit(solution)/shard_map/pallas_call | solution.py:107
  80.8 1.8 %collective-permute-done.23.refs_5_ = bf16[64,1024]{1,0:T(8,128)(2,1)S(1)} collective-permute-done((bf16[64,1024]{1,0:T(8,128)(2,1)}, bf16[64,1024]{1,0:T(8,128)(2,1)S(1)}, u32[]{:S(2)}, u32[]{:S(2)}) %collective-permute-start.23) | collective-permute-done | bytes 131104 | tf_op jit(solution)/shard_map/ppermute | solution.py:464
  83.5 1.5 %shard_map.143 = bf16[128,1024]{1,0:T(8,128)(2,1)S(1)} custom-call(s32[1]{0:T(128)} %bitcast.refs_0_, bf16[16,1024]{1,0:T(8,128)(2,1)S(1)} %copy-done.13, bf16[64,1024]{1,0:T(8,128)(2,1)S(1)} %copy-done.17, bf16[64,1024]{1,0:T(8,128)(2,1)S(1)} %collective-permute-done.19.refs_3_, bf16[64,1024]{1,0:T(8,128)(2,1)S(1)} %collective-permute-done.22.refs_4_, ...), custom_call_target="tpu_custom_call" | custom-call | flops 1 | bytes 1 | tf_op jit(solution)/shard_map/pallas_call | solution.py:107
  87.7 1.7 %collective-permute-start.25 = (bf16[64,1024]{1,0:T(8,128)(2,1)}, bf16[64,1024]{1,0:T(8,128)(2,1)S(1)}, u32[]{:S(2)}, u32[]{:S(2)}) collective-permute-start(bf16[64,1024]{1,0:T(8,128)(2,1)} %get-tuple-element.212), channel_id=1, source_target_pairs={{0,4},{1,5},{2,6},{3,7},{4,0},{5,1},{6,2},{7,3},{8,12},{9,13},{10,... | collective-permute-start | bytes 393224 | tf_op jit(solution)/shard_map/ppermute | solution.py:464
  89.8 1.8 %collective-permute-start.34 = (bf16[128,1024]{1,0:T(8,128)(2,1)S(1)}, bf16[128,1024]{1,0:T(8,128)(2,1)S(1)}, u32[]{:S(2)}, u32[]{:S(2)}) collective-permute-start(bf16[128,1024]{1,0:T(8,128)(2,1)S(1)} %get-tuple-element.235), channel_id=1, source_target_pairs={{0,8},{1,9},{2,10},{3,11},{4,12},{5,13},{6,14},{7,15},{8,0},{9,1},... | collective-permute-start | bytes 786440 | tf_op jit(solution)/shard_map/ppermute | solution.py:464
  91.6 1.6 %copy-done.3 = bf16[1024,1024]{1,0:T(8,128)(2,1)S(1)} copy-done((bf16[1024,1024]{1,0:T(8,128)(2,1)S(1)}, bf16[1024,1024]{1,0:T(8,128)(2,1)}, u32[]{:S(2)}) %copy-start.3) | copy-done | bytes 2097176
  93.1 6.7 %shard_map.141 = (bf16[1024,1024]{1,0:T(8,128)(2,1)}, bf16[1024,1024]{1,0:T(8,128)(2,1)}) custom-call(bf16[512,1024]{1,0:T(8,128)(2,1)S(1)} %copy-done.2, bf16[1024,1024]{1,0:T(8,128)(2,1)S(1)} %copy-done.3, bf16[1024,1024]{1,0:T(8,128)(2,1)S(1)} %collective-permute-done.20.refs_2_.refs_6_, bf16[1024,1024]{1,0:T(8,128)(2,1)S(1)} %collective-permute-done.21.refs_3_.refs_7_, ...), custom_call_target="tpu_custom_call" | custom-call | flops 1 | bytes 2160001 | tf_op jit(solution)/shard_map/pallas_call | solution.py:107
  102.2 3.4 %shard_map.144 = (f32[128,1024]{1,0:T(8,128)S(1)}, f32[128,1024]{1,0:T(8,128)S(1)}, bf16[128,1024]{1,0:T(8,128)(2,1)S(1)}, bf16[16,1024]{1,0:T(8,128)(2,1)S(1)},...) custom-call(s32[1]{0:T(128)} %bitcast.1.refs_1_.refs_0_, ...), custom_call_target="tpu_custom_call" | custom-call | flops 1 | bytes 1 | tf_op jit(solution)/shard_map/pallas_call | solution.py:107
  106.9 1.5 %collective-permute-start.31 = (f32[40,512]{1,0:T(8,128)S(1)}, f32[40,512]{1,0:T(8,128)S(1)}, u32[]{:S(2)}, u32[]{:S(2)}) collective-permute-start(f32[40,512]{1,0:T(8,128)S(1)} %add.29), channel_id=1, source_target_pairs={{0,6},{1,7},{2,4},{3,5},{4,2},{5,3},{6,0},{7,1},{8,14},{9,15},{10,... | collective-permute-start | bytes 245768 | tf_op jit(solution)/shard_map/ppermute | solution.py:464
  114.2 3.9 %collective-permute-start.35 = (f32[40,512]{1,0:T(8,128)S(1)}, f32[40,512]{1,0:T(8,128)S(1)}, u32[]{:S(2)}, u32[]{:S(2)}) collective-permute-start(f32[40,512]{1,0:T(8,128)S(1)} %add_add_fusion), channel_id=1, source_target_pairs={{0,8},{1,9},{2,10},{3,11},{4,12},{5,13},{6,14},{7,15},{8,0},{9,1},... | collective-permute-start | bytes 245768 | tf_op jit(solution)/shard_map/ppermute | solution.py:464
  118.1 3.7 %shard_map.146 = bf16[128,1024]{1,0:T(8,128)(2,1)} custom-call(s32[1]{0:T(128)} %bitcast.1.refs_1_.refs_0_, f32[128,1024]{1,0:T(8,128)S(1)} %get-tuple-element.240.refs_1_, bf16[128,1024]{1,0:T(8,128)(2,1)S(1)} %get-tuple-element.241.refs_2_, bf16[16,1024]{1,0:T(8,128)(2,1)S(1)} %collective-permute-done.32.refs_3_, ...), custom_call_target="tpu_custom_call" | custom-call | flops 1 | bytes 1 | tf_op jit(solution)/shard_map/pallas_call | solution.py:107
  (139 shorter events, 37.6 us)
Async XLA Ops:
  0.6 11.0 %collective-permute-start.2 = (bf16[1024,1024]{1,0:T(8,128)(2,1)}, bf16[1024,1024]{1,0:T(8,128)(2,1)}, u32[]{:S(2)}, u32[]{:S(2)}) collective-permute-start(bf16[1024,1024]{1,0:T(8,128)(2,1)} %bitcast.11), channel_id=1, source_target_pairs={{0,1},{1,0},{2,3},{3,2},{4,5},{5,4},{6,7},{7,6},{8,9},{9,8},{10,11... | collective-permute-start | bytes 6291464 | tf_op jit(solution)/shard_map/ppermute | solution.py:464
  1.1 10.5 %collective-permute-start.3 = (bf16[1024,1024]{1,0:T(8,128)(2,1)}, bf16[1024,1024]{1,0:T(8,128)(2,1)}, u32[]{:S(2)}, u32[]{:S(2)}) collective-permute-start(bf16[1024,1024]{1,0:T(8,128)(2,1)} %bitcast.14), channel_id=1, source_target_pairs={{0,1},{1,0},{2,3},{3,2},{4,5},{5,4},{6,7},{7,6},{8,9},{9,8},{10,11... | collective-permute-start | bytes 6291464 | tf_op jit(solution)/shard_map/ppermute | solution.py:464
  2.0 9.6 %collective-permute-start = (bf16[16,1024]{1,0:T(8,128)(2,1)S(1)}, bf16[16,1024]{1,0:T(8,128)(2,1)S(1)}, u32[]{:S(2)}, u32[]{:S(2)}) collective-permute-start(bf16[16,1024]{1,0:T(8,128)(2,1)S(1)} %get-tuple-element.130), channel_id=1, source_target_pairs={{0,1},{1,0},{2,3},{3,2},{4,5},{5,4},{6,7},{7,6},{8,9},{9,8},{10,11... | collective-permute-start | bytes 98312 | tf_op jit(solution)/shard_map/ppermute | solution.py:464
  2.5 9.1 %collective-permute-start.1 = (bf16[16,1024]{1,0:T(8,128)(2,1)S(1)}, bf16[16,1024]{1,0:T(8,128)(2,1)S(1)}, u32[]{:S(2)}, u32[]{:S(2)}) collective-permute-start(bf16[16,1024]{1,0:T(8,128)(2,1)S(1)} %get-tuple-element.131), channel_id=1, source_target_pairs={{1,2},{3,4},{5,6},{7,8},{9,10},{11,12},{13,14},{2,1},{4,3},{6,5},{... | collective-permute-start | bytes 98312 | tf_op jit(solution)/shard_map/ppermute | solution.py:460
  3.2 21.5 %collective-permute-start.8 = (bf16[128,1024]{1,0:T(8,128)(2,1)}, bf16[128,1024]{1,0:T(8,128)(2,1)S(1)}, u32[]{:S(2)}, u32[]{:S(2)}) collective-permute-start(bf16[128,1024]{1,0:T(8,128)(2,1)} %refs_1_), channel_id=1, source_target_pairs={{0,8},{1,9},{2,10},{3,11},{4,12},{5,13},{6,14},{7,15},{8,0},{9,1},... | collective-permute-start | bytes 786440 | tf_op jit(solution)/shard_map/ppermute | solution.py:464
  11.7 13.7 %collective-permute-start.7 = (bf16[32,1024]{1,0:T(8,128)(2,1)S(1)}, bf16[32,1024]{1,0:T(8,128)(2,1)S(1)}, u32[]{:S(2)}, u32[]{:S(2)}) collective-permute-start(bf16[32,1024]{1,0:T(8,128)(2,1)S(1)} %maximum_select_fusion), channel_id=1, source_target_pairs={{0,8},{1,9},{2,10},{3,11},{4,12},{5,13},{6,14},{7,15},{8,0},{9,1},... | collective-permute-start | bytes 196616 | tf_op jit(solution)/shard_map/ppermute | solution.py:464
  19.6 12.2 %collective-permute-start.4 = (bf16[64,1024]{1,0:T(8,128)(2,1)}, bf16[64,1024]{1,0:T(8,128)(2,1)S(1)}, u32[]{:S(2)}, u32[]{:S(2)}) collective-permute-start(bf16[64,1024]{1,0:T(8,128)(2,1)} %get-tuple-element.135), channel_id=1, source_target_pairs={{0,2},{1,3},{2,0},{3,1},{4,6},{5,7},{6,4},{7,5},{8,10},{9,11},{10,... | collective-permute-start | bytes 393224 | tf_op jit(solution)/shard_map/ppermute | solution.py:464
  21.1 10.7 %collective-permute-start.5 = (bf16[64,1024]{1,0:T(8,128)(2,1)}, bf16[64,1024]{1,0:T(8,128)(2,1)S(1)}, u32[]{:S(2)}, u32[]{:S(2)}) collective-permute-start(bf16[64,1024]{1,0:T(8,128)(2,1)} %get-tuple-element.136), channel_id=1, source_target_pairs={{0,4},{1,5},{2,6},{3,7},{4,0},{5,1},{6,2},{7,3},{8,12},{9,13},{10,... | collective-permute-start | bytes 393224 | tf_op jit(solution)/shard_map/ppermute | solution.py:464
  23.3 9.4 %collective-permute-start.6 = (bf16[64,1024]{1,0:T(8,128)(2,1)}, bf16[64,1024]{1,0:T(8,128)(2,1)S(1)}, u32[]{:S(2)}, u32[]{:S(2)}) collective-permute-start(bf16[64,1024]{1,0:T(8,128)(2,1)} %get-tuple-element.137), channel_id=1, source_target_pairs={{0,6},{1,7},{2,4},{3,5},{4,2},{5,3},{6,0},{7,1},{8,14},{9,15},{10,... | collective-permute-start | bytes 393224 | tf_op jit(solution)/shard_map/ppermute | solution.py:464
  25.4 14.6 %collective-permute-start.12 = (bf16[128,1024]{1,0:T(8,128)(2,1)}, bf16[128,1024]{1,0:T(8,128)(2,1)S(1)}, u32[]{:S(2)}, u32[]{:S(2)}) collective-permute-start(bf16[128,1024]{1,0:T(8,128)(2,1)} %refs_5_), channel_id=1, source_target_pairs={{0,8},{1,9},{2,10},{3,11},{4,12},{5,13},{6,14},{7,15},{8,0},{9,1},... | collective-permute-start | bytes 786440 | tf_op jit(solution)/shard_map/ppermute | solution.py:464
  32.7 11.4 %collective-permute-start.9 = (bf16[64,1024]{1,0:T(8,128)(2,1)}, bf16[64,1024]{1,0:T(8,128)(2,1)S(1)}, u32[]{:S(2)}, u32[]{:S(2)}) collective-permute-start(bf16[64,1024]{1,0:T(8,128)(2,1)} %get-tuple-element.149), channel_id=1, source_target_pairs={{0,2},{1,3},{2,0},{3,1},{4,6},{5,7},{6,4},{7,5},{8,10},{9,11},{10,... | collective-permute-start | bytes 393224 | tf_op jit(solution)/shard_map/ppermute | solution.py:464
  34.4 9.7 %collective-permute-start.10 = (bf16[64,1024]{1,0:T(8,128)(2,1)}, bf16[64,1024]{1,0:T(8,128)(2,1)S(1)}, u32[]{:S(2)}, u32[]{:S(2)}) collective-permute-start(bf16[64,1024]{1,0:T(8,128)(2,1)} %get-tuple-element.150), channel_id=1, source_target_pairs={{0,4},{1,5},{2,6},{3,7},{4,0},{5,1},{6,2},{7,3},{8,12},{9,13},{10,... | collective-permute-start | bytes 393224 | tf_op jit(solution)/shard_map/ppermute | solution.py:464
  35.1 10.7 %collective-permute-start.11 = (bf16[64,1024]{1,0:T(8,128)(2,1)}, bf16[64,1024]{1,0:T(8,128)(2,1)S(1)}, u32[]{:S(2)}, u32[]{:S(2)}) collective-permute-start(bf16[64,1024]{1,0:T(8,128)(2,1)} %get-tuple-element.151), channel_id=1, source_target_pairs={{0,6},{1,7},{2,4},{3,5},{4,2},{5,3},{6,0},{7,1},{8,14},{9,15},{10,... | collective-permute-start | bytes 393224 | tf_op jit(solution)/shard_map/ppermute | solution.py:464
  45.8 13.4 %collective-permute-start.16 = (bf16[128,1024]{1,0:T(8,128)(2,1)}, bf16[128,1024]{1,0:T(8,128)(2,1)S(1)}, u32[]{:S(2)}, u32[]{:S(2)}) collective-permute-start(bf16[128,1024]{1,0:T(8,128)(2,1)} %get-tuple-element.169), channel_id=1, source_target_pairs={{0,2},{1,3},{2,0},{3,1},{4,6},{5,7},{6,4},{7,5},{8,10},{9,11},{10,... | collective-permute-start | bytes 786440 | tf_op jit(solution)/shard_map/ppermute | solution.py:464
  47.0 14.6 %collective-permute-start.17 = (bf16[128,1024]{1,0:T(8,128)(2,1)}, bf16[128,1024]{1,0:T(8,128)(2,1)S(1)}, u32[]{:S(2)}, u32[]{:S(2)}) collective-permute-start(bf16[128,1024]{1,0:T(8,128)(2,1)} %get-tuple-element.170), channel_id=1, source_target_pairs={{0,4},{1,5},{2,6},{3,7},{4,0},{5,1},{6,2},{7,3},{8,12},{9,13},{10,... | collective-permute-start | bytes 786440 | tf_op jit(solution)/shard_map/ppermute | solution.py:464
  47.0 14.6 %collective-permute-start.18 = (bf16[128,1024]{1,0:T(8,128)(2,1)}, bf16[128,1024]{1,0:T(8,128)(2,1)S(1)}, u32[]{:S(2)}, u32[]{:S(2)}) collective-permute-start(bf16[128,1024]{1,0:T(8,128)(2,1)} %get-tuple-element.171), channel_id=1, source_target_pairs={{0,6},{1,7},{2,4},{3,5},{4,2},{5,3},{6,0},{7,1},{8,14},{9,15},{10,... | collective-permute-start | bytes 786440 | tf_op jit(solution)/shard_map/ppermute | solution.py:464
  58.0 14.1 %collective-permute-start.13 = (bf16[128,1024]{1,0:T(8,128)(2,1)}, bf16[128,1024]{1,0:T(8,128)(2,1)S(1)}, u32[]{:S(2)}, u32[]{:S(2)}) collective-permute-start(bf16[128,1024]{1,0:T(8,128)(2,1)} %get-tuple-element.165), channel_id=1, source_target_pairs={{0,2},{1,3},{2,0},{3,1},{4,6},{5,7},{6,4},{7,5},{8,10},{9,11},{10,... | collective-permute-start | bytes 786440 | tf_op jit(solution)/shard_map/ppermute | solution.py:464
  59.2 12.8 %collective-permute-start.14 = (bf16[128,1024]{1,0:T(8,128)(2,1)}, bf16[128,1024]{1,0:T(8,128)(2,1)S(1)}, u32[]{:S(2)}, u32[]{:S(2)}) collective-permute-start(bf16[128,1024]{1,0:T(8,128)(2,1)} %get-tuple-element.166), channel_id=1, source_target_pairs={{0,4},{1,5},{2,6},{3,7},{4,0},{5,1},{6,2},{7,3},{8,12},{9,13},{10,... | collective-permute-start | bytes 786440 | tf_op jit(solution)/shard_map/ppermute | solution.py:464
  59.2 13.2 %collective-permute-start.15 = (bf16[128,1024]{1,0:T(8,128)(2,1)}, bf16[128,1024]{1,0:T(8,128)(2,1)S(1)}, u32[]{:S(2)}, u32[]{:S(2)}) collective-permute-start(bf16[128,1024]{1,0:T(8,128)(2,1)} %get-tuple-element.167), channel_id=1, source_target_pairs={{0,6},{1,7},{2,4},{3,5},{4,2},{5,3},{6,0},{7,1},{8,14},{9,15},{10,... | collective-permute-start | bytes 786440 | tf_op jit(solution)/shard_map/ppermute | solution.py:464
  85.1 17.1 %collective-permute-start.27 = (bf16[128,1024]{1,0:T(8,128)(2,1)S(1)}, bf16[128,1024]{1,0:T(8,128)(2,1)S(1)}, u32[]{:S(2)}, u32[]{:S(2)}) collective-permute-start(bf16[128,1024]{1,0:T(8,128)(2,1)S(1)} %shard_map.143), channel_id=1, source_target_pairs={{0,8},{1,9},{2,10},{3,11},{4,12},{5,13},{6,14},{7,15},{8,0},{9,1},... | collective-permute-start | bytes 786440 | tf_op jit(solution)/shard_map/ppermute | solution.py:464
  86.3 13.6 %collective-permute-start.24 = (bf16[64,1024]{1,0:T(8,128)(2,1)}, bf16[64,1024]{1,0:T(8,128)(2,1)S(1)}, u32[]{:S(2)}, u32[]{:S(2)}) collective-permute-start(bf16[64,1024]{1,0:T(8,128)(2,1)} %get-tuple-element.211), channel_id=1, source_target_pairs={{0,2},{1,3},{2,0},{3,1},{4,6},{5,7},{6,4},{7,5},{8,10},{9,11},{10,... | collective-permute-start | bytes 393224 | tf_op jit(solution)/shard_map/ppermute | solution.py:464
  87.7 12.1 %collective-permute-start.25 = (bf16[64,1024]{1,0:T(8,128)(2,1)}, bf16[64,1024]{1,0:T(8,128)(2,1)S(1)}, u32[]{:S(2)}, u32[]{:S(2)}) collective-permute-start(bf16[64,1024]{1,0:T(8,128)(2,1)} %get-tuple-element.212), channel_id=1, source_target_pairs={{0,4},{1,5},{2,6},{3,7},{4,0},{5,1},{6,2},{7,3},{8,12},{9,13},{10,... | collective-permute-start | bytes 393224 | tf_op jit(solution)/shard_map/ppermute | solution.py:464
  89.5 11.1 %collective-permute-start.26 = (bf16[64,1024]{1,0:T(8,128)(2,1)}, bf16[64,1024]{1,0:T(8,128)(2,1)S(1)}, u32[]{:S(2)}, u32[]{:S(2)}) collective-permute-start(bf16[64,1024]{1,0:T(8,128)(2,1)} %get-tuple-element.213), channel_id=1, source_target_pairs={{0,6},{1,7},{2,4},{3,5},{4,2},{5,3},{6,0},{7,1},{8,14},{9,15},{10,... | collective-permute-start | bytes 393224 | tf_op jit(solution)/shard_map/ppermute | solution.py:464
  89.8 20.7 %collective-permute-start.34 = (bf16[128,1024]{1,0:T(8,128)(2,1)S(1)}, bf16[128,1024]{1,0:T(8,128)(2,1)S(1)}, u32[]{:S(2)}, u32[]{:S(2)}) collective-permute-start(bf16[128,1024]{1,0:T(8,128)(2,1)S(1)} %get-tuple-element.235), channel_id=1, source_target_pairs={{0,8},{1,9},{2,10},{3,11},{4,12},{5,13},{6,14},{7,15},{8,0},{9,1},... | collective-permute-start | bytes 786440 | tf_op jit(solution)/shard_map/ppermute | solution.py:464
  (45 other events, 387.0 us)
